TPU v7x, 32 devices: a whole 2x2x4 slice. The times are simulated.
32 devices in a mesh: groups: 2 (over y), gz: 4 (over z), gy: 2 (over x), col: 2 (over core).
Axes of the slice: x: 2, y: 2, z: 4, core: 2. Of those that a mesh axis runs over, the one named last changes fastest.
Arguments:
- fields: float32 [4, 6, 32, 32, 256], P('groups', None, ('gz', 'col'), 'gy'), parts along dimension 0, may hold values from -6 to 6
- eps_inv: float32 [64, 32, 256], P(('groups', 'gz', 'col'), 'gy'), parts along dimension 0, may hold values from 0.0826 to 1
- row_counts: int32 [4, 8], P(('groups', 'gy')), parts along dimension 0, may hold values from 1 to 4, 16 in all within a row
- col_counts: int32 [256], P('groups'), parts along dimension 0, may hold values from 1 to 4, 256 in all
- density: float32 [32, 128], P(('groups', 'gy')), parts along dimension 0, may hold values from 0 to 1
Outputs:
- fields_out: float32 [4, 6, 32, 32, 256], P('groups', None, ('gz', 'col'), 'gy'), parts along dimension 0
- design_gradient: float32 [32, 128], P(('groups', 'gy'), ('gz', 'col')), parts along dimension 0
There are 2 independent parts, one for each index of `groups`. A program takes and returns all parts, laid end to end along the dimension named above; each array names one. Nothing has to cross between parts.
Inputs may be any that keep to these rules, and one draw needn't show every extreme that they name: `row_counts`: each row of 8 counts sums to 16, so a y-block of the field maps onto the design rows of that block. `col_counts`: the 128 counts sum to 256.
All inputs are finite; a program needn't handle non-finite values.
Results may differ from a plain program's by a relative error of at most 0.0003.
Values sent between devices are 32-bit elements; how exact they have to be, the bound alone decides.
No kernel may reach another device: no remote copies, remote signals or barrier semaphores. Data moves between devices by JAX's collectives and lax.ppermute only.
A program may use at most 64 MiB of HBM per device.

v0:
```python
import math

import jax
import jax.numpy as jnp
from jax import lax
from jax.sharding import PartitionSpec as P

STEPS = 8
FILTER_LEN = 12


courant = 0.5
omega_step = 0.7
beta_proj = 4.0
eta_proj = 0.5
eps_span = 11.1
highest = lax.Precision.HIGHEST


def from_behind(x, axis, by):
    devices = lax.axis_size(axis)
    pairs = [(i, i + by) for i in range(devices) if 0 <= i + by < devices]
    return lax.ppermute(x, axis, pairs)


def step_ahead(field, axis, plane):
    size = field.shape[axis]
    return jnp.concatenate([lax.slice_in_dim(field, 1, size, axis=axis), plane], axis=axis) - field


def step_behind(field, axis, plane):
    size = field.shape[axis]
    return field - jnp.concatenate(
        [plane, lax.slice_in_dim(field, 0, size - 1, axis=axis)], axis=axis
    )


def blank(field, axis):
    return jnp.zeros_like(lax.slice_in_dim(field, 0, 1, axis=axis))


def magnetic(state, next_z, next_y):
    ex, ey, ez, hx, hy, hz = state
    hx = hx - courant * (step_ahead(ez, 2, next_y[0]) - step_ahead(ey, 1, next_z[1]))
    hy = hy - courant * (step_ahead(ex, 1, next_z[0]) - step_ahead(ez, 3, blank(ez, 3)))
    hz = hz - courant * (step_ahead(ey, 3, blank(ey, 3)) - step_ahead(ex, 2, next_y[1]))
    return (ex, ey, ez, hx, hy, hz)


def electric(state, scale, prev_z, prev_y):
    ex, ey, ez, hx, hy, hz = state
    ex = ex + scale * (step_behind(hz, 2, prev_y[0]) - step_behind(hy, 1, prev_z[1]))
    ey = ey + scale * (step_behind(hx, 1, prev_z[0]) - step_behind(hz, 3, blank(hz, 3)))
    ez = ez + scale * (step_behind(hy, 3, blank(hy, 3)) - step_behind(hx, 2, prev_y[1]))
    return (ex, ey, ez, hx, hy, hz)


def accumulate(totals, state, step):
    angle = omega_step * (step + 1)
    electric_now = jnp.stack(state[:3], axis=1)
    return (totals[0] + electric_now * math.cos(angle), totals[1] - electric_now * math.sin(angle))


def slope_of(density):
    norm = math.tanh(beta_proj * eta_proj) + math.tanh(beta_proj * (1.0 - eta_proj))
    bent = jnp.tanh(beta_proj * (density - eta_proj))
    return beta_proj * (1.0 - bent * bent) / norm


def band_table(counts, length):
    ends = jnp.cumsum(counts)
    starts = ends - counts
    place = jnp.arange(length, dtype=jnp.int32)[:, None]
    return ((place >= starts[None, :]) & (place < ends[None, :])).astype(jnp.float32)


def phase(first, second, modulus):
    turns = first[:, None] * second[None, :] % modulus
    return turns.astype(jnp.float32) * (2.0 * math.pi / modulus)


def matmul(left, right):
    return jnp.dot(left, right, precision=highest, preferred_element_type=jnp.float32)


def column_fold(ky_all, tall):

    def fold_y(carry, pieces, start):
        count = pieces[0].shape[0]
        angle = phase(ky_all, jnp.arange(count, dtype=jnp.int32), tall)
        cos_part = jnp.cos(angle)
        sin_part = jnp.sin(angle)
        grown_re = matmul(cos_part, pieces[0]) + matmul(sin_part, pieces[1])
        grown_im = matmul(cos_part, pieces[1]) - matmul(sin_part, pieces[0])
        return (grown_re, grown_im)

    return fold_y


def filtered_back(rows_re, rows_im, response, back_angle, tall):
    kept_re = rows_re * response
    kept_im = rows_im * response
    back_re = (matmul(jnp.cos(back_angle), kept_re) - matmul(jnp.sin(back_angle), kept_im)) / tall
    back_im = (matmul(jnp.cos(back_angle), kept_im) + matmul(jnp.sin(back_angle), kept_re)) / tall
    return (back_re, back_im)


def inverse_part(back_re, back_im, kx_mine, design_cols, count):
    angle = phase(jnp.arange(count, dtype=jnp.int32), kx_mine, design_cols)
    return (matmul(jnp.cos(angle), back_re.T) - matmul(jnp.sin(angle), back_im.T)) / design_cols


def body(fields, eps_inv, row_counts, col_counts, density):
    depth_z, rows_y, cols_x = eps_inv.shape
    state = tuple((fields[:, c] for c in range(6)))
    empty = jnp.zeros((2, 3, depth_z, rows_y, cols_x), jnp.float32)
    totals = (empty, empty)
    scale = courant * eps_inv
    for step in range(STEPS):
        ex, ey, ez = state[:3]
        upper_z = from_behind(jnp.stack([ex[:, 0:1], ey[:, 0:1]]), ("gz", "col"), -1)
        upper_y = from_behind(jnp.stack([ez[:, :, 0:1], ex[:, :, 0:1]]), "gy", -1)
        state = magnetic(state, (upper_z[0], upper_z[1]), (upper_y[0], upper_y[1]))
        hx, hy, hz = state[3:]
        lower_z = from_behind(jnp.stack([hx[:, -1:], hy[:, -1:]]), ("gz", "col"), 1)
        lower_y = from_behind(jnp.stack([hz[:, :, -1:], hx[:, :, -1:]]), "gy", 1)
        state = electric(state, scale, (lower_z[0], lower_z[1]), (lower_y[0], lower_y[1]))
        totals = accumulate(totals, state, step)
    fields_out = jnp.stack(state, axis=1)
    product = jnp.sum(totals[0][0] * totals[0][1] - totals[1][0] * totals[1][1], axis=0)
    layer_start = depth_z * lax.axis_size(("gz", "col")) // 2 - depth_z - depth_z // 2
    layer_depth = 3 * depth_z
    z_here = lax.axis_index(("gz", "col")) * depth_z + jnp.arange(depth_z, dtype=jnp.int32)
    in_layer = ((z_here >= layer_start) & (z_here < layer_start + layer_depth)).astype(jnp.float32)
    column_sum = jnp.sum(product * in_layer[:, None, None], axis=0)
    band = rows_y // 2
    design_cols = cols_x // 2
    row_table = band_table(row_counts[0], rows_y)
    col_table = band_table(col_counts, cols_x)
    partial_value = matmul(row_table.T, matmul(column_sum, col_table)) * (
        eps_span / (STEPS * layer_depth)
    )
    slope = slope_of(density)
    owners = lax.axis_size(("gz", "col"))
    mine = lax.axis_index(("gz", "col"))
    width = design_cols // owners
    tall = band * lax.axis_size("gy")
    ky_all = jnp.arange(tall, dtype=jnp.int32)
    y_mine = lax.axis_index("gy") * band + jnp.arange(band, dtype=jnp.int32)
    wave_y = jnp.sin(math.pi * ky_all.astype(jnp.float32) / tall)
    kx_mine = mine * width + jnp.arange(width, dtype=jnp.int32)
    fold_y = column_fold(ky_all, tall)
    start_rows = jnp.zeros((tall, width), jnp.float32)
    wave_x = jnp.sin(math.pi * kx_mine.astype(jnp.float32) / design_cols)
    response = 1.0 / (
        1.0 + FILTER_LEN**2 * (4.0 * wave_y[:, None] ** 2 + 4.0 * wave_x[None, :] ** 2)
    )
    back_angle = phase(y_mine, ky_all, tall)
    sens = lax.psum_scatter(partial_value, ("gz", "col"), scatter_dimension=1, tiled=True)
    weighted = sens * lax.dynamic_slice_in_dim(slope, mine * width, width, 1)
    start_spec = jnp.zeros((band, width), jnp.float32)
    piece = lax.all_gather(weighted, ("gz", "col"), axis=1, tiled=True)
    count = piece.shape[1]
    angle = phase(jnp.arange(count, dtype=jnp.int32), kx_mine, design_cols)
    spec_re = matmul(piece, jnp.cos(angle))
    spec_im = (start_spec, start_spec)[1] - matmul(piece, jnp.sin(angle))
    rows_re, rows_im = fold_y(
        (start_rows, start_rows),
        (
            lax.all_gather(spec_re, "gy", axis=0, tiled=True),
            lax.all_gather(spec_im, "gy", axis=0, tiled=True),
        ),
        jnp.int32(0),
    )
    back_re, back_im = filtered_back(rows_re, rows_im, response, back_angle, tall)
    gradient = lax.psum_scatter(
        inverse_part(back_re, back_im, kx_mine, design_cols, width * lax.axis_size(("gz", "col"))),
        ("gz", "col"),
        scatter_dimension=0,
        tiled=True,
    ).T
    return (fields_out, gradient)


def solution(mesh):
    in_specs = (
        P("groups", None, ("gz", "col"), "gy", None),
        P(("groups", "gz", "col"), "gy", None),
        P(("groups", "gy"), None),
        P("groups"),
        P(("groups", "gy"), None),
    )
    out_specs = (P("groups", None, ("gz", "col"), "gy", None), P(("groups", "gy"), ("gz", "col")))
    return jax.shard_map(body, mesh=mesh, in_specs=in_specs, out_specs=out_specs, check_vma=False)
```

profile of v0, /device:TPU:0, one launch (start us, length us, event | category | flops | bytes accessed | tf_op | source)
XLA Modules:
  0.0 238.0 jit_solution(8619174922094549900)
XLA Ops:
  7.2 1.3 fusion.245
  8.6 1.3 collective-permute-start.1
  10.0 1.3 collective-permute-start
  11.5 0.6 copy-done.6
  12.6 0.7 copy-done.5
  13.6 2.3 collective-permute-done
  16.2 2.6 %collective-permute-start.2 = (f32[2,2,4,1,256]{4,1,2,3,0:T(2,128)S(1)}, f32[2,2,4,1,256]{4,1,2,3,0:T(2,128)S(1)}, u32[]{:S(2)}, u32[]{:S(2)}) collective-permute-start(f32[2,2,4,1,256]{4,1,2,3,0:T(2,128)S(1)} %pad_maximum_fusion.25), channel_id=1, source_target_pairs={{0,2},{1,3},{4,6},{5,7},{8,10},{9,11},{12,14},{13,15},{16,18},{17,... | collective-permute-start | bytes 49160 | tf_op jit(solution)/shard_map/ppermute | solution.py:23
  18.9 2.8 %collective-permute-start.3 = (f32[2,2,1,16,256]{4,3,1,2,0:T(8,128)S(1)}, f32[2,2,1,16,256]{4,3,1,2,0:T(8,128)S(1)}, u32[]{:S(2)}, u32[]{:S(2)}) collective-permute-start(f32[2,2,1,16,256]{4,3,1,2,0:T(8,128)S(1)} %pad_maximum_fusion.9), channel_id=1, source_target_pairs={{0,1},{1,4},{4,5},{5,8},{8,9},{9,12},{12,13},{2,3},{3,6},{6,7},{7,... | collective-permute-start | bytes 196616 | tf_op jit(solution)/shard_map/ppermute | solution.py:23
  21.7 0.8 collective-permute-done.3
  22.8 0.9 bitcast_add_fusion
  23.8 1.3 collective-permute-start.4
  25.2 1.3 collective-permute-start.5
  26.5 2.9 %collective-permute-done.4 = f32[2,2,4,1,256]{4,1,2,3,0:T(2,128)S(1)} collective-permute-done((f32[2,2,4,1,256]{4,1,2,3,0:T(2,128)S(1)}, f32[2,2,4,1,256]{4,1,2,3,0:T(2,128)S(1)}, u32[]{:S(2)}, u32[]{:S(2)}) %collective-permute-start.4) | collective-permute-done | bytes 16416 | tf_op jit(solution)/shard_map/ppermute | solution.py:23
  29.4 1.5 collective-permute-done.5
  31.2 4.3 %collective-permute-start.6 = (f32[2,2,4,1,256]{4,1,2,3,0:T(2,128)S(1)}, f32[2,2,4,1,256]{4,1,2,3,0:T(2,128)S(1)}, u32[]{:S(2)}, u32[]{:S(2)}) collective-permute-start(f32[2,2,4,1,256]{4,1,2,3,0:T(2,128)S(1)} %pad_maximum_fusion.27), channel_id=1, source_target_pairs={{0,2},{1,3},{4,6},{5,7},{8,10},{9,11},{12,14},{13,15},{16,18},{17,... | collective-permute-start | bytes 49160 | tf_op jit(solution)/shard_map/ppermute | solution.py:23
  35.5 5.5 %collective-permute-start.7 = (f32[2,2,1,16,256]{4,3,1,2,0:T(8,128)S(1)}, f32[2,2,1,16,256]{4,3,1,2,0:T(8,128)S(1)}, u32[]{:S(2)}, u32[]{:S(2)}) collective-permute-start(f32[2,2,1,16,256]{4,3,1,2,0:T(8,128)S(1)} %pad_maximum_fusion.11), channel_id=1, source_target_pairs={{0,1},{1,4},{4,5},{5,8},{8,9},{9,12},{12,13},{2,3},{3,6},{6,7},{7,... | collective-permute-start | bytes 196616 | tf_op jit(solution)/shard_map/ppermute | solution.py:23
  41.1 0.8 collective-permute-done.7
  42.2 1.3 collective-permute-start.8
  43.7 1.3 collective-permute-start.9
  45.0 2.9 %collective-permute-done.8 = f32[2,2,4,1,256]{4,1,2,3,0:T(2,128)S(1)} collective-permute-done((f32[2,2,4,1,256]{4,1,2,3,0:T(2,128)S(1)}, f32[2,2,4,1,256]{4,1,2,3,0:T(2,128)S(1)}, u32[]{:S(2)}, u32[]{:S(2)}) %collective-permute-start.8) | collective-permute-done | bytes 16416 | tf_op jit(solution)/shard_map/ppermute | solution.py:23
  48.2 3.5 %collective-permute-start.10 = (f32[2,2,4,1,256]{4,1,2,3,0:T(2,128)S(1)}, f32[2,2,4,1,256]{4,1,2,3,0:T(2,128)S(1)}, u32[]{:S(2)}, u32[]{:S(2)}) collective-permute-start(f32[2,2,4,1,256]{4,1,2,3,0:T(2,128)S(1)} %pad_maximum_fusion.29), channel_id=1, source_target_pairs={{0,2},{1,3},{4,6},{5,7},{8,10},{9,11},{12,14},{13,15},{16,18},{17,... | collective-permute-start | bytes 49160 | tf_op jit(solution)/shard_map/ppermute | solution.py:23
  51.7 5.4 %collective-permute-start.11 = (f32[2,2,1,16,256]{4,3,1,2,0:T(8,128)S(1)}, f32[2,2,1,16,256]{4,3,1,2,0:T(8,128)S(1)}, u32[]{:S(2)}, u32[]{:S(2)}) collective-permute-start(f32[2,2,1,16,256]{4,3,1,2,0:T(8,128)S(1)} %pad_maximum_fusion.13), channel_id=1, source_target_pairs={{0,1},{1,4},{4,5},{5,8},{8,9},{9,12},{12,13},{2,3},{3,6},{6,7},{7,... | collective-permute-start | bytes 196616 | tf_op jit(solution)/shard_map/ppermute | solution.py:23
  57.2 0.8 collective-permute-done.11
  58.3 1.3 collective-permute-start.12
  59.8 1.3 collective-permute-start.13
  61.1 2.9 %collective-permute-done.12 = f32[2,2,4,1,256]{4,1,2,3,0:T(2,128)S(1)} collective-permute-done((f32[2,2,4,1,256]{4,1,2,3,0:T(2,128)S(1)}, f32[2,2,4,1,256]{4,1,2,3,0:T(2,128)S(1)}, u32[]{:S(2)}, u32[]{:S(2)}) %collective-permute-start.12) | collective-permute-done | bytes 16416 | tf_op jit(solution)/shard_map/ppermute | solution.py:23
  64.3 3.5 %collective-permute-start.14 = (f32[2,2,4,1,256]{4,1,2,3,0:T(2,128)S(1)}, f32[2,2,4,1,256]{4,1,2,3,0:T(2,128)S(1)}, u32[]{:S(2)}, u32[]{:S(2)}) collective-permute-start(f32[2,2,4,1,256]{4,1,2,3,0:T(2,128)S(1)} %pad_maximum_fusion.31), channel_id=1, source_target_pairs={{0,2},{1,3},{4,6},{5,7},{8,10},{9,11},{12,14},{13,15},{16,18},{17,... | collective-permute-start | bytes 49160 | tf_op jit(solution)/shard_map/ppermute | solution.py:23
  67.8 5.4 %collective-permute-start.15 = (f32[2,2,1,16,256]{4,3,1,2,0:T(8,128)S(1)}, f32[2,2,1,16,256]{4,3,1,2,0:T(8,128)S(1)}, u32[]{:S(2)}, u32[]{:S(2)}) collective-permute-start(f32[2,2,1,16,256]{4,3,1,2,0:T(8,128)S(1)} %pad_maximum_fusion.15), channel_id=1, source_target_pairs={{0,1},{1,4},{4,5},{5,8},{8,9},{9,12},{12,13},{2,3},{3,6},{6,7},{7,... | collective-permute-start | bytes 196616 | tf_op jit(solution)/shard_map/ppermute | solution.py:23
  73.2 0.8 collective-permute-done.15
  74.4 1.3 collective-permute-start.16
  75.9 1.3 collective-permute-start.17
  77.2 2.9 %collective-permute-done.16 = f32[2,2,4,1,256]{4,1,2,3,0:T(2,128)S(1)} collective-permute-done((f32[2,2,4,1,256]{4,1,2,3,0:T(2,128)S(1)}, f32[2,2,4,1,256]{4,1,2,3,0:T(2,128)S(1)}, u32[]{:S(2)}, u32[]{:S(2)}) %collective-permute-start.16) | collective-permute-done | bytes 16416 | tf_op jit(solution)/shard_map/ppermute | solution.py:23
  80.4 3.5 %collective-permute-start.18 = (f32[2,2,4,1,256]{4,1,2,3,0:T(2,128)S(1)}, f32[2,2,4,1,256]{4,1,2,3,0:T(2,128)S(1)}, u32[]{:S(2)}, u32[]{:S(2)}) collective-permute-start(f32[2,2,4,1,256]{4,1,2,3,0:T(2,128)S(1)} %pad_maximum_fusion.33), channel_id=1, source_target_pairs={{0,2},{1,3},{4,6},{5,7},{8,10},{9,11},{12,14},{13,15},{16,18},{17,... | collective-permute-start | bytes 49160 | tf_op jit(solution)/shard_map/ppermute | solution.py:23
  83.9 5.4 %collective-permute-start.19 = (f32[2,2,1,16,256]{4,3,1,2,0:T(8,128)S(1)}, f32[2,2,1,16,256]{4,3,1,2,0:T(8,128)S(1)}, u32[]{:S(2)}, u32[]{:S(2)}) collective-permute-start(f32[2,2,1,16,256]{4,3,1,2,0:T(8,128)S(1)} %pad_maximum_fusion.17), channel_id=1, source_target_pairs={{0,1},{1,4},{4,5},{5,8},{8,9},{9,12},{12,13},{2,3},{3,6},{6,7},{7,... | collective-permute-start | bytes 196616 | tf_op jit(solution)/shard_map/ppermute | solution.py:23
  89.3 0.8 collective-permute-done.19
  90.5 1.3 collective-permute-start.20
  92.0 1.3 collective-permute-start.21
  93.3 2.9 %collective-permute-done.20 = f32[2,2,4,1,256]{4,1,2,3,0:T(2,128)S(1)} collective-permute-done((f32[2,2,4,1,256]{4,1,2,3,0:T(2,128)S(1)}, f32[2,2,4,1,256]{4,1,2,3,0:T(2,128)S(1)}, u32[]{:S(2)}, u32[]{:S(2)}) %collective-permute-start.20) | collective-permute-done | bytes 16416 | tf_op jit(solution)/shard_map/ppermute | solution.py:23
  96.5 3.5 %collective-permute-start.22 = (f32[2,2,4,1,256]{4,1,2,3,0:T(2,128)S(1)}, f32[2,2,4,1,256]{4,1,2,3,0:T(2,128)S(1)}, u32[]{:S(2)}, u32[]{:S(2)}) collective-permute-start(f32[2,2,4,1,256]{4,1,2,3,0:T(2,128)S(1)} %pad_maximum_fusion.35), channel_id=1, source_target_pairs={{0,2},{1,3},{4,6},{5,7},{8,10},{9,11},{12,14},{13,15},{16,18},{17,... | collective-permute-start | bytes 49160 | tf_op jit(solution)/shard_map/ppermute | solution.py:23
  100.0 5.4 %collective-permute-start.23 = (f32[2,2,1,16,256]{4,3,1,2,0:T(8,128)S(1)}, f32[2,2,1,16,256]{4,3,1,2,0:T(8,128)S(1)}, u32[]{:S(2)}, u32[]{:S(2)}) collective-permute-start(f32[2,2,1,16,256]{4,3,1,2,0:T(8,128)S(1)} %pad_maximum_fusion.19), channel_id=1, source_target_pairs={{0,1},{1,4},{4,5},{5,8},{8,9},{9,12},{12,13},{2,3},{3,6},{6,7},{7,... | collective-permute-start | bytes 196616 | tf_op jit(solution)/shard_map/ppermute | solution.py:23
  105.4 0.8 collective-permute-done.23
  106.6 1.3 collective-permute-start.24
  108.1 1.3 collective-permute-start.25
  109.4 2.9 %collective-permute-done.24 = f32[2,2,4,1,256]{4,1,2,3,0:T(2,128)S(1)} collective-permute-done((f32[2,2,4,1,256]{4,1,2,3,0:T(2,128)S(1)}, f32[2,2,4,1,256]{4,1,2,3,0:T(2,128)S(1)}, u32[]{:S(2)}, u32[]{:S(2)}) %collective-permute-start.24) | collective-permute-done | bytes 16416 | tf_op jit(solution)/shard_map/ppermute | solution.py:23
  112.5 3.5 %collective-permute-start.26 = (f32[2,2,4,1,256]{4,1,2,3,0:T(2,128)S(1)}, f32[2,2,4,1,256]{4,1,2,3,0:T(2,128)S(1)}, u32[]{:S(2)}, u32[]{:S(2)}) collective-permute-start(f32[2,2,4,1,256]{4,1,2,3,0:T(2,128)S(1)} %pad_maximum_fusion.37), channel_id=1, source_target_pairs={{0,2},{1,3},{4,6},{5,7},{8,10},{9,11},{12,14},{13,15},{16,18},{17,... | collective-permute-start | bytes 49160 | tf_op jit(solution)/shard_map/ppermute | solution.py:23
  116.1 5.4 %collective-permute-start.27 = (f32[2,2,1,16,256]{4,3,1,2,0:T(8,128)S(1)}, f32[2,2,1,16,256]{4,3,1,2,0:T(8,128)S(1)}, u32[]{:S(2)}, u32[]{:S(2)}) collective-permute-start(f32[2,2,1,16,256]{4,3,1,2,0:T(8,128)S(1)} %pad_maximum_fusion.21), channel_id=1, source_target_pairs={{0,1},{1,4},{4,5},{5,8},{8,9},{9,12},{12,13},{2,3},{3,6},{6,7},{7,... | collective-permute-start | bytes 196616 | tf_op jit(solution)/shard_map/ppermute | solution.py:23
  121.5 0.8 collective-permute-done.27
  122.7 1.3 collective-permute-start.28
  124.2 1.3 collective-permute-start.29
  125.5 2.9 %collective-permute-done.28 = f32[2,2,4,1,256]{4,1,2,3,0:T(2,128)S(1)} collective-permute-done((f32[2,2,4,1,256]{4,1,2,3,0:T(2,128)S(1)}, f32[2,2,4,1,256]{4,1,2,3,0:T(2,128)S(1)}, u32[]{:S(2)}, u32[]{:S(2)}) %collective-permute-start.28) | collective-permute-done | bytes 16416 | tf_op jit(solution)/shard_map/ppermute | solution.py:23
  128.7 3.5 %collective-permute-start.30 = (f32[2,2,4,1,256]{4,1,2,3,0:T(2,128)S(1)}, f32[2,2,4,1,256]{4,1,2,3,0:T(2,128)S(1)}, u32[]{:S(2)}, u32[]{:S(2)}) collective-permute-start(f32[2,2,4,1,256]{4,1,2,3,0:T(2,128)S(1)} %pad_maximum_fusion.39), channel_id=1, source_target_pairs={{0,2},{1,3},{4,6},{5,7},{8,10},{9,11},{12,14},{13,15},{16,18},{17,... | collective-permute-start | bytes 49160 | tf_op jit(solution)/shard_map/ppermute | solution.py:23
  132.2 5.4 %collective-permute-start.31 = (f32[2,2,1,16,256]{4,3,1,2,0:T(8,128)S(1)}, f32[2,2,1,16,256]{4,3,1,2,0:T(8,128)S(1)}, u32[]{:S(2)}, u32[]{:S(2)}) collective-permute-start(f32[2,2,1,16,256]{4,3,1,2,0:T(8,128)S(1)} %pad_maximum_fusion.23), channel_id=1, source_target_pairs={{0,1},{1,4},{4,5},{5,8},{8,9},{9,12},{12,13},{2,3},{3,6},{6,7},{7,... | collective-permute-start | bytes 196616 | tf_op jit(solution)/shard_map/ppermute | solution.py:23
  137.7 0.8 collective-permute-done.31
  138.6 0.9 copy-done.1
  141.0 0.7 copy.498
  141.9 31.7 %reduce-scatter.7.cloned.1.call-done = f32[16,8]{1,0:T(8,128)} async-done(((f32[128,8]{1,0:T(8,128)}), f32[16,8]{1,0:T(8,128)}) %reduce-scatter.7.cloned.1.call-update) | async-done | bytes 528
  173.6 0.8 copy.499
  174.4 14.0 %all-gather = f32[8,16,8]{1,2,0:T(8,128)S(1)} all-gather(f32[1,16,8]{1,2,0:T(8,128)S(1)} %multiply_bitcast_fusion), channel_id=1, replica_groups=mesh['groups'=2,'gz'=4,'gy'=2,'col'=2] {'gz','col'}, dimensions={0}, use_global_device_ids=true | all-gather | bytes 4608 | tf_op jit(solution)/shard_map/all_gather | solution.py:162
  189.4 4.4 %all_gather.11 = f32[16,16]{1,0:T(8,128)S(1)} all-gather(f32[8,16]{1,0:T(8,128)S(1)} %convolution_subtract_fusion.3), channel_id=1, replica_groups=mesh['groups'=2,'gz'=4,'gy'=2,'col'=2] {'gy'}, dimensions={0}, use_global_device_ids=true | all-gather | bytes 1536 | tf_op jit(solution)/shard_map/all_gather | solution.py:171
  193.9 4.3 %all_gather.10 = f32[16,16]{1,0:T(8,128)S(1)} all-gather(f32[8,16]{1,0:T(8,128)S(1)} %fusion.158), channel_id=1, replica_groups=mesh['groups'=2,'gz'=4,'gy'=2,'col'=2] {'gy'}, dimensions={0}, use_global_device_ids=true | all-gather | bytes 1536 | tf_op jit(solution)/shard_map/all_gather | solution.py:170
  199.8 0.5 fusion.156
  200.7 0.8 copy.500
  201.5 28.3 %reduce-scatter.9.cloned.1.call-done = f32[16,8]{1,0:T(8,128)} async-done(((f32[128,8]{1,0:T(8,128)}), f32[16,8]{1,0:T(8,128)}) %reduce-scatter.9.cloned.1.call-update) | async-done | bytes 528
  229.8 1.4 copy.501
  (338 shorter events, 11.2 us)
Async XLA Ops:
  7.2 166.4 %reduce-scatter.7.cloned.1.call-start = ((), (), s32[]{:S(2)}) async-start(), calls=%async_computation.2 | async-start | bytes 73728
  8.6 7.4 %collective-permute-start.1 = (f32[2,2,1,16,256]{4,3,1,2,0:T(8,128)S(1)}, f32[2,2,1,16,256]{4,3,1,2,0:T(8,128)S(1)}, u32[]{:S(2)}, u32[]{:S(2)}) collective-permute-start(f32[2,2,1,16,256]{4,3,1,2,0:T(8,128)S(1)} %pad_maximum_fusion.8), channel_id=1, source_target_pairs={{1,0},{4,1},{5,4},{8,5},{9,8},{12,9},{13,12},{3,2},{6,3},{7,6},{10... | collective-permute-start | bytes 196616 | tf_op jit(solution)/shard_map/ppermute | solution.py:23
  9.9 1.5 copy-start.2
  10.0 5.9 %collective-permute-start = (f32[2,2,4,1,256]{4,1,2,3,0:T(2,128)S(1)}, f32[2,2,4,1,256]{4,1,2,3,0:T(2,128)S(1)}, u32[]{:S(2)}, u32[]{:S(2)}) collective-permute-start(f32[2,2,4,1,256]{4,1,2,3,0:T(2,128)S(1)} %pad_maximum_fusion.24), channel_id=1, source_target_pairs={{2,0},{3,1},{6,4},{7,5},{10,8},{11,9},{14,12},{15,13},{18,16},{19,... | collective-permute-start | bytes 49160 | tf_op jit(solution)/shard_map/ppermute | solution.py:23
  11.4 0.7 copy-start.6
  11.4 0.8 copy-start.4
  12.5 0.7 copy-start.5
  16.2 5.4 %collective-permute-start.2 = (f32[2,2,4,1,256]{4,1,2,3,0:T(2,128)S(1)}, f32[2,2,4,1,256]{4,1,2,3,0:T(2,128)S(1)}, u32[]{:S(2)}, u32[]{:S(2)}) collective-permute-start(f32[2,2,4,1,256]{4,1,2,3,0:T(2,128)S(1)} %pad_maximum_fusion.25), channel_id=1, source_target_pairs={{0,2},{1,3},{4,6},{5,7},{8,10},{9,11},{12,14},{13,15},{16,18},{17,... | collective-permute-start | bytes 49160 | tf_op jit(solution)/shard_map/ppermute | solution.py:23
  18.9 3.6 %collective-permute-start.3 = (f32[2,2,1,16,256]{4,3,1,2,0:T(8,128)S(1)}, f32[2,2,1,16,256]{4,3,1,2,0:T(8,128)S(1)}, u32[]{:S(2)}, u32[]{:S(2)}) collective-permute-start(f32[2,2,1,16,256]{4,3,1,2,0:T(8,128)S(1)} %pad_maximum_fusion.9), channel_id=1, source_target_pairs={{0,1},{1,4},{4,5},{5,8},{8,9},{9,12},{12,13},{2,3},{3,6},{6,7},{7,... | collective-permute-start | bytes 196616 | tf_op jit(solution)/shard_map/ppermute | solution.py:23
  23.8 5.6 %collective-permute-start.4 = (f32[2,2,4,1,256]{4,1,2,3,0:T(2,128)S(1)}, f32[2,2,4,1,256]{4,1,2,3,0:T(2,128)S(1)}, u32[]{:S(2)}, u32[]{:S(2)}) collective-permute-start(f32[2,2,4,1,256]{4,1,2,3,0:T(2,128)S(1)} %pad_maximum_fusion.26), channel_id=1, source_target_pairs={{2,0},{3,1},{6,4},{7,5},{10,8},{11,9},{14,12},{15,13},{18,16},{19,... | collective-permute-start | bytes 49160 | tf_op jit(solution)/shard_map/ppermute | solution.py:23
  25.2 5.7 %collective-permute-start.5 = (f32[2,2,1,16,256]{4,3,1,2,0:T(8,128)S(1)}, f32[2,2,1,16,256]{4,3,1,2,0:T(8,128)S(1)}, u32[]{:S(2)}, u32[]{:S(2)}) collective-permute-start(f32[2,2,1,16,256]{4,3,1,2,0:T(8,128)S(1)} %pad_maximum_fusion.10), channel_id=1, source_target_pairs={{1,0},{4,1},{5,4},{8,5},{9,8},{12,9},{13,12},{3,2},{6,3},{7,6},{10... | collective-permute-start | bytes 196616 | tf_op jit(solution)/shard_map/ppermute | solution.py:23
  31.2 9.8 %collective-permute-start.6 = (f32[2,2,4,1,256]{4,1,2,3,0:T(2,128)S(1)}, f32[2,2,4,1,256]{4,1,2,3,0:T(2,128)S(1)}, u32[]{:S(2)}, u32[]{:S(2)}) collective-permute-start(f32[2,2,4,1,256]{4,1,2,3,0:T(2,128)S(1)} %pad_maximum_fusion.27), channel_id=1, source_target_pairs={{0,2},{1,3},{4,6},{5,7},{8,10},{9,11},{12,14},{13,15},{16,18},{17,... | collective-permute-start | bytes 49160 | tf_op jit(solution)/shard_map/ppermute | solution.py:23
  35.5 6.4 %collective-permute-start.7 = (f32[2,2,1,16,256]{4,3,1,2,0:T(8,128)S(1)}, f32[2,2,1,16,256]{4,3,1,2,0:T(8,128)S(1)}, u32[]{:S(2)}, u32[]{:S(2)}) collective-permute-start(f32[2,2,1,16,256]{4,3,1,2,0:T(8,128)S(1)} %pad_maximum_fusion.11), channel_id=1, source_target_pairs={{0,1},{1,4},{4,5},{5,8},{8,9},{9,12},{12,13},{2,3},{3,6},{6,7},{7,... | collective-permute-start | bytes 196616 | tf_op jit(solution)/shard_map/ppermute | solution.py:23
  42.2 5.6 %collective-permute-start.8 = (f32[2,2,4,1,256]{4,1,2,3,0:T(2,128)S(1)}, f32[2,2,4,1,256]{4,1,2,3,0:T(2,128)S(1)}, u32[]{:S(2)}, u32[]{:S(2)}) collective-permute-start(f32[2,2,4,1,256]{4,1,2,3,0:T(2,128)S(1)} %pad_maximum_fusion.28), channel_id=1, source_target_pairs={{2,0},{3,1},{6,4},{7,5},{10,8},{11,9},{14,12},{15,13},{18,16},{19,... | collective-permute-start | bytes 49160 | tf_op jit(solution)/shard_map/ppermute | solution.py:23
  43.7 4.2 %collective-permute-start.9 = (f32[2,2,1,16,256]{4,3,1,2,0:T(8,128)S(1)}, f32[2,2,1,16,256]{4,3,1,2,0:T(8,128)S(1)}, u32[]{:S(2)}, u32[]{:S(2)}) collective-permute-start(f32[2,2,1,16,256]{4,3,1,2,0:T(8,128)S(1)} %pad_maximum_fusion.12), channel_id=1, source_target_pairs={{1,0},{4,1},{5,4},{8,5},{9,8},{12,9},{13,12},{3,2},{6,3},{7,6},{10... | collective-permute-start | bytes 196616 | tf_op jit(solution)/shard_map/ppermute | solution.py:23
  48.2 8.9 %collective-permute-start.10 = (f32[2,2,4,1,256]{4,1,2,3,0:T(2,128)S(1)}, f32[2,2,4,1,256]{4,1,2,3,0:T(2,128)S(1)}, u32[]{:S(2)}, u32[]{:S(2)}) collective-permute-start(f32[2,2,4,1,256]{4,1,2,3,0:T(2,128)S(1)} %pad_maximum_fusion.29), channel_id=1, source_target_pairs={{0,2},{1,3},{4,6},{5,7},{8,10},{9,11},{12,14},{13,15},{16,18},{17,... | collective-permute-start | bytes 49160 | tf_op jit(solution)/shard_map/ppermute | solution.py:23
  51.7 6.2 %collective-permute-start.11 = (f32[2,2,1,16,256]{4,3,1,2,0:T(8,128)S(1)}, f32[2,2,1,16,256]{4,3,1,2,0:T(8,128)S(1)}, u32[]{:S(2)}, u32[]{:S(2)}) collective-permute-start(f32[2,2,1,16,256]{4,3,1,2,0:T(8,128)S(1)} %pad_maximum_fusion.13), channel_id=1, source_target_pairs={{0,1},{1,4},{4,5},{5,8},{8,9},{9,12},{12,13},{2,3},{3,6},{6,7},{7,... | collective-permute-start | bytes 196616 | tf_op jit(solution)/shard_map/ppermute | solution.py:23
  58.3 5.6 %collective-permute-start.12 = (f32[2,2,4,1,256]{4,1,2,3,0:T(2,128)S(1)}, f32[2,2,4,1,256]{4,1,2,3,0:T(2,128)S(1)}, u32[]{:S(2)}, u32[]{:S(2)}) collective-permute-start(f32[2,2,4,1,256]{4,1,2,3,0:T(2,128)S(1)} %pad_maximum_fusion.30), channel_id=1, source_target_pairs={{2,0},{3,1},{6,4},{7,5},{10,8},{11,9},{14,12},{15,13},{18,16},{19,... | collective-permute-start | bytes 49160 | tf_op jit(solution)/shard_map/ppermute | solution.py:23
  59.8 4.2 %collective-permute-start.13 = (f32[2,2,1,16,256]{4,3,1,2,0:T(8,128)S(1)}, f32[2,2,1,16,256]{4,3,1,2,0:T(8,128)S(1)}, u32[]{:S(2)}, u32[]{:S(2)}) collective-permute-start(f32[2,2,1,16,256]{4,3,1,2,0:T(8,128)S(1)} %pad_maximum_fusion.14), channel_id=1, source_target_pairs={{1,0},{4,1},{5,4},{8,5},{9,8},{12,9},{13,12},{3,2},{6,3},{7,6},{10... | collective-permute-start | bytes 196616 | tf_op jit(solution)/shard_map/ppermute | solution.py:23
  64.3 8.9 %collective-permute-start.14 = (f32[2,2,4,1,256]{4,1,2,3,0:T(2,128)S(1)}, f32[2,2,4,1,256]{4,1,2,3,0:T(2,128)S(1)}, u32[]{:S(2)}, u32[]{:S(2)}) collective-permute-start(f32[2,2,4,1,256]{4,1,2,3,0:T(2,128)S(1)} %pad_maximum_fusion.31), channel_id=1, source_target_pairs={{0,2},{1,3},{4,6},{5,7},{8,10},{9,11},{12,14},{13,15},{16,18},{17,... | collective-permute-start | bytes 49160 | tf_op jit(solution)/shard_map/ppermute | solution.py:23
  67.8 6.2 %collective-permute-start.15 = (f32[2,2,1,16,256]{4,3,1,2,0:T(8,128)S(1)}, f32[2,2,1,16,256]{4,3,1,2,0:T(8,128)S(1)}, u32[]{:S(2)}, u32[]{:S(2)}) collective-permute-start(f32[2,2,1,16,256]{4,3,1,2,0:T(8,128)S(1)} %pad_maximum_fusion.15), channel_id=1, source_target_pairs={{0,1},{1,4},{4,5},{5,8},{8,9},{9,12},{12,13},{2,3},{3,6},{6,7},{7,... | collective-permute-start | bytes 196616 | tf_op jit(solution)/shard_map/ppermute | solution.py:23
  74.4 5.6 %collective-permute-start.16 = (f32[2,2,4,1,256]{4,1,2,3,0:T(2,128)S(1)}, f32[2,2,4,1,256]{4,1,2,3,0:T(2,128)S(1)}, u32[]{:S(2)}, u32[]{:S(2)}) collective-permute-start(f32[2,2,4,1,256]{4,1,2,3,0:T(2,128)S(1)} %pad_maximum_fusion.32), channel_id=1, source_target_pairs={{2,0},{3,1},{6,4},{7,5},{10,8},{11,9},{14,12},{15,13},{18,16},{19,... | collective-permute-start | bytes 49160 | tf_op jit(solution)/shard_map/ppermute | solution.py:23
  75.9 4.2 %collective-permute-start.17 = (f32[2,2,1,16,256]{4,3,1,2,0:T(8,128)S(1)}, f32[2,2,1,16,256]{4,3,1,2,0:T(8,128)S(1)}, u32[]{:S(2)}, u32[]{:S(2)}) collective-permute-start(f32[2,2,1,16,256]{4,3,1,2,0:T(8,128)S(1)} %pad_maximum_fusion.16), channel_id=1, source_target_pairs={{1,0},{4,1},{5,4},{8,5},{9,8},{12,9},{13,12},{3,2},{6,3},{7,6},{10... | collective-permute-start | bytes 196616 | tf_op jit(solution)/shard_map/ppermute | solution.py:23
  80.4 8.9 %collective-permute-start.18 = (f32[2,2,4,1,256]{4,1,2,3,0:T(2,128)S(1)}, f32[2,2,4,1,256]{4,1,2,3,0:T(2,128)S(1)}, u32[]{:S(2)}, u32[]{:S(2)}) collective-permute-start(f32[2,2,4,1,256]{4,1,2,3,0:T(2,128)S(1)} %pad_maximum_fusion.33), channel_id=1, source_target_pairs={{0,2},{1,3},{4,6},{5,7},{8,10},{9,11},{12,14},{13,15},{16,18},{17,... | collective-permute-start | bytes 49160 | tf_op jit(solution)/shard_map/ppermute | solution.py:23
  83.9 6.2 %collective-permute-start.19 = (f32[2,2,1,16,256]{4,3,1,2,0:T(8,128)S(1)}, f32[2,2,1,16,256]{4,3,1,2,0:T(8,128)S(1)}, u32[]{:S(2)}, u32[]{:S(2)}) collective-permute-start(f32[2,2,1,16,256]{4,3,1,2,0:T(8,128)S(1)} %pad_maximum_fusion.17), channel_id=1, source_target_pairs={{0,1},{1,4},{4,5},{5,8},{8,9},{9,12},{12,13},{2,3},{3,6},{6,7},{7,... | collective-permute-start | bytes 196616 | tf_op jit(solution)/shard_map/ppermute | solution.py:23
  90.5 5.6 %collective-permute-start.20 = (f32[2,2,4,1,256]{4,1,2,3,0:T(2,128)S(1)}, f32[2,2,4,1,256]{4,1,2,3,0:T(2,128)S(1)}, u32[]{:S(2)}, u32[]{:S(2)}) collective-permute-start(f32[2,2,4,1,256]{4,1,2,3,0:T(2,128)S(1)} %pad_maximum_fusion.34), channel_id=1, source_target_pairs={{2,0},{3,1},{6,4},{7,5},{10,8},{11,9},{14,12},{15,13},{18,16},{19,... | collective-permute-start | bytes 49160 | tf_op jit(solution)/shard_map/ppermute | solution.py:23
  92.0 4.2 %collective-permute-start.21 = (f32[2,2,1,16,256]{4,3,1,2,0:T(8,128)S(1)}, f32[2,2,1,16,256]{4,3,1,2,0:T(8,128)S(1)}, u32[]{:S(2)}, u32[]{:S(2)}) collective-permute-start(f32[2,2,1,16,256]{4,3,1,2,0:T(8,128)S(1)} %pad_maximum_fusion.18), channel_id=1, source_target_pairs={{1,0},{4,1},{5,4},{8,5},{9,8},{12,9},{13,12},{3,2},{6,3},{7,6},{10... | collective-permute-start | bytes 196616 | tf_op jit(solution)/shard_map/ppermute | solution.py:23
  96.5 8.9 %collective-permute-start.22 = (f32[2,2,4,1,256]{4,1,2,3,0:T(2,128)S(1)}, f32[2,2,4,1,256]{4,1,2,3,0:T(2,128)S(1)}, u32[]{:S(2)}, u32[]{:S(2)}) collective-permute-start(f32[2,2,4,1,256]{4,1,2,3,0:T(2,128)S(1)} %pad_maximum_fusion.35), channel_id=1, source_target_pairs={{0,2},{1,3},{4,6},{5,7},{8,10},{9,11},{12,14},{13,15},{16,18},{17,... | collective-permute-start | bytes 49160 | tf_op jit(solution)/shard_map/ppermute | solution.py:23
  100.0 6.2 %collective-permute-start.23 = (f32[2,2,1,16,256]{4,3,1,2,0:T(8,128)S(1)}, f32[2,2,1,16,256]{4,3,1,2,0:T(8,128)S(1)}, u32[]{:S(2)}, u32[]{:S(2)}) collective-permute-start(f32[2,2,1,16,256]{4,3,1,2,0:T(8,128)S(1)} %pad_maximum_fusion.19), channel_id=1, source_target_pairs={{0,1},{1,4},{4,5},{5,8},{8,9},{9,12},{12,13},{2,3},{3,6},{6,7},{7,... | collective-permute-start | bytes 196616 | tf_op jit(solution)/shard_map/ppermute | solution.py:23
  106.6 5.6 %collective-permute-start.24 = (f32[2,2,4,1,256]{4,1,2,3,0:T(2,128)S(1)}, f32[2,2,4,1,256]{4,1,2,3,0:T(2,128)S(1)}, u32[]{:S(2)}, u32[]{:S(2)}) collective-permute-start(f32[2,2,4,1,256]{4,1,2,3,0:T(2,128)S(1)} %pad_maximum_fusion.36), channel_id=1, source_target_pairs={{2,0},{3,1},{6,4},{7,5},{10,8},{11,9},{14,12},{15,13},{18,16},{19,... | collective-permute-start | bytes 49160 | tf_op jit(solution)/shard_map/ppermute | solution.py:23
  108.1 4.2 %collective-permute-start.25 = (f32[2,2,1,16,256]{4,3,1,2,0:T(8,128)S(1)}, f32[2,2,1,16,256]{4,3,1,2,0:T(8,128)S(1)}, u32[]{:S(2)}, u32[]{:S(2)}) collective-permute-start(f32[2,2,1,16,256]{4,3,1,2,0:T(8,128)S(1)} %pad_maximum_fusion.20), channel_id=1, source_target_pairs={{1,0},{4,1},{5,4},{8,5},{9,8},{12,9},{13,12},{3,2},{6,3},{7,6},{10... | collective-permute-start | bytes 196616 | tf_op jit(solution)/shard_map/ppermute | solution.py:23
  112.5 8.9 %collective-permute-start.26 = (f32[2,2,4,1,256]{4,1,2,3,0:T(2,128)S(1)}, f32[2,2,4,1,256]{4,1,2,3,0:T(2,128)S(1)}, u32[]{:S(2)}, u32[]{:S(2)}) collective-permute-start(f32[2,2,4,1,256]{4,1,2,3,0:T(2,128)S(1)} %pad_maximum_fusion.37), channel_id=1, source_target_pairs={{0,2},{1,3},{4,6},{5,7},{8,10},{9,11},{12,14},{13,15},{16,18},{17,... | collective-permute-start | bytes 49160 | tf_op jit(solution)/shard_map/ppermute | solution.py:23
  116.1 6.2 %collective-permute-start.27 = (f32[2,2,1,16,256]{4,3,1,2,0:T(8,128)S(1)}, f32[2,2,1,16,256]{4,3,1,2,0:T(8,128)S(1)}, u32[]{:S(2)}, u32[]{:S(2)}) collective-permute-start(f32[2,2,1,16,256]{4,3,1,2,0:T(8,128)S(1)} %pad_maximum_fusion.21), channel_id=1, source_target_pairs={{0,1},{1,4},{4,5},{5,8},{8,9},{9,12},{12,13},{2,3},{3,6},{6,7},{7,... | collective-permute-start | bytes 196616 | tf_op jit(solution)/shard_map/ppermute | solution.py:23
  122.7 5.6 %collective-permute-start.28 = (f32[2,2,4,1,256]{4,1,2,3,0:T(2,128)S(1)}, f32[2,2,4,1,256]{4,1,2,3,0:T(2,128)S(1)}, u32[]{:S(2)}, u32[]{:S(2)}) collective-permute-start(f32[2,2,4,1,256]{4,1,2,3,0:T(2,128)S(1)} %pad_maximum_fusion.38), channel_id=1, source_target_pairs={{2,0},{3,1},{6,4},{7,5},{10,8},{11,9},{14,12},{15,13},{18,16},{19,... | collective-permute-start | bytes 49160 | tf_op jit(solution)/shard_map/ppermute | solution.py:23
  124.2 4.2 %collective-permute-start.29 = (f32[2,2,1,16,256]{4,3,1,2,0:T(8,128)S(1)}, f32[2,2,1,16,256]{4,3,1,2,0:T(8,128)S(1)}, u32[]{:S(2)}, u32[]{:S(2)}) collective-permute-start(f32[2,2,1,16,256]{4,3,1,2,0:T(8,128)S(1)} %pad_maximum_fusion.22), channel_id=1, source_target_pairs={{1,0},{4,1},{5,4},{8,5},{9,8},{12,9},{13,12},{3,2},{6,3},{7,6},{10... | collective-permute-start | bytes 196616 | tf_op jit(solution)/shard_map/ppermute | solution.py:23
  128.6 3.7 %copy-start = (f32[2,4,16,256]{3,2,1,0:T(8,128)}, f32[2,4,16,256]{3,2,1,0:T(8,128)S(1)}, u32[]{:S(2)}) copy-start(f32[2,4,16,256]{3,2,1,0:T(8,128)S(1)} %copy_subtract_fusion) | copy-start | bytes 393220
  128.7 8.9 %collective-permute-start.30 = (f32[2,2,4,1,256]{4,1,2,3,0:T(2,128)S(1)}, f32[2,2,4,1,256]{4,1,2,3,0:T(2,128)S(1)}, u32[]{:S(2)}, u32[]{:S(2)}) collective-permute-start(f32[2,2,4,1,256]{4,1,2,3,0:T(2,128)S(1)} %pad_maximum_fusion.39), channel_id=1, source_target_pairs={{0,2},{1,3},{4,6},{5,7},{8,10},{9,11},{12,14},{13,15},{16,18},{17,... | collective-permute-start | bytes 49160 | tf_op jit(solution)/shard_map/ppermute | solution.py:23
  132.2 6.2 %collective-permute-start.31 = (f32[2,2,1,16,256]{4,3,1,2,0:T(8,128)S(1)}, f32[2,2,1,16,256]{4,3,1,2,0:T(8,128)S(1)}, u32[]{:S(2)}, u32[]{:S(2)}) collective-permute-start(f32[2,2,1,16,256]{4,3,1,2,0:T(8,128)S(1)} %pad_maximum_fusion.23), channel_id=1, source_target_pairs={{0,1},{1,4},{4,5},{5,8},{8,9},{9,12},{12,13},{2,3},{3,6},{6,7},{7,... | collective-permute-start | bytes 196616 | tf_op jit(solution)/shard_map/ppermute | solution.py:23
  138.6 0.9 copy-start.1
  138.6 1.0 slice-start
  141.8 88.0 %reduce-scatter.9.cloned.1.call-start = ((), (), s32[]{:S(2)}) async-start(), calls=%async_computation.3 | async-start | bytes 73728
  201.5 29.7 %copy-start.3 = (f32[2,6,4,16,256]{4,3,2,1,0:T(8,128)}, f32[2,6,4,16,256]{4,3,2,1,0:T(8,128)S(1)}, u32[]{:S(2)}) copy-start(f32[2,6,4,16,256]{4,3,2,1,0:T(8,128)S(1)} %bitcast_dynamic-update-slice_fusion.3) | copy-start | bytes 2359300
Sparse Core Ops, SparseCore 0:
  141.9 31.6 reduce-scatter.6
  201.6 28.1 reduce-scatter.8
where the time goes:
time: 239 us; the launch traced here: 238 us
  waiting for transfers between devices  90.5 us (38%)
  starting transfers between devices  88.9 us (37%)
  blocking collectives  22.7 us (9%)
  between operations  16.5 us (7%)
  local copies, waits for them, and re-layouts  9.64 us (4%)
  other arithmetic  6.03 us (3%)
  matrix products  3.85 us (2%)
    ppermute x32, starting transfers between devices, from_behind(): return lax.ppermute(x, axis, pairs)  88.8 us
    unnamed x4, waiting for transfers between devices  60.1 us
    ppermute x32, waiting for transfers between devices, from_behind(): return lax.ppermute(x, axis, pairs)  30.4 us
    all_gather x1, blocking collectives, body(): piece = lax.all_gather(weighted, ('gz', 'col'), axis=1, tiled=True)  14 us
    unnamed x57, local copies, waits for them, and re-layouts  6.11 us
  transfers between devices with their start and end apart: 34, of which 19 were waited for; matrix products, arithmetic and copies ran while one was open for 1% of the time, Pallas kernels for 0%

commit v1 on v0

v1 whole, which is shorter than its diff:
```python
import functools
import math

import jax
import jax.numpy as jnp
import numpy as np
from jax import lax
from jax.experimental import pallas as pl
from jax.experimental.pallas import tpu as pltpu
from jax.sharding import PartitionSpec as P

STEPS = 8
FILTER_LEN = 12

courant = 0.5
omega_step = 0.7
beta_proj = 4.0
eta_proj = 0.5
eps_span = 11.1
highest = lax.Precision.HIGHEST

PLANES = 13
Z = ("gz", "col")


def slope_of(density):
    norm = math.tanh(beta_proj * eta_proj) + math.tanh(beta_proj * (1.0 - eta_proj))
    bent = jnp.tanh(beta_proj * (density - eta_proj))
    return beta_proj * (1.0 - bent * bent) / norm


def real_basis(size):
    place = np.arange(size)
    rows, waves = [], []
    for k in range(size // 2 + 1):
        angle = 2.0 * np.pi * ((k * place) % size) / size
        edge = k == 0 or 2 * k == size
        rows.append(np.cos(angle) * math.sqrt((1.0 if edge else 2.0) / size))
        waves.append(k)
        if not edge:
            rows.append(np.sin(angle) * math.sqrt(2.0 / size))
            waves.append(k)
    return np.array(rows), np.array(waves)


def band_table(counts, place):
    ends = jnp.cumsum(counts)
    starts = ends - counts
    return ((place >= starts[None, :]) & (place < ends[None, :])).astype(jnp.float32)


def mm(left, right):
    return jnp.dot(left, right, precision=highest, preferred_element_type=jnp.float32)


def window_kernel(cfg, *refs):
    depth, rows_own, rows, sides, masked_rows = cfg
    n_blocks = 5
    it = iter(refs)
    info = next(it)
    full = [next(it) for _ in range(n_blocks)]
    halo = [[next(it) for _ in range(n_blocks)] for _ in range(sides)]
    row_table, col_table, slope, basis_x, basis_xt, basis_y, own_y, response = (next(it) for _ in range(8))
    out, share = next(it), next(it)
    st, acc, sem_full, sem_halo, sem_out = (next(it) for _ in range(5))

    halo_rows = STEPS
    core = info[0]
    row_own = pl.multiple_of(info[1], 8)
    copies = []
    for b in range(n_blocks):
        place = jnp.where(core == 0, b * depth, (n_blocks - 1 - b) * depth)
        layers = pl.ds(place, depth)
        copies.append(
            pltpu.make_async_copy(full[b], st.at[:, layers, pl.ds(row_own, rows_own), :], sem_full.at[b])
        )
        for s in range(sides):
            row_at = pl.multiple_of(info[2 + s], 8)
            copies.append(
                pltpu.make_async_copy(
                    halo[s][b], st.at[:, layers, pl.ds(row_at, halo_rows), :], sem_halo.at[s, b]
                )
            )
    for copy in copies:
        copy.start()
    acc[...] = jnp.zeros_like(acc)
    for copy in copies:
        copy.wait()

    nx = st.shape[-1]
    row_at = lax.broadcasted_iota(jnp.int32, (rows, nx), 0)
    lane_at = lax.broadcasted_iota(jnp.int32, (rows, nx), 1)
    last_row, first_row = row_at == rows - 1, row_at == 0
    last_lane, first_lane = lane_at == nx - 1, lane_at == 0
    if masked_rows:
        row_ok = (row_at >= info[6]) & (row_at < info[7])

    def y_ahead(f):
        return jnp.where(last_row, 0.0, pltpu.roll(f, rows - 1, 0))

    def y_behind(f):
        return jnp.where(first_row, 0.0, pltpu.roll(f, 1, 0))

    def x_ahead(f):
        return jnp.where(last_lane, 0.0, pltpu.roll(f, nx - 1, 1))

    def x_behind(f):
        return jnp.where(first_lane, 0.0, pltpu.roll(f, 1, 1))

    low_layer, high_layer = info[4], info[5]

    def layer(z, carry, weights):
        coef = jnp.where((z >= low_layer) & (z < high_layer), courant, 0.0)
        coef = jnp.full((rows, nx), coef, jnp.float32)
        if masked_rows:
            coef = jnp.where(row_ok, coef, 0.0)
        scale = st[12, z]
        carried = []
        for r in range(2):
            hx_p, hy_p = carry[r]
            b = 6 * r
            ex, ey, ez = st[b, z], st[b + 1, z], st[b + 2, z]
            ex_n, ey_n = st[b, z + 1], st[b + 1, z + 1]
            hx = st[b + 3, z] - coef * ((y_ahead(ez) - ez) - (ey_n - ey))
            hy = st[b + 4, z] - coef * ((ex_n - ex) - (x_ahead(ez) - ez))
            hz = st[b + 5, z] - coef * ((x_ahead(ey) - ey) - (y_ahead(ex) - ex))
            ex = ex + scale * ((hz - y_behind(hz)) - (hy - hy_p))
            ey = ey + scale * ((hx - hx_p) - (hz - x_behind(hz)))
            ez = ez + scale * ((hy - x_behind(hy)) - (hx - y_behind(hx)))
            st[b, z], st[b + 1, z], st[b + 2, z] = ex, ey, ez
            st[b + 3, z], st[b + 4, z], st[b + 5, z] = hx, hy, hz
            if weights is not None:
                own = z - 2 * depth
                for c, e in enumerate((ex, ey, ez)):
                    acc[0, 3 * r + c, own] = acc[0, 3 * r + c, own] + e * weights[0]
                    acc[1, 3 * r + c, own] = acc[1, 3 * r + c, own] - e * weights[1]
            carried.append((hx, hy))
        return tuple(carried)

    layers_all = n_blocks * depth
    for n in range(1, STEPS + 1):
        angle = omega_step * n
        weights = (math.cos(angle), math.sin(angle))
        zero = jnp.zeros((rows, nx), jnp.float32)
        carry = ((zero, zero), (zero, zero))
        carry = lax.fori_loop(n - 1, 2 * depth, lambda z, c: layer(z, c, None), carry)
        carry = lax.fori_loop(2 * depth, 3 * depth, lambda z, c: layer(z, c, weights), carry)
        lax.fori_loop(3 * depth, layers_all - n, lambda z, c: layer(z, c, None), carry)

    result = pltpu.make_async_copy(
        st.at[pl.ds(0, 12), pl.ds(2 * depth, depth), pl.ds(row_own, rows_own), :], out, sem_out
    )
    result.start()
    column_sum = jnp.zeros((rows, nx), jnp.float32)
    for own in range(depth):
        g = jnp.zeros((rows, nx), jnp.float32)
        for c in range(3):
            g = g + acc[0, c, own] * acc[0, 3 + c, own] - acc[1, c, own] * acc[1, 3 + c, own]
        in_layer = (info[8] + own >= 0) & (info[8] + own < info[9])
        column_sum = column_sum + jnp.where(in_layer, g, 0.0)
    sens = mm(row_table[...], mm(column_sum, col_table[...])) * (eps_span / (STEPS * 3 * depth))
    weighted = sens * slope[...]
    spectrum = mm(own_y[...], mm(weighted, basis_xt[...])) * response[...]
    share[...] = mm(basis_y[...], mm(spectrum, basis_x[...]))
    result.wait()


def body(fields, eps_inv, row_counts, col_counts, density):
    runs, comps, depth, rows_own, nx = fields.shape
    n_gz, n_gy = lax.axis_size("gz"), lax.axis_size("gy")
    gz, gy, core = lax.axis_index("gz"), lax.axis_index("gy"), lax.axis_index("col")
    index = gz * 2 + core
    n_z = n_gz * 2
    assert STEPS == 2 * depth and rows_own >= STEPS

    own = jnp.concatenate([fields.reshape(runs * comps, depth, rows_own, nx), (courant * eps_inv)[None]])

    def swap_core(x):
        return lax.ppermute(x, "col", [(0, 1), (1, 0)])

    def cross(x):
        pairs = []
        for c in range(n_gz - 1):
            a, b = 2 * c + 1, 2 * c + 2
            pairs += [(a, b), (b, a)]
        return lax.ppermute(x, Z, pairs)

    if n_gy == 2:
        rows = rows_own + STEPS
        row_own = gy * STEPS
        halo_at = [(1 - gy) * rows_own]
        ways = [{0: 1, 1: 0}]
        starts = [(1 - gy) * (rows_own - STEPS)]
    else:
        rows = rows_own + 2 * STEPS
        row_own = jnp.int32(STEPS)
        halo_at = [jnp.int32(0), jnp.int32(STEPS + rows_own)]
        ways = [{y: y + 1 for y in range(n_gy - 1)}, {y: y - 1 for y in range(1, n_gy)}]
        starts = [rows_own - STEPS, 0]
    sides = len(ways)

    def edge(x, s):
        return lax.dynamic_slice_in_dim(x, starts[s], STEPS, axis=2)

    def along_y(x, s):
        return lax.ppermute(x, "gy", list(ways[s].items()))

    def across(x, s):
        pairs = []
        for c in range(n_gz - 1):
            for y, to in ways[s].items():
                a, b = ((c, y, 1), (c + 1, to, 0)), ((c + 1, y, 0), (c, to, 1))
                for src, dst in (a, b):
                    pairs.append(tuple((p[0] * n_gy + p[1]) * 2 + p[2] for p in (src, dst)))
        return lax.ppermute(x, ("gz", "gy", "col"), pairs)

    sibling = swap_core(own)
    near = cross(own)
    far = cross(sibling)
    near_sib = swap_core(near)
    full = [far, near, own, sibling, near_sib]
    halos = []
    for s in range(sides):
        mine, theirs = edge(own, s), edge(sibling, s)
        y_own = along_y(mine, s)
        y_near = across(mine, s)
        y_far = across(theirs, s)
        halos.append([y_far, y_near, y_own, swap_core(y_own), swap_core(y_near)])

    layer_start = depth * n_z // 2 - depth - depth // 2
    info = [core, row_own]
    info += halo_at + [jnp.int32(0)] * (2 - sides)
    info += [2 * depth - index * depth, depth * n_z - index * depth + 2 * depth]
    info += [
        jnp.where(gy == 0, STEPS, 0) if sides == 2 else jnp.int32(0),
        jnp.where(gy == n_gy - 1, STEPS + rows_own, rows) if sides == 2 else jnp.int32(rows),
    ]
    info += [index * depth - layer_start, jnp.int32(3 * depth)]
    info = jnp.stack([jnp.asarray(v, jnp.int32) for v in info])

    band, design_cols = density.shape
    tall = band * n_gy
    place_y = jnp.arange(rows, dtype=jnp.int32)[:, None] - row_own
    row_table = band_table(row_counts[0], place_y).T
    col_table = band_table(col_counts, jnp.arange(nx, dtype=jnp.int32)[:, None])
    basis_x, wave_x = real_basis(design_cols)
    basis_y, wave_y = real_basis(tall)
    response = 1.0 / (
        1.0
        + FILTER_LEN**2
        * (
            4.0 * np.sin(math.pi * wave_y / tall)[:, None] ** 2
            + 4.0 * np.sin(math.pi * wave_x / design_cols)[None, :] ** 2
        )
    )
    const = lambda a: jnp.asarray(a, jnp.float32)
    own_y = lax.dynamic_slice_in_dim(const(basis_y), gy * band, band, 1)

    operands = [info] + full + [h for side in halos for h in side]
    operands += [row_table, col_table, slope_of(density), const(basis_x), const(basis_x.T), const(basis_y.T), own_y, const(response)]
    n_any = 5 * (1 + sides)
    anywhere = pl.BlockSpec(memory_space=pl.ANY)
    vmem = pl.BlockSpec(memory_space=pltpu.VMEM)
    fields_out, share = pl.pallas_call(
        functools.partial(window_kernel, (depth, rows_own, rows, sides, sides == 2)),
        out_shape=(
            jax.ShapeDtypeStruct((runs * comps, depth, rows_own, nx), jnp.float32),
            jax.ShapeDtypeStruct((tall, design_cols), jnp.float32),
        ),
        in_specs=[pl.BlockSpec(memory_space=pltpu.SMEM)] + [anywhere] * n_any + [vmem] * 8,
        out_specs=(anywhere, vmem),
        scratch_shapes=[
            pltpu.VMEM((PLANES, 5 * depth, rows, nx), jnp.float32),
            pltpu.VMEM((2, 6, depth, rows, nx), jnp.float32),
            pltpu.SemaphoreType.DMA((5,)),
            pltpu.SemaphoreType.DMA((sides, 5)),
            pltpu.SemaphoreType.DMA,
        ],
        compiler_params=pltpu.CompilerParams(vmem_limit_bytes=24 * 1024 * 1024),
        cost_estimate=pl.CostEstimate(flops=60_000_000, bytes_accessed=8_000_000, transcendentals=0),
    )(*operands)

    width = design_cols // n_z
    blocks = share.reshape(n_gy, band, n_gz, 2, width).transpose(2, 0, 3, 1, 4)
    blocks = blocks.reshape(n_gz * n_gy * 2, band, width)
    got = lax.all_to_all(blocks, ("gz", "gy", "col"), 0, 0)
    gradient = jnp.sum(got, axis=0)
    return fields_out.reshape(fields.shape), gradient


def solution(mesh):
    in_specs = (
        P("groups", None, ("gz", "col"), "gy", None),
        P(("groups", "gz", "col"), "gy", None),
        P(("groups", "gy"), None),
        P("groups"),
        P(("groups", "gy"), None),
    )
    out_specs = (P("groups", None, ("gz", "col"), "gy", None), P(("groups", "gy"), ("gz", "col")))
    return jax.shard_map(body, mesh=mesh, in_specs=in_specs, out_specs=out_specs, check_vma=False)
```

time: 239 us -> 81.1 us (0.34)
  waiting for transfers between devices: 90.5 us -> 0.74 us
  starting transfers between devices: 88.9 us -> 19.1 us
  Pallas kernels: 0 us -> 22.7 us
  between operations: 16.5 us -> 0.84 us
  local copies, waits for them, and re-layouts: 9.64 us -> 2.48 us
  blocking collectives: 22.7 us -> 29 us
  matrix products: 3.85 us -> 0 us
    ppermute x32 -> x9, starting transfers between devices: 88.8 us -> 19.1 us  [the longest x4 13.1 us: swap_core(): return lax.ppermute(x, 'col', [(0, 1), (1, 0)])]
    unnamed x4 -> x0, waiting for transfers between devices: 60.1 us -> none
    ppermute x32 -> x9, waiting for transfers between devices: 30.4 us -> 0.74 us  [the longest x4 0.72 us: swap_core(): return lax.ppermute(x, 'col', [(0, 1), (1, 0)])]
    all_to_all x0 -> x1, blocking collectives: none -> 29 us  [body(): got = lax.all_to_all(blocks, ('gz', 'gy', 'col'), 0, 0)]
    pallas_call x0 -> x1, Pallas kernels: none -> 22.7 us  [body(): pl.pallas_call(functools.partial(window_kernel, (depth, rows_own, rows, s...]
    all_gather x3 -> x0, blocking collectives: 22.7 us -> none  [the longest x1 14 us: body(): piece = lax.all_gather(weighted, ('gz', 'col'), axis=1, tiled=True)]
    unnamed x57 -> x24, local copies, waits for them, and re-layouts: 6.11 us -> 1.52 us
    dot_general x14 -> x0, matrix products: 3.85 us -> none  [matmul(): jnp.dot(left, right, precision=highest, preferred_element_type=jnp.float32)]
  transfers between devices with their start and end apart: 34 -> 9, of which waited for: 19 -> 1; matrix products, arithmetic and copies ran while one was open for 1% -> 3% of each run, Pallas kernels for 0% -> 0%
where the time goes in v1:
time: 81.1 us; the launch traced here: 80.7 us
  blocking collectives  29 us (36%)
  Pallas kernels  22.7 us (28%)
  starting transfers between devices  19.1 us (24%)
  other arithmetic  5.81 us (7%)
  local copies, waits for them, and re-layouts  2.48 us (3%)
  between operations  0.84 us (1%)
    all_to_all x1, blocking collectives, body(): got = lax.all_to_all(blocks, ('gz', 'gy', 'col'), 0, 0)  29 us
    pallas_call x1, Pallas kernels, body(): pl.pallas_call(functools.partial(window_kernel, (depth, rows_own, rows, s...  22.7 us
    ppermute x4, starting transfers between devices, swap_core(): return lax.ppermute(x, 'col', [(0, 1), (1, 0)])  13.1 us
    ppermute x1, starting transfers between devices, along_y(): return lax.ppermute(x, 'gy', list(ways[s].items()))  2.51 us
    ppermute x2, starting transfers between devices, across(): return lax.ppermute(x, ('gz', 'gy', 'col'), pairs)  2.11 us
    concatenate x2, other arithmetic, body(): jnp.concatenate([fields.reshape(runs * comps, depth, rows_own, nx), (cour...  2.08 us
  transfers between devices with their start and end apart: 9, of which 1 were waited for; matrix products, arithmetic and copies ran while one was open for 3% of the time, Pallas kernels for 0%

profile of v1, /device:TPU:0, one launch (start us, length us, event | category | flops | bytes accessed | tf_op | source)
XLA Modules:
  0.0 80.7 jit_solution(10234930058625571160)
XLA Ops:
  0.6 0.8 %multiply_bitcast_fusion = f32[1,4,16,256]{3,2,1,0:T(8,128)S(1)} fusion(f32[4,16,256]{2,1,0:T(8,128)} %param.11), kind=kLoop, calls=%fused_computation.8 | loop fusion | flops 16384 | bytes 131072 | tf_op jit(solution)/shard_map/broadcast_in_dim | solution.py:176
  1.5 0.0 copy-start.4
  1.5 1.3 %pad_maximum_fusion.refs_3_ = f32[13,4,16,256]{3,2,1,0:T(8,128)S(1)} fusion(f32[1,4,16,256]{3,2,1,0:T(8,128)S(1)} %multiply_bitcast_fusion, f32[12,4,16,256]{3,2,1,0:T(8,128)} %bitcast.22), kind=kLoop, calls=%fused_computation.1 | loop fusion | flops 212992 | bytes 1703936 | tf_op jit(solution)/shard_map/concatenate | solution.py:176
  2.8 0.5 collective-permute-start
  3.3 0.7 collective-permute-start.2
  4.0 0.0 copy-done.4
  4.0 0.0 copy-start.10
  4.0 0.8 fusion
  4.8 0.0 copy-start.5
  4.8 2.5 %collective-permute-start.6 = (f32[13,4,8,256]{3,2,1,0:T(8,128)}, f32[13,4,8,256]{3,2,1,0:T(8,128)}, u32[]{:S(2)}, u32[]{:S(2)}) collective-permute-start(f32[13,4,8,256]{3,2,1,0:T(8,128)} %fusion), channel_id=1, source_target_pairs={{0,2},{2,0},{1,3},{3,1},{4,6},{6,4},{5,7},{7,5},{8,10},{10,8},{9,1... | collective-permute-start | bytes 1277960 | tf_op jit(solution)/shard_map/ppermute | solution.py:206
  7.3 1.4 %collective-permute-start.5 = (f32[13,4,8,256]{3,2,1,0:T(8,128)}, f32[13,4,8,256]{3,2,1,0:T(8,128)}, u32[]{:S(2)}, u32[]{:S(2)}) collective-permute-start(f32[13,4,8,256]{3,2,1,0:T(8,128)} %fusion), channel_id=1, source_target_pairs={{1,6},{4,3},{3,4},{6,1},{5,10},{8,7},{7,8},{10,5},{9,14},{12,11},{... | collective-permute-start | bytes 1277960 | tf_op jit(solution)/shard_map/ppermute | solution.py:215
  8.8 0.0 copy-done.10
  8.8 0.2 reduce-window.13
  8.9 0.5 fusion.3
  9.5 0.0 copy-done.5
  9.5 0.1 constant_dynamic-slice_fusion.refs_17_
  9.5 0.0 collective-permute-done.refs_4_
  9.5 0.7 collective-permute-start.1
  10.3 0.0 collective-permute-done.2.refs_2_
  10.3 8.0 %collective-permute-start.3 = (f32[13,4,16,256]{3,2,1,0:T(8,128)S(1)}, f32[13,4,16,256]{3,2,1,0:T(8,128)}, u32[]{:S(2)}, u32[]{:S(2)}) collective-permute-start(f32[13,4,16,256]{3,2,1,0:T(8,128)S(1)} %collective-permute-done.2.refs_2_), channel_id=1, source_target_pairs={{0,1},{1,0},{2,3},{3,2},{4,5},{5,4},{6,7},{7,6},{8,9},{9,8},{10,11... | collective-permute-start | bytes 2555912 | tf_op jit(solution)/shard_map/ppermute | solution.py:179
  18.3 0.5 iota_subtract_fusion
  18.8 0.0 copy-start.7
  18.8 0.7 copy-done.7
  19.4 0.1 copy.13
  19.6 0.2 reduce-window.14
  19.7 0.1 reduce
  19.8 0.0 copy-start.6
  19.9 0.1 stack.27.refs_0_
  19.9 0.6 copy-done.6
  20.5 0.0 collective-permute-done.6.refs_8_
  20.6 2.0 %collective-permute-start.7 = (f32[13,4,8,256]{3,2,1,0:T(8,128)}, f32[13,4,8,256]{3,2,1,0:T(8,128)S(1)}, u32[]{:S(2)}, u32[]{:S(2)}) collective-permute-start(f32[13,4,8,256]{3,2,1,0:T(8,128)} %collective-permute-done.6.refs_8_), channel_id=1, source_target_pairs={{0,1},{1,0},{2,3},{3,2},{4,5},{5,4},{6,7},{7,6},{8,9},{9,8},{10,11... | collective-permute-start | bytes 1277960 | tf_op jit(solution)/shard_map/ppermute | solution.py:179
  22.6 0.0 collective-permute-done.5.refs_7_
  22.6 2.5 %collective-permute-start.8 = (f32[13,4,8,256]{3,2,1,0:T(8,128)}, f32[13,4,8,256]{3,2,1,0:T(8,128)S(1)}, u32[]{:S(2)}, u32[]{:S(2)}) collective-permute-start(f32[13,4,8,256]{3,2,1,0:T(8,128)} %collective-permute-done.5.refs_7_), channel_id=1, source_target_pairs={{0,1},{1,0},{2,3},{3,2},{4,5},{5,4},{6,7},{7,6},{8,9},{9,8},{10,11... | collective-permute-start | bytes 1277960 | tf_op jit(solution)/shard_map/ppermute | solution.py:179
  25.1 0.0 copy-start.2
  25.1 0.0 copy-start.3
  25.1 0.0 copy-start.8
  25.1 0.0 copy-start.9
  25.2 0.7 collective-permute-start.4
  25.9 0.0 copy-done.8
  25.9 0.0 copy-done.9
  25.9 0.1 and_convert_fusion.refs_11_
  25.9 0.0 copy-start
  25.9 0.0 copy-start.1
  26.0 0.0 collective-permute-done.7.refs_9_
  26.0 0.7 collective-permute-done.8.refs_10_
  26.7 0.0 collective-permute-done.4.refs_6_
  26.7 0.0 collective-permute-done.1.refs_1_
  26.7 0.0 collective-permute-done.3.refs_5_
  26.7 0.0 copy-done.2
  26.7 0.0 copy-done.3
  26.7 0.0 copy-done
  26.8 0.0 copy-done.1
  26.8 22.7 %shard_map.113 = (f32[12,4,16,256]{3,2,1,0:T(8,128)}, f32[16,128]{1,0:T(8,128)S(1)}) custom-call(s32[10]{0:T(128)S(1)} %stack.27.refs_0_, f32[13,4,16,256]{3,2,1,0:T(8,128)S(1)} %collective-permute-done.1.refs_1_, f32[13,4,16,256]{3,2,1,0:T(8,128)S(1)} %collective-permute-done.2.refs_2_, f32[13,4,16,256]{3,2,1,0:T(8,128)S(1)} %pad_maximum_fusion.refs_3_, ...), custom_call_target="tpu_custom_call" | custom-call | flops 60000000 | bytes 8000000 | tf_op jit(solution)/shard_map/pallas_call | solution.py:264
  49.6 0.1 reshape.61
  49.7 0.1 reshape.64
  49.8 29.0 %all_to_all.5 = f32[16,1,128]{2,1,0:T(1,128)S(1)} all-to-all(f32[16,1,128]{2,1,0:T(1,128)S(1)} %reshape.64), channel_id=1, replica_groups=mesh['groups'=2,'gz'=4,'gy'=2,'col'=2] {'gz','gy','col'}, dimensions={0} | all-to-all | bytes 16384 | tf_op jit(solution)/shard_map/all_to_all | solution.py:286
  78.8 0.5 broadcast.22
  79.3 0.7 reduce.1
  80.0 0.1 reshape.65
  80.1 0.6 reduce_sum.9
  (5 shorter events, 0.1 us)
Async XLA Ops:
  1.5 2.5 %copy-start.4 = (f32[2,6,4,16,256]{4,3,2,1,0:T(8,128)S(1)}, f32[2,6,4,16,256]{4,3,2,1,0:T(8,128)}, u32[]{:S(2)}) copy-start(f32[2,6,4,16,256]{4,3,2,1,0:T(8,128)} %param.10) | copy-start | bytes 2359300
  2.8 6.8 %collective-permute-start = (f32[13,4,16,256]{3,2,1,0:T(8,128)S(1)}, f32[13,4,16,256]{3,2,1,0:T(8,128)S(1)}, u32[]{:S(2)}, u32[]{:S(2)}) collective-permute-start(f32[13,4,16,256]{3,2,1,0:T(8,128)S(1)} %pad_maximum_fusion.refs_3_), channel_id=1, source_target_pairs={{0,1},{1,0},{2,3},{3,2},{4,5},{5,4},{6,7},{7,6},{8,9},{9,8},{10,11... | collective-permute-start | bytes 2555912 | tf_op jit(solution)/shard_map/ppermute | solution.py:179
  3.3 7.0 %collective-permute-start.2 = (f32[13,4,16,256]{3,2,1,0:T(8,128)S(1)}, f32[13,4,16,256]{3,2,1,0:T(8,128)S(1)}, u32[]{:S(2)}, u32[]{:S(2)}) collective-permute-start(f32[13,4,16,256]{3,2,1,0:T(8,128)S(1)} %pad_maximum_fusion.refs_3_), channel_id=1, source_target_pairs={{1,4},{4,1},{5,8},{8,5},{9,12},{12,9},{3,6},{6,3},{7,10},{10,7},{1... | collective-permute-start | bytes 2555912 | tf_op jit(solution)/shard_map/ppermute | solution.py:186
  4.0 4.7 %copy-start.10 = (s32[1,8]{1,0:T(1,128)S(1)}, s32[1,8]{1,0:T(1,128)}, u32[]{:S(2)}) copy-start(s32[1,8]{1,0:T(1,128)} %param.12) | copy-start | bytes 100
  4.8 4.6 %copy-start.5 = (f32[16,16]{1,0:T(8,128)S(1)}, f32[16,16]{1,0:T(8,128)}, u32[]{:S(2)}) copy-start(f32[16,16]{1,0:T(8,128)} %constant.66.clone) | copy-start | bytes 3076
  4.8 15.7 %collective-permute-start.6 = (f32[13,4,8,256]{3,2,1,0:T(8,128)}, f32[13,4,8,256]{3,2,1,0:T(8,128)}, u32[]{:S(2)}, u32[]{:S(2)}) collective-permute-start(f32[13,4,8,256]{3,2,1,0:T(8,128)} %fusion), channel_id=1, source_target_pairs={{0,2},{2,0},{1,3},{3,1},{4,6},{6,4},{5,7},{7,5},{8,10},{10,8},{9,1... | collective-permute-start | bytes 1277960 | tf_op jit(solution)/shard_map/ppermute | solution.py:206
  7.3 15.2 %collective-permute-start.5 = (f32[13,4,8,256]{3,2,1,0:T(8,128)}, f32[13,4,8,256]{3,2,1,0:T(8,128)}, u32[]{:S(2)}, u32[]{:S(2)}) collective-permute-start(f32[13,4,8,256]{3,2,1,0:T(8,128)} %fusion), channel_id=1, source_target_pairs={{1,6},{4,3},{3,4},{6,1},{5,10},{8,7},{7,8},{10,5},{9,14},{12,11},{... | collective-permute-start | bytes 1277960 | tf_op jit(solution)/shard_map/ppermute | solution.py:215
  9.5 17.2 %collective-permute-start.1 = (f32[13,4,16,256]{3,2,1,0:T(8,128)S(1)}, f32[13,4,16,256]{3,2,1,0:T(8,128)S(1)}, u32[]{:S(2)}, u32[]{:S(2)}) collective-permute-start(f32[13,4,16,256]{3,2,1,0:T(8,128)S(1)} %collective-permute-done.refs_4_), channel_id=1, source_target_pairs={{1,4},{4,1},{5,8},{8,5},{9,12},{12,9},{3,6},{6,3},{7,10},{10,7},{1... | collective-permute-start | bytes 2555912 | tf_op jit(solution)/shard_map/ppermute | solution.py:186
  10.3 16.4 %collective-permute-start.3 = (f32[13,4,16,256]{3,2,1,0:T(8,128)S(1)}, f32[13,4,16,256]{3,2,1,0:T(8,128)}, u32[]{:S(2)}, u32[]{:S(2)}) collective-permute-start(f32[13,4,16,256]{3,2,1,0:T(8,128)S(1)} %collective-permute-done.2.refs_2_), channel_id=1, source_target_pairs={{0,1},{1,0},{2,3},{3,2},{4,5},{5,4},{6,7},{7,6},{8,9},{9,8},{10,11... | collective-permute-start | bytes 2555912 | tf_op jit(solution)/shard_map/ppermute | solution.py:179
  18.8 0.7 copy-start.7
  19.8 0.7 copy-start.6
  20.6 5.4 %collective-permute-start.7 = (f32[13,4,8,256]{3,2,1,0:T(8,128)}, f32[13,4,8,256]{3,2,1,0:T(8,128)S(1)}, u32[]{:S(2)}, u32[]{:S(2)}) collective-permute-start(f32[13,4,8,256]{3,2,1,0:T(8,128)} %collective-permute-done.6.refs_8_), channel_id=1, source_target_pairs={{0,1},{1,0},{2,3},{3,2},{4,5},{5,4},{6,7},{7,6},{8,9},{9,8},{10,11... | collective-permute-start | bytes 1277960 | tf_op jit(solution)/shard_map/ppermute | solution.py:179
  22.6 4.1 %collective-permute-start.8 = (f32[13,4,8,256]{3,2,1,0:T(8,128)}, f32[13,4,8,256]{3,2,1,0:T(8,128)S(1)}, u32[]{:S(2)}, u32[]{:S(2)}) collective-permute-start(f32[13,4,8,256]{3,2,1,0:T(8,128)} %collective-permute-done.5.refs_7_), channel_id=1, source_target_pairs={{0,1},{1,0},{2,3},{3,2},{4,5},{5,4},{6,7},{7,6},{8,9},{9,8},{10,11... | collective-permute-start | bytes 1277960 | tf_op jit(solution)/shard_map/ppermute | solution.py:179
  25.1 1.6 %copy-start.2 = (f32[16,16]{1,0:T(8,128)S(1)}, f32[16,16]{1,0:T(8,128)}, u32[]{:S(2)}) copy-start(f32[16,16]{1,0:T(8,128)} %constant.69.clone.refs_16_) | copy-start | bytes 3076
  25.1 1.6 %copy-start.3 = (f32[16,128]{1,0:T(8,128)S(1)}, f32[16,128]{1,0:T(8,128)}, u32[]{:S(2)}) copy-start(f32[16,128]{1,0:T(8,128)} %constant.70.clone.refs_18_) | copy-start | bytes 24580
  25.1 0.7 copy-start.8
  25.1 0.7 copy-start.9
  25.2 1.6 %collective-permute-start.4 = (f32[13,4,8,256]{3,2,1,0:T(8,128)S(1)}, f32[13,4,8,256]{3,2,1,0:T(8,128)S(1)}, u32[]{:S(2)}, u32[]{:S(2)}) collective-permute-start(f32[13,4,8,256]{3,2,1,0:T(8,128)S(1)} %constant_dynamic-slice_fusion.1), channel_id=1, source_target_pairs={{1,6},{4,3},{3,4},{6,1},{5,10},{8,7},{7,8},{10,5},{9,14},{12,11},{... | collective-permute-start | bytes 1277960 | tf_op jit(solution)/shard_map/ppermute | solution.py:215
  25.9 0.8 %copy-start = (f32[128,128]{1,0:T(8,128)S(1)}, f32[128,128]{1,0:T(8,128)}, u32[]{:S(2)}) copy-start(f32[128,128]{1,0:T(8,128)} %constant.67.clone.refs_14_) | copy-start | bytes 196612
  25.9 0.9 %copy-start.1 = (f32[128,128]{1,0:T(8,128)S(1)}, f32[128,128]{1,0:T(8,128)}, u32[]{:S(2)}) copy-start(f32[128,128]{1,0:T(8,128)} %constant.68.clone.refs_15_) | copy-start | bytes 196612

commit v2 on v1

v2 whole, which is shorter than its diff:
```python
import functools
import math

import jax
import jax.numpy as jnp
import numpy as np
from jax import lax
from jax.experimental import pallas as pl
from jax.experimental.pallas import tpu as pltpu
from jax.sharding import PartitionSpec as P

STEPS = 8
FILTER_LEN = 12

courant = 0.5
omega_step = 0.7
beta_proj = 4.0
eta_proj = 0.5
eps_span = 11.1
highest = lax.Precision.HIGHEST

Z = ("gz", "col")
HALF = STEPS // 2


def slope_of(density):
    norm = math.tanh(beta_proj * eta_proj) + math.tanh(beta_proj * (1.0 - eta_proj))
    bent = jnp.tanh(beta_proj * (density - eta_proj))
    return beta_proj * (1.0 - bent * bent) / norm


def real_basis(size):
    place = np.arange(size)
    rows, waves = [], []
    for k in range(size // 2 + 1):
        angle = 2.0 * np.pi * ((k * place) % size) / size
        edge = k == 0 or 2 * k == size
        rows.append(np.cos(angle) * math.sqrt((1.0 if edge else 2.0) / size))
        waves.append(k)
        if not edge:
            rows.append(np.sin(angle) * math.sqrt(2.0 / size))
            waves.append(k)
    return np.array(rows), np.array(waves)


def band_table(counts, place):
    ends = jnp.cumsum(counts)
    starts = ends - counts
    return ((place >= starts[None, :]) & (place < ends[None, :])).astype(jnp.float32)


def mm(left, right):
    return jnp.dot(left, right, precision=highest, preferred_element_type=jnp.float32)


def strip_of(block, up):
    low_half = lax.broadcasted_iota(jnp.int32, (8, 128), 0) < HALF
    rows = block.shape[0]
    if up:
        a, b = block[rows - 8 :, :128], block[rows - 8 :, 128:]
        return jnp.where(low_half, pltpu.roll(a, HALF, 0), b)
    a, b = block[:8, :128], block[:8, 128:]
    return jnp.where(low_half, a, pltpu.roll(b, HALF, 0))


def strips_of(block, info, sides):
    if sides == 2:
        return [strip_of(block, True), strip_of(block, False)]
    return [jnp.where(info[1] == 0, strip_of(block, True), strip_of(block, False))]


def edge_kernel(sides, info, fields, eps, scaled, *strips):
    for l in range(eps.shape[0]):
        scale = courant * eps[l]
        scaled[l] = scale
        for c in range(13):
            block = fields[c, l] if c < 12 else scale
            for s, strip in enumerate(strips_of(block, info, sides)):
                strips[s][c, l] = strip


def window_kernel(cfg, *refs):
    depth, rows_own, sides, second = cfg
    it = iter(refs)
    take = lambda n: [next(it) for _ in range(n)]
    info = next(it)
    full = take(3)
    strip_in = [take(3) for _ in range(sides)]
    if second:
        (scale_in, acc_in) = take(2)
        row_table, col_table, slope, basis_x, basis_xt, basis_y, own_y, response = take(8)
        out, share = take(2)
    else:
        eps_full = take(3)
        out, scale_out, acc_out = take(3)
        strip_out = take(sides)
    if second:
        st, strips, acc, sem_full, sem_strip, sem_out = take(6)
        scale_ref = scale_in
    else:
        st, strips, sem_full, sem_strip, sem_eps, sem_out = take(6)
        scale_ref = scale_out
        acc = acc_out

    core, gy = info[0], info[1]
    copies = []
    for b in range(3):
        place = jnp.where(core == 0, b * depth, (2 - b) * depth)
        layers = pl.ds(place, depth)
        copies.append(pltpu.make_async_copy(full[b], st.at[:, layers, pl.ds(0, rows_own), :], sem_full.at[b]))
        for s in range(sides):
            copies.append(pltpu.make_async_copy(strip_in[s][b], strips.at[s, :, layers], sem_strip.at[s, b]))
        if not second:
            copies.append(
                pltpu.make_async_copy(eps_full[b], scale_ref.at[layers, pl.ds(0, rows_own), :], sem_eps.at[b])
            )
    for copy in copies:
        copy.start()
    for copy in copies:
        copy.wait()

    nx = st.shape[-1]
    rows = st.shape[-2]
    low_half = lax.broadcasted_iota(jnp.int32, (8, 128), 0) < HALF
    low_half_at = jnp.where(low_half, 0, 1)
    n_layers = 3 * depth
    planes = 12 if second else 13
    for c in range(planes):
        for l in range(n_layers):
            if sides == 2:
                lo, hi = strips[0, c, l], strips[1, c, l]
                left = jnp.where(low_half, hi, pltpu.roll(lo, HALF, 0))
                right = jnp.where(low_half, pltpu.roll(hi, HALF, 0), lo)
            else:
                v = strips[0, c, l]
                w = pltpu.roll(v, HALF, 0)
                keep = low_half_at == gy
                left = jnp.where(keep, jnp.where(low_half, v, w), 0.0)
                right = jnp.where(keep, jnp.where(low_half, w, v), 0.0)
            tile = jnp.concatenate([left, right], axis=1)
            if c == 12:
                scale_ref[l, rows_own:rows, :] = tile
            else:
                st[c, l, rows_own:rows, :] = tile

    row_at = lax.broadcasted_iota(jnp.int32, (rows, nx), 0)
    lane_at = lax.broadcasted_iota(jnp.int32, (rows, 128), 1)
    last_lane, first_lane = lane_at == 127, lane_at == 0
    ahead = jnp.where(info[4] > 0, courant, 0.0)
    behind = jnp.where(info[5] > 0, courant, 0.0)
    coef_in = jnp.where(row_at < rows_own, courant, jnp.where(row_at < rows_own + HALF, ahead, behind))
    low_layer, high_layer = info[2], info[3]

    def y_ahead(f):
        return pltpu.roll(f, rows - 1, 0)

    def y_behind(f):
        return pltpu.roll(f, 1, 0)

    def x_ahead(f):
        a, b = pltpu.roll(f[:, :128], 127, 1), pltpu.roll(f[:, 128:], 127, 1)
        return jnp.concatenate([jnp.where(last_lane, b, a), jnp.where(last_lane, 0.0, b)], axis=1)

    def x_behind(f):
        a, b = pltpu.roll(f[:, :128], 1, 1), pltpu.roll(f[:, 128:], 1, 1)
        return jnp.concatenate([jnp.where(first_lane, 0.0, a), jnp.where(first_lane, a, b)], axis=1)

    for m in range(1, HALF + 1):
        angle = omega_step * (m + (HALF if second else 0))
        w_re, w_im = math.cos(angle), math.sin(angle)
        prev = [None, None]
        for z in range(m - 1, n_layers - m):
            coef = coef_in * jnp.where((z >= low_layer) & (z < high_layer), 1.0, 0.0)
            scale = scale_ref[z]
            for r in range(2):
                b = 6 * r
                ex, ey, ez = st[b, z], st[b + 1, z], st[b + 2, z]
                ex_n, ey_n = st[b, z + 1], st[b + 1, z + 1]
                hx = st[b + 3, z] - coef * ((y_ahead(ez) - ez) - (ey_n - ey))
                hy = st[b + 4, z] - coef * ((ex_n - ex) - (x_ahead(ez) - ez))
                if z >= m:
                    hx_p, hy_p = prev[r]
                    hz = st[b + 5, z] - coef * ((x_ahead(ey) - ey) - (y_ahead(ex) - ex))
                    ex = ex + scale * ((hz - y_behind(hz)) - (hy - hy_p))
                    ey = ey + scale * ((hx - hx_p) - (hz - x_behind(hz)))
                    ez = ez + scale * ((hy - x_behind(hy)) - (hx - y_behind(hx)))
                    st[b, z], st[b + 1, z], st[b + 2, z] = ex, ey, ez
                    st[b + 3, z], st[b + 4, z], st[b + 5, z] = hx, hy, hz
                    own = z - depth
                    if 0 <= own < depth:
                        for c, e in enumerate((ex, ey, ez)):
                            e = e[:rows_own]
                            re, im = e * w_re, e * w_im
                            if m > 1:
                                acc[0, 3 * r + c, own] = acc[0, 3 * r + c, own] + re
                                acc[1, 3 * r + c, own] = acc[1, 3 * r + c, own] - im
                            elif second:
                                acc[0, 3 * r + c, own] = acc_in[0, 3 * r + c, own] + re
                                acc[1, 3 * r + c, own] = acc_in[1, 3 * r + c, own] - im
                            else:
                                acc[0, 3 * r + c, own] = re
                                acc[1, 3 * r + c, own] = -im
                else:
                    st[b + 3, z], st[b + 4, z] = hx, hy
                prev[r] = (hx, hy)

    result = pltpu.make_async_copy(st.at[:, pl.ds(depth, depth), pl.ds(0, rows_own), :], out, sem_out)
    result.start()
    if not second:
        for c in range(12):
            for l in range(depth):
                for s, strip in enumerate(strips_of(st[c, depth + l, :rows_own, :], info, sides)):
                    strip_out[s][c, l] = strip
    else:
        column_sum = jnp.zeros((rows_own, nx), jnp.float32)
        for own in range(depth):
            g = jnp.zeros((rows_own, nx), jnp.float32)
            for c in range(3):
                g = g + acc[0, c, own] * acc[0, 3 + c, own] - acc[1, c, own] * acc[1, 3 + c, own]
            in_layer = (info[6] + own >= 0) & (info[6] + own < 3 * depth)
            column_sum = column_sum + jnp.where(in_layer, g, 0.0)
        sens = mm(row_table[...], mm(column_sum, col_table[...])) * (eps_span / (STEPS * 3 * depth))
        weighted = sens * slope[...]
        spectrum = mm(own_y[...], mm(weighted, basis_xt[...])) * response[...]
        share[...] = mm(basis_y[...], mm(spectrum, basis_x[...]))
    result.wait()


def body(fields, eps_inv, row_counts, col_counts, density):
    runs, comps, depth, rows_own, nx = fields.shape
    n_gz, n_gy = lax.axis_size("gz"), lax.axis_size("gy")
    gz, gy, core = lax.axis_index("gz"), lax.axis_index("gy"), lax.axis_index("col")
    index = gz * 2 + core
    n_z = n_gz * 2
    assert HALF == depth and rows_own == 16 and nx == 256
    rows = rows_own + 2 * HALF
    own = fields.reshape(runs * comps, depth, rows_own, nx)

    def swap_core(x):
        return lax.ppermute(x, "col", [(0, 1), (1, 0)])

    def cross(x):
        pairs = []
        for c in range(n_gz - 1):
            a, b = 2 * c + 1, 2 * c + 2
            pairs += [(a, b), (b, a)]
        return lax.ppermute(x, Z, pairs)

    if n_gy == 2:
        ways = [{0: 1, 1: 0}]
    else:
        ways = [{y: y + 1 for y in range(n_gy - 1)}, {y: y - 1 for y in range(1, n_gy)}]
    sides = len(ways)

    def along_y(x, s):
        return lax.ppermute(x, "gy", list(ways[s].items()))

    def across(x, s):
        pairs = []
        for c in range(n_gz - 1):
            for y, to in ways[s].items():
                for src, dst in (((c, y, 1), (c + 1, to, 0)), ((c + 1, y, 0), (c, to, 1))):
                    pairs.append(tuple((p[0] * n_gy + p[1]) * 2 + p[2] for p in (src, dst)))
        return lax.ppermute(x, ("gz", "gy", "col"), pairs)

    layer_start = depth * n_z // 2 - depth - depth // 2
    info = [
        core,
        gy,
        depth - index * depth,
        depth * n_z - index * depth + depth,
        jnp.where(gy < n_gy - 1, 1, 0),
        jnp.where(gy > 0, 1, 0),
        index * depth - layer_start,
    ]
    info = jnp.stack([jnp.asarray(v, jnp.int32) for v in info])

    anywhere = pl.BlockSpec(memory_space=pl.ANY)
    vmem = pl.BlockSpec(memory_space=pltpu.VMEM)
    smem = pl.BlockSpec(memory_space=pltpu.SMEM)
    shape = lambda *s: jax.ShapeDtypeStruct(s, jnp.float32)
    limit = pltpu.CompilerParams(vmem_limit_bytes=24 * 1024 * 1024)

    def strips_sent(strips):
        sent = []
        for s, strip in enumerate(strips):
            mine = along_y(strip, s)
            sent += [across(strip, s), mine, swap_core(mine)]
        return sent

    full = [cross(own), own, swap_core(own)]
    scaled, *strips = pl.pallas_call(
        functools.partial(edge_kernel, sides),
        out_shape=(shape(depth, rows_own, nx),) + (shape(13, depth, 8, 128),) * sides,
        in_specs=[smem, vmem, vmem],
        out_specs=(vmem,) * (1 + sides),
        compiler_params=limit,
    )(info, own, eps_inv)
    operands = [info] + full + strips_sent(strips) + [cross(scaled), scaled, swap_core(scaled)]
    cost = pl.CostEstimate(flops=20_000_000, bytes_accessed=4_000_000, transcendentals=0)
    state, scale, acc, *strips = pl.pallas_call(
        functools.partial(window_kernel, (depth, rows_own, sides, False)),
        out_shape=(
            shape(runs * comps, depth, rows_own, nx),
            shape(3 * depth, rows, nx),
            shape(2, 6, depth, rows_own, nx),
        )
        + (shape(12, depth, 8, 128),) * sides,
        in_specs=[smem] + [anywhere] * (6 + 3 * sides),
        out_specs=(anywhere, vmem, vmem) + (vmem,) * sides,
        scratch_shapes=[
            pltpu.VMEM((12, 3 * depth, rows, nx), jnp.float32),
            pltpu.VMEM((sides, 13, 3 * depth, 8, 128), jnp.float32),
            pltpu.SemaphoreType.DMA((3,)),
            pltpu.SemaphoreType.DMA((sides, 3)),
            pltpu.SemaphoreType.DMA((3,)),
            pltpu.SemaphoreType.DMA,
        ],
        compiler_params=limit,
        cost_estimate=cost,
    )(*operands)

    band, design_cols = density.shape
    tall = band * n_gy
    row_table = band_table(row_counts[0], jnp.arange(rows_own, dtype=jnp.int32)[:, None]).T
    col_table = band_table(col_counts, jnp.arange(nx, dtype=jnp.int32)[:, None])
    basis_x, wave_x = real_basis(design_cols)
    basis_y, wave_y = real_basis(tall)
    response = 1.0 / (
        1.0
        + FILTER_LEN**2
        * (
            4.0 * np.sin(math.pi * wave_y / tall)[:, None] ** 2
            + 4.0 * np.sin(math.pi * wave_x / design_cols)[None, :] ** 2
        )
    )
    const = lambda a: jnp.asarray(a, jnp.float32)
    own_y = lax.dynamic_slice_in_dim(const(basis_y), gy * band, band, 1)
    operands = [info, cross(state), state, swap_core(state)] + strips_sent(strips) + [scale, acc]
    operands += [row_table, col_table, slope_of(density), const(basis_x), const(basis_x.T), const(basis_y.T), own_y, const(response)]
    fields_out, share = pl.pallas_call(
        functools.partial(window_kernel, (depth, rows_own, sides, True)),
        out_shape=(shape(runs * comps, depth, rows_own, nx), shape(tall, design_cols)),
        in_specs=[smem] + [anywhere] * (3 + 3 * sides) + [vmem] * 10,
        out_specs=(anywhere, vmem),
        scratch_shapes=[
            pltpu.VMEM((12, 3 * depth, rows, nx), jnp.float32),
            pltpu.VMEM((sides, 12, 3 * depth, 8, 128), jnp.float32),
            pltpu.VMEM((2, 6, depth, rows_own, nx), jnp.float32),
            pltpu.SemaphoreType.DMA((3,)),
            pltpu.SemaphoreType.DMA((sides, 3)),
            pltpu.SemaphoreType.DMA,
        ],
        compiler_params=limit,
        cost_estimate=cost,
    )(*operands)

    width = design_cols // n_z
    blocks = share.reshape(n_gy, band, n_gz, 2, width).transpose(2, 0, 3, 1, 4)
    blocks = blocks.reshape(n_gz * n_gy * 2, band, width)
    got = lax.all_to_all(blocks, ("gz", "gy", "col"), 0, 0)
    gradient = jnp.sum(got, axis=0)
    return fields_out.reshape(fields.shape), gradient


def solution(mesh):
    in_specs = (
        P("groups", None, ("gz", "col"), "gy", None),
        P(("groups", "gz", "col"), "gy", None),
        P(("groups", "gy"), None),
        P("groups"),
        P(("groups", "gy"), None),
    )
    out_specs = (P("groups", None, ("gz", "col"), "gy", None), P(("groups", "gy"), ("gz", "col")))
    return jax.shard_map(body, mesh=mesh, in_specs=in_specs, out_specs=out_specs, check_vma=False)
```

time: 81.1 us -> 68.5 us (0.84)
  blocking collectives: 29 us -> 16.2 us
  Pallas kernels: 22.7 us -> 11.8 us
  waiting for transfers between devices: 0.74 us -> 7.43 us
  starting transfers between devices: 19.1 us -> 25.6 us
  other arithmetic: 5.81 us -> 1.85 us
  local copies, waits for them, and re-layouts: 2.48 us -> 4.4 us
    all_to_all x1, blocking collectives: 29 us -> 16.2 us  [body(): got = lax.all_to_all(blocks, ('gz', 'gy', 'col'), 0, 0)]
    pallas_call x1 -> x3, Pallas kernels: 22.7 us -> 11.8 us  [the longest x2 11.2 us: body(): pl.pallas_call(functools.partial(window_kernel, (depth, rows_own, sides,...]
    ppermute x1 -> x2, waiting for transfers between devices: 0.01 us -> 6.04 us  [along_y(): return lax.ppermute(x, 'gy', list(ways[s].items()))]
    ppermute x4 -> x5, starting transfers between devices: 13.1 us -> 19.1 us  [swap_core(): return lax.ppermute(x, 'col', [(0, 1), (1, 0)])]
    concatenate x2 -> x0, other arithmetic: 2.08 us -> none  [body(): jnp.concatenate([fields.reshape(runs * comps, depth, rows_own, nx), (cour...]
    unnamed x24, local copies, waits for them, and re-layouts: 1.52 us -> 3.47 us
    broadcast_in_dim x1 -> x0, other arithmetic: 0.85 us -> none  [body(): (courant * eps_inv)[None]]
    ppermute x2 -> x3, starting transfers between devices: 1.41 us -> 2.07 us  [cross(): return lax.ppermute(x, Z, pairs)]
  transfers between devices with their start and end apart: 9 -> 12, of which waited for: 1 -> 3; matrix products, arithmetic and copies ran while one was open for 3% -> 1% of each run, Pallas kernels for 0% -> 1%
where the time goes in v2:
time: 68.5 us; the launch traced here: 68.1 us
  starting transfers between devices  25.6 us (37%)
  blocking collectives  16.2 us (24%)
  Pallas kernels  11.8 us (17%)
  waiting for transfers between devices  7.43 us (11%)
  local copies, waits for them, and re-layouts  4.4 us (6%)
  other arithmetic  1.85 us (3%)
  between operations  0.84 us (1%)
    ppermute x5, starting transfers between devices, swap_core(): return lax.ppermute(x, 'col', [(0, 1), (1, 0)])  19.1 us
    all_to_all x1, blocking collectives, body(): got = lax.all_to_all(blocks, ('gz', 'gy', 'col'), 0, 0)  16.2 us
    pallas_call x2, Pallas kernels, body(): pl.pallas_call(functools.partial(window_kernel, (depth, rows_own, sides,...  11.2 us
    ppermute x2, waiting for transfers between devices, along_y(): return lax.ppermute(x, 'gy', list(ways[s].items()))  6.04 us
    unnamed x24, local copies, waits for them, and re-layouts  3.47 us
    ppermute x2, starting transfers between devices, along_y(): return lax.ppermute(x, 'gy', list(ways[s].items()))  3.11 us
    ppermute x3, starting transfers between devices, cross(): return lax.ppermute(x, Z, pairs)  2.07 us
    ppermute x5, waiting for transfers between devices, swap_core(): return lax.ppermute(x, 'col', [(0, 1), (1, 0)])  1.37 us
  transfers between devices with their start and end apart: 12, of which 3 were waited for; matrix products, arithmetic and copies ran while one was open for 1% of the time, Pallas kernels for 1%

profile of v2, /device:TPU:0, one launch (start us, length us, event | category | flops | bytes accessed | tf_op | source)
XLA Modules:
  0.0 68.1 jit_solution(6564420899569671626)
XLA Ops:
  0.6 0.7 %collective-permute-start = (f32[12,4,16,256]{3,2,1,0:T(8,128)}, f32[12,4,16,256]{3,2,1,0:T(8,128)S(1)}, u32[]{:S(2)}, u32[]{:S(2)}) collective-permute-start(f32[12,4,16,256]{3,2,1,0:T(8,128)} %bitcast.21), channel_id=1, source_target_pairs={{1,4},{4,1},{5,8},{8,5},{9,12},{12,9},{3,6},{6,3},{7,10},{10,7},{1... | collective-permute-start | bytes 2359304 | tf_op jit(solution)/shard_map/ppermute | solution.py:247
  1.3 4.4 %collective-permute-start.1 = (f32[12,4,16,256]{3,2,1,0:T(8,128)}, f32[12,4,16,256]{3,2,1,0:T(8,128)S(1)}, u32[]{:S(2)}, u32[]{:S(2)}) collective-permute-start(f32[12,4,16,256]{3,2,1,0:T(8,128)} %bitcast.22), channel_id=1, source_target_pairs={{0,1},{1,0},{2,3},{3,2},{4,5},{5,4},{6,7},{7,6},{8,9},{9,8},{10,11... | collective-permute-start | bytes 2359304 | tf_op jit(solution)/shard_map/ppermute | solution.py:240
  5.8 0.1 stack.31.info.refs_0_
  5.8 0.0 copy-start
  5.8 1.1 %copy-done = f32[2,6,4,16,256]{4,3,2,1,0:T(8,128)S(1)} copy-done((f32[2,6,4,16,256]{4,3,2,1,0:T(8,128)S(1)}, f32[2,6,4,16,256]{4,3,2,1,0:T(8,128)}, u32[]{:S(2)}) %copy-start) | copy-done | bytes 786456
  7.0 0.0 copy-start.4
  7.0 0.8 %copy-done.4 = f32[4,16,256]{2,1,0:T(8,128)S(1)} copy-done((f32[4,16,256]{2,1,0:T(8,128)S(1)}, f32[4,16,256]{2,1,0:T(8,128)}, u32[]{:S(2)}) %copy-start.4) | copy-done | bytes 65560
  7.8 0.0 copy-start.8
  7.8 0.0 copy-start.1
  7.8 0.6 shard_map.113
  8.4 1.6 %collective-permute-start.3 = (f32[13,4,8,128]{3,2,1,0:T(8,128)S(1)}, f32[13,4,8,128]{3,2,1,0:T(8,128)S(1)}, u32[]{:S(2)}, u32[]{:S(2)}) collective-permute-start(f32[13,4,8,128]{3,2,1,0:T(8,128)S(1)} %get-tuple-element.10), channel_id=1, source_target_pairs={{0,2},{2,0},{1,3},{3,1},{4,6},{6,4},{5,7},{7,5},{8,10},{10,8},{9,1... | collective-permute-start | bytes 638984 | tf_op jit(solution)/shard_map/ppermute | solution.py:256
  10.0 0.7 collective-permute-start.5
  10.6 3.0 %collective-permute-start.6 = (f32[4,16,256]{2,1,0:T(8,128)S(1)}, f32[4,16,256]{2,1,0:T(8,128)S(1)}, u32[]{:S(2)}, u32[]{:S(2)}) collective-permute-start(f32[4,16,256]{2,1,0:T(8,128)S(1)} %get-tuple-element.11.refs_8_), channel_id=1, source_target_pairs={{0,1},{1,0},{2,3},{3,2},{4,5},{5,4},{6,7},{7,6},{8,9},{9,8},{10,11... | collective-permute-start | bytes 196616 | tf_op jit(solution)/shard_map/ppermute | solution.py:240
  13.6 0.0 collective-permute-done.5.refs_7_
  13.6 0.7 collective-permute-start.2
  14.3 1.4 %collective-permute-done.3.refs_5_ = f32[13,4,8,128]{3,2,1,0:T(8,128)S(1)} collective-permute-done((f32[13,4,8,128]{3,2,1,0:T(8,128)S(1)}, f32[13,4,8,128]{3,2,1,0:T(8,128)S(1)}, u32[]{:S(2)}, u32[]{:S(2)}) %collective-permute-start.3) | collective-permute-done | bytes 213024 | tf_op jit(solution)/shard_map/ppermute | solution.py:256
  15.7 5.2 %collective-permute-start.4 = (f32[13,4,8,128]{3,2,1,0:T(8,128)S(1)}, f32[13,4,8,128]{3,2,1,0:T(8,128)S(1)}, u32[]{:S(2)}, u32[]{:S(2)}) collective-permute-start(f32[13,4,8,128]{3,2,1,0:T(8,128)S(1)} %collective-permute-done.3.refs_5_), channel_id=1, source_target_pairs={{0,1},{1,0},{2,3},{3,2},{4,5},{5,4},{6,7},{7,6},{8,9},{9,8},{10,11... | collective-permute-start | bytes 638984 | tf_op jit(solution)/shard_map/ppermute | solution.py:240
  20.9 0.0 copy-done.8
  20.9 0.0 copy-start.9
  20.9 0.6 copy-done.9
  21.6 0.1 copy.13
  21.7 0.2 reduce-window.14
  21.9 0.1 reduce
  22.0 0.0 copy-start.10
  22.0 0.6 copy-done.10
  22.6 0.2 reduce-window.13
  22.8 0.0 copy-start.7
  22.8 0.0 collective-permute-done.6.refs_9_
  22.8 0.0 collective-permute-done.2.refs_4_
  22.8 0.0 collective-permute-done.4.refs_6_
  22.8 0.0 collective-permute-done.refs_1_
  22.8 0.0 collective-permute-done.1.refs_3_
  22.9 0.0 copy-done.1
  22.9 6.5 %shard_map.114 = (f32[12,4,16,256]{3,2,1,0:T(8,128)S(1)}, f32[12,24,256]{2,1,0:T(8,128)S(1)}, f32[2,6,4,16,256]{4,3,2,1,0:T(8,128)S(1)}, f32[12,4,8,128]{3,2,1,0:T(8,128)S(1)}) custom-call(s32[7]{0:T(128)S(1)} %stack.31.info.refs_0_, f32[12,4,16,256]{3,2,1,0:T(8,128)S(1)} %collective-permute-done.refs_1_, f32[12,4,16,256]{3,2,1,0:T(8,128)S(1)} %bitcast.24, ...), custom_call_target="tpu_custom_call" | custom-call | flops 20000000 | bytes 4000000 | tf_op jit(solution)/shard_map/pallas_call | solution.py:301
  29.4 0.7 %collective-permute-start.7 = (f32[12,4,16,256]{3,2,1,0:T(8,128)S(1)}, f32[12,4,16,256]{3,2,1,0:T(8,128)S(1)}, u32[]{:S(2)}, u32[]{:S(2)}) collective-permute-start(f32[12,4,16,256]{3,2,1,0:T(8,128)S(1)} %get-tuple-element.12.refs_2_), channel_id=1, source_target_pairs={{1,4},{4,1},{5,8},{8,5},{9,12},{12,9},{3,6},{6,3},{7,10},{10,7},{1... | collective-permute-start | bytes 2359304 | tf_op jit(solution)/shard_map/ppermute | solution.py:247
  30.1 6.4 %collective-permute-start.8 = (f32[12,4,16,256]{3,2,1,0:T(8,128)S(1)}, f32[12,4,16,256]{3,2,1,0:T(8,128)S(1)}, u32[]{:S(2)}, u32[]{:S(2)}) collective-permute-start(f32[12,4,16,256]{3,2,1,0:T(8,128)S(1)} %get-tuple-element.12.refs_2_), channel_id=1, source_target_pairs={{0,1},{1,0},{2,3},{3,2},{4,5},{5,4},{6,7},{7,6},{8,9},{9,8},{10,11... | collective-permute-start | bytes 2359304 | tf_op jit(solution)/shard_map/ppermute | solution.py:240
  36.5 0.0 copy-done.7
  36.5 0.0 copy-start.6
  36.5 0.1 constant_dynamic-slice_fusion.refs_15_
  36.6 0.0 copy-start.2
  36.6 0.0 copy-start.3
  36.6 0.0 copy-start.5
  36.7 1.6 %collective-permute-start.10 = (f32[12,4,8,128]{3,2,1,0:T(8,128)S(1)}, f32[12,4,8,128]{3,2,1,0:T(8,128)S(1)}, u32[]{:S(2)}, u32[]{:S(2)}) collective-permute-start(f32[12,4,8,128]{3,2,1,0:T(8,128)S(1)} %get-tuple-element.13), channel_id=1, source_target_pairs={{0,2},{2,0},{1,3},{3,1},{4,6},{6,4},{5,7},{7,5},{8,10},{10,8},{9,1... | collective-permute-start | bytes 589832 | tf_op jit(solution)/shard_map/ppermute | solution.py:256
  38.2 0.7 collective-permute-start.9
  38.9 4.7 %collective-permute-done.10.refs_5_ = f32[12,4,8,128]{3,2,1,0:T(8,128)S(1)} collective-permute-done((f32[12,4,8,128]{3,2,1,0:T(8,128)S(1)}, f32[12,4,8,128]{3,2,1,0:T(8,128)S(1)}, u32[]{:S(2)}, u32[]{:S(2)}) %collective-permute-start.10) | collective-permute-done | bytes 196640 | tf_op jit(solution)/shard_map/ppermute | solution.py:256
  43.6 0.0 collective-permute-start.11
  43.6 0.1 fusion.3.refs_9_
  43.6 0.0 collective-permute-done.9.refs_4_
  43.6 1.4 %collective-permute-done.11.refs_6_ = f32[12,4,8,128]{3,2,1,0:T(8,128)S(1)} collective-permute-done((f32[12,4,8,128]{3,2,1,0:T(8,128)S(1)}, f32[12,4,8,128]{3,2,1,0:T(8,128)S(1)}, u32[]{:S(2)}, u32[]{:S(2)}) %collective-permute-start.11) | collective-permute-done | bytes 196640 | tf_op jit(solution)/shard_map/ppermute | solution.py:240
  45.0 0.0 collective-permute-done.7.refs_1_
  45.0 0.0 collective-permute-done.8.refs_3_
  45.0 0.0 copy-done.6
  45.0 0.0 copy-done.2
  45.0 0.0 copy-done.3
  45.0 0.0 copy-done.5
  45.1 4.7 %shard_map.115 = (f32[12,4,16,256]{3,2,1,0:T(8,128)}, f32[16,128]{1,0:T(8,128)S(1)}) custom-call(s32[7]{0:T(128)S(1)} %stack.31.info.refs_0_, f32[12,4,16,256]{3,2,1,0:T(8,128)S(1)} %collective-permute-done.7.refs_1_, f32[12,4,16,256]{3,2,1,0:T(8,128)S(1)} %get-tuple-element.12.refs_2_, f32[12,4,16,256]{3,2,1,0:T(8,128)S(1)} %collective-permute-done.8.refs_3_, ...), custom_call_target="tpu_custom_call" | custom-call | flops 20000000 | bytes 4000000 | tf_op jit(solution)/shard_map/pallas_call | solution.py:341
  49.8 0.1 reshape.56
  50.0 0.1 reshape.59
  50.1 16.2 %all_to_all.5 = f32[16,1,128]{2,1,0:T(1,128)S(1)} all-to-all(f32[16,1,128]{2,1,0:T(1,128)S(1)} %reshape.59), channel_id=1, replica_groups=mesh['groups'=2,'gz'=4,'gy'=2,'col'=2] {'gz','gy','col'}, dimensions={0} | all-to-all | bytes 16384 | tf_op jit(solution)/shard_map/all_to_all | solution.py:361
  66.2 0.5 broadcast.17
  66.8 0.7 reduce.1
  67.4 0.1 reshape.60
  67.5 0.6 reduce_sum.9
  (5 shorter events, 0.1 us)
Async XLA Ops:
  0.6 22.2 %collective-permute-start = (f32[12,4,16,256]{3,2,1,0:T(8,128)}, f32[12,4,16,256]{3,2,1,0:T(8,128)S(1)}, u32[]{:S(2)}, u32[]{:S(2)}) collective-permute-start(f32[12,4,16,256]{3,2,1,0:T(8,128)} %bitcast.21), channel_id=1, source_target_pairs={{1,4},{4,1},{5,8},{8,5},{9,12},{12,9},{3,6},{6,3},{7,10},{10,7},{1... | collective-permute-start | bytes 2359304 | tf_op jit(solution)/shard_map/ppermute | solution.py:247
  1.3 21.5 %collective-permute-start.1 = (f32[12,4,16,256]{3,2,1,0:T(8,128)}, f32[12,4,16,256]{3,2,1,0:T(8,128)S(1)}, u32[]{:S(2)}, u32[]{:S(2)}) collective-permute-start(f32[12,4,16,256]{3,2,1,0:T(8,128)} %bitcast.22), channel_id=1, source_target_pairs={{0,1},{1,0},{2,3},{3,2},{4,5},{5,4},{6,7},{7,6},{8,9},{9,8},{10,11... | collective-permute-start | bytes 2359304 | tf_op jit(solution)/shard_map/ppermute | solution.py:240
  5.8 1.1 %copy-start = (f32[2,6,4,16,256]{4,3,2,1,0:T(8,128)S(1)}, f32[2,6,4,16,256]{4,3,2,1,0:T(8,128)}, u32[]{:S(2)}) copy-start(f32[2,6,4,16,256]{4,3,2,1,0:T(8,128)} %param.10) | copy-start | bytes 2359300
  7.0 0.8 %copy-start.4 = (f32[4,16,256]{2,1,0:T(8,128)S(1)}, f32[4,16,256]{2,1,0:T(8,128)}, u32[]{:S(2)}) copy-start(f32[4,16,256]{2,1,0:T(8,128)} %eps.1) | copy-start | bytes 196612
  7.8 13.1 %copy-start.8 = (f32[8,128]{1,0:T(8,128)S(1)}, f32[8,128]{1,0:T(8,128)}, u32[]{:S(2)}) copy-start(f32[8,128]{1,0:T(8,128)} %param.14) | copy-start | bytes 12292
  7.8 15.0 %copy-start.1 = (f32[2,6,4,16,256]{4,3,2,1,0:T(8,128)S(1)}, f32[2,6,4,16,256]{4,3,2,1,0:T(8,128)}, u32[]{:S(2)}) copy-start(f32[2,6,4,16,256]{4,3,2,1,0:T(8,128)} %param.10) | copy-start | bytes 2359300
  8.4 7.3 %collective-permute-start.3 = (f32[13,4,8,128]{3,2,1,0:T(8,128)S(1)}, f32[13,4,8,128]{3,2,1,0:T(8,128)S(1)}, u32[]{:S(2)}, u32[]{:S(2)}) collective-permute-start(f32[13,4,8,128]{3,2,1,0:T(8,128)S(1)} %get-tuple-element.10), channel_id=1, source_target_pairs={{0,2},{2,0},{1,3},{3,1},{4,6},{6,4},{5,7},{7,5},{8,10},{10,8},{9,1... | collective-permute-start | bytes 638984 | tf_op jit(solution)/shard_map/ppermute | solution.py:256
  10.0 3.7 %collective-permute-start.5 = (f32[4,16,256]{2,1,0:T(8,128)S(1)}, f32[4,16,256]{2,1,0:T(8,128)S(1)}, u32[]{:S(2)}, u32[]{:S(2)}) collective-permute-start(f32[4,16,256]{2,1,0:T(8,128)S(1)} %get-tuple-element.11.refs_8_), channel_id=1, source_target_pairs={{1,4},{4,1},{5,8},{8,5},{9,12},{12,9},{3,6},{6,3},{7,10},{10,7},{1... | collective-permute-start | bytes 196616 | tf_op jit(solution)/shard_map/ppermute | solution.py:247
  10.6 12.2 %collective-permute-start.6 = (f32[4,16,256]{2,1,0:T(8,128)S(1)}, f32[4,16,256]{2,1,0:T(8,128)S(1)}, u32[]{:S(2)}, u32[]{:S(2)}) collective-permute-start(f32[4,16,256]{2,1,0:T(8,128)S(1)} %get-tuple-element.11.refs_8_), channel_id=1, source_target_pairs={{0,1},{1,0},{2,3},{3,2},{4,5},{5,4},{6,7},{7,6},{8,9},{9,8},{10,11... | collective-permute-start | bytes 196616 | tf_op jit(solution)/shard_map/ppermute | solution.py:240
  13.6 9.2 %collective-permute-start.2 = (f32[13,4,8,128]{3,2,1,0:T(8,128)S(1)}, f32[13,4,8,128]{3,2,1,0:T(8,128)S(1)}, u32[]{:S(2)}, u32[]{:S(2)}) collective-permute-start(f32[13,4,8,128]{3,2,1,0:T(8,128)S(1)} %get-tuple-element.10), channel_id=1, source_target_pairs={{1,6},{4,3},{3,4},{6,1},{5,10},{8,7},{7,8},{10,5},{9,14},{12,11},{... | collective-permute-start | bytes 638984 | tf_op jit(solution)/shard_map/ppermute | solution.py:264
  15.7 7.2 %collective-permute-start.4 = (f32[13,4,8,128]{3,2,1,0:T(8,128)S(1)}, f32[13,4,8,128]{3,2,1,0:T(8,128)S(1)}, u32[]{:S(2)}, u32[]{:S(2)}) collective-permute-start(f32[13,4,8,128]{3,2,1,0:T(8,128)S(1)} %collective-permute-done.3.refs_5_), channel_id=1, source_target_pairs={{0,1},{1,0},{2,3},{3,2},{4,5},{5,4},{6,7},{7,6},{8,9},{9,8},{10,11... | collective-permute-start | bytes 638984 | tf_op jit(solution)/shard_map/ppermute | solution.py:240
  20.9 0.7 copy-start.9
  22.0 0.7 copy-start.10
  22.8 13.7 %copy-start.7 = (f32[16,16]{1,0:T(8,128)S(1)}, f32[16,16]{1,0:T(8,128)}, u32[]{:S(2)}) copy-start(f32[16,16]{1,0:T(8,128)} %constant.58.clone) | copy-start | bytes 3076
  29.4 15.6 %collective-permute-start.7 = (f32[12,4,16,256]{3,2,1,0:T(8,128)S(1)}, f32[12,4,16,256]{3,2,1,0:T(8,128)S(1)}, u32[]{:S(2)}, u32[]{:S(2)}) collective-permute-start(f32[12,4,16,256]{3,2,1,0:T(8,128)S(1)} %get-tuple-element.12.refs_2_), channel_id=1, source_target_pairs={{1,4},{4,1},{5,8},{8,5},{9,12},{12,9},{3,6},{6,3},{7,10},{10,7},{1... | collective-permute-start | bytes 2359304 | tf_op jit(solution)/shard_map/ppermute | solution.py:247
  30.1 14.9 %collective-permute-start.8 = (f32[12,4,16,256]{3,2,1,0:T(8,128)S(1)}, f32[12,4,16,256]{3,2,1,0:T(8,128)S(1)}, u32[]{:S(2)}, u32[]{:S(2)}) collective-permute-start(f32[12,4,16,256]{3,2,1,0:T(8,128)S(1)} %get-tuple-element.12.refs_2_), channel_id=1, source_target_pairs={{0,1},{1,0},{2,3},{3,2},{4,5},{5,4},{6,7},{7,6},{8,9},{9,8},{10,11... | collective-permute-start | bytes 2359304 | tf_op jit(solution)/shard_map/ppermute | solution.py:240
  36.5 8.5 %copy-start.6 = (f32[16,128]{1,0:T(8,128)S(1)}, f32[16,128]{1,0:T(8,128)}, u32[]{:S(2)}) copy-start(f32[16,128]{1,0:T(8,128)} %constant.62.clone.refs_16_) | copy-start | bytes 24580
  36.6 8.4 %copy-start.2 = (f32[128,128]{1,0:T(8,128)S(1)}, f32[128,128]{1,0:T(8,128)}, u32[]{:S(2)}) copy-start(f32[128,128]{1,0:T(8,128)} %constant.59.clone.refs_12_) | copy-start | bytes 196612
  36.6 8.4 %copy-start.3 = (f32[128,128]{1,0:T(8,128)S(1)}, f32[128,128]{1,0:T(8,128)}, u32[]{:S(2)}) copy-start(f32[128,128]{1,0:T(8,128)} %constant.60.clone.refs_13_) | copy-start | bytes 196612
  36.6 8.4 %copy-start.5 = (f32[16,16]{1,0:T(8,128)S(1)}, f32[16,16]{1,0:T(8,128)}, u32[]{:S(2)}) copy-start(f32[16,16]{1,0:T(8,128)} %constant.61.clone.refs_14_) | copy-start | bytes 3076
  36.7 6.9 %collective-permute-start.10 = (f32[12,4,8,128]{3,2,1,0:T(8,128)S(1)}, f32[12,4,8,128]{3,2,1,0:T(8,128)S(1)}, u32[]{:S(2)}, u32[]{:S(2)}) collective-permute-start(f32[12,4,8,128]{3,2,1,0:T(8,128)S(1)} %get-tuple-element.13), channel_id=1, source_target_pairs={{0,2},{2,0},{1,3},{3,1},{4,6},{6,4},{5,7},{7,5},{8,10},{10,8},{9,1... | collective-permute-start | bytes 589832 | tf_op jit(solution)/shard_map/ppermute | solution.py:256
  38.2 5.4 %collective-permute-start.9 = (f32[12,4,8,128]{3,2,1,0:T(8,128)S(1)}, f32[12,4,8,128]{3,2,1,0:T(8,128)S(1)}, u32[]{:S(2)}, u32[]{:S(2)}) collective-permute-start(f32[12,4,8,128]{3,2,1,0:T(8,128)S(1)} %get-tuple-element.13), channel_id=1, source_target_pairs={{1,6},{4,3},{3,4},{6,1},{5,10},{8,7},{7,8},{10,5},{9,14},{12,11},{... | collective-permute-start | bytes 589832 | tf_op jit(solution)/shard_map/ppermute | solution.py:264
  43.6 1.4 %collective-permute-start.11 = (f32[12,4,8,128]{3,2,1,0:T(8,128)S(1)}, f32[12,4,8,128]{3,2,1,0:T(8,128)S(1)}, u32[]{:S(2)}, u32[]{:S(2)}) collective-permute-start(f32[12,4,8,128]{3,2,1,0:T(8,128)S(1)} %collective-permute-done.10.refs_5_), channel_id=1, source_target_pairs={{0,1},{1,0},{2,3},{3,2},{4,5},{5,4},{6,7},{7,6},{8,9},{9,8},{10,11... | collective-permute-start | bytes 589832 | tf_op jit(solution)/shard_map/ppermute | solution.py:240

commit v3 on v2

--- a/solution.py
+++ b/solution.py
@@ -53,30 +53,37 @@
     return jnp.dot(left, right, precision=highest, preferred_element_type=jnp.float32)
 
 
-def strip_of(block, up):
+def strip_of(tile, up):
     low_half = lax.broadcasted_iota(jnp.int32, (8, 128), 0) < HALF
-    rows = block.shape[0]
+    a, b = tile[:, :128], tile[:, 128:]
     if up:
-        a, b = block[rows - 8 :, :128], block[rows - 8 :, 128:]
         return jnp.where(low_half, pltpu.roll(a, HALF, 0), b)
-    a, b = block[:8, :128], block[:8, 128:]
     return jnp.where(low_half, a, pltpu.roll(b, HALF, 0))
 
 
-def strips_of(block, info, sides):
-    if sides == 2:
-        return [strip_of(block, True), strip_of(block, False)]
-    return [jnp.where(info[1] == 0, strip_of(block, True), strip_of(block, False))]
-
-
-def edge_kernel(sides, info, fields, eps, scaled, *strips):
-    for l in range(eps.shape[0]):
-        scale = courant * eps[l]
-        scaled[l] = scale
+def edge_kernel(depth, rows_own, sides, info, fields, eps, *refs):
+    strips, tiles, sems = refs[:sides], refs[sides], refs[sides + 1]
+    gy = info[1]
+    copies = []
+    for s in range(sides):
+        at = rows_own - 8 if s == 0 else 0
+        if sides == 1:
+            at = pl.multiple_of((1 - gy) * (rows_own - 8), 8)
+        rows = pl.ds(at, 8)
+        copies.append(pltpu.make_async_copy(fields.at[:, :, rows, :], tiles.at[s, pl.ds(0, 12)], sems.at[s, 0]))
+        copies.append(pltpu.make_async_copy(eps.at[:, rows, :], tiles.at[s, 12], sems.at[s, 1]))
+    for copy in copies:
+        copy.start()
+    for copy in copies:
+        copy.wait()
+    for s in range(sides):
         for c in range(13):
-            block = fields[c, l] if c < 12 else scale
-            for s, strip in enumerate(strips_of(block, info, sides)):
-                strips[s][c, l] = strip
+            for l in range(depth):
+                tile = tiles[s, c, l]
+                if sides == 2:
+                    strips[s][c, l] = strip_of(tile, s == 0)
+                else:
+                    strips[s][c, l] = jnp.where(gy == 0, strip_of(tile, True), strip_of(tile, False))
 
 
 def window_kernel(cfg, *refs):
@@ -87,61 +94,66 @@
     full = take(3)
     strip_in = [take(3) for _ in range(sides)]
     if second:
-        (scale_in, acc_in) = take(2)
+        (scale_ref, acc_in) = take(2)
         row_table, col_table, slope, basis_x, basis_xt, basis_y, own_y, response = take(8)
         out, share = take(2)
+        st, strips, acc, done, sem_full, sem_strip, sem_out = take(7)
     else:
         eps_full = take(3)
-        out, scale_out, acc_out = take(3)
+        done, scale_ref, acc = take(3)
         strip_out = take(sides)
-    if second:
-        st, strips, acc, sem_full, sem_strip, sem_out = take(6)
-        scale_ref = scale_in
-    else:
-        st, strips, sem_full, sem_strip, sem_eps, sem_out = take(6)
-        scale_ref = scale_out
-        acc = acc_out
+        st, strips, eps, sem_full, sem_strip, sem_eps = take(6)
 
     core, gy = info[0], info[1]
-    copies = []
-    for b in range(3):
-        place = jnp.where(core == 0, b * depth, (2 - b) * depth)
-        layers = pl.ds(place, depth)
-        copies.append(pltpu.make_async_copy(full[b], st.at[:, layers, pl.ds(0, rows_own), :], sem_full.at[b]))
+
+    def copies_of(b, place):
+        layers = pl.ds(place * depth, depth)
+        found = [pltpu.make_async_copy(full[b], st.at[:, layers, pl.ds(0, rows_own), :], sem_full.at[place])]
         for s in range(sides):
-            copies.append(pltpu.make_async_copy(strip_in[s][b], strips.at[s, :, layers], sem_strip.at[s, b]))
+            found.append(pltpu.make_async_copy(strip_in[s][b], strips.at[s, :, layers], sem_strip.at[s, place]))
         if not second:
-            copies.append(
-                pltpu.make_async_copy(eps_full[b], scale_ref.at[layers, pl.ds(0, rows_own), :], sem_eps.at[b])
-            )
-    for copy in copies:
-        copy.start()
-    for copy in copies:
-        copy.wait()
+            found.append(pltpu.make_async_copy(eps_full[b], eps.at[layers], sem_eps.at[place]))
+        return found
+
+    @pl.when(core == 0)
+    def _():
+        for b in range(3):
+            for copy in copies_of(b, b):
+                copy.start()
+
+    @pl.when(core != 0)
+    def _():
+        for b in (2, 1, 0):
+            for copy in copies_of(b, 2 - b):
+                copy.start()
 
     nx = st.shape[-1]
     rows = st.shape[-2]
     low_half = lax.broadcasted_iota(jnp.int32, (8, 128), 0) < HALF
     low_half_at = jnp.where(low_half, 0, 1)
     n_layers = 3 * depth
-    planes = 12 if second else 13
-    for c in range(planes):
-        for l in range(n_layers):
-            if sides == 2:
-                lo, hi = strips[0, c, l], strips[1, c, l]
-                left = jnp.where(low_half, hi, pltpu.roll(lo, HALF, 0))
-                right = jnp.where(low_half, pltpu.roll(hi, HALF, 0), lo)
-            else:
-                v = strips[0, c, l]
-                w = pltpu.roll(v, HALF, 0)
-                keep = low_half_at == gy
-                left = jnp.where(keep, jnp.where(low_half, v, w), 0.0)
-                right = jnp.where(keep, jnp.where(low_half, w, v), 0.0)
-            tile = jnp.concatenate([left, right], axis=1)
-            if c == 12:
-                scale_ref[l, rows_own:rows, :] = tile
-            else:
-                st[c, l, rows_own:rows, :] = tile
+
+    def arrive(place):
+        for copy in copies_of(place, place):
+            copy.wait()
+        for l in range(place * depth, (place + 1) * depth):
+            for c in range(12 if second else 13):
+                if sides == 2:
+                    lo, hi = strips[0, c, l], strips[1, c, l]
+                    left = jnp.where(low_half, hi, pltpu.roll(lo, HALF, 0))
+                    right = jnp.where(low_half, pltpu.roll(hi, HALF, 0), lo)
+                else:
+                    v = strips[0, c, l]
+                    w = pltpu.roll(v, HALF, 0)
+                    keep = low_half_at == gy
+                    left = jnp.where(keep, jnp.where(low_half, v, w), 0.0)
+                    right = jnp.where(keep, jnp.where(low_half, w, v), 0.0)
+                tile = jnp.concatenate([left, right], axis=1)
+                if c == 12:
+                    scale_ref[l, rows_own:rows, :] = courant * tile
+                    scale_ref[l, :rows_own, :] = courant * eps[l]
+                else:
+                    st[c, l, rows_own:rows, :] = tile
 
     row_at = lax.broadcasted_iota(jnp.int32, (rows, nx), 0)
     lane_at = lax.broadcasted_iota(jnp.int32, (rows, 128), 1)
@@ -170,8 +182,13 @@
         w_re, w_im = math.cos(angle), math.sin(angle)
         prev = [None, None]
         for z in range(m - 1, n_layers - m):
+            if m == 1 and z == 0:
+                arrive(0)
+            if m == 1 and (z + 1) % depth == 0:
+                arrive((z + 1) // depth)
             coef = coef_in * jnp.where((z >= low_layer) & (z < high_layer), 1.0, 0.0)
             scale = scale_ref[z]
+            own = z - depth
             for r in range(2):
                 b = 6 * r
                 ex, ey, ez = st[b, z], st[b + 1, z], st[b + 2, z]
@@ -184,9 +201,20 @@
                     ex = ex + scale * ((hz - y_behind(hz)) - (hy - hy_p))
                     ey = ey + scale * ((hx - hx_p) - (hz - x_behind(hz)))
                     ez = ez + scale * ((hy - x_behind(hy)) - (hx - y_behind(hx)))
-                    st[b, z], st[b + 1, z], st[b + 2, z] = ex, ey, ez
-                    st[b + 3, z], st[b + 4, z], st[b + 5, z] = hx, hy, hz
-                    own = z - depth
+                    for c, f in enumerate((ex, ey, ez, hx, hy, hz)):
+                        if m < HALF:
+                            st[b + c, z] = f
+                            continue
+                        done[b + c, own] = f[:rows_own]
+                        if not second:
+                            up, down = f[rows_own - 8 : rows_own], f[:8]
+                            if sides == 2:
+                                strip_out[0][b + c, own] = strip_of(up, True)
+                                strip_out[1][b + c, own] = strip_of(down, False)
+                            else:
+                                strip_out[0][b + c, own] = jnp.where(
+                                    gy == 0, strip_of(up, True), strip_of(down, False)
+                                )
                     if 0 <= own < depth:
                         for c, e in enumerate((ex, ey, ez)):
                             e = e[:rows_own]
@@ -204,14 +232,9 @@
                     st[b + 3, z], st[b + 4, z] = hx, hy
                 prev[r] = (hx, hy)
 
-    result = pltpu.make_async_copy(st.at[:, pl.ds(depth, depth), pl.ds(0, rows_own), :], out, sem_out)
-    result.start()
-    if not second:
-        for c in range(12):
-            for l in range(depth):
-                for s, strip in enumerate(strips_of(st[c, depth + l, :rows_own, :], info, sides)):
-                    strip_out[s][c, l] = strip
-    else:
+    if second:
+        result = pltpu.make_async_copy(done, out, sem_out)
+        result.start()
         column_sum = jnp.zeros((rows_own, nx), jnp.float32)
         for own in range(depth):
             g = jnp.zeros((rows_own, nx), jnp.float32)
@@ -222,8 +245,22 @@
         sens = mm(row_table[...], mm(column_sum, col_table[...])) * (eps_span / (STEPS * 3 * depth))
         weighted = sens * slope[...]
         spectrum = mm(own_y[...], mm(weighted, basis_xt[...])) * response[...]
-        share[...] = mm(basis_y[...], mm(spectrum, basis_x[...]))
-    result.wait()
+        shares = mm(basis_y[...], mm(spectrum, basis_x[...]))
+        count, band, _ = share.shape
+        n_gy = shares.shape[0] // band
+        for d in range(count):
+            y = d // 2 % n_gy
+            share[d] = shares[y * band : (y + 1) * band]
+        result.wait()
+
+
+def sum_kernel(info, got, out):
+    total = got[0]
+    for d in range(1, got.shape[0]):
+        total = total + got[d]
+    width = out.shape[1]
+    columns = total.shape[1]
+    out[...] = pltpu.roll(total, lax.rem(columns - info[7], columns), 1)[:, :width]
 
 
 def body(fields, eps_inv, row_counts, col_counts, density):
@@ -255,14 +292,6 @@
     def along_y(x, s):
         return lax.ppermute(x, "gy", list(ways[s].items()))
 
-    def across(x, s):
-        pairs = []
-        for c in range(n_gz - 1):
-            for y, to in ways[s].items():
-                for src, dst in (((c, y, 1), (c + 1, to, 0)), ((c + 1, y, 0), (c, to, 1))):
-                    pairs.append(tuple((p[0] * n_gy + p[1]) * 2 + p[2] for p in (src, dst)))
-        return lax.ppermute(x, ("gz", "gy", "col"), pairs)
-
     layer_start = depth * n_z // 2 - depth - depth // 2
     info = [
         core,
@@ -272,6 +301,7 @@
         jnp.where(gy < n_gy - 1, 1, 0),
         jnp.where(gy > 0, 1, 0),
         index * depth - layer_start,
+        index * (density.shape[1] // n_z),
     ]
     info = jnp.stack([jnp.asarray(v, jnp.int32) for v in info])
 
@@ -285,19 +315,26 @@
         sent = []
         for s, strip in enumerate(strips):
             mine = along_y(strip, s)
-            sent += [across(strip, s), mine, swap_core(mine)]
+            sent += [cross(mine), mine, swap_core(mine)]
         return sent
 
-    full = [cross(own), own, swap_core(own)]
-    scaled, *strips = pl.pallas_call(
-        functools.partial(edge_kernel, sides),
-        out_shape=(shape(depth, rows_own, nx),) + (shape(13, depth, 8, 128),) * sides,
-        in_specs=[smem, vmem, vmem],
-        out_specs=(vmem,) * (1 + sides),
+    strips = pl.pallas_call(
+        functools.partial(edge_kernel, depth, rows_own, sides),
+        out_shape=(shape(13, depth, 8, 128),) * sides,
+        in_specs=[smem, anywhere, anywhere],
+        out_specs=(vmem,) * sides,
+        scratch_shapes=[
+            pltpu.VMEM((sides, 13, depth, 8, nx), jnp.float32),
+            pltpu.SemaphoreType.DMA((sides, 2)),
+        ],
         compiler_params=limit,
     )(info, own, eps_inv)
-    operands = [info] + full + strips_sent(strips) + [cross(scaled), scaled, swap_core(scaled)]
+    operands = [info, cross(own), own, swap_core(own)] + strips_sent(strips)
+    operands += [cross(eps_inv), eps_inv, swap_core(eps_inv)]
     cost = pl.CostEstimate(flops=20_000_000, bytes_accessed=4_000_000, transcendentals=0)
+    window = pltpu.VMEM((12, 3 * depth, rows, nx), jnp.float32)
+    block = pltpu.VMEM((12, depth, rows_own, nx), jnp.float32)
+    arrivals = [pltpu.SemaphoreType.DMA((3,)), pltpu.SemaphoreType.DMA((sides, 3))]
     state, scale, acc, *strips = pl.pallas_call(
         functools.partial(window_kernel, (depth, rows_own, sides, False)),
         out_shape=(
@@ -307,15 +344,14 @@
         )
         + (shape(12, depth, 8, 128),) * sides,
         in_specs=[smem] + [anywhere] * (6 + 3 * sides),
-        out_specs=(anywhere, vmem, vmem) + (vmem,) * sides,
+        out_specs=(vmem, vmem, vmem) + (vmem,) * sides,
         scratch_shapes=[
-            pltpu.VMEM((12, 3 * depth, rows, nx), jnp.float32),
+            window,
             pltpu.VMEM((sides, 13, 3 * depth, 8, 128), jnp.float32),
-            pltpu.SemaphoreType.DMA((3,)),
-            pltpu.SemaphoreType.DMA((sides, 3)),
-            pltpu.SemaphoreType.DMA((3,)),
-            pltpu.SemaphoreType.DMA,
-        ],
+            pltpu.VMEM((3 * depth, rows_own, nx), jnp.float32),
+        ]
+        + arrivals
+        + [pltpu.SemaphoreType.DMA((3,))],
         compiler_params=limit,
         cost_estimate=cost,
     )(*operands)
@@ -338,28 +374,31 @@
     own_y = lax.dynamic_slice_in_dim(const(basis_y), gy * band, band, 1)
     operands = [info, cross(state), state, swap_core(state)] + strips_sent(strips) + [scale, acc]
     operands += [row_table, col_table, slope_of(density), const(basis_x), const(basis_x.T), const(basis_y.T), own_y, const(response)]
+    n_all = n_z * n_gy
     fields_out, share = pl.pallas_call(
         functools.partial(window_kernel, (depth, rows_own, sides, True)),
-        out_shape=(shape(runs * comps, depth, rows_own, nx), shape(tall, design_cols)),
+        out_shape=(shape(runs * comps, depth, rows_own, nx), shape(n_all, band, design_cols)),
         in_specs=[smem] + [anywhere] * (3 + 3 * sides) + [vmem] * 10,
         out_specs=(anywhere, vmem),
         scratch_shapes=[
-            pltpu.VMEM((12, 3 * depth, rows, nx), jnp.float32),
+            window,
             pltpu.VMEM((sides, 12, 3 * depth, 8, 128), jnp.float32),
             pltpu.VMEM((2, 6, depth, rows_own, nx), jnp.float32),
-            pltpu.SemaphoreType.DMA((3,)),
-            pltpu.SemaphoreType.DMA((sides, 3)),
-            pltpu.SemaphoreType.DMA,
-        ],
+            block,
+        ]
+        + arrivals
+        + [pltpu.SemaphoreType.DMA],
         compiler_params=limit,
         cost_estimate=cost,
     )(*operands)
 
-    width = design_cols // n_z
-    blocks = share.reshape(n_gy, band, n_gz, 2, width).transpose(2, 0, 3, 1, 4)
-    blocks = blocks.reshape(n_gz * n_gy * 2, band, width)
-    got = lax.all_to_all(blocks, ("gz", "gy", "col"), 0, 0)
-    gradient = jnp.sum(got, axis=0)
+    got = lax.all_to_all(share, ("gz", "gy", "col"), 0, 0)
+    gradient = pl.pallas_call(
+        sum_kernel,
+        out_shape=shape(band, design_cols // n_z),
+        in_specs=[smem, vmem],
+        out_specs=vmem,
+    )(info, got)
     return fields_out.reshape(fields.shape), gradient
 
 

time: 68.5 us -> 66.5 us (0.971)
  waiting for transfers between devices: 7.43 us -> 4.01 us
  blocking collectives: 16.2 us -> 19.4 us
  Pallas kernels: 11.8 us -> 14.5 us
  local copies, waits for them, and re-layouts: 4.4 us -> 2.76 us
  starting transfers between devices: 25.6 us -> 24 us
  other arithmetic: 1.85 us -> 0.57 us
    all_to_all x1, blocking collectives: 16.2 us -> 19.4 us  [body(): got = lax.all_to_all(share, ('gz', 'gy', 'col'), 0, 0)]
    ppermute x5, starting transfers between devices: 19.1 us -> 15.9 us  [swap_core(): return lax.ppermute(x, 'col', [(0, 1), (1, 0)])]
    ppermute x2, waiting for transfers between devices: 6.04 us -> 3.65 us  [along_y(): return lax.ppermute(x, 'gy', list(ways[s].items()))]
    pallas_call x1 -> x2, Pallas kernels: 0.58 us -> 2.91 us  [the longest x1 1.52 us: body(): pl.pallas_call(sum_kernel, out_shape=shape(band, design_cols // n_z), in_...]
    ppermute x2, starting transfers between devices: 3.11 us -> 4.66 us  [along_y(): return lax.ppermute(x, 'gy', list(ways[s].items()))]
    ppermute x2 -> x0, starting transfers between devices: 1.32 us -> none  [across(): return lax.ppermute(x, ('gz', 'gy', 'col'), pairs)]
    ppermute x3 -> x5, starting transfers between devices: 2.07 us -> 3.37 us  [cross(): return lax.ppermute(x, Z, pairs)]
    ppermute x5, waiting for transfers between devices: 1.37 us -> 0.34 us  [swap_core(): return lax.ppermute(x, 'col', [(0, 1), (1, 0)])]
  transfers between devices with their start and end apart: 12 -> 12, of which waited for: 3 -> 2; matrix products, arithmetic and copies ran while one was open for 1% -> 1% of each run, Pallas kernels for 1% -> 2%
where the time goes in v3:
time: 66.5 us; the launch traced here: 66.1 us
  starting transfers between devices  24 us (36%)
  blocking collectives  19.4 us (29%)
  Pallas kernels  14.5 us (22%)
  waiting for transfers between devices  4.01 us (6%)
  local copies, waits for them, and re-layouts  2.76 us (4%)
  between operations  0.89 us (1%)
    all_to_all x1, blocking collectives, body(): got = lax.all_to_all(share, ('gz', 'gy', 'col'), 0, 0)  19.4 us
    ppermute x5, starting transfers between devices, swap_core(): return lax.ppermute(x, 'col', [(0, 1), (1, 0)])  15.9 us
    pallas_call x2, Pallas kernels, body(): pl.pallas_call(functools.partial(window_kernel, (depth, rows_own, sides,...  11.6 us
    ppermute x2, starting transfers between devices, along_y(): return lax.ppermute(x, 'gy', list(ways[s].items()))  4.66 us
    ppermute x2, waiting for transfers between devices, along_y(): return lax.ppermute(x, 'gy', list(ways[s].items()))  3.65 us
    ppermute x5, starting transfers between devices, cross(): return lax.ppermute(x, Z, pairs)  3.37 us
    unnamed x22, local copies, waits for them, and re-layouts  2.48 us
    pallas_call x1, Pallas kernels, body(): pl.pallas_call(sum_kernel, out_shape=shape(band, design_cols // n_z), in_...  1.52 us
  transfers between devices with their start and end apart: 12, of which 2 were waited for; matrix products, arithmetic and copies ran while one was open for 1% of the time, Pallas kernels for 2%

profile of v3, /device:TPU:0, one launch (start us, length us, event | category | flops | bytes accessed | tf_op | source)
XLA Modules:
  0.0 66.1 jit_solution(4517118156777056994)
XLA Ops:
  0.6 0.5 collective-permute-start.1
  1.1 0.7 %collective-permute-start = (f32[12,4,16,256]{3,2,1,0:T(8,128)}, f32[12,4,16,256]{3,2,1,0:T(8,128)S(1)}, u32[]{:S(2)}, u32[]{:S(2)}) collective-permute-start(f32[12,4,16,256]{3,2,1,0:T(8,128)} %bitcast.20), channel_id=1, source_target_pairs={{1,4},{4,1},{5,8},{8,5},{9,12},{12,9},{3,6},{6,3},{7,10},{10,7},{1... | collective-permute-start | bytes 2359304 | tf_op jit(solution)/shard_map/ppermute | solution.py:284
  1.9 0.1 stack.35.info.refs_0_
  2.0 0.0 copy-start
  2.0 1.1 %copy-done = f32[2,6,4,16,256]{4,3,2,1,0:T(8,128)S(1)} copy-done((f32[2,6,4,16,256]{4,3,2,1,0:T(8,128)S(1)}, f32[2,6,4,16,256]{4,3,2,1,0:T(8,128)}, u32[]{:S(2)}) %copy-start) | copy-done | bytes 786456
  3.1 0.0 copy-start.4
  3.1 0.0 copy-start.8
  3.1 0.0 copy-start.1
  3.1 1.4 %shard_map.113 = f32[13,4,8,128]{3,2,1,0:T(8,128)S(1)} custom-call(s32[8]{0:T(128)S(1)} %stack.35.info.refs_0_, f32[12,4,16,256]{3,2,1,0:T(8,128)S(1)} %bitcast.21, f32[4,16,256]{2,1,0:T(8,128)} %refs_8_.1), custom_call_target="tpu_custom_call" | custom-call | tf_op jit(solution)/shard_map/pallas_call | solution.py:321
  4.5 2.6 %collective-permute-start.2 = (f32[13,4,8,128]{3,2,1,0:T(8,128)S(1)}, f32[13,4,8,128]{3,2,1,0:T(8,128)S(1)}, u32[]{:S(2)}, u32[]{:S(2)}) collective-permute-start(f32[13,4,8,128]{3,2,1,0:T(8,128)S(1)} %shard_map.113), channel_id=1, source_target_pairs={{0,2},{2,0},{1,3},{3,1},{4,6},{6,4},{5,7},{7,5},{8,10},{10,8},{9,1... | collective-permute-start | bytes 638984 | tf_op jit(solution)/shard_map/ppermute | solution.py:293
  7.1 0.7 collective-permute-start.5
  7.7 4.7 %collective-permute-start.6 = (f32[4,16,256]{2,1,0:T(8,128)}, f32[4,16,256]{2,1,0:T(8,128)S(1)}, u32[]{:S(2)}, u32[]{:S(2)}) collective-permute-start(f32[4,16,256]{2,1,0:T(8,128)} %refs_8_.1), channel_id=1, source_target_pairs={{0,1},{1,0},{2,3},{3,2},{4,5},{5,4},{6,7},{7,6},{8,9},{9,8},{10,11... | collective-permute-start | bytes 196616 | tf_op jit(solution)/shard_map/ppermute | solution.py:277
  12.5 0.0 collective-permute-done.2.refs_5_
  12.5 0.7 %collective-permute-start.4 = (f32[13,4,8,128]{3,2,1,0:T(8,128)S(1)}, f32[13,4,8,128]{3,2,1,0:T(8,128)S(1)}, u32[]{:S(2)}, u32[]{:S(2)}) collective-permute-start(f32[13,4,8,128]{3,2,1,0:T(8,128)S(1)} %collective-permute-done.2.refs_5_), channel_id=1, source_target_pairs={{0,1},{1,0},{2,3},{3,2},{4,5},{5,4},{6,7},{7,6},{8,9},{9,8},{10,11... | collective-permute-start | bytes 638984 | tf_op jit(solution)/shard_map/ppermute | solution.py:277
  13.2 0.0 collective-permute-done.5.refs_7_
  13.2 0.7 %collective-permute-start.3 = (f32[13,4,8,128]{3,2,1,0:T(8,128)S(1)}, f32[13,4,8,128]{3,2,1,0:T(8,128)S(1)}, u32[]{:S(2)}, u32[]{:S(2)}) collective-permute-start(f32[13,4,8,128]{3,2,1,0:T(8,128)S(1)} %collective-permute-done.2.refs_5_), channel_id=1, source_target_pairs={{1,4},{4,1},{5,8},{8,5},{9,12},{12,9},{3,6},{6,3},{7,10},{10,7},{1... | collective-permute-start | bytes 638984 | tf_op jit(solution)/shard_map/ppermute | solution.py:284
  13.8 0.0 copy-done.8
  13.9 0.0 copy-start.10
  13.9 0.6 copy-done.10
  14.5 0.2 reduce-window.13
  14.7 0.0 copy-start.9
  14.7 0.7 copy-done.9
  15.4 0.1 copy.13
  15.5 0.2 reduce-window.14
  15.6 0.1 reduce
  15.8 0.0 copy-start.7
  15.8 0.0 collective-permute-done.6.refs_9_
  15.8 0.0 collective-permute-done.4.refs_6_
  15.8 0.0 collective-permute-done.3.refs_4_
  15.8 0.0 collective-permute-done.1.refs_3_
  15.8 0.0 collective-permute-done.refs_1_
  15.8 0.0 copy-done.1
  15.8 6.2 %shard_map.114 = (f32[12,4,16,256]{3,2,1,0:T(8,128)S(1)}, f32[12,24,256]{2,1,0:T(8,128)S(1)}, f32[2,6,4,16,256]{4,3,2,1,0:T(8,128)S(1)}, f32[12,4,8,128]{3,2,1,0:T(8,128)S(1)}) custom-call(s32[8]{0:T(128)S(1)} %stack.35.info.refs_0_, f32[12,4,16,256]{3,2,1,0:T(8,128)S(1)} %collective-permute-done.refs_1_, f32[12,4,16,256]{3,2,1,0:T(8,128)S(1)} %bitcast.22, ...), custom_call_target="tpu_custom_call" | custom-call | flops 20000000 | bytes 4000000 | tf_op jit(solution)/shard_map/pallas_call | solution.py:338
  22.0 7.7 %collective-permute-start.8 = (f32[12,4,16,256]{3,2,1,0:T(8,128)S(1)}, f32[12,4,16,256]{3,2,1,0:T(8,128)S(1)}, u32[]{:S(2)}, u32[]{:S(2)}) collective-permute-start(f32[12,4,16,256]{3,2,1,0:T(8,128)S(1)} %get-tuple-element.8.refs_2_), channel_id=1, source_target_pairs={{0,1},{1,0},{2,3},{3,2},{4,5},{5,4},{6,7},{7,6},{8,9},{9,8},{10,11... | collective-permute-start | bytes 2359304 | tf_op jit(solution)/shard_map/ppermute | solution.py:277
  29.8 0.7 %collective-permute-start.7 = (f32[12,4,16,256]{3,2,1,0:T(8,128)S(1)}, f32[12,4,16,256]{3,2,1,0:T(8,128)S(1)}, u32[]{:S(2)}, u32[]{:S(2)}) collective-permute-start(f32[12,4,16,256]{3,2,1,0:T(8,128)S(1)} %get-tuple-element.8.refs_2_), channel_id=1, source_target_pairs={{1,4},{4,1},{5,8},{8,5},{9,12},{12,9},{3,6},{6,3},{7,10},{10,7},{1... | collective-permute-start | bytes 2359304 | tf_op jit(solution)/shard_map/ppermute | solution.py:284
  30.5 0.0 copy-done.7
  30.5 0.0 copy-start.6
  30.5 0.1 constant_dynamic-slice_fusion.refs_15_
  30.6 0.0 copy-start.2
  30.6 0.0 copy-start.3
  30.6 0.0 copy-start.5
  30.6 2.1 %collective-permute-start.9 = (f32[12,4,8,128]{3,2,1,0:T(8,128)S(1)}, f32[12,4,8,128]{3,2,1,0:T(8,128)S(1)}, u32[]{:S(2)}, u32[]{:S(2)}) collective-permute-start(f32[12,4,8,128]{3,2,1,0:T(8,128)S(1)} %get-tuple-element.9), channel_id=1, source_target_pairs={{0,2},{2,0},{1,3},{3,1},{4,6},{6,4},{5,7},{7,5},{8,10},{10,8},{9,1... | collective-permute-start | bytes 589832 | tf_op jit(solution)/shard_map/ppermute | solution.py:293
  32.7 3.6 %collective-permute-done.9.refs_5_ = f32[12,4,8,128]{3,2,1,0:T(8,128)S(1)} collective-permute-done((f32[12,4,8,128]{3,2,1,0:T(8,128)S(1)}, f32[12,4,8,128]{3,2,1,0:T(8,128)S(1)}, u32[]{:S(2)}, u32[]{:S(2)}) %collective-permute-start.9) | collective-permute-done | bytes 196640 | tf_op jit(solution)/shard_map/ppermute | solution.py:293
  36.4 2.3 %collective-permute-start.11 = (f32[12,4,8,128]{3,2,1,0:T(8,128)S(1)}, f32[12,4,8,128]{3,2,1,0:T(8,128)S(1)}, u32[]{:S(2)}, u32[]{:S(2)}) collective-permute-start(f32[12,4,8,128]{3,2,1,0:T(8,128)S(1)} %collective-permute-done.9.refs_5_), channel_id=1, source_target_pairs={{0,1},{1,0},{2,3},{3,2},{4,5},{5,4},{6,7},{7,6},{8,9},{9,8},{10,11... | collective-permute-start | bytes 589832 | tf_op jit(solution)/shard_map/ppermute | solution.py:277
  38.6 0.7 %collective-permute-start.10 = (f32[12,4,8,128]{3,2,1,0:T(8,128)S(1)}, f32[12,4,8,128]{3,2,1,0:T(8,128)S(1)}, u32[]{:S(2)}, u32[]{:S(2)}) collective-permute-start(f32[12,4,8,128]{3,2,1,0:T(8,128)S(1)} %collective-permute-done.9.refs_5_), channel_id=1, source_target_pairs={{1,4},{4,1},{5,8},{8,5},{9,12},{12,9},{3,6},{6,3},{7,10},{10,7},{1... | collective-permute-start | bytes 589832 | tf_op jit(solution)/shard_map/ppermute | solution.py:284
  39.3 0.1 fusion.3.refs_9_
  39.4 0.3 collective-permute-done.11.refs_6_
  39.7 0.0 collective-permute-done.10.refs_4_
  39.7 0.0 collective-permute-done.8.refs_3_
  39.7 0.0 collective-permute-done.7.refs_1_
  39.7 0.0 copy-done.4
  39.7 0.0 copy-done.6
  39.7 0.0 copy-done.2
  39.7 0.0 copy-done.3
  39.7 0.0 copy-done.5
  39.8 5.4 %shard_map.115 = (f32[12,4,16,256]{3,2,1,0:T(8,128)}, f32[16,8,128]{2,1,0:T(8,128)S(1)}) custom-call(s32[8]{0:T(128)S(1)} %stack.35.info.refs_0_, f32[12,4,16,256]{3,2,1,0:T(8,128)S(1)} %collective-permute-done.7.refs_1_, f32[12,4,16,256]{3,2,1,0:T(8,128)S(1)} %get-tuple-element.8.refs_2_, f32[12,4,16,256]{3,2,1,0:T(8,128)S(1)} %collective-permute-done.8.refs_3_, ...), custom_call_target="tpu_custom_call" | custom-call | flops 20000000 | bytes 4000000 | tf_op jit(solution)/shard_map/pallas_call | solution.py:378
  45.2 19.4 %all_to_all.5.got = f32[16,8,128]{2,1,0:T(8,128)} all-to-all(f32[16,8,128]{2,1,0:T(8,128)S(1)} %get-tuple-element.13), channel_id=1, replica_groups=mesh['groups'=2,'gz'=4,'gy'=2,'col'=2] {'gz','gy','col'}, dimensions={0} | all-to-all | bytes 131072 | tf_op jit(solution)/shard_map/all_to_all | solution.py:395
  64.6 1.5 %shard_map.116 = f32[8,16]{1,0:T(8,128)} custom-call(s32[8]{0:T(128)} %copy-done.4, f32[16,8,128]{2,1,0:T(8,128)} %all_to_all.5.got), custom_call_target="tpu_custom_call" | custom-call | tf_op jit(solution)/shard_map/pallas_call | solution.py:396
  (4 shorter events, 0.0 us)
Async XLA Ops:
  0.6 15.2 %collective-permute-start.1 = (f32[12,4,16,256]{3,2,1,0:T(8,128)}, f32[12,4,16,256]{3,2,1,0:T(8,128)S(1)}, u32[]{:S(2)}, u32[]{:S(2)}) collective-permute-start(f32[12,4,16,256]{3,2,1,0:T(8,128)} %bitcast.19), channel_id=1, source_target_pairs={{0,1},{1,0},{2,3},{3,2},{4,5},{5,4},{6,7},{7,6},{8,9},{9,8},{10,11... | collective-permute-start | bytes 2359304 | tf_op jit(solution)/shard_map/ppermute | solution.py:277
  1.1 14.7 %collective-permute-start = (f32[12,4,16,256]{3,2,1,0:T(8,128)}, f32[12,4,16,256]{3,2,1,0:T(8,128)S(1)}, u32[]{:S(2)}, u32[]{:S(2)}) collective-permute-start(f32[12,4,16,256]{3,2,1,0:T(8,128)} %bitcast.20), channel_id=1, source_target_pairs={{1,4},{4,1},{5,8},{8,5},{9,12},{12,9},{3,6},{6,3},{7,10},{10,7},{1... | collective-permute-start | bytes 2359304 | tf_op jit(solution)/shard_map/ppermute | solution.py:284
  2.0 1.1 %copy-start = (f32[2,6,4,16,256]{4,3,2,1,0:T(8,128)S(1)}, f32[2,6,4,16,256]{4,3,2,1,0:T(8,128)}, u32[]{:S(2)}) copy-start(f32[2,6,4,16,256]{4,3,2,1,0:T(8,128)} %param.10) | copy-start | bytes 2359300
  3.1 36.6 %copy-start.4 = (s32[8]{0:T(128)}, s32[8]{0:T(128)S(1)}, u32[]{:S(2)}) copy-start(s32[8]{0:T(128)S(1)} %stack.35.info.refs_0_) | copy-start | bytes 100
  3.1 10.7 %copy-start.8 = (f32[8,128]{1,0:T(8,128)S(1)}, f32[8,128]{1,0:T(8,128)}, u32[]{:S(2)}) copy-start(f32[8,128]{1,0:T(8,128)} %param.14) | copy-start | bytes 12292
  3.1 12.7 %copy-start.1 = (f32[2,6,4,16,256]{4,3,2,1,0:T(8,128)S(1)}, f32[2,6,4,16,256]{4,3,2,1,0:T(8,128)}, u32[]{:S(2)}) copy-start(f32[2,6,4,16,256]{4,3,2,1,0:T(8,128)} %param.10) | copy-start | bytes 2359300
  4.5 8.0 %collective-permute-start.2 = (f32[13,4,8,128]{3,2,1,0:T(8,128)S(1)}, f32[13,4,8,128]{3,2,1,0:T(8,128)S(1)}, u32[]{:S(2)}, u32[]{:S(2)}) collective-permute-start(f32[13,4,8,128]{3,2,1,0:T(8,128)S(1)} %shard_map.113), channel_id=1, source_target_pairs={{0,2},{2,0},{1,3},{3,1},{4,6},{6,4},{5,7},{7,5},{8,10},{10,8},{9,1... | collective-permute-start | bytes 638984 | tf_op jit(solution)/shard_map/ppermute | solution.py:293
  7.1 6.1 %collective-permute-start.5 = (f32[4,16,256]{2,1,0:T(8,128)}, f32[4,16,256]{2,1,0:T(8,128)S(1)}, u32[]{:S(2)}, u32[]{:S(2)}) collective-permute-start(f32[4,16,256]{2,1,0:T(8,128)} %refs_8_.1), channel_id=1, source_target_pairs={{1,4},{4,1},{5,8},{8,5},{9,12},{12,9},{3,6},{6,3},{7,10},{10,7},{1... | collective-permute-start | bytes 196616 | tf_op jit(solution)/shard_map/ppermute | solution.py:284
  7.7 8.0 %collective-permute-start.6 = (f32[4,16,256]{2,1,0:T(8,128)}, f32[4,16,256]{2,1,0:T(8,128)S(1)}, u32[]{:S(2)}, u32[]{:S(2)}) collective-permute-start(f32[4,16,256]{2,1,0:T(8,128)} %refs_8_.1), channel_id=1, source_target_pairs={{0,1},{1,0},{2,3},{3,2},{4,5},{5,4},{6,7},{7,6},{8,9},{9,8},{10,11... | collective-permute-start | bytes 196616 | tf_op jit(solution)/shard_map/ppermute | solution.py:277
  12.5 3.3 %collective-permute-start.4 = (f32[13,4,8,128]{3,2,1,0:T(8,128)S(1)}, f32[13,4,8,128]{3,2,1,0:T(8,128)S(1)}, u32[]{:S(2)}, u32[]{:S(2)}) collective-permute-start(f32[13,4,8,128]{3,2,1,0:T(8,128)S(1)} %collective-permute-done.2.refs_5_), channel_id=1, source_target_pairs={{0,1},{1,0},{2,3},{3,2},{4,5},{5,4},{6,7},{7,6},{8,9},{9,8},{10,11... | collective-permute-start | bytes 638984 | tf_op jit(solution)/shard_map/ppermute | solution.py:277
  13.2 2.6 %collective-permute-start.3 = (f32[13,4,8,128]{3,2,1,0:T(8,128)S(1)}, f32[13,4,8,128]{3,2,1,0:T(8,128)S(1)}, u32[]{:S(2)}, u32[]{:S(2)}) collective-permute-start(f32[13,4,8,128]{3,2,1,0:T(8,128)S(1)} %collective-permute-done.2.refs_5_), channel_id=1, source_target_pairs={{1,4},{4,1},{5,8},{8,5},{9,12},{12,9},{3,6},{6,3},{7,10},{10,7},{1... | collective-permute-start | bytes 638984 | tf_op jit(solution)/shard_map/ppermute | solution.py:284
  13.9 0.7 copy-start.10
  14.7 0.7 copy-start.9
  15.8 14.7 %copy-start.7 = (f32[16,16]{1,0:T(8,128)S(1)}, f32[16,16]{1,0:T(8,128)}, u32[]{:S(2)}) copy-start(f32[16,16]{1,0:T(8,128)} %constant.56.clone) | copy-start | bytes 3076
  22.0 17.7 %collective-permute-start.8 = (f32[12,4,16,256]{3,2,1,0:T(8,128)S(1)}, f32[12,4,16,256]{3,2,1,0:T(8,128)S(1)}, u32[]{:S(2)}, u32[]{:S(2)}) collective-permute-start(f32[12,4,16,256]{3,2,1,0:T(8,128)S(1)} %get-tuple-element.8.refs_2_), channel_id=1, source_target_pairs={{0,1},{1,0},{2,3},{3,2},{4,5},{5,4},{6,7},{7,6},{8,9},{9,8},{10,11... | collective-permute-start | bytes 2359304 | tf_op jit(solution)/shard_map/ppermute | solution.py:277
  29.8 9.9 %collective-permute-start.7 = (f32[12,4,16,256]{3,2,1,0:T(8,128)S(1)}, f32[12,4,16,256]{3,2,1,0:T(8,128)S(1)}, u32[]{:S(2)}, u32[]{:S(2)}) collective-permute-start(f32[12,4,16,256]{3,2,1,0:T(8,128)S(1)} %get-tuple-element.8.refs_2_), channel_id=1, source_target_pairs={{1,4},{4,1},{5,8},{8,5},{9,12},{12,9},{3,6},{6,3},{7,10},{10,7},{1... | collective-permute-start | bytes 2359304 | tf_op jit(solution)/shard_map/ppermute | solution.py:284
  30.5 9.2 %copy-start.6 = (f32[16,16]{1,0:T(8,128)S(1)}, f32[16,16]{1,0:T(8,128)}, u32[]{:S(2)}) copy-start(f32[16,16]{1,0:T(8,128)} %constant.59.clone.refs_14_) | copy-start | bytes 3076
  30.6 9.2 %copy-start.2 = (f32[128,128]{1,0:T(8,128)S(1)}, f32[128,128]{1,0:T(8,128)}, u32[]{:S(2)}) copy-start(f32[128,128]{1,0:T(8,128)} %constant.58.clone.refs_13_) | copy-start | bytes 196612
  30.6 9.2 %copy-start.3 = (f32[128,128]{1,0:T(8,128)S(1)}, f32[128,128]{1,0:T(8,128)}, u32[]{:S(2)}) copy-start(f32[128,128]{1,0:T(8,128)} %constant.57.clone.refs_12_) | copy-start | bytes 196612
  30.6 9.1 %copy-start.5 = (f32[16,128]{1,0:T(8,128)S(1)}, f32[16,128]{1,0:T(8,128)}, u32[]{:S(2)}) copy-start(f32[16,128]{1,0:T(8,128)} %constant.60.clone.refs_16_) | copy-start | bytes 24580
  30.6 5.7 %collective-permute-start.9 = (f32[12,4,8,128]{3,2,1,0:T(8,128)S(1)}, f32[12,4,8,128]{3,2,1,0:T(8,128)S(1)}, u32[]{:S(2)}, u32[]{:S(2)}) collective-permute-start(f32[12,4,8,128]{3,2,1,0:T(8,128)S(1)} %get-tuple-element.9), channel_id=1, source_target_pairs={{0,2},{2,0},{1,3},{3,1},{4,6},{6,4},{5,7},{7,5},{8,10},{10,8},{9,1... | collective-permute-start | bytes 589832 | tf_op jit(solution)/shard_map/ppermute | solution.py:293
  36.4 3.3 %collective-permute-start.11 = (f32[12,4,8,128]{3,2,1,0:T(8,128)S(1)}, f32[12,4,8,128]{3,2,1,0:T(8,128)S(1)}, u32[]{:S(2)}, u32[]{:S(2)}) collective-permute-start(f32[12,4,8,128]{3,2,1,0:T(8,128)S(1)} %collective-permute-done.9.refs_5_), channel_id=1, source_target_pairs={{0,1},{1,0},{2,3},{3,2},{4,5},{5,4},{6,7},{7,6},{8,9},{9,8},{10,11... | collective-permute-start | bytes 589832 | tf_op jit(solution)/shard_map/ppermute | solution.py:277
  38.6 1.1 %collective-permute-start.10 = (f32[12,4,8,128]{3,2,1,0:T(8,128)S(1)}, f32[12,4,8,128]{3,2,1,0:T(8,128)S(1)}, u32[]{:S(2)}, u32[]{:S(2)}) collective-permute-start(f32[12,4,8,128]{3,2,1,0:T(8,128)S(1)} %collective-permute-done.9.refs_5_), channel_id=1, source_target_pairs={{1,4},{4,1},{5,8},{8,5},{9,12},{12,9},{3,6},{6,3},{7,10},{10,7},{1... | collective-permute-start | bytes 589832 | tf_op jit(solution)/shard_map/ppermute | solution.py:284

commit v4 on v3

--- a/solution.py
+++ b/solution.py
@@ -59,31 +59,6 @@
     if up:
         return jnp.where(low_half, pltpu.roll(a, HALF, 0), b)
     return jnp.where(low_half, a, pltpu.roll(b, HALF, 0))
-
-
-def edge_kernel(depth, rows_own, sides, info, fields, eps, *refs):
-    strips, tiles, sems = refs[:sides], refs[sides], refs[sides + 1]
-    gy = info[1]
-    copies = []
-    for s in range(sides):
-        at = rows_own - 8 if s == 0 else 0
-        if sides == 1:
-            at = pl.multiple_of((1 - gy) * (rows_own - 8), 8)
-        rows = pl.ds(at, 8)
-        copies.append(pltpu.make_async_copy(fields.at[:, :, rows, :], tiles.at[s, pl.ds(0, 12)], sems.at[s, 0]))
-        copies.append(pltpu.make_async_copy(eps.at[:, rows, :], tiles.at[s, 12], sems.at[s, 1]))
-    for copy in copies:
-        copy.start()
-    for copy in copies:
-        copy.wait()
-    for s in range(sides):
-        for c in range(13):
-            for l in range(depth):
-                tile = tiles[s, c, l]
-                if sides == 2:
-                    strips[s][c, l] = strip_of(tile, s == 0)
-                else:
-                    strips[s][c, l] = jnp.where(gy == 0, strip_of(tile, True), strip_of(tile, False))
 
 
 def window_kernel(cfg, *refs):
@@ -99,10 +74,9 @@
         out, share = take(2)
         st, strips, acc, done, sem_full, sem_strip, sem_out = take(7)
     else:
-        eps_full = take(3)
         done, scale_ref, acc = take(3)
         strip_out = take(sides)
-        st, strips, eps, sem_full, sem_strip, sem_eps = take(6)
+        st, strips, sem_full, sem_strip = take(4)
 
     core, gy = info[0], info[1]
 
@@ -110,9 +84,8 @@
         layers = pl.ds(place * depth, depth)
         found = [pltpu.make_async_copy(full[b], st.at[:, layers, pl.ds(0, rows_own), :], sem_full.at[place])]
         for s in range(sides):
-            found.append(pltpu.make_async_copy(strip_in[s][b], strips.at[s, :, layers], sem_strip.at[s, place]))
-        if not second:
-            found.append(pltpu.make_async_copy(eps_full[b], eps.at[layers], sem_eps.at[place]))
+            planes = pl.ds(0, strip_in[s][b].shape[0])
+            found.append(pltpu.make_async_copy(strip_in[s][b], strips.at[s, planes, layers], sem_strip.at[s, place]))
         return found
 
     @pl.when(core == 0)
@@ -151,7 +124,9 @@
                 tile = jnp.concatenate([left, right], axis=1)
                 if c == 12:
                     scale_ref[l, rows_own:rows, :] = courant * tile
-                    scale_ref[l, :rows_own, :] = courant * eps[l]
+                    for t in range(2):
+                        pair = [strips[0, 13 + 2 * t + half, l] for half in range(2)]
+                        scale_ref[l, 8 * t : 8 * t + 8, :] = courant * jnp.concatenate(pair, axis=1)
                 else:
                     st[c, l, rows_own:rows, :] = tile
 
@@ -180,57 +155,55 @@
     for m in range(1, HALF + 1):
         angle = omega_step * (m + (HALF if second else 0))
         w_re, w_im = math.cos(angle), math.sin(angle)
-        prev = [None, None]
         for z in range(m - 1, n_layers - m):
             if m == 1 and z == 0:
                 arrive(0)
             if m == 1 and (z + 1) % depth == 0:
                 arrive((z + 1) // depth)
             coef = coef_in * jnp.where((z >= low_layer) & (z < high_layer), 1.0, 0.0)
+            for b in (0, 6):
+                ex, ey, ez = st[b, z], st[b + 1, z], st[b + 2, z]
+                ex_n, ey_n = st[b, z + 1], st[b + 1, z + 1]
+                st[b + 3, z] = st[b + 3, z] - coef * ((y_ahead(ez) - ez) - (ey_n - ey))
+                st[b + 4, z] = st[b + 4, z] - coef * ((ex_n - ex) - (x_ahead(ez) - ez))
+                if z >= m:
+                    st[b + 5, z] = st[b + 5, z] - coef * ((x_ahead(ey) - ey) - (y_ahead(ex) - ex))
+        for z in range(m, n_layers - m):
             scale = scale_ref[z]
             own = z - depth
             for r in range(2):
                 b = 6 * r
-                ex, ey, ez = st[b, z], st[b + 1, z], st[b + 2, z]
-                ex_n, ey_n = st[b, z + 1], st[b + 1, z + 1]
-                hx = st[b + 3, z] - coef * ((y_ahead(ez) - ez) - (ey_n - ey))
-                hy = st[b + 4, z] - coef * ((ex_n - ex) - (x_ahead(ez) - ez))
-                if z >= m:
-                    hx_p, hy_p = prev[r]
-                    hz = st[b + 5, z] - coef * ((x_ahead(ey) - ey) - (y_ahead(ex) - ex))
-                    ex = ex + scale * ((hz - y_behind(hz)) - (hy - hy_p))
-                    ey = ey + scale * ((hx - hx_p) - (hz - x_behind(hz)))
-                    ez = ez + scale * ((hy - x_behind(hy)) - (hx - y_behind(hx)))
-                    for c, f in enumerate((ex, ey, ez, hx, hy, hz)):
-                        if m < HALF:
+                hx_p, hy_p = st[b + 3, z - 1], st[b + 4, z - 1]
+                hx, hy, hz = st[b + 3, z], st[b + 4, z], st[b + 5, z]
+                ex = st[b, z] + scale * ((hz - y_behind(hz)) - (hy - hy_p))
+                ey = st[b + 1, z] + scale * ((hx - hx_p) - (hz - x_behind(hz)))
+                ez = st[b + 2, z] + scale * ((hy - x_behind(hy)) - (hx - y_behind(hx)))
+                for c, f in enumerate((ex, ey, ez, hx, hy, hz)):
+                    if m < HALF:
+                        if c < 3:
                             st[b + c, z] = f
-                            continue
-                        done[b + c, own] = f[:rows_own]
-                        if not second:
-                            up, down = f[rows_own - 8 : rows_own], f[:8]
-                            if sides == 2:
-                                strip_out[0][b + c, own] = strip_of(up, True)
-                                strip_out[1][b + c, own] = strip_of(down, False)
-                            else:
-                                strip_out[0][b + c, own] = jnp.where(
-                                    gy == 0, strip_of(up, True), strip_of(down, False)
-                                )
-                    if 0 <= own < depth:
-                        for c, e in enumerate((ex, ey, ez)):
-                            e = e[:rows_own]
-                            re, im = e * w_re, e * w_im
-                            if m > 1:
-                                acc[0, 3 * r + c, own] = acc[0, 3 * r + c, own] + re
-                                acc[1, 3 * r + c, own] = acc[1, 3 * r + c, own] - im
-                            elif second:
-                                acc[0, 3 * r + c, own] = acc_in[0, 3 * r + c, own] + re
-                                acc[1, 3 * r + c, own] = acc_in[1, 3 * r + c, own] - im
-                            else:
-                                acc[0, 3 * r + c, own] = re
-                                acc[1, 3 * r + c, own] = -im
-                else:
-                    st[b + 3, z], st[b + 4, z] = hx, hy
-                prev[r] = (hx, hy)
+                        continue
+                    done[b + c, own] = f[:rows_own]
+                    if not second:
+                        up, down = f[rows_own - 8 : rows_own], f[:8]
+                        if sides == 2:
+                            strip_out[0][b + c, own] = strip_of(up, True)
+                            strip_out[1][b + c, own] = strip_of(down, False)
+                        else:
+                            strip_out[0][b + c, own] = jnp.where(gy == 0, strip_of(up, True), strip_of(down, False))
+                if 0 <= own < depth:
+                    for c, e in enumerate((ex, ey, ez)):
+                        e = e[:rows_own]
+                        re, im = e * w_re, e * w_im
+                        if m > 1:
+                            acc[0, 3 * r + c, own] = acc[0, 3 * r + c, own] + re
+                            acc[1, 3 * r + c, own] = acc[1, 3 * r + c, own] - im
+                        elif second:
+                            acc[0, 3 * r + c, own] = acc_in[0, 3 * r + c, own] + re
+                            acc[1, 3 * r + c, own] = acc_in[1, 3 * r + c, own] - im
+                        else:
+                            acc[0, 3 * r + c, own] = re
+                            acc[1, 3 * r + c, own] = -im
 
     if second:
         result = pltpu.make_async_copy(done, out, sem_out)
@@ -254,15 +227,6 @@
         result.wait()
 
 
-def sum_kernel(info, got, out):
-    total = got[0]
-    for d in range(1, got.shape[0]):
-        total = total + got[d]
-    width = out.shape[1]
-    columns = total.shape[1]
-    out[...] = pltpu.roll(total, lax.rem(columns - info[7], columns), 1)[:, :width]
-
-
 def body(fields, eps_inv, row_counts, col_counts, density):
     runs, comps, depth, rows_own, nx = fields.shape
     n_gz, n_gy = lax.axis_size("gz"), lax.axis_size("gy")
@@ -301,7 +265,6 @@
         jnp.where(gy < n_gy - 1, 1, 0),
         jnp.where(gy > 0, 1, 0),
         index * depth - layer_start,
-        index * (density.shape[1] // n_z),
     ]
     info = jnp.stack([jnp.asarray(v, jnp.int32) for v in info])
 
@@ -311,26 +274,25 @@
     shape = lambda *s: jax.ShapeDtypeStruct(s, jnp.float32)
     limit = pltpu.CompilerParams(vmem_limit_bytes=24 * 1024 * 1024)
 
-    def strips_sent(strips):
+    def strips_sent(strips, more=None):
         sent = []
         for s, strip in enumerate(strips):
             mine = along_y(strip, s)
+            if more is not None and s == 0:
+                mine = jnp.concatenate([mine, more])
             sent += [cross(mine), mine, swap_core(mine)]
         return sent
 
-    strips = pl.pallas_call(
-        functools.partial(edge_kernel, depth, rows_own, sides),
-        out_shape=(shape(13, depth, 8, 128),) * sides,
-        in_specs=[smem, anywhere, anywhere],
-        out_specs=(vmem,) * sides,
-        scratch_shapes=[
-            pltpu.VMEM((sides, 13, depth, 8, nx), jnp.float32),
-            pltpu.SemaphoreType.DMA((sides, 2)),
-        ],
-        compiler_params=limit,
-    )(info, own, eps_inv)
-    operands = [info, cross(own), own, swap_core(own)] + strips_sent(strips)
-    operands += [cross(eps_inv), eps_inv, swap_core(eps_inv)]
+    starts = [(1 - gy) * (rows_own - HALF)] if sides == 1 else [rows_own - HALF, 0]
+    strips = []
+    for start in starts:
+        rows_f = lax.dynamic_slice_in_dim(own, start, HALF, 2)
+        rows_e = lax.dynamic_slice_in_dim(eps_inv, start, HALF, 1)[None]
+        halves = [jnp.concatenate([f[..., :128], f[..., 128:]], 2) for f in (rows_f, rows_e)]
+        strips.append(jnp.concatenate(halves))
+    tiles = eps_inv.reshape(depth, 2, 8, 2, 128).transpose(1, 3, 0, 2, 4).reshape(4, depth, 8, 128)
+    sent = strips_sent(strips, tiles)
+    operands = [info, cross(own), own, swap_core(own)] + sent
     cost = pl.CostEstimate(flops=20_000_000, bytes_accessed=4_000_000, transcendentals=0)
     window = pltpu.VMEM((12, 3 * depth, rows, nx), jnp.float32)
     block = pltpu.VMEM((12, depth, rows_own, nx), jnp.float32)
@@ -343,15 +305,13 @@
             shape(2, 6, depth, rows_own, nx),
         )
         + (shape(12, depth, 8, 128),) * sides,
-        in_specs=[smem] + [anywhere] * (6 + 3 * sides),
+        in_specs=[smem] + [anywhere] * (3 + 3 * sides),
         out_specs=(vmem, vmem, vmem) + (vmem,) * sides,
         scratch_shapes=[
             window,
-            pltpu.VMEM((sides, 13, 3 * depth, 8, 128), jnp.float32),
-            pltpu.VMEM((3 * depth, rows_own, nx), jnp.float32),
+            pltpu.VMEM((sides, 17, 3 * depth, 8, 128), jnp.float32),
         ]
-        + arrivals
-        + [pltpu.SemaphoreType.DMA((3,))],
+        + arrivals,
         compiler_params=limit,
         cost_estimate=cost,
     )(*operands)
@@ -372,7 +332,8 @@
     )
     const = lambda a: jnp.asarray(a, jnp.float32)
     own_y = lax.dynamic_slice_in_dim(const(basis_y), gy * band, band, 1)
-    operands = [info, cross(state), state, swap_core(state)] + strips_sent(strips) + [scale, acc]
+    sent = strips_sent(strips)
+    operands = [info, cross(state), state, swap_core(state)] + sent + [scale, acc]
     operands += [row_table, col_table, slope_of(density), const(basis_x), const(basis_x.T), const(basis_y.T), own_y, const(response)]
     n_all = n_z * n_gy
     fields_out, share = pl.pallas_call(
@@ -393,12 +354,8 @@
     )(*operands)
 
     got = lax.all_to_all(share, ("gz", "gy", "col"), 0, 0)
-    gradient = pl.pallas_call(
-        sum_kernel,
-        out_shape=shape(band, design_cols // n_z),
-        in_specs=[smem, vmem],
-        out_specs=vmem,
-    )(info, got)
+    width = design_cols // n_z
+    gradient = lax.dynamic_slice_in_dim(jnp.sum(got, axis=0), index * width, width, 1)
     return fields_out.reshape(fields.shape), gradient
 
 

time: 66.5 us -> 62 us (0.932)
  blocking collectives: 19.4 us -> 0 us
  waiting for transfers between devices: 4.01 us -> 14.7 us
  starting transfers between devices: 24 us -> 31 us
  Pallas kernels: 14.5 us -> 9.51 us
  local copies, waits for them, and re-layouts: 2.76 us -> 4.85 us
    all_to_all x1 -> x0, blocking collectives: 19.4 us -> none  [body(): got = lax.all_to_all(share, ('gz', 'gy', 'col'), 0, 0)]
    all_to_all x0 -> x1, starting transfers between devices: none -> 12.1 us  [body(): got = lax.all_to_all(share, ('gz', 'gy', 'col'), 0, 0)]
    all_to_all x0 -> x1, waiting for transfers between devices: none -> 6.9 us  [body(): got = lax.all_to_all(share, ('gz', 'gy', 'col'), 0, 0)]
    ppermute x5 -> x4, starting transfers between devices: 15.9 us -> 11.5 us  [swap_core(): return lax.ppermute(x, 'col', [(0, 1), (1, 0)])]
    ppermute x2, waiting for transfers between devices: 3.65 us -> 7.46 us  [along_y(): return lax.ppermute(x, 'gy', list(ways[s].items()))]
    pallas_call x2 -> x0, Pallas kernels: 2.91 us -> none  [the longest x1 1.52 us: body(): pl.pallas_call(sum_kernel, out_shape=shape(band, design_cols // n_z), in_...]
    pallas_call x2, Pallas kernels: 11.6 us -> 9.51 us  [body(): pl.pallas_call(functools.partial(window_kernel, (depth, rows_own, sides,...]
    slice x0 -> x2, local copies, waits for them, and re-layouts: none -> 1.19 us  [body(): f[..., :128]]
  transfers between devices with their start and end apart: 12 -> 11, of which waited for: 2 -> 4; matrix products, arithmetic and copies ran while one was open for 1% -> 5% of each run, Pallas kernels for 2% -> 0%
where the time goes in v4:
time: 62 us; the launch traced here: 61.6 us
  starting transfers between devices  31 us (50%)
  waiting for transfers between devices  14.7 us (24%)
  Pallas kernels  9.51 us (15%)
  local copies, waits for them, and re-layouts  4.85 us (8%)
  between operations  0.88 us (1%)
  other arithmetic  0.65 us (1%)
    all_to_all x1, starting transfers between devices, body(): got = lax.all_to_all(share, ('gz', 'gy', 'col'), 0, 0)  12.1 us
    ppermute x4, starting transfers between devices, swap_core(): return lax.ppermute(x, 'col', [(0, 1), (1, 0)])  11.5 us
    pallas_call x2, Pallas kernels, body(): pl.pallas_call(functools.partial(window_kernel, (depth, rows_own, sides,...  9.51 us
    ppermute x2, waiting for transfers between devices, along_y(): return lax.ppermute(x, 'gy', list(ways[s].items()))  7.46 us
    all_to_all x1, waiting for transfers between devices, body(): got = lax.all_to_all(share, ('gz', 'gy', 'col'), 0, 0)  6.9 us
    ppermute x2, starting transfers between devices, along_y(): return lax.ppermute(x, 'gy', list(ways[s].items()))  4.66 us
    ppermute x4, starting transfers between devices, cross(): return lax.ppermute(x, Z, pairs)  2.73 us
    unnamed x20, local copies, waits for them, and re-layouts  1.93 us
  transfers between devices with their start and end apart: 11, of which 4 were waited for; matrix products, arithmetic and copies ran while one was open for 5% of the time, Pallas kernels for 0%

profile of v4, /device:TPU:0, one launch (start us, length us, event | category | flops | bytes accessed | tf_op | source)
XLA Modules:
  0.0 61.6 jit_solution(5298123960168854562)
XLA Ops:
  0.6 0.5 collective-permute-start.1
  1.1 0.7 %collective-permute-start = (f32[12,4,16,256]{3,2,1,0:T(8,128)}, f32[12,4,16,256]{3,2,1,0:T(8,128)S(1)}, u32[]{:S(2)}, u32[]{:S(2)}) collective-permute-start(f32[12,4,16,256]{3,2,1,0:T(8,128)} %bitcast.25), channel_id=1, source_target_pairs={{1,4},{4,1},{5,8},{8,5},{9,12},{12,9},{3,6},{6,3},{7,10},{10,7},{1... | collective-permute-start | bytes 2359304 | tf_op jit(solution)/shard_map/ppermute | solution.py:248
  1.9 0.8 %dynamic-slice_bitcast_fusion = f32[1,4,4,256]{3,2,1,0:T(4,128)S(1)} fusion(f32[4,16,256]{2,1,0:T(8,128)} %param.11, s32[]{:T(128)S(6)} %select_n.19), kind=kLoop, calls=%fused_computation.6 | loop fusion | bytes 32772 | tf_op jit(solution)/shard_map/broadcast_in_dim | solution.py:290
  2.6 0.0 copy-start.5
  2.7 1.2 %constant_dynamic-slice_fusion = (f32[12,4,4,128]{3,2,1,0:T(4,128)S(1)}, f32[12,4,4,128]{3,2,1,0:T(4,128)S(1)}) fusion(f32[12,4,16,256]{3,2,1,0:T(8,128)} %bitcast.26, s32[]{:T(128)S(6)} %select_n.19, s32[]{:T(128)S(6)} %add.25), kind=kLoop, calls=%fused_computation.12 | loop fusion | bytes 393224 | tf_op jit(solution)/shard_map/slice | solution.py:291
  3.8 0.0 copy-start
  3.9 2.6 %collective-permute-start.2 = (f32[13,4,8,128]{3,2,1,0:T(8,128)S(1)}, f32[13,4,8,128]{3,2,1,0:T(8,128)S(1)}, u32[]{:S(2)}, u32[]{:S(2)}) collective-permute-start(f32[13,4,8,128]{3,2,1,0:T(8,128)S(1)} %maximum_maximum_fusion), channel_id=1, source_target_pairs={{0,2},{2,0},{1,3},{3,1},{4,6},{6,4},{5,7},{7,5},{8,10},{10,8},{9,1... | collective-permute-start | bytes 638984 | tf_op jit(solution)/shard_map/ppermute | solution.py:257
  6.5 0.0 copy-done.5
  6.5 3.8 %collective-permute-done.2 = f32[13,4,8,128]{3,2,1,0:T(8,128)S(1)} collective-permute-done((f32[13,4,8,128]{3,2,1,0:T(8,128)S(1)}, f32[13,4,8,128]{3,2,1,0:T(8,128)S(1)}, u32[]{:S(2)}, u32[]{:S(2)}) %collective-permute-start.2) | collective-permute-done | bytes 213024 | tf_op jit(solution)/shard_map/ppermute | solution.py:257
  10.3 2.3 %collective-permute-start.4 = (f32[17,4,8,128]{3,2,1,0:T(8,128)S(1)}, f32[17,4,8,128]{3,2,1,0:T(8,128)S(1)}, u32[]{:S(2)}, u32[]{:S(2)}) collective-permute-start(f32[17,4,8,128]{3,2,1,0:T(8,128)S(1)} %pad_maximum_fusion.refs_5_), channel_id=1, source_target_pairs={{0,1},{1,0},{2,3},{3,2},{4,5},{5,4},{6,7},{7,6},{8,9},{9,8},{10,11... | collective-permute-start | bytes 835592 | tf_op jit(solution)/shard_map/ppermute | solution.py:241
  12.7 0.7 %collective-permute-start.3 = (f32[17,4,8,128]{3,2,1,0:T(8,128)S(1)}, f32[17,4,8,128]{3,2,1,0:T(8,128)S(1)}, u32[]{:S(2)}, u32[]{:S(2)}) collective-permute-start(f32[17,4,8,128]{3,2,1,0:T(8,128)S(1)} %pad_maximum_fusion.refs_5_), channel_id=1, source_target_pairs={{1,4},{4,1},{5,8},{8,5},{9,12},{12,9},{3,6},{6,3},{7,10},{10,7},{1... | collective-permute-start | bytes 835592 | tf_op jit(solution)/shard_map/ppermute | solution.py:248
  13.4 0.0 copy-start.9
  13.4 0.6 %copy-done.9 = s32[1,8]{1,0:T(1,128)S(1)} copy-done((s32[1,8]{1,0:T(1,128)S(1)}, s32[1,8]{1,0:T(1,128)}, u32[]{:S(2)}) %copy-start.9) | copy-done | bytes 56
  14.0 0.2 reduce-window.13
  14.2 0.0 copy-start.8
  14.2 0.7 %copy-done.8 = s32[128]{0:T(128)S(1)} copy-done((s32[128]{0:T(128)S(1)}, s32[128]{0:T(128)}, u32[]{:S(2)}) %copy-start.8) | copy-done | bytes 536
  14.9 0.1 copy.15
  15.0 0.2 reduce-window.14
  15.1 0.1 reduce
  15.3 0.0 copy-start.7
  15.3 0.1 stack.31.refs_0_
  15.4 0.6 copy-done.7
  16.0 0.0 copy-start.6
  16.0 0.0 collective-permute-done.4.refs_6_
  16.0 0.0 collective-permute-done.3.refs_4_
  16.0 0.0 collective-permute-done.1.refs_3_
  16.0 0.0 collective-permute-done.refs_1_
  16.0 0.0 copy-done
  16.0 3.5 %shard_map.113 = (f32[12,4,16,256]{3,2,1,0:T(8,128)S(1)}, f32[12,24,256]{2,1,0:T(8,128)S(1)}, f32[2,6,4,16,256]{4,3,2,1,0:T(8,128)S(1)}, f32[12,4,8,128]{3,2,1,0:T(8,128)S(1)}) custom-call(s32[7]{0:T(128)S(1)} %stack.31.refs_0_, f32[12,4,16,256]{3,2,1,0:T(8,128)S(1)} %collective-permute-done.refs_1_, f32[12,4,16,256]{3,2,1,0:T(8,128)S(1)} %bitcast.27, ...), custom_call_target="tpu_custom_call" | custom-call | flops 20000000 | bytes 4000000 | tf_op jit(solution)/shard_map/pallas_call | solution.py:300
  19.5 6.4 %collective-permute-start.6 = (f32[12,4,16,256]{3,2,1,0:T(8,128)S(1)}, f32[12,4,16,256]{3,2,1,0:T(8,128)S(1)}, u32[]{:S(2)}, u32[]{:S(2)}) collective-permute-start(f32[12,4,16,256]{3,2,1,0:T(8,128)S(1)} %get-tuple-element.8.refs_2_), channel_id=1, source_target_pairs={{0,1},{1,0},{2,3},{3,2},{4,5},{5,4},{6,7},{7,6},{8,9},{9,8},{10,11... | collective-permute-start | bytes 2359304 | tf_op jit(solution)/shard_map/ppermute | solution.py:241
  26.0 0.7 %collective-permute-start.5 = (f32[12,4,16,256]{3,2,1,0:T(8,128)S(1)}, f32[12,4,16,256]{3,2,1,0:T(8,128)S(1)}, u32[]{:S(2)}, u32[]{:S(2)}) collective-permute-start(f32[12,4,16,256]{3,2,1,0:T(8,128)S(1)} %get-tuple-element.8.refs_2_), channel_id=1, source_target_pairs={{1,4},{4,1},{5,8},{8,5},{9,12},{12,9},{3,6},{6,3},{7,10},{10,7},{1... | collective-permute-start | bytes 2359304 | tf_op jit(solution)/shard_map/ppermute | solution.py:248
  26.7 0.0 copy-done.6
  26.7 0.0 copy-start.4
  26.7 0.1 constant_dynamic-slice_fusion.2.refs_15_
  26.8 0.0 copy-start.1
  26.8 0.0 copy-start.2
  26.8 0.0 copy-start.3
  26.8 2.1 %collective-permute-start.7 = (f32[12,4,8,128]{3,2,1,0:T(8,128)S(1)}, f32[12,4,8,128]{3,2,1,0:T(8,128)S(1)}, u32[]{:S(2)}, u32[]{:S(2)}) collective-permute-start(f32[12,4,8,128]{3,2,1,0:T(8,128)S(1)} %get-tuple-element.9), channel_id=1, source_target_pairs={{0,2},{2,0},{1,3},{3,1},{4,6},{6,4},{5,7},{7,5},{8,10},{10,8},{9,1... | collective-permute-start | bytes 589832 | tf_op jit(solution)/shard_map/ppermute | solution.py:257
  28.9 3.6 %collective-permute-done.7.refs_5_ = f32[12,4,8,128]{3,2,1,0:T(8,128)S(1)} collective-permute-done((f32[12,4,8,128]{3,2,1,0:T(8,128)S(1)}, f32[12,4,8,128]{3,2,1,0:T(8,128)S(1)}, u32[]{:S(2)}, u32[]{:S(2)}) %collective-permute-start.7) | collective-permute-done | bytes 196640 | tf_op jit(solution)/shard_map/ppermute | solution.py:257
  32.5 2.3 %collective-permute-start.9 = (f32[12,4,8,128]{3,2,1,0:T(8,128)S(1)}, f32[12,4,8,128]{3,2,1,0:T(8,128)S(1)}, u32[]{:S(2)}, u32[]{:S(2)}) collective-permute-start(f32[12,4,8,128]{3,2,1,0:T(8,128)S(1)} %collective-permute-done.7.refs_5_), channel_id=1, source_target_pairs={{0,1},{1,0},{2,3},{3,2},{4,5},{5,4},{6,7},{7,6},{8,9},{9,8},{10,11... | collective-permute-start | bytes 589832 | tf_op jit(solution)/shard_map/ppermute | solution.py:241
  34.8 0.7 %collective-permute-start.8 = (f32[12,4,8,128]{3,2,1,0:T(8,128)S(1)}, f32[12,4,8,128]{3,2,1,0:T(8,128)S(1)}, u32[]{:S(2)}, u32[]{:S(2)}) collective-permute-start(f32[12,4,8,128]{3,2,1,0:T(8,128)S(1)} %collective-permute-done.7.refs_5_), channel_id=1, source_target_pairs={{1,4},{4,1},{5,8},{8,5},{9,12},{12,9},{3,6},{6,3},{7,10},{10,7},{1... | collective-permute-start | bytes 589832 | tf_op jit(solution)/shard_map/ppermute | solution.py:248
  35.5 0.1 fusion.3.refs_9_
  35.6 0.3 collective-permute-done.9.refs_6_
  35.9 0.0 collective-permute-done.8.refs_4_
  35.9 0.0 collective-permute-done.6.refs_3_
  35.9 0.0 collective-permute-done.5.refs_1_
  35.9 0.0 copy-done.4
  35.9 0.0 copy-done.1
  35.9 0.0 copy-done.2
  35.9 0.0 copy-done.3
  35.9 6.0 %shard_map.114 = (f32[12,4,16,256]{3,2,1,0:T(8,128)}, f32[16,8,128]{2,1,0:T(8,128)}) custom-call(s32[7]{0:T(128)S(1)} %stack.31.refs_0_, f32[12,4,16,256]{3,2,1,0:T(8,128)S(1)} %collective-permute-done.5.refs_1_, f32[12,4,16,256]{3,2,1,0:T(8,128)S(1)} %get-tuple-element.8.refs_2_, f32[12,4,16,256]{3,2,1,0:T(8,128)S(1)} %collective-permute-done.6.refs_3_, ...), custom_call_target="tpu_custom_call" | custom-call | flops 20000000 | bytes 4000000 | tf_op jit(solution)/shard_map/pallas_call | solution.py:339
  41.9 12.1 %all-to-all-start = ((f32[16,8,128]{2,1,0:T(8,128)}), f32[16,8,128]{2,1,0:T(8,128)S(1)}, u32[]{:S(2)}, u32[]{:S(2)}) async-start(f32[16,8,128]{2,1,0:T(8,128)} %get-tuple-element.13), calls=%async_computation | async-start | bytes 131072 | tf_op jit(solution)/shard_map/all_to_all | solution.py:356
  54.0 6.9 %all-to-all-done = f32[16,8,128]{2,1,0:T(8,128)S(1)} async-done(((f32[16,8,128]{2,1,0:T(8,128)}), f32[16,8,128]{2,1,0:T(8,128)S(1)}, u32[]{:S(2)}, u32[]{:S(2)}) %all-to-all-start) | async-done | bytes 65568 | tf_op jit(solution)/shard_map/all_to_all | solution.py:356
  60.9 0.7 %constant_dynamic-slice_fusion.1 = f32[8,16]{1,0:T(8,128)} fusion(f32[8,128]{1,0:T(8,128)S(1)} %reduce_sum.9, s32[]{:T(128)S(6)} %select_n.21), kind=kLoop, calls=%fused_computation.13 | loop fusion | bytes 1028 | tf_op jit(solution)/shard_map/dynamic_slice | solution.py:358
  (9 shorter events, 0.1 us)
Async XLA Ops:
  0.6 15.3 %collective-permute-start.1 = (f32[12,4,16,256]{3,2,1,0:T(8,128)}, f32[12,4,16,256]{3,2,1,0:T(8,128)S(1)}, u32[]{:S(2)}, u32[]{:S(2)}) collective-permute-start(f32[12,4,16,256]{3,2,1,0:T(8,128)} %bitcast.24), channel_id=1, source_target_pairs={{0,1},{1,0},{2,3},{3,2},{4,5},{5,4},{6,7},{7,6},{8,9},{9,8},{10,11... | collective-permute-start | bytes 2359304 | tf_op jit(solution)/shard_map/ppermute | solution.py:241
  1.1 14.8 %collective-permute-start = (f32[12,4,16,256]{3,2,1,0:T(8,128)}, f32[12,4,16,256]{3,2,1,0:T(8,128)S(1)}, u32[]{:S(2)}, u32[]{:S(2)}) collective-permute-start(f32[12,4,16,256]{3,2,1,0:T(8,128)} %bitcast.25), channel_id=1, source_target_pairs={{1,4},{4,1},{5,8},{8,5},{9,12},{12,9},{3,6},{6,3},{7,10},{10,7},{1... | collective-permute-start | bytes 2359304 | tf_op jit(solution)/shard_map/ppermute | solution.py:248
  2.6 3.8 %copy-start.5 = (f32[4,16,256]{2,1,0:T(8,128)S(1)}, f32[4,16,256]{2,1,0:T(8,128)}, u32[]{:S(2)}) copy-start(f32[4,16,256]{2,1,0:T(8,128)} %param.11) | copy-start | bytes 196612
  3.8 12.2 %copy-start = (f32[2,6,4,16,256]{4,3,2,1,0:T(8,128)S(1)}, f32[2,6,4,16,256]{4,3,2,1,0:T(8,128)}, u32[]{:S(2)}) copy-start(f32[2,6,4,16,256]{4,3,2,1,0:T(8,128)} %param.10) | copy-start | bytes 2359300
  3.9 6.4 %collective-permute-start.2 = (f32[13,4,8,128]{3,2,1,0:T(8,128)S(1)}, f32[13,4,8,128]{3,2,1,0:T(8,128)S(1)}, u32[]{:S(2)}, u32[]{:S(2)}) collective-permute-start(f32[13,4,8,128]{3,2,1,0:T(8,128)S(1)} %maximum_maximum_fusion), channel_id=1, source_target_pairs={{0,2},{2,0},{1,3},{3,1},{4,6},{6,4},{5,7},{7,5},{8,10},{10,8},{9,1... | collective-permute-start | bytes 638984 | tf_op jit(solution)/shard_map/ppermute | solution.py:257
  10.3 5.6 %collective-permute-start.4 = (f32[17,4,8,128]{3,2,1,0:T(8,128)S(1)}, f32[17,4,8,128]{3,2,1,0:T(8,128)S(1)}, u32[]{:S(2)}, u32[]{:S(2)}) collective-permute-start(f32[17,4,8,128]{3,2,1,0:T(8,128)S(1)} %pad_maximum_fusion.refs_5_), channel_id=1, source_target_pairs={{0,1},{1,0},{2,3},{3,2},{4,5},{5,4},{6,7},{7,6},{8,9},{9,8},{10,11... | collective-permute-start | bytes 835592 | tf_op jit(solution)/shard_map/ppermute | solution.py:241
  12.7 3.3 %collective-permute-start.3 = (f32[17,4,8,128]{3,2,1,0:T(8,128)S(1)}, f32[17,4,8,128]{3,2,1,0:T(8,128)S(1)}, u32[]{:S(2)}, u32[]{:S(2)}) collective-permute-start(f32[17,4,8,128]{3,2,1,0:T(8,128)S(1)} %pad_maximum_fusion.refs_5_), channel_id=1, source_target_pairs={{1,4},{4,1},{5,8},{8,5},{9,12},{12,9},{3,6},{6,3},{7,10},{10,7},{1... | collective-permute-start | bytes 835592 | tf_op jit(solution)/shard_map/ppermute | solution.py:248
  13.4 0.7 %copy-start.9 = (s32[1,8]{1,0:T(1,128)S(1)}, s32[1,8]{1,0:T(1,128)}, u32[]{:S(2)}) copy-start(s32[1,8]{1,0:T(1,128)} %param.12) | copy-start | bytes 100
  14.2 0.7 %copy-start.8 = (s32[128]{0:T(128)S(1)}, s32[128]{0:T(128)}, u32[]{:S(2)}) copy-start(s32[128]{0:T(128)} %param.13) | copy-start | bytes 1540
  15.3 0.7 %copy-start.7 = (f32[8,128]{1,0:T(8,128)S(1)}, f32[8,128]{1,0:T(8,128)}, u32[]{:S(2)}) copy-start(f32[8,128]{1,0:T(8,128)} %param.14) | copy-start | bytes 12292
  16.0 10.7 %copy-start.6 = (f32[16,16]{1,0:T(8,128)S(1)}, f32[16,16]{1,0:T(8,128)}, u32[]{:S(2)}) copy-start(f32[16,16]{1,0:T(8,128)} %constant.62.clone) | copy-start | bytes 3076
  19.5 16.4 %collective-permute-start.6 = (f32[12,4,16,256]{3,2,1,0:T(8,128)S(1)}, f32[12,4,16,256]{3,2,1,0:T(8,128)S(1)}, u32[]{:S(2)}, u32[]{:S(2)}) collective-permute-start(f32[12,4,16,256]{3,2,1,0:T(8,128)S(1)} %get-tuple-element.8.refs_2_), channel_id=1, source_target_pairs={{0,1},{1,0},{2,3},{3,2},{4,5},{5,4},{6,7},{7,6},{8,9},{9,8},{10,11... | collective-permute-start | bytes 2359304 | tf_op jit(solution)/shard_map/ppermute | solution.py:241
  26.0 9.9 %collective-permute-start.5 = (f32[12,4,16,256]{3,2,1,0:T(8,128)S(1)}, f32[12,4,16,256]{3,2,1,0:T(8,128)S(1)}, u32[]{:S(2)}, u32[]{:S(2)}) collective-permute-start(f32[12,4,16,256]{3,2,1,0:T(8,128)S(1)} %get-tuple-element.8.refs_2_), channel_id=1, source_target_pairs={{1,4},{4,1},{5,8},{8,5},{9,12},{12,9},{3,6},{6,3},{7,10},{10,7},{1... | collective-permute-start | bytes 2359304 | tf_op jit(solution)/shard_map/ppermute | solution.py:248
  26.7 9.2 %copy-start.4 = (f32[16,16]{1,0:T(8,128)S(1)}, f32[16,16]{1,0:T(8,128)}, u32[]{:S(2)}) copy-start(f32[16,16]{1,0:T(8,128)} %constant.65.clone.refs_14_) | copy-start | bytes 3076
  26.8 9.1 %copy-start.1 = (f32[128,128]{1,0:T(8,128)S(1)}, f32[128,128]{1,0:T(8,128)}, u32[]{:S(2)}) copy-start(f32[128,128]{1,0:T(8,128)} %constant.64.clone.refs_13_) | copy-start | bytes 196612
  26.8 9.2 %copy-start.2 = (f32[128,128]{1,0:T(8,128)S(1)}, f32[128,128]{1,0:T(8,128)}, u32[]{:S(2)}) copy-start(f32[128,128]{1,0:T(8,128)} %constant.63.clone.refs_12_) | copy-start | bytes 196612
  26.8 9.1 %copy-start.3 = (f32[16,128]{1,0:T(8,128)S(1)}, f32[16,128]{1,0:T(8,128)}, u32[]{:S(2)}) copy-start(f32[16,128]{1,0:T(8,128)} %constant.66.clone.refs_16_) | copy-start | bytes 24580
  26.8 5.7 %collective-permute-start.7 = (f32[12,4,8,128]{3,2,1,0:T(8,128)S(1)}, f32[12,4,8,128]{3,2,1,0:T(8,128)S(1)}, u32[]{:S(2)}, u32[]{:S(2)}) collective-permute-start(f32[12,4,8,128]{3,2,1,0:T(8,128)S(1)} %get-tuple-element.9), channel_id=1, source_target_pairs={{0,2},{2,0},{1,3},{3,1},{4,6},{6,4},{5,7},{7,5},{8,10},{10,8},{9,1... | collective-permute-start | bytes 589832 | tf_op jit(solution)/shard_map/ppermute | solution.py:257
  32.5 3.3 %collective-permute-start.9 = (f32[12,4,8,128]{3,2,1,0:T(8,128)S(1)}, f32[12,4,8,128]{3,2,1,0:T(8,128)S(1)}, u32[]{:S(2)}, u32[]{:S(2)}) collective-permute-start(f32[12,4,8,128]{3,2,1,0:T(8,128)S(1)} %collective-permute-done.7.refs_5_), channel_id=1, source_target_pairs={{0,1},{1,0},{2,3},{3,2},{4,5},{5,4},{6,7},{7,6},{8,9},{9,8},{10,11... | collective-permute-start | bytes 589832 | tf_op jit(solution)/shard_map/ppermute | solution.py:241
  34.8 1.1 %collective-permute-start.8 = (f32[12,4,8,128]{3,2,1,0:T(8,128)S(1)}, f32[12,4,8,128]{3,2,1,0:T(8,128)S(1)}, u32[]{:S(2)}, u32[]{:S(2)}) collective-permute-start(f32[12,4,8,128]{3,2,1,0:T(8,128)S(1)} %collective-permute-done.7.refs_5_), channel_id=1, source_target_pairs={{1,4},{4,1},{5,8},{8,5},{9,12},{12,9},{3,6},{6,3},{7,10},{10,7},{1... | collective-permute-start | bytes 589832 | tf_op jit(solution)/shard_map/ppermute | solution.py:248
  41.9 19.0 %all-to-all-start = ((f32[16,8,128]{2,1,0:T(8,128)}), f32[16,8,128]{2,1,0:T(8,128)S(1)}, u32[]{:S(2)}, u32[]{:S(2)}) async-start(f32[16,8,128]{2,1,0:T(8,128)} %get-tuple-element.13), calls=%async_computation | async-start | bytes 131072 | tf_op jit(solution)/shard_map/all_to_all | solution.py:356

commit v5 on v4

--- a/solution.py
+++ b/solution.py
@@ -61,20 +61,48 @@
     return jnp.where(low_half, a, pltpu.roll(b, HALF, 0))
 
 
+def split(x):
+    high = x.astype(jnp.bfloat16).astype(jnp.float32)
+    return high, x - high
+
+
+def mix(table, x, start=0):
+    total = table[start] * x[:1]
+    for k in range(1, x.shape[0]):
+        total = total + table[start + k] * x[k : k + 1]
+    return total
+
+
+def placed(x, at, size):
+    rows = x.shape[0]
+    block = lax.broadcasted_iota(jnp.int32, (size, x.shape[1]), 0) // rows
+    return jnp.where(block == at, jnp.concatenate([x] * (size // rows)), 0.0)
+
+
+def transform(x, basis):
+    rows, columns = x.shape
+    parts = jnp.concatenate(split(x)).astype(jnp.bfloat16)
+    product = jnp.dot(parts, basis[...].astype(jnp.bfloat16), preferred_element_type=jnp.float32)
+    small = product[rows:, :columns] + product[:rows, columns:] + product[rows:, columns:]
+    return product[:rows, :columns] + small
+
+
 def window_kernel(cfg, *refs):
     depth, rows_own, sides, second = cfg
     it = iter(refs)
     take = lambda n: [next(it) for _ in range(n)]
     info = next(it)
-    full = take(3)
+    pieces = 2 if second else 1
+    full = [take(3) for _ in range(pieces)]
     strip_in = [take(3) for _ in range(sides)]
     if second:
         (scale_ref, acc_in) = take(2)
-        row_table, col_table, slope, basis_x, basis_xt, basis_y, own_y, response = take(8)
+        row_wide, col_table, slope, basis_x, basis_xt, basis_y, basis_yt, response = take(8)
         out, share = take(2)
         st, strips, acc, done, sem_full, sem_strip, sem_out = take(7)
     else:
-        done, scale_ref, acc = take(3)
+        done = take(2)
+        scale_ref, acc = take(2)
         strip_out = take(sides)
         st, strips, sem_full, sem_strip = take(4)
 
@@ -82,7 +110,14 @@
 
     def copies_of(b, place):
         layers = pl.ds(place * depth, depth)
-        found = [pltpu.make_async_copy(full[b], st.at[:, layers, pl.ds(0, rows_own), :], sem_full.at[place])]
+        found = []
+        for p in range(pieces):
+            planes = pl.ds(12 // pieces * p, 12 // pieces)
+            found.append(
+                pltpu.make_async_copy(
+                    full[p][b], st.at[planes, layers, pl.ds(0, rows_own), :], sem_full.at[p, place]
+                )
+            )
         for s in range(sides):
             planes = pl.ds(0, strip_in[s][b].shape[0])
             found.append(pltpu.make_async_copy(strip_in[s][b], strips.at[s, planes, layers], sem_strip.at[s, place]))
@@ -183,8 +218,10 @@
                         if c < 3:
                             st[b + c, z] = f
                         continue
-                    done[b + c, own] = f[:rows_own]
-                    if not second:
+                    if second:
+                        done[b + c, own] = f[:rows_own]
+                    else:
+                        done[r][c, own] = f[:rows_own]
                         up, down = f[rows_own - 8 : rows_own], f[:8]
                         if sides == 2:
                             strip_out[0][b + c, own] = strip_of(up, True)
@@ -215,11 +252,24 @@
                 g = g + acc[0, c, own] * acc[0, 3 + c, own] - acc[1, c, own] * acc[1, 3 + c, own]
             in_layer = (info[6] + own >= 0) & (info[6] + own < 3 * depth)
             column_sum = column_sum + jnp.where(in_layer, g, 0.0)
-        sens = mm(row_table[...], mm(column_sum, col_table[...])) * (eps_span / (STEPS * 3 * depth))
+        pooled = jnp.zeros(row_wide.shape[1:], jnp.float32)
+        for k in range(rows_own):
+            pooled = pooled + row_wide[k] * column_sum[k : k + 1]
+        high, rest = split(pooled)
+        mid, low = split(rest)
+        parts = jnp.concatenate([high, mid, low, jnp.zeros_like(low)]).astype(jnp.bfloat16)
+        parts = jnp.dot(parts, col_table[...].astype(jnp.bfloat16), preferred_element_type=jnp.float32)
+        band = pooled.shape[0]
+        sens = (parts[:band] + parts[band : 2 * band] + parts[2 * band : 3 * band]) * (eps_span / (STEPS * 3 * depth))
         weighted = sens * slope[...]
-        spectrum = mm(own_y[...], mm(weighted, basis_xt[...])) * response[...]
-        shares = mm(basis_y[...], mm(spectrum, basis_x[...]))
-        count, band, _ = share.shape
+        tall = response.shape[0]
+        if len(basis_y.shape) == 3:
+            spectrum = transform(mix(basis_yt, weighted, gy * band), basis_xt) * response[...]
+            shares = mix(basis_y, transform(spectrum, basis_x))
+        else:
+            spectrum = transform(mm(basis_y[...], placed(weighted, gy, tall)), basis_xt) * response[...]
+            shares = mm(basis_yt[...], transform(spectrum, basis_x))
+        count = share.shape[0]
         n_gy = shares.shape[0] // band
         for d in range(count):
             y = d // 2 % n_gy
@@ -296,17 +346,18 @@
     cost = pl.CostEstimate(flops=20_000_000, bytes_accessed=4_000_000, transcendentals=0)
     window = pltpu.VMEM((12, 3 * depth, rows, nx), jnp.float32)
     block = pltpu.VMEM((12, depth, rows_own, nx), jnp.float32)
-    arrivals = [pltpu.SemaphoreType.DMA((3,)), pltpu.SemaphoreType.DMA((sides, 3))]
-    state, scale, acc, *strips = pl.pallas_call(
+    arrivals = [pltpu.SemaphoreType.DMA((2, 3)), pltpu.SemaphoreType.DMA((sides, 3))]
+    half_0, half_1, scale, acc, *strips = pl.pallas_call(
         functools.partial(window_kernel, (depth, rows_own, sides, False)),
         out_shape=(
-            shape(runs * comps, depth, rows_own, nx),
+            shape(comps, depth, rows_own, nx),
+            shape(comps, depth, rows_own, nx),
             shape(3 * depth, rows, nx),
             shape(2, 6, depth, rows_own, nx),
         )
         + (shape(12, depth, 8, 128),) * sides,
         in_specs=[smem] + [anywhere] * (3 + 3 * sides),
-        out_specs=(vmem, vmem, vmem) + (vmem,) * sides,
+        out_specs=(vmem,) * (4 + sides),
         scratch_shapes=[
             window,
             pltpu.VMEM((sides, 17, 3 * depth, 8, 128), jnp.float32),
@@ -318,7 +369,8 @@
 
     band, design_cols = density.shape
     tall = band * n_gy
-    row_table = band_table(row_counts[0], jnp.arange(rows_own, dtype=jnp.int32)[:, None]).T
+    row_table = band_table(row_counts[0], jnp.arange(rows_own, dtype=jnp.int32)[:, None])
+    row_wide = jnp.broadcast_to(row_table[:, :, None], (rows_own, band, nx))
     col_table = band_table(col_counts, jnp.arange(nx, dtype=jnp.int32)[:, None])
     basis_x, wave_x = real_basis(design_cols)
     basis_y, wave_y = real_basis(tall)
@@ -331,15 +383,26 @@
         )
     )
     const = lambda a: jnp.asarray(a, jnp.float32)
-    own_y = lax.dynamic_slice_in_dim(const(basis_y), gy * band, band, 1)
+    tables = [basis_y, basis_y.T]
+    if tall <= 16:
+        tables = [np.broadcast_to(t[:, :, None], (tall, tall, design_cols)) for t in tables]
+
+    def halves(matrix):
+        high = matrix.astype(jnp.bfloat16).astype(np.float64)
+        return const(np.concatenate([high, matrix - high], axis=1))
+
     sent = strips_sent(strips)
-    operands = [info, cross(state), state, swap_core(state)] + sent + [scale, acc]
-    operands += [row_table, col_table, slope_of(density), const(basis_x), const(basis_x.T), const(basis_y.T), own_y, const(response)]
+    operands = [info]
+    for half in (half_0, half_1):
+        operands += [cross(half), half, swap_core(half)]
+    operands += sent + [scale, acc]
+    operands += [row_wide, col_table, slope_of(density), halves(basis_x), halves(basis_x.T)]
+    operands += [const(tables[0]), const(tables[1]), const(response)]
     n_all = n_z * n_gy
     fields_out, share = pl.pallas_call(
         functools.partial(window_kernel, (depth, rows_own, sides, True)),
         out_shape=(shape(runs * comps, depth, rows_own, nx), shape(n_all, band, design_cols)),
-        in_specs=[smem] + [anywhere] * (3 + 3 * sides) + [vmem] * 10,
+        in_specs=[smem] + [anywhere] * (6 + 3 * sides) + [vmem] * 10,
         out_specs=(anywhere, vmem),
         scratch_shapes=[
             window,

time: 62 us -> 61.5 us (level)
  starting transfers between devices: 31 us -> 34.2 us
  waiting for transfers between devices: 14.7 us -> 11.8 us
  Pallas kernels: 9.51 us -> 8.73 us
    ppermute x4 -> x5, starting transfers between devices: 11.5 us -> 15.9 us  [swap_core(): return lax.ppermute(x, 'col', [(0, 1), (1, 0)])]
    ppermute x2, waiting for transfers between devices: 7.46 us -> 3.82 us  [along_y(): return lax.ppermute(x, 'gy', list(ways[s].items()))]
    all_to_all x1, starting transfers between devices: 12.1 us -> 10.4 us  [body(): got = lax.all_to_all(share, ('gz', 'gy', 'col'), 0, 0)]
    pallas_call x2, Pallas kernels: 9.51 us -> 8.73 us  [body(): pl.pallas_call(functools.partial(window_kernel, (depth, rows_own, sides,...]
    ppermute x4 -> x5, waiting for transfers between devices: 0.34 us -> 1.07 us  [swap_core(): return lax.ppermute(x, 'col', [(0, 1), (1, 0)])]
    ppermute x4 -> x5, starting transfers between devices: 2.73 us -> 3.37 us  [cross(): return lax.ppermute(x, Z, pairs)]
  transfers between devices with their start and end apart: 11 -> 13, of which waited for: 4 -> 3; matrix products, arithmetic and copies ran while one was open for 5% -> 4% of each run, Pallas kernels for 0% -> 0%
where the time goes in v5:
time: 61.5 us; the launch traced here: 61.1 us
  starting transfers between devices  34.2 us (56%)
  waiting for transfers between devices  11.8 us (19%)
  Pallas kernels  8.73 us (14%)
  local copies, waits for them, and re-layouts  4.83 us (8%)
  between operations  0.97 us (2%)
    ppermute x5, starting transfers between devices, swap_core(): return lax.ppermute(x, 'col', [(0, 1), (1, 0)])  15.9 us
    all_to_all x1, starting transfers between devices, body(): got = lax.all_to_all(share, ('gz', 'gy', 'col'), 0, 0)  10.4 us
    pallas_call x2, Pallas kernels, body(): pl.pallas_call(functools.partial(window_kernel, (depth, rows_own, sides,...  8.73 us
    all_to_all x1, waiting for transfers between devices, body(): got = lax.all_to_all(share, ('gz', 'gy', 'col'), 0, 0)  6.9 us
    ppermute x2, starting transfers between devices, along_y(): return lax.ppermute(x, 'gy', list(ways[s].items()))  4.5 us
    ppermute x2, waiting for transfers between devices, along_y(): return lax.ppermute(x, 'gy', list(ways[s].items()))  3.82 us
    ppermute x5, starting transfers between devices, cross(): return lax.ppermute(x, Z, pairs)  3.37 us
    unnamed x20, local copies, waits for them, and re-layouts  1.92 us
  transfers between devices with their start and end apart: 13, of which 3 were waited for; matrix products, arithmetic and copies ran while one was open for 4% of the time, Pallas kernels for 0%

profile of v5, /device:TPU:0, one launch (start us, length us, event | category | flops | bytes accessed | tf_op | source)
XLA Modules:
  0.0 61.1 jit_solution(9425659768672161059)
XLA Ops:
  0.6 0.5 collective-permute-start.1
  1.1 0.7 %collective-permute-start = (f32[12,4,16,256]{3,2,1,0:T(8,128)}, f32[12,4,16,256]{3,2,1,0:T(8,128)S(1)}, u32[]{:S(2)}, u32[]{:S(2)}) collective-permute-start(f32[12,4,16,256]{3,2,1,0:T(8,128)} %bitcast.25), channel_id=1, source_target_pairs={{1,4},{4,1},{5,8},{8,5},{9,12},{12,9},{3,6},{6,3},{7,10},{10,7},{1... | collective-permute-start | bytes 2359304 | tf_op jit(solution)/shard_map/ppermute | solution.py:298
  1.9 0.8 %dynamic-slice_bitcast_fusion = f32[1,4,4,256]{3,2,1,0:T(4,128)S(1)} fusion(f32[4,16,256]{2,1,0:T(8,128)} %param.11, s32[]{:T(128)S(6)} %select_n.16), kind=kLoop, calls=%fused_computation.6 | loop fusion | bytes 32772 | tf_op jit(solution)/shard_map/broadcast_in_dim | solution.py:340
  2.6 0.0 copy-start.6
  2.7 1.2 %constant_dynamic-slice_fusion = (f32[12,4,4,128]{3,2,1,0:T(4,128)S(1)}, f32[12,4,4,128]{3,2,1,0:T(4,128)S(1)}) fusion(f32[12,4,16,256]{3,2,1,0:T(8,128)} %bitcast.26, s32[]{:T(128)S(6)} %select_n.16, s32[]{:T(128)S(6)} %add.21), kind=kLoop, calls=%fused_computation.12 | loop fusion | bytes 393224 | tf_op jit(solution)/shard_map/slice | solution.py:341
  3.8 0.0 copy-start
  3.9 2.6 %collective-permute-start.2 = (f32[13,4,8,128]{3,2,1,0:T(8,128)S(1)}, f32[13,4,8,128]{3,2,1,0:T(8,128)S(1)}, u32[]{:S(2)}, u32[]{:S(2)}) collective-permute-start(f32[13,4,8,128]{3,2,1,0:T(8,128)S(1)} %maximum_maximum_fusion), channel_id=1, source_target_pairs={{0,2},{2,0},{1,3},{3,1},{4,6},{6,4},{5,7},{7,5},{8,10},{10,8},{9,1... | collective-permute-start | bytes 638984 | tf_op jit(solution)/shard_map/ppermute | solution.py:307
  6.5 0.0 copy-done.6
  6.5 3.8 %collective-permute-done.2 = f32[13,4,8,128]{3,2,1,0:T(8,128)S(1)} collective-permute-done((f32[13,4,8,128]{3,2,1,0:T(8,128)S(1)}, f32[13,4,8,128]{3,2,1,0:T(8,128)S(1)}, u32[]{:S(2)}, u32[]{:S(2)}) %collective-permute-start.2) | collective-permute-done | bytes 213024 | tf_op jit(solution)/shard_map/ppermute | solution.py:307
  10.3 2.3 %collective-permute-start.4 = (f32[17,4,8,128]{3,2,1,0:T(8,128)S(1)}, f32[17,4,8,128]{3,2,1,0:T(8,128)S(1)}, u32[]{:S(2)}, u32[]{:S(2)}) collective-permute-start(f32[17,4,8,128]{3,2,1,0:T(8,128)S(1)} %pad_maximum_fusion.refs_5_), channel_id=1, source_target_pairs={{0,1},{1,0},{2,3},{3,2},{4,5},{5,4},{6,7},{7,6},{8,9},{9,8},{10,11... | collective-permute-start | bytes 835592 | tf_op jit(solution)/shard_map/ppermute | solution.py:291
  12.7 0.7 %collective-permute-start.3 = (f32[17,4,8,128]{3,2,1,0:T(8,128)S(1)}, f32[17,4,8,128]{3,2,1,0:T(8,128)S(1)}, u32[]{:S(2)}, u32[]{:S(2)}) collective-permute-start(f32[17,4,8,128]{3,2,1,0:T(8,128)S(1)} %pad_maximum_fusion.refs_5_), channel_id=1, source_target_pairs={{1,4},{4,1},{5,8},{8,5},{9,12},{12,9},{3,6},{6,3},{7,10},{10,7},{1... | collective-permute-start | bytes 835592 | tf_op jit(solution)/shard_map/ppermute | solution.py:298
  13.4 0.0 copy-start.9
  13.4 0.6 %copy-done.9 = s32[1,8]{1,0:T(1,128)S(1)} copy-done((s32[1,8]{1,0:T(1,128)S(1)}, s32[1,8]{1,0:T(1,128)}, u32[]{:S(2)}) %copy-start.9) | copy-done | bytes 56
  14.0 0.2 reduce-window.13
  14.2 0.0 copy-start.8
  14.2 0.7 %copy-done.8 = s32[128]{0:T(128)S(1)} copy-done((s32[128]{0:T(128)S(1)}, s32[128]{0:T(128)}, u32[]{:S(2)}) %copy-start.8) | copy-done | bytes 536
  14.9 0.1 copy.15
  15.0 0.2 reduce-window.14
  15.1 0.1 reduce
  15.3 0.1 stack.31.refs_0_
  15.4 0.0 collective-permute-done.4.refs_6_
  15.4 0.0 collective-permute-done.3.refs_4_
  15.4 0.0 collective-permute-done.1.refs_3_
  15.4 0.0 collective-permute-done.refs_1_
  15.4 0.0 copy-done
  15.4 0.0 copy-start.7
  15.4 0.0 copy-start.2
  15.5 0.0 copy-start.3
  15.5 0.0 copy-start.4
  15.5 3.6 %shard_map.113 = (f32[6,4,16,256]{3,2,1,0:T(8,128)S(1)}, f32[6,4,16,256]{3,2,1,0:T(8,128)S(1)}, f32[12,24,256]{2,1,0:T(8,128)S(1)}, f32[2,6,4,16,256]{4,3,2,1,0:T(8,128)S(1)}, f32[12,4,8,128]{3,2,1,0:T(8,128)S(1)}) custom-call(s32[7]{0:T(128)S(1)} %stack.31.refs_0_, f32[12,4,16,256]{3,2,1,0:T(8,128)S(1)} %collective-permute-done.refs_1_, ...), custom_call_target="tpu_custom_call" | custom-call | flops 20000000 | bytes 4000000 | tf_op jit(solution)/shard_map/pallas_call | solution.py:350
  19.0 0.0 copy-start.1
  19.1 1.9 %collective-permute-start.9 = (f32[12,4,8,128]{3,2,1,0:T(8,128)S(1)}, f32[12,4,8,128]{3,2,1,0:T(8,128)S(1)}, u32[]{:S(2)}, u32[]{:S(2)}) collective-permute-start(f32[12,4,8,128]{3,2,1,0:T(8,128)S(1)} %get-tuple-element.11), channel_id=1, source_target_pairs={{0,2},{2,0},{1,3},{3,1},{4,6},{6,4},{5,7},{7,5},{8,10},{10,8},{9,1... | collective-permute-start | bytes 589832 | tf_op jit(solution)/shard_map/ppermute | solution.py:307
  21.0 7.1 %collective-permute-start.6 = (f32[6,4,16,256]{3,2,1,0:T(8,128)S(1)}, f32[6,4,16,256]{3,2,1,0:T(8,128)S(1)}, u32[]{:S(2)}, u32[]{:S(2)}) collective-permute-start(f32[6,4,16,256]{3,2,1,0:T(8,128)S(1)} %get-tuple-element.9.refs_2_), channel_id=1, source_target_pairs={{0,1},{1,0},{2,3},{3,2},{4,5},{5,4},{6,7},{7,6},{8,9},{9,8},{10,11... | collective-permute-start | bytes 1179656 | tf_op jit(solution)/shard_map/ppermute | solution.py:291
  28.1 0.7 %collective-permute-start.5 = (f32[6,4,16,256]{3,2,1,0:T(8,128)S(1)}, f32[6,4,16,256]{3,2,1,0:T(8,128)S(1)}, u32[]{:S(2)}, u32[]{:S(2)}) collective-permute-start(f32[6,4,16,256]{3,2,1,0:T(8,128)S(1)} %get-tuple-element.9.refs_2_), channel_id=1, source_target_pairs={{1,4},{4,1},{5,8},{8,5},{9,12},{12,9},{3,6},{6,3},{7,10},{10,7},{1... | collective-permute-start | bytes 1179656 | tf_op jit(solution)/shard_map/ppermute | solution.py:298
  28.8 3.0 %collective-permute-start.8 = (f32[6,4,16,256]{3,2,1,0:T(8,128)S(1)}, f32[6,4,16,256]{3,2,1,0:T(8,128)S(1)}, u32[]{:S(2)}, u32[]{:S(2)}) collective-permute-start(f32[6,4,16,256]{3,2,1,0:T(8,128)S(1)} %get-tuple-element.10.refs_5_), channel_id=1, source_target_pairs={{0,1},{1,0},{2,3},{3,2},{4,5},{5,4},{6,7},{7,6},{8,9},{9,8},{10,11... | collective-permute-start | bytes 1179656 | tf_op jit(solution)/shard_map/ppermute | solution.py:291
  31.8 0.7 %collective-permute-start.7 = (f32[6,4,16,256]{3,2,1,0:T(8,128)S(1)}, f32[6,4,16,256]{3,2,1,0:T(8,128)S(1)}, u32[]{:S(2)}, u32[]{:S(2)}) collective-permute-start(f32[6,4,16,256]{3,2,1,0:T(8,128)S(1)} %get-tuple-element.10.refs_5_), channel_id=1, source_target_pairs={{1,4},{4,1},{5,8},{8,5},{9,12},{12,9},{3,6},{6,3},{7,10},{10,7},{1... | collective-permute-start | bytes 1179656 | tf_op jit(solution)/shard_map/ppermute | solution.py:298
  32.5 0.0 collective-permute-done.9.refs_8_
  32.5 3.0 %collective-permute-start.11 = (f32[12,4,8,128]{3,2,1,0:T(8,128)S(1)}, f32[12,4,8,128]{3,2,1,0:T(8,128)S(1)}, u32[]{:S(2)}, u32[]{:S(2)}) collective-permute-start(f32[12,4,8,128]{3,2,1,0:T(8,128)S(1)} %collective-permute-done.9.refs_8_), channel_id=1, source_target_pairs={{0,1},{1,0},{2,3},{3,2},{4,5},{5,4},{6,7},{7,6},{8,9},{9,8},{10,11... | collective-permute-start | bytes 589832 | tf_op jit(solution)/shard_map/ppermute | solution.py:291
  35.5 1.1 %collective-permute-done.11.refs_9_ = f32[12,4,8,128]{3,2,1,0:T(8,128)S(1)} collective-permute-done((f32[12,4,8,128]{3,2,1,0:T(8,128)S(1)}, f32[12,4,8,128]{3,2,1,0:T(8,128)S(1)}, u32[]{:S(2)}, u32[]{:S(2)}) %collective-permute-start.11) | collective-permute-done | bytes 196640 | tf_op jit(solution)/shard_map/ppermute | solution.py:291
  36.5 0.7 %collective-permute-start.10 = (f32[12,4,8,128]{3,2,1,0:T(8,128)S(1)}, f32[12,4,8,128]{3,2,1,0:T(8,128)S(1)}, u32[]{:S(2)}, u32[]{:S(2)}) collective-permute-start(f32[12,4,8,128]{3,2,1,0:T(8,128)S(1)} %collective-permute-done.9.refs_8_), channel_id=1, source_target_pairs={{1,4},{4,1},{5,8},{8,5},{9,12},{12,9},{3,6},{6,3},{7,10},{10,7},{1... | collective-permute-start | bytes 589832 | tf_op jit(solution)/shard_map/ppermute | solution.py:298
  37.2 0.0 copy-done.7
  37.2 0.0 collective-permute-done.10.refs_7_
  37.2 0.0 collective-permute-done.6.refs_3_
  37.2 0.0 collective-permute-done.5.refs_1_
  37.2 0.0 collective-permute-done.8.refs_6_
  37.3 0.0 collective-permute-done.7.refs_4_
  37.3 0.0 copy-start.5
  37.3 0.1 broadcast_in_dim.5.refs_12_
  37.4 0.0 copy-done.2
  37.4 0.0 copy-done.3
  37.4 0.0 copy-done.4
  37.4 0.0 copy-done.1
  37.4 0.6 copy-done.5
  38.0 5.2 %shard_map.114 = (f32[12,4,16,256]{3,2,1,0:T(8,128)}, f32[16,8,128]{2,1,0:T(8,128)}) custom-call(s32[7]{0:T(128)S(1)} %stack.31.refs_0_, f32[6,4,16,256]{3,2,1,0:T(8,128)S(1)} %collective-permute-done.5.refs_1_, f32[6,4,16,256]{3,2,1,0:T(8,128)S(1)} %get-tuple-element.9.refs_2_, f32[6,4,16,256]{3,2,1,0:T(8,128)S(1)} %collective-permute-done.6.refs_3_, ...), custom_call_target="tpu_custom_call" | custom-call | flops 20000000 | bytes 4000000 | tf_op jit(solution)/shard_map/pallas_call | solution.py:402
  43.1 10.4 %all-to-all-start = ((f32[16,8,128]{2,1,0:T(8,128)}), f32[16,8,128]{2,1,0:T(8,128)S(1)}, u32[]{:S(2)}, u32[]{:S(2)}) async-start(f32[16,8,128]{2,1,0:T(8,128)} %get-tuple-element.15), calls=%async_computation | async-start | bytes 131072 | tf_op jit(solution)/shard_map/all_to_all | solution.py:419
  53.5 6.9 %all-to-all-done = f32[16,8,128]{2,1,0:T(8,128)S(1)} async-done(((f32[16,8,128]{2,1,0:T(8,128)}), f32[16,8,128]{2,1,0:T(8,128)S(1)}, u32[]{:S(2)}, u32[]{:S(2)}) %all-to-all-start) | async-done | bytes 65568 | tf_op jit(solution)/shard_map/all_to_all | solution.py:419
  60.4 0.7 %constant_dynamic-slice_fusion.1 = f32[8,16]{1,0:T(8,128)} fusion(f32[8,128]{1,0:T(8,128)S(1)} %reduce_sum.9, s32[]{:T(128)S(6)} %select_n.17), kind=kLoop, calls=%fused_computation.13 | loop fusion | bytes 1028 | tf_op jit(solution)/shard_map/dynamic_slice | solution.py:421
  (10 shorter events, 0.1 us)
Async XLA Ops:
  0.6 14.8 %collective-permute-start.1 = (f32[12,4,16,256]{3,2,1,0:T(8,128)}, f32[12,4,16,256]{3,2,1,0:T(8,128)S(1)}, u32[]{:S(2)}, u32[]{:S(2)}) collective-permute-start(f32[12,4,16,256]{3,2,1,0:T(8,128)} %bitcast.24), channel_id=1, source_target_pairs={{0,1},{1,0},{2,3},{3,2},{4,5},{5,4},{6,7},{7,6},{8,9},{9,8},{10,11... | collective-permute-start | bytes 2359304 | tf_op jit(solution)/shard_map/ppermute | solution.py:291
  1.1 14.3 %collective-permute-start = (f32[12,4,16,256]{3,2,1,0:T(8,128)}, f32[12,4,16,256]{3,2,1,0:T(8,128)S(1)}, u32[]{:S(2)}, u32[]{:S(2)}) collective-permute-start(f32[12,4,16,256]{3,2,1,0:T(8,128)} %bitcast.25), channel_id=1, source_target_pairs={{1,4},{4,1},{5,8},{8,5},{9,12},{12,9},{3,6},{6,3},{7,10},{10,7},{1... | collective-permute-start | bytes 2359304 | tf_op jit(solution)/shard_map/ppermute | solution.py:298
  2.6 3.8 %copy-start.6 = (f32[4,16,256]{2,1,0:T(8,128)S(1)}, f32[4,16,256]{2,1,0:T(8,128)}, u32[]{:S(2)}) copy-start(f32[4,16,256]{2,1,0:T(8,128)} %param.11) | copy-start | bytes 196612
  3.8 11.6 %copy-start = (f32[2,6,4,16,256]{4,3,2,1,0:T(8,128)S(1)}, f32[2,6,4,16,256]{4,3,2,1,0:T(8,128)}, u32[]{:S(2)}) copy-start(f32[2,6,4,16,256]{4,3,2,1,0:T(8,128)} %param.10) | copy-start | bytes 2359300
  3.9 6.4 %collective-permute-start.2 = (f32[13,4,8,128]{3,2,1,0:T(8,128)S(1)}, f32[13,4,8,128]{3,2,1,0:T(8,128)S(1)}, u32[]{:S(2)}, u32[]{:S(2)}) collective-permute-start(f32[13,4,8,128]{3,2,1,0:T(8,128)S(1)} %maximum_maximum_fusion), channel_id=1, source_target_pairs={{0,2},{2,0},{1,3},{3,1},{4,6},{6,4},{5,7},{7,5},{8,10},{10,8},{9,1... | collective-permute-start | bytes 638984 | tf_op jit(solution)/shard_map/ppermute | solution.py:307
  10.3 5.1 %collective-permute-start.4 = (f32[17,4,8,128]{3,2,1,0:T(8,128)S(1)}, f32[17,4,8,128]{3,2,1,0:T(8,128)S(1)}, u32[]{:S(2)}, u32[]{:S(2)}) collective-permute-start(f32[17,4,8,128]{3,2,1,0:T(8,128)S(1)} %pad_maximum_fusion.refs_5_), channel_id=1, source_target_pairs={{0,1},{1,0},{2,3},{3,2},{4,5},{5,4},{6,7},{7,6},{8,9},{9,8},{10,11... | collective-permute-start | bytes 835592 | tf_op jit(solution)/shard_map/ppermute | solution.py:291
  12.7 2.7 %collective-permute-start.3 = (f32[17,4,8,128]{3,2,1,0:T(8,128)S(1)}, f32[17,4,8,128]{3,2,1,0:T(8,128)S(1)}, u32[]{:S(2)}, u32[]{:S(2)}) collective-permute-start(f32[17,4,8,128]{3,2,1,0:T(8,128)S(1)} %pad_maximum_fusion.refs_5_), channel_id=1, source_target_pairs={{1,4},{4,1},{5,8},{8,5},{9,12},{12,9},{3,6},{6,3},{7,10},{10,7},{1... | collective-permute-start | bytes 835592 | tf_op jit(solution)/shard_map/ppermute | solution.py:298
  13.4 0.7 %copy-start.9 = (s32[1,8]{1,0:T(1,128)S(1)}, s32[1,8]{1,0:T(1,128)}, u32[]{:S(2)}) copy-start(s32[1,8]{1,0:T(1,128)} %param.12) | copy-start | bytes 100
  14.2 0.7 %copy-start.8 = (s32[128]{0:T(128)S(1)}, s32[128]{0:T(128)}, u32[]{:S(2)}) copy-start(s32[128]{0:T(128)} %param.13) | copy-start | bytes 1540
  15.4 21.8 %copy-start.7 = (f32[8,128]{1,0:T(8,128)S(1)}, f32[8,128]{1,0:T(8,128)}, u32[]{:S(2)}) copy-start(f32[8,128]{1,0:T(8,128)} %param.14) | copy-start | bytes 12292
  15.4 21.9 %copy-start.2 = (f32[16,16,128]{2,1,0:T(8,128)S(1)}, f32[16,16,128]{2,1,0:T(8,128)}, u32[]{:S(2)}) copy-start(f32[16,16,128]{2,1,0:T(8,128)} %constant.62.clone.refs_17_) | copy-start | bytes 393220
  15.5 21.9 %copy-start.3 = (f32[128,256]{1,0:T(8,128)S(1)}, f32[128,256]{1,0:T(8,128)}, u32[]{:S(2)}) copy-start(f32[128,256]{1,0:T(8,128)} %constant.61.clone.refs_16_) | copy-start | bytes 393220
  15.5 21.9 %copy-start.4 = (f32[128,256]{1,0:T(8,128)S(1)}, f32[128,256]{1,0:T(8,128)}, u32[]{:S(2)}) copy-start(f32[128,256]{1,0:T(8,128)} %constant.60.clone.refs_15_) | copy-start | bytes 393220
  19.0 18.4 %copy-start.1 = (f32[16,16,128]{2,1,0:T(8,128)S(1)}, f32[16,16,128]{2,1,0:T(8,128)}, u32[]{:S(2)}) copy-start(f32[16,16,128]{2,1,0:T(8,128)} %constant.63.clone.refs_18_) | copy-start | bytes 393220
  19.1 13.4 %collective-permute-start.9 = (f32[12,4,8,128]{3,2,1,0:T(8,128)S(1)}, f32[12,4,8,128]{3,2,1,0:T(8,128)S(1)}, u32[]{:S(2)}, u32[]{:S(2)}) collective-permute-start(f32[12,4,8,128]{3,2,1,0:T(8,128)S(1)} %get-tuple-element.11), channel_id=1, source_target_pairs={{0,2},{2,0},{1,3},{3,1},{4,6},{6,4},{5,7},{7,5},{8,10},{10,8},{9,1... | collective-permute-start | bytes 589832 | tf_op jit(solution)/shard_map/ppermute | solution.py:307
  21.0 16.2 %collective-permute-start.6 = (f32[6,4,16,256]{3,2,1,0:T(8,128)S(1)}, f32[6,4,16,256]{3,2,1,0:T(8,128)S(1)}, u32[]{:S(2)}, u32[]{:S(2)}) collective-permute-start(f32[6,4,16,256]{3,2,1,0:T(8,128)S(1)} %get-tuple-element.9.refs_2_), channel_id=1, source_target_pairs={{0,1},{1,0},{2,3},{3,2},{4,5},{5,4},{6,7},{7,6},{8,9},{9,8},{10,11... | collective-permute-start | bytes 1179656 | tf_op jit(solution)/shard_map/ppermute | solution.py:291
  28.1 9.2 %collective-permute-start.5 = (f32[6,4,16,256]{3,2,1,0:T(8,128)S(1)}, f32[6,4,16,256]{3,2,1,0:T(8,128)S(1)}, u32[]{:S(2)}, u32[]{:S(2)}) collective-permute-start(f32[6,4,16,256]{3,2,1,0:T(8,128)S(1)} %get-tuple-element.9.refs_2_), channel_id=1, source_target_pairs={{1,4},{4,1},{5,8},{8,5},{9,12},{12,9},{3,6},{6,3},{7,10},{10,7},{1... | collective-permute-start | bytes 1179656 | tf_op jit(solution)/shard_map/ppermute | solution.py:298
  28.8 8.5 %collective-permute-start.8 = (f32[6,4,16,256]{3,2,1,0:T(8,128)S(1)}, f32[6,4,16,256]{3,2,1,0:T(8,128)S(1)}, u32[]{:S(2)}, u32[]{:S(2)}) collective-permute-start(f32[6,4,16,256]{3,2,1,0:T(8,128)S(1)} %get-tuple-element.10.refs_5_), channel_id=1, source_target_pairs={{0,1},{1,0},{2,3},{3,2},{4,5},{5,4},{6,7},{7,6},{8,9},{9,8},{10,11... | collective-permute-start | bytes 1179656 | tf_op jit(solution)/shard_map/ppermute | solution.py:291
  31.8 5.5 %collective-permute-start.7 = (f32[6,4,16,256]{3,2,1,0:T(8,128)S(1)}, f32[6,4,16,256]{3,2,1,0:T(8,128)S(1)}, u32[]{:S(2)}, u32[]{:S(2)}) collective-permute-start(f32[6,4,16,256]{3,2,1,0:T(8,128)S(1)} %get-tuple-element.10.refs_5_), channel_id=1, source_target_pairs={{1,4},{4,1},{5,8},{8,5},{9,12},{12,9},{3,6},{6,3},{7,10},{10,7},{1... | collective-permute-start | bytes 1179656 | tf_op jit(solution)/shard_map/ppermute | solution.py:298
  32.5 4.1 %collective-permute-start.11 = (f32[12,4,8,128]{3,2,1,0:T(8,128)S(1)}, f32[12,4,8,128]{3,2,1,0:T(8,128)S(1)}, u32[]{:S(2)}, u32[]{:S(2)}) collective-permute-start(f32[12,4,8,128]{3,2,1,0:T(8,128)S(1)} %collective-permute-done.9.refs_8_), channel_id=1, source_target_pairs={{0,1},{1,0},{2,3},{3,2},{4,5},{5,4},{6,7},{7,6},{8,9},{9,8},{10,11... | collective-permute-start | bytes 589832 | tf_op jit(solution)/shard_map/ppermute | solution.py:291
  36.5 0.7 %collective-permute-start.10 = (f32[12,4,8,128]{3,2,1,0:T(8,128)S(1)}, f32[12,4,8,128]{3,2,1,0:T(8,128)S(1)}, u32[]{:S(2)}, u32[]{:S(2)}) collective-permute-start(f32[12,4,8,128]{3,2,1,0:T(8,128)S(1)} %collective-permute-done.9.refs_8_), channel_id=1, source_target_pairs={{1,4},{4,1},{5,8},{8,5},{9,12},{12,9},{3,6},{6,3},{7,10},{10,7},{1... | collective-permute-start | bytes 589832 | tf_op jit(solution)/shard_map/ppermute | solution.py:298
  37.3 0.7 %copy-start.5 = (f32[16,128]{1,0:T(8,128)S(1)}, f32[16,128]{1,0:T(8,128)}, u32[]{:S(2)}) copy-start(f32[16,128]{1,0:T(8,128)} %constant.64.clone.refs_19_) | copy-start | bytes 24580
  43.1 17.3 %all-to-all-start = ((f32[16,8,128]{2,1,0:T(8,128)}), f32[16,8,128]{2,1,0:T(8,128)S(1)}, u32[]{:S(2)}, u32[]{:S(2)}) async-start(f32[16,8,128]{2,1,0:T(8,128)} %get-tuple-element.15), calls=%async_computation | async-start | bytes 131072 | tf_op jit(solution)/shard_map/all_to_all | solution.py:419

commit v6 on v5

--- a/solution.py
+++ b/solution.py
@@ -43,12 +43,6 @@
     return np.array(rows), np.array(waves)
 
 
-def band_table(counts, place):
-    ends = jnp.cumsum(counts)
-    starts = ends - counts
-    return ((place >= starts[None, :]) & (place < ends[None, :])).astype(jnp.float32)
-
-
 def mm(left, right):
     return jnp.dot(left, right, precision=highest, preferred_element_type=jnp.float32)
 
@@ -91,9 +85,12 @@
     depth, rows_own, sides, second = cfg
     it = iter(refs)
     take = lambda n: [next(it) for _ in range(n)]
-    info = next(it)
+    n_z, n_gy = 2 * lax.axis_size("gz"), lax.axis_size("gy")
+    core, gy = lax.axis_index("col"), lax.axis_index("gy")
+    first_layer = (2 * lax.axis_index("gz") + core) * depth
+    layer_start = depth * n_z // 2 - depth - depth // 2
     pieces = 2 if second else 1
-    full = [take(3) for _ in range(pieces)]
+    full = [take(pieces), take(1), take(1)]
     strip_in = [take(3) for _ in range(sides)]
     if second:
         (scale_ref, acc_in) = take(2)
@@ -101,26 +98,26 @@
         out, share = take(2)
         st, strips, acc, done, sem_full, sem_strip, sem_out = take(7)
     else:
-        done = take(2)
+        done = take(3)
         scale_ref, acc = take(2)
         strip_out = take(sides)
-        st, strips, sem_full, sem_strip = take(4)
-
-    core, gy = info[0], info[1]
+        st, strips, eps, sem_full, sem_strip, sem_eps = take(6)
 
     def copies_of(b, place):
         layers = pl.ds(place * depth, depth)
         found = []
-        for p in range(pieces):
-            planes = pl.ds(12 // pieces * p, 12 // pieces)
+        for p, ref in enumerate(full[b]):
+            count = min(ref.shape[0], 12)
+            planes = pl.ds(count * p, count)
             found.append(
                 pltpu.make_async_copy(
-                    full[p][b], st.at[planes, layers, pl.ds(0, rows_own), :], sem_full.at[p, place]
+                    ref.at[pl.ds(0, count)], st.at[planes, layers, pl.ds(0, rows_own), :], sem_full.at[p, place]
                 )
             )
         for s in range(sides):
-            planes = pl.ds(0, strip_in[s][b].shape[0])
-            found.append(pltpu.make_async_copy(strip_in[s][b], strips.at[s, planes, layers], sem_strip.at[s, place]))
+            found.append(pltpu.make_async_copy(strip_in[s][b], strips.at[s, :, layers], sem_strip.at[s, place]))
+        if not second:
+            found.append(pltpu.make_async_copy(full[b][0].at[12], eps.at[layers], sem_eps.at[place]))
         return found
 
     @pl.when(core == 0)
@@ -142,8 +139,22 @@
     n_layers = 3 * depth
 
     def arrive(place):
-        for copy in copies_of(place, place):
-            copy.wait()
+        if place == 1:
+            for copy in copies_of(1, 1):
+                copy.wait()
+        else:
+            here = core == place // 2
+
+            @pl.when(here)
+            def _():
+                for copy in copies_of(0, place):
+                    copy.wait()
+
+            @pl.when(jnp.logical_not(here))
+            def _():
+                for copy in copies_of(2, place):
+                    copy.wait()
+
         for l in range(place * depth, (place + 1) * depth):
             for c in range(12 if second else 13):
                 if sides == 2:
@@ -159,19 +170,18 @@
                 tile = jnp.concatenate([left, right], axis=1)
                 if c == 12:
                     scale_ref[l, rows_own:rows, :] = courant * tile
-                    for t in range(2):
-                        pair = [strips[0, 13 + 2 * t + half, l] for half in range(2)]
-                        scale_ref[l, 8 * t : 8 * t + 8, :] = courant * jnp.concatenate(pair, axis=1)
+                    scale_ref[l, :rows_own, :] = courant * eps[l]
                 else:
                     st[c, l, rows_own:rows, :] = tile
 
     row_at = lax.broadcasted_iota(jnp.int32, (rows, nx), 0)
     lane_at = lax.broadcasted_iota(jnp.int32, (rows, 128), 1)
     last_lane, first_lane = lane_at == 127, lane_at == 0
-    ahead = jnp.where(info[4] > 0, courant, 0.0)
-    behind = jnp.where(info[5] > 0, courant, 0.0)
+    ahead = jnp.where(gy < n_gy - 1, courant, 0.0)
+    behind = jnp.where(gy > 0, courant, 0.0)
     coef_in = jnp.where(row_at < rows_own, courant, jnp.where(row_at < rows_own + HALF, ahead, behind))
-    low_layer, high_layer = info[2], info[3]
+    low_layer = depth - first_layer
+    high_layer = low_layer + depth * n_z
 
     def y_ahead(f):
         return pltpu.roll(f, rows - 1, 0)
@@ -222,6 +232,7 @@
                         done[b + c, own] = f[:rows_own]
                     else:
                         done[r][c, own] = f[:rows_own]
+                        done[2][b + c, own] = f[:rows_own]
                         up, down = f[rows_own - 8 : rows_own], f[:8]
                         if sides == 2:
                             strip_out[0][b + c, own] = strip_of(up, True)
@@ -250,7 +261,8 @@
             g = jnp.zeros((rows_own, nx), jnp.float32)
             for c in range(3):
                 g = g + acc[0, c, own] * acc[0, 3 + c, own] - acc[1, c, own] * acc[1, 3 + c, own]
-            in_layer = (info[6] + own >= 0) & (info[6] + own < 3 * depth)
+            layer = first_layer + own - layer_start
+            in_layer = (layer >= 0) & (layer < 3 * depth)
             column_sum = column_sum + jnp.where(in_layer, g, 0.0)
         pooled = jnp.zeros(row_wide.shape[1:], jnp.float32)
         for k in range(rows_own):
@@ -270,11 +282,32 @@
             spectrum = transform(mm(basis_y[...], placed(weighted, gy, tall)), basis_xt) * response[...]
             shares = mm(basis_yt[...], transform(spectrum, basis_x))
         count = share.shape[0]
-        n_gy = shares.shape[0] // band
         for d in range(count):
             y = d // 2 % n_gy
             share[d] = shares[y * band : (y + 1) * band]
         result.wait()
+
+
+def table_kernel(row_counts, col_counts, row_wide, col_table):
+    band, nx = row_wide.shape[1:]
+    row = lax.broadcasted_iota(jnp.int32, (band, nx), 0)
+    start = jnp.zeros((band, nx), jnp.int32)
+    stop = jnp.zeros((band, nx), jnp.int32)
+    total = jnp.int32(0)
+    for k in range(band):
+        start = jnp.where(row == k, total, start)
+        total = total + row_counts[0, k]
+        stop = jnp.where(row == k, total, stop)
+    for p in range(row_wide.shape[0]):
+        row_wide[p] = jnp.where((start <= p) & (p < stop), 1.0, 0.0)
+    width = col_table.shape[1]
+    counts = jnp.broadcast_to(col_counts[...].astype(jnp.float32), (16, width))
+    before = lax.broadcasted_iota(jnp.int32, (width, width), 0) <= lax.broadcasted_iota(jnp.int32, (width, width), 1)
+    upto = jnp.where(before, 1.0, 0.0).astype(jnp.bfloat16)
+    ends = jnp.dot(counts.astype(jnp.bfloat16), upto, preferred_element_type=jnp.float32)
+    starts = ends - counts
+    place = lax.broadcasted_iota(jnp.int32, col_table.shape, 0).astype(jnp.float32)
+    col_table[...] = jnp.where((place >= starts[:1]) & (place < ends[:1]), 1.0, 0.0)
 
 
 def body(fields, eps_inv, row_counts, col_counts, density):
@@ -285,7 +318,7 @@
     n_z = n_gz * 2
     assert HALF == depth and rows_own == 16 and nx == 256
     rows = rows_own + 2 * HALF
-    own = fields.reshape(runs * comps, depth, rows_own, nx)
+    own = jnp.concatenate([fields.reshape(runs * comps, depth, rows_own, nx), eps_inv[None]])
 
     def swap_core(x):
         return lax.ppermute(x, "col", [(0, 1), (1, 0)])
@@ -306,72 +339,63 @@
     def along_y(x, s):
         return lax.ppermute(x, "gy", list(ways[s].items()))
 
-    layer_start = depth * n_z // 2 - depth - depth // 2
-    info = [
-        core,
-        gy,
-        depth - index * depth,
-        depth * n_z - index * depth + depth,
-        jnp.where(gy < n_gy - 1, 1, 0),
-        jnp.where(gy > 0, 1, 0),
-        index * depth - layer_start,
-    ]
-    info = jnp.stack([jnp.asarray(v, jnp.int32) for v in info])
-
     anywhere = pl.BlockSpec(memory_space=pl.ANY)
     vmem = pl.BlockSpec(memory_space=pltpu.VMEM)
     smem = pl.BlockSpec(memory_space=pltpu.SMEM)
     shape = lambda *s: jax.ShapeDtypeStruct(s, jnp.float32)
     limit = pltpu.CompilerParams(vmem_limit_bytes=24 * 1024 * 1024)
 
-    def strips_sent(strips, more=None):
+    def strips_sent(strips):
         sent = []
         for s, strip in enumerate(strips):
             mine = along_y(strip, s)
-            if more is not None and s == 0:
-                mine = jnp.concatenate([mine, more])
-            sent += [cross(mine), mine, swap_core(mine)]
+            far = cross(mine)
+            sent += [far, mine, swap_core(mine)]
         return sent
 
     starts = [(1 - gy) * (rows_own - HALF)] if sides == 1 else [rows_own - HALF, 0]
     strips = []
     for start in starts:
-        rows_f = lax.dynamic_slice_in_dim(own, start, HALF, 2)
-        rows_e = lax.dynamic_slice_in_dim(eps_inv, start, HALF, 1)[None]
-        halves = [jnp.concatenate([f[..., :128], f[..., 128:]], 2) for f in (rows_f, rows_e)]
-        strips.append(jnp.concatenate(halves))
-    tiles = eps_inv.reshape(depth, 2, 8, 2, 128).transpose(1, 3, 0, 2, 4).reshape(4, depth, 8, 128)
-    sent = strips_sent(strips, tiles)
-    operands = [info, cross(own), own, swap_core(own)] + sent
+        edge = lax.dynamic_slice_in_dim(own, start, HALF, 2)
+        strips.append(jnp.concatenate([edge[..., :128], edge[..., 128:]], 2))
+    sent = strips_sent(strips)
+    operands = [cross(own), own, swap_core(own)] + sent
     cost = pl.CostEstimate(flops=20_000_000, bytes_accessed=4_000_000, transcendentals=0)
     window = pltpu.VMEM((12, 3 * depth, rows, nx), jnp.float32)
     block = pltpu.VMEM((12, depth, rows_own, nx), jnp.float32)
     arrivals = [pltpu.SemaphoreType.DMA((2, 3)), pltpu.SemaphoreType.DMA((sides, 3))]
-    half_0, half_1, scale, acc, *strips = pl.pallas_call(
+    half_0, half_1, state, scale, acc, *strips = pl.pallas_call(
         functools.partial(window_kernel, (depth, rows_own, sides, False)),
         out_shape=(
             shape(comps, depth, rows_own, nx),
             shape(comps, depth, rows_own, nx),
+            shape(runs * comps, depth, rows_own, nx),
             shape(3 * depth, rows, nx),
             shape(2, 6, depth, rows_own, nx),
         )
         + (shape(12, depth, 8, 128),) * sides,
-        in_specs=[smem] + [anywhere] * (3 + 3 * sides),
-        out_specs=(vmem,) * (4 + sides),
+        in_specs=[anywhere] * (3 + 3 * sides),
+        out_specs=(vmem,) * (5 + sides),
         scratch_shapes=[
             window,
-            pltpu.VMEM((sides, 17, 3 * depth, 8, 128), jnp.float32),
+            pltpu.VMEM((sides, 13, 3 * depth, 8, 128), jnp.float32),
+            pltpu.VMEM((3 * depth, rows_own, nx), jnp.float32),
         ]
-        + arrivals,
+        + arrivals
+        + [pltpu.SemaphoreType.DMA((3,))],
         compiler_params=limit,
         cost_estimate=cost,
     )(*operands)
 
     band, design_cols = density.shape
     tall = band * n_gy
-    row_table = band_table(row_counts[0], jnp.arange(rows_own, dtype=jnp.int32)[:, None])
-    row_wide = jnp.broadcast_to(row_table[:, :, None], (rows_own, band, nx))
-    col_table = band_table(col_counts, jnp.arange(nx, dtype=jnp.int32)[:, None])
+    row_wide, col_table = pl.pallas_call(
+        table_kernel,
+        out_shape=(shape(rows_own, band, nx), shape(nx, design_cols)),
+        in_specs=[smem, vmem],
+        out_specs=(vmem, vmem),
+        compiler_params=pltpu.CompilerParams(vmem_limit_bytes=4 * 1024 * 1024),
+    )(row_counts, col_counts.reshape(1, design_cols))
     basis_x, wave_x = real_basis(design_cols)
     basis_y, wave_y = real_basis(tall)
     response = 1.0 / (
@@ -392,9 +416,7 @@
         return const(np.concatenate([high, matrix - high], axis=1))
 
     sent = strips_sent(strips)
-    operands = [info]
-    for half in (half_0, half_1):
-        operands += [cross(half), half, swap_core(half)]
+    operands = [cross(half_0), cross(half_1), state, swap_core(state)]
     operands += sent + [scale, acc]
     operands += [row_wide, col_table, slope_of(density), halves(basis_x), halves(basis_x.T)]
     operands += [const(tables[0]), const(tables[1]), const(response)]
@@ -402,7 +424,7 @@
     fields_out, share = pl.pallas_call(
         functools.partial(window_kernel, (depth, rows_own, sides, True)),
         out_shape=(shape(runs * comps, depth, rows_own, nx), shape(n_all, band, design_cols)),
-        in_specs=[smem] + [anywhere] * (6 + 3 * sides) + [vmem] * 10,
+        in_specs=[anywhere] * (4 + 3 * sides) + [vmem] * 10,
         out_specs=(anywhere, vmem),
         scratch_shapes=[
             window,

time: 61.5 us -> 58.5 us (0.951)
  waiting for transfers between devices: 11.8 us -> 17.3 us
  starting transfers between devices: 34.2 us -> 29.3 us
  local copies, waits for them, and re-layouts: 4.83 us -> 0.76 us
  other arithmetic: 0.59 us -> 1.46 us
    ppermute x2, waiting for transfers between devices: 3.82 us -> 8.97 us  [along_y(): return lax.ppermute(x, 'gy', list(ways[s].items()))]
    ppermute x5 -> x4, starting transfers between devices: 15.9 us -> 11 us  [swap_core(): return lax.ppermute(x, 'col', [(0, 1), (1, 0)])]
    unnamed x20, local copies, waits for them, and re-layouts: 1.92 us -> 0.06 us
    all_to_all x1, starting transfers between devices: 10.4 us -> 11.9 us  [body(): got = lax.all_to_all(share, ('gz', 'gy', 'col'), 0, 0)]
    ppermute x2, starting transfers between devices: 4.5 us -> 3.05 us  [along_y(): return lax.ppermute(x, 'gy', list(ways[s].items()))]
    concatenate x2 -> x3, other arithmetic: 0.07 us -> 1.43 us  [the longest x2 1.37 us: body(): jnp.concatenate([fields.reshape(runs * comps, depth, rows_own, nx), eps_i...]
    slice x2 -> x1, local copies, waits for them, and re-layouts: 1.19 us -> 0.04 us  [body(): strips.append(jnp.concatenate([edge[..., :128], edge[..., 128:]], 2))]
    pallas_call x2, Pallas kernels: 8.73 us -> 7.68 us  [body(): pl.pallas_call(functools.partial(window_kernel, (depth, rows_own, sides,...]
  transfers between devices with their start and end apart: 13 -> 12, of which waited for: 3 -> 5; matrix products, arithmetic and copies ran while one was open for 4% -> 0% of each run, Pallas kernels for 0% -> 1%
where the time goes in v6:
time: 58.5 us; the launch traced here: 58.2 us
  starting transfers between devices  29.3 us (50%)
  waiting for transfers between devices  17.3 us (30%)
  Pallas kernels  8.38 us (14%)
  other arithmetic  1.46 us (2%)
  between operations  0.89 us (2%)
  local copies, waits for them, and re-layouts  0.76 us (1%)
    all_to_all x1, starting transfers between devices, body(): got = lax.all_to_all(share, ('gz', 'gy', 'col'), 0, 0)  11.9 us
    ppermute x4, starting transfers between devices, swap_core(): return lax.ppermute(x, 'col', [(0, 1), (1, 0)])  11 us
    ppermute x2, waiting for transfers between devices, along_y(): return lax.ppermute(x, 'gy', list(ways[s].items()))  8.97 us
    pallas_call x2, Pallas kernels, body(): pl.pallas_call(functools.partial(window_kernel, (depth, rows_own, sides,...  7.68 us
    all_to_all x1, waiting for transfers between devices, body(): got = lax.all_to_all(share, ('gz', 'gy', 'col'), 0, 0)  6.89 us
    ppermute x5, starting transfers between devices, cross(): return lax.ppermute(x, Z, pairs)  3.4 us
    ppermute x2, starting transfers between devices, along_y(): return lax.ppermute(x, 'gy', list(ways[s].items()))  3.05 us
    ppermute x4, waiting for transfers between devices, swap_core(): return lax.ppermute(x, 'col', [(0, 1), (1, 0)])  1.47 us
  transfers between devices with their start and end apart: 12, of which 5 were waited for; matrix products, arithmetic and copies ran while one was open for 0% of the time, Pallas kernels for 1%

profile of v6, /device:TPU:0, one launch (start us, length us, event | category | flops | bytes accessed | tf_op | source)
XLA Modules:
  0.0 58.2 jit_solution(16919349826065104187)
XLA Ops:
  0.6 0.0 copy-start.7
  0.6 0.0 copy-start.8
  0.6 1.3 %pad_maximum_fusion.refs_1_ = f32[13,4,16,256]{3,2,1,0:T(8,128)S(1)} fusion(f32[1,4,16,256]{3,2,1,0:T(8,128)} %bitcast.7, f32[12,4,16,256]{3,2,1,0:T(8,128)} %bitcast.5), kind=kLoop, calls=%fused_computation.1 | loop fusion | flops 212992 | bytes 1703936 | tf_op jit(solution)/shard_map/concatenate | solution.py:321
  2.0 0.7 %collective-permute-start = (f32[13,4,16,256]{3,2,1,0:T(8,128)S(1)}, f32[13,4,16,256]{3,2,1,0:T(8,128)S(1)}, u32[]{:S(2)}, u32[]{:S(2)}) collective-permute-start(f32[13,4,16,256]{3,2,1,0:T(8,128)S(1)} %pad_maximum_fusion.refs_1_), channel_id=1, source_target_pairs={{1,4},{4,1},{5,8},{8,5},{9,12},{12,9},{3,6},{6,3},{7,10},{10,7},{1... | collective-permute-start | bytes 2555912 | tf_op jit(solution)/shard_map/ppermute | solution.py:331
  2.7 4.4 %collective-permute-start.1 = (f32[13,4,16,256]{3,2,1,0:T(8,128)S(1)}, f32[13,4,16,256]{3,2,1,0:T(8,128)S(1)}, u32[]{:S(2)}, u32[]{:S(2)}) collective-permute-start(f32[13,4,16,256]{3,2,1,0:T(8,128)S(1)} %pad_maximum_fusion.refs_1_), channel_id=1, source_target_pairs={{0,1},{1,0},{2,3},{3,2},{4,5},{5,4},{6,7},{7,6},{8,9},{9,8},{10,11... | collective-permute-start | bytes 2555912 | tf_op jit(solution)/shard_map/ppermute | solution.py:324
  7.1 0.0 copy-done.7
  7.1 0.0 copy-done.8
  7.1 0.1 fusion
  7.2 0.1 pad_maximum_fusion.1
  7.3 0.0 copy-start
  7.3 0.0 copy-start.1
  7.3 0.0 copy-start.2
  7.3 0.0 copy-start.3
  7.3 1.6 %collective-permute-start.2 = (f32[13,4,8,128]{3,2,1,0:T(8,128)S(1)}, f32[13,4,8,128]{3,2,1,0:T(8,128)S(1)}, u32[]{:S(2)}, u32[]{:S(2)}) collective-permute-start(f32[13,4,8,128]{3,2,1,0:T(8,128)S(1)} %pad_maximum_fusion.1), channel_id=1, source_target_pairs={{0,2},{2,0},{1,3},{3,1},{4,6},{6,4},{5,7},{7,5},{8,10},{10,8},{9,1... | collective-permute-start | bytes 638984 | tf_op jit(solution)/shard_map/ppermute | solution.py:340
  8.9 5.7 %collective-permute-done.2.refs_4_ = f32[13,4,8,128]{3,2,1,0:T(8,128)S(1)} collective-permute-done((f32[13,4,8,128]{3,2,1,0:T(8,128)S(1)}, f32[13,4,8,128]{3,2,1,0:T(8,128)S(1)}, u32[]{:S(2)}, u32[]{:S(2)}) %collective-permute-start.2) | collective-permute-done | bytes 213024 | tf_op jit(solution)/shard_map/ppermute | solution.py:340
  14.6 0.7 %collective-permute-start.3 = (f32[13,4,8,128]{3,2,1,0:T(8,128)S(1)}, f32[13,4,8,128]{3,2,1,0:T(8,128)S(1)}, u32[]{:S(2)}, u32[]{:S(2)}) collective-permute-start(f32[13,4,8,128]{3,2,1,0:T(8,128)S(1)} %collective-permute-done.2.refs_4_), channel_id=1, source_target_pairs={{1,4},{4,1},{5,8},{8,5},{9,12},{12,9},{3,6},{6,3},{7,10},{10,7},{1... | collective-permute-start | bytes 638984 | tf_op jit(solution)/shard_map/ppermute | solution.py:331
  15.3 3.0 %collective-permute-start.4 = (f32[13,4,8,128]{3,2,1,0:T(8,128)S(1)}, f32[13,4,8,128]{3,2,1,0:T(8,128)S(1)}, u32[]{:S(2)}, u32[]{:S(2)}) collective-permute-start(f32[13,4,8,128]{3,2,1,0:T(8,128)S(1)} %collective-permute-done.2.refs_4_), channel_id=1, source_target_pairs={{0,1},{1,0},{2,3},{3,2},{4,5},{5,4},{6,7},{7,6},{8,9},{9,8},{10,11... | collective-permute-start | bytes 638984 | tf_op jit(solution)/shard_map/ppermute | solution.py:324
  18.2 0.0 collective-permute-done.3.refs_3_
  18.2 1.1 %collective-permute-done.4.refs_5_ = f32[13,4,8,128]{3,2,1,0:T(8,128)S(1)} collective-permute-done((f32[13,4,8,128]{3,2,1,0:T(8,128)S(1)}, f32[13,4,8,128]{3,2,1,0:T(8,128)S(1)}, u32[]{:S(2)}, u32[]{:S(2)}) %collective-permute-start.4) | collective-permute-done | bytes 213024 | tf_op jit(solution)/shard_map/ppermute | solution.py:324
  19.3 0.0 collective-permute-done.refs_0_
  19.3 0.0 collective-permute-done.1.refs_2_
  19.3 3.2 %shard_map.113 = (f32[6,4,16,256]{3,2,1,0:T(8,128)S(1)}, f32[6,4,16,256]{3,2,1,0:T(8,128)S(1)}, f32[12,4,16,256]{3,2,1,0:T(8,128)S(1)}, f32[12,24,256]{2,1,0:T(8...) custom-call(f32[13,4,16,256]{3,2,1,0:T(8,128)S(1)} %collective-permute-done.refs_0_, ...), custom_call_target="tpu_custom_call" | custom-call | flops 20000000 | bytes 4000000 | tf_op jit(solution)/shard_map/pallas_call | solution.py:367
  22.5 2.4 %collective-permute-start.7 = (f32[12,4,16,256]{3,2,1,0:T(8,128)S(1)}, f32[12,4,16,256]{3,2,1,0:T(8,128)S(1)}, u32[]{:S(2)}, u32[]{:S(2)}) collective-permute-start(f32[12,4,16,256]{3,2,1,0:T(8,128)S(1)} %get-tuple-element.14.refs_2_), channel_id=1, source_target_pairs={{0,1},{1,0},{2,3},{3,2},{4,5},{5,4},{6,7},{7,6},{8,9},{9,8},{10,11... | collective-permute-start | bytes 2359304 | tf_op jit(solution)/shard_map/ppermute | solution.py:324
  25.0 0.0 copy-start.9
  25.0 1.5 %collective-permute-start.8 = (f32[12,4,8,128]{3,2,1,0:T(8,128)S(1)}, f32[12,4,8,128]{3,2,1,0:T(8,128)S(1)}, u32[]{:S(2)}, u32[]{:S(2)}) collective-permute-start(f32[12,4,8,128]{3,2,1,0:T(8,128)S(1)} %get-tuple-element.15), channel_id=1, source_target_pairs={{0,2},{2,0},{1,3},{3,1},{4,6},{6,4},{5,7},{7,5},{8,10},{10,8},{9,1... | collective-permute-start | bytes 589832 | tf_op jit(solution)/shard_map/ppermute | solution.py:340
  26.5 0.7 %collective-permute-start.5 = (f32[6,4,16,256]{3,2,1,0:T(8,128)S(1)}, f32[6,4,16,256]{3,2,1,0:T(8,128)S(1)}, u32[]{:S(2)}, u32[]{:S(2)}) collective-permute-start(f32[6,4,16,256]{3,2,1,0:T(8,128)S(1)} %get-tuple-element.12), channel_id=1, source_target_pairs={{1,4},{4,1},{5,8},{8,5},{9,12},{12,9},{3,6},{6,3},{7,10},{10,7},{1... | collective-permute-start | bytes 1179656 | tf_op jit(solution)/shard_map/ppermute | solution.py:331
  27.1 0.0 copy-start.5
  27.2 0.0 copy-start.6
  27.2 0.7 %collective-permute-start.6 = (f32[6,4,16,256]{3,2,1,0:T(8,128)S(1)}, f32[6,4,16,256]{3,2,1,0:T(8,128)S(1)}, u32[]{:S(2)}, u32[]{:S(2)}) collective-permute-start(f32[6,4,16,256]{3,2,1,0:T(8,128)S(1)} %get-tuple-element.13), channel_id=1, source_target_pairs={{1,4},{4,1},{5,8},{8,5},{9,12},{12,9},{3,6},{6,3},{7,10},{10,7},{1... | collective-permute-start | bytes 1179656 | tf_op jit(solution)/shard_map/ppermute | solution.py:331
  27.9 0.0 copy-done.5
  27.9 0.0 copy-done.6
  27.9 0.7 %shard_map.114 = (f32[16,8,256]{2,1,0:T(8,128)S(1)}, f32[256,128]{1,0:T(8,128)S(1)}) custom-call(s32[1,8]{1,0:T(1,128)S(1)} %copy-done.5, s32[1,128]{1,0:T(1,128)S(1)} %bitcast.4), custom_call_target="tpu_custom_call" | custom-call | tf_op jit(solution)/shard_map/pallas_call | solution.py:392
  28.6 0.0 copy-start.4
  28.6 3.3 %collective-permute-done.8.refs_5_ = f32[12,4,8,128]{3,2,1,0:T(8,128)S(1)} collective-permute-done((f32[12,4,8,128]{3,2,1,0:T(8,128)S(1)}, f32[12,4,8,128]{3,2,1,0:T(8,128)S(1)}, u32[]{:S(2)}, u32[]{:S(2)}) %collective-permute-start.8) | collective-permute-done | bytes 196640 | tf_op jit(solution)/shard_map/ppermute | solution.py:340
  31.9 1.2 %collective-permute-start.10 = (f32[12,4,8,128]{3,2,1,0:T(8,128)S(1)}, f32[12,4,8,128]{3,2,1,0:T(8,128)S(1)}, u32[]{:S(2)}, u32[]{:S(2)}) collective-permute-start(f32[12,4,8,128]{3,2,1,0:T(8,128)S(1)} %collective-permute-done.8.refs_5_), channel_id=1, source_target_pairs={{0,1},{1,0},{2,3},{3,2},{4,5},{5,4},{6,7},{7,6},{8,9},{9,8},{10,11... | collective-permute-start | bytes 589832 | tf_op jit(solution)/shard_map/ppermute | solution.py:324
  33.0 0.7 %collective-permute-start.9 = (f32[12,4,8,128]{3,2,1,0:T(8,128)S(1)}, f32[12,4,8,128]{3,2,1,0:T(8,128)S(1)}, u32[]{:S(2)}, u32[]{:S(2)}) collective-permute-start(f32[12,4,8,128]{3,2,1,0:T(8,128)S(1)} %collective-permute-done.8.refs_5_), channel_id=1, source_target_pairs={{1,4},{4,1},{5,8},{8,5},{9,12},{12,9},{3,6},{6,3},{7,10},{10,7},{1... | collective-permute-start | bytes 589832 | tf_op jit(solution)/shard_map/ppermute | solution.py:331
  33.7 0.0 copy-done.9
  33.7 0.4 collective-permute-done.10.refs_6_
  34.1 0.0 collective-permute-done.9.refs_4_
  34.1 0.0 collective-permute-done.5.refs_0_
  34.1 0.0 collective-permute-done.6.refs_1_
  34.1 0.0 collective-permute-done.7.refs_3_
  34.1 0.0 copy-done
  34.1 0.0 copy-done.1
  34.1 0.0 copy-done.2
  34.1 0.0 copy-done.3
  34.2 0.0 copy-done.4
  34.2 4.5 %shard_map.115 = (f32[12,4,16,256]{3,2,1,0:T(8,128)}, f32[16,8,128]{2,1,0:T(8,128)}) custom-call(f32[6,4,16,256]{3,2,1,0:T(8,128)S(1)} %collective-permute-done.5.refs_0_, f32[6,4,16,256]{3,2,1,0:T(8,128)S(1)} %collective-permute-done.6.refs_1_, f32[12,4,16,256]{3,2,1,0:T(8,128)S(1)} %get-tuple-element.14.refs_2_, ...), custom_call_target="tpu_custom_call" | custom-call | flops 20000000 | bytes 4000000 | tf_op jit(solution)/shard_map/pallas_call | solution.py:424
  38.7 11.9 %all-to-all-start = ((f32[16,8,128]{2,1,0:T(8,128)}), f32[16,8,128]{2,1,0:T(8,128)S(1)}, u32[]{:S(2)}, u32[]{:S(2)}) async-start(f32[16,8,128]{2,1,0:T(8,128)} %get-tuple-element.21), calls=%async_computation | async-start | bytes 131072 | tf_op jit(solution)/shard_map/all_to_all | solution.py:441
  50.6 6.9 %all-to-all-done = f32[16,8,128]{2,1,0:T(8,128)S(1)} async-done(((f32[16,8,128]{2,1,0:T(8,128)}), f32[16,8,128]{2,1,0:T(8,128)S(1)}, u32[]{:S(2)}, u32[]{:S(2)}) %all-to-all-start) | async-done | bytes 65568 | tf_op jit(solution)/shard_map/all_to_all | solution.py:441
  57.5 0.7 %constant_dynamic-slice_fusion = f32[8,16]{1,0:T(8,128)} fusion(f32[8,128]{1,0:T(8,128)S(1)} %reduce_sum.9, s32[]{:T(128)S(6)} %select_n.7), kind=kLoop, calls=%fused_computation.6 | loop fusion | bytes 1028 | tf_op jit(solution)/shard_map/dynamic_slice | solution.py:443
  (3 shorter events, 0.1 us)
Async XLA Ops:
  0.6 6.5 %copy-start.7 = (f32[2,6,4,16,256]{4,3,2,1,0:T(8,128)S(1)}, f32[2,6,4,16,256]{4,3,2,1,0:T(8,128)}, u32[]{:S(2)}) copy-start(f32[2,6,4,16,256]{4,3,2,1,0:T(8,128)} %param.10) | copy-start | bytes 2359300
  0.6 6.5 %copy-start.8 = (f32[4,16,256]{2,1,0:T(8,128)S(1)}, f32[4,16,256]{2,1,0:T(8,128)}, u32[]{:S(2)}) copy-start(f32[4,16,256]{2,1,0:T(8,128)} %param.11) | copy-start | bytes 196612
  2.0 17.4 %collective-permute-start = (f32[13,4,16,256]{3,2,1,0:T(8,128)S(1)}, f32[13,4,16,256]{3,2,1,0:T(8,128)S(1)}, u32[]{:S(2)}, u32[]{:S(2)}) collective-permute-start(f32[13,4,16,256]{3,2,1,0:T(8,128)S(1)} %pad_maximum_fusion.refs_1_), channel_id=1, source_target_pairs={{1,4},{4,1},{5,8},{8,5},{9,12},{12,9},{3,6},{6,3},{7,10},{10,7},{1... | collective-permute-start | bytes 2555912 | tf_op jit(solution)/shard_map/ppermute | solution.py:331
  2.7 16.6 %collective-permute-start.1 = (f32[13,4,16,256]{3,2,1,0:T(8,128)S(1)}, f32[13,4,16,256]{3,2,1,0:T(8,128)S(1)}, u32[]{:S(2)}, u32[]{:S(2)}) collective-permute-start(f32[13,4,16,256]{3,2,1,0:T(8,128)S(1)} %pad_maximum_fusion.refs_1_), channel_id=1, source_target_pairs={{0,1},{1,0},{2,3},{3,2},{4,5},{5,4},{6,7},{7,6},{8,9},{9,8},{10,11... | collective-permute-start | bytes 2555912 | tf_op jit(solution)/shard_map/ppermute | solution.py:324
  7.3 26.8 %copy-start = (f32[128,256]{1,0:T(8,128)S(1)}, f32[128,256]{1,0:T(8,128)}, u32[]{:S(2)}) copy-start(f32[128,256]{1,0:T(8,128)} %constant.46.clone.refs_12_) | copy-start | bytes 393220
  7.3 26.8 %copy-start.1 = (f32[128,256]{1,0:T(8,128)S(1)}, f32[128,256]{1,0:T(8,128)}, u32[]{:S(2)}) copy-start(f32[128,256]{1,0:T(8,128)} %constant.47.clone.refs_13_) | copy-start | bytes 393220
  7.3 26.8 %copy-start.2 = (f32[16,16,128]{2,1,0:T(8,128)S(1)}, f32[16,16,128]{2,1,0:T(8,128)}, u32[]{:S(2)}) copy-start(f32[16,16,128]{2,1,0:T(8,128)} %constant.48.clone.refs_14_) | copy-start | bytes 393220
  7.3 26.8 %copy-start.3 = (f32[16,16,128]{2,1,0:T(8,128)S(1)}, f32[16,16,128]{2,1,0:T(8,128)}, u32[]{:S(2)}) copy-start(f32[16,16,128]{2,1,0:T(8,128)} %constant.49.clone.refs_15_) | copy-start | bytes 393220
  7.3 7.3 %collective-permute-start.2 = (f32[13,4,8,128]{3,2,1,0:T(8,128)S(1)}, f32[13,4,8,128]{3,2,1,0:T(8,128)S(1)}, u32[]{:S(2)}, u32[]{:S(2)}) collective-permute-start(f32[13,4,8,128]{3,2,1,0:T(8,128)S(1)} %pad_maximum_fusion.1), channel_id=1, source_target_pairs={{0,2},{2,0},{1,3},{3,1},{4,6},{6,4},{5,7},{7,5},{8,10},{10,8},{9,1... | collective-permute-start | bytes 638984 | tf_op jit(solution)/shard_map/ppermute | solution.py:340
  14.6 3.7 %collective-permute-start.3 = (f32[13,4,8,128]{3,2,1,0:T(8,128)S(1)}, f32[13,4,8,128]{3,2,1,0:T(8,128)S(1)}, u32[]{:S(2)}, u32[]{:S(2)}) collective-permute-start(f32[13,4,8,128]{3,2,1,0:T(8,128)S(1)} %collective-permute-done.2.refs_4_), channel_id=1, source_target_pairs={{1,4},{4,1},{5,8},{8,5},{9,12},{12,9},{3,6},{6,3},{7,10},{10,7},{1... | collective-permute-start | bytes 638984 | tf_op jit(solution)/shard_map/ppermute | solution.py:331
  15.3 4.1 %collective-permute-start.4 = (f32[13,4,8,128]{3,2,1,0:T(8,128)S(1)}, f32[13,4,8,128]{3,2,1,0:T(8,128)S(1)}, u32[]{:S(2)}, u32[]{:S(2)}) collective-permute-start(f32[13,4,8,128]{3,2,1,0:T(8,128)S(1)} %collective-permute-done.2.refs_4_), channel_id=1, source_target_pairs={{0,1},{1,0},{2,3},{3,2},{4,5},{5,4},{6,7},{7,6},{8,9},{9,8},{10,11... | collective-permute-start | bytes 638984 | tf_op jit(solution)/shard_map/ppermute | solution.py:324
  22.5 11.6 %collective-permute-start.7 = (f32[12,4,16,256]{3,2,1,0:T(8,128)S(1)}, f32[12,4,16,256]{3,2,1,0:T(8,128)S(1)}, u32[]{:S(2)}, u32[]{:S(2)}) collective-permute-start(f32[12,4,16,256]{3,2,1,0:T(8,128)S(1)} %get-tuple-element.14.refs_2_), channel_id=1, source_target_pairs={{0,1},{1,0},{2,3},{3,2},{4,5},{5,4},{6,7},{7,6},{8,9},{9,8},{10,11... | collective-permute-start | bytes 2359304 | tf_op jit(solution)/shard_map/ppermute | solution.py:324
  25.0 8.7 %copy-start.9 = (f32[8,128]{1,0:T(8,128)S(1)}, f32[8,128]{1,0:T(8,128)}, u32[]{:S(2)}) copy-start(f32[8,128]{1,0:T(8,128)} %param.14) | copy-start | bytes 12292
  25.0 6.9 %collective-permute-start.8 = (f32[12,4,8,128]{3,2,1,0:T(8,128)S(1)}, f32[12,4,8,128]{3,2,1,0:T(8,128)S(1)}, u32[]{:S(2)}, u32[]{:S(2)}) collective-permute-start(f32[12,4,8,128]{3,2,1,0:T(8,128)S(1)} %get-tuple-element.15), channel_id=1, source_target_pairs={{0,2},{2,0},{1,3},{3,1},{4,6},{6,4},{5,7},{7,5},{8,10},{10,8},{9,1... | collective-permute-start | bytes 589832 | tf_op jit(solution)/shard_map/ppermute | solution.py:340
  26.5 7.6 %collective-permute-start.5 = (f32[6,4,16,256]{3,2,1,0:T(8,128)S(1)}, f32[6,4,16,256]{3,2,1,0:T(8,128)S(1)}, u32[]{:S(2)}, u32[]{:S(2)}) collective-permute-start(f32[6,4,16,256]{3,2,1,0:T(8,128)S(1)} %get-tuple-element.12), channel_id=1, source_target_pairs={{1,4},{4,1},{5,8},{8,5},{9,12},{12,9},{3,6},{6,3},{7,10},{10,7},{1... | collective-permute-start | bytes 1179656 | tf_op jit(solution)/shard_map/ppermute | solution.py:331
  27.1 0.7 %copy-start.5 = (s32[1,8]{1,0:T(1,128)S(1)}, s32[1,8]{1,0:T(1,128)}, u32[]{:S(2)}) copy-start(s32[1,8]{1,0:T(1,128)} %row_counts.1) | copy-start | bytes 100
  27.2 0.7 %copy-start.6 = (s32[128]{0:T(128)S(1)}, s32[128]{0:T(128)}, u32[]{:S(2)}) copy-start(s32[128]{0:T(128)} %param.13) | copy-start | bytes 1540
  27.2 6.9 %collective-permute-start.6 = (f32[6,4,16,256]{3,2,1,0:T(8,128)S(1)}, f32[6,4,16,256]{3,2,1,0:T(8,128)S(1)}, u32[]{:S(2)}, u32[]{:S(2)}) collective-permute-start(f32[6,4,16,256]{3,2,1,0:T(8,128)S(1)} %get-tuple-element.13), channel_id=1, source_target_pairs={{1,4},{4,1},{5,8},{8,5},{9,12},{12,9},{3,6},{6,3},{7,10},{10,7},{1... | collective-permute-start | bytes 1179656 | tf_op jit(solution)/shard_map/ppermute | solution.py:331
  28.6 5.6 %copy-start.4 = (f32[16,128]{1,0:T(8,128)S(1)}, f32[16,128]{1,0:T(8,128)}, u32[]{:S(2)}) copy-start(f32[16,128]{1,0:T(8,128)} %constant.50.clone.refs_16_) | copy-start | bytes 24580
  31.9 2.2 %collective-permute-start.10 = (f32[12,4,8,128]{3,2,1,0:T(8,128)S(1)}, f32[12,4,8,128]{3,2,1,0:T(8,128)S(1)}, u32[]{:S(2)}, u32[]{:S(2)}) collective-permute-start(f32[12,4,8,128]{3,2,1,0:T(8,128)S(1)} %collective-permute-done.8.refs_5_), channel_id=1, source_target_pairs={{0,1},{1,0},{2,3},{3,2},{4,5},{5,4},{6,7},{7,6},{8,9},{9,8},{10,11... | collective-permute-start | bytes 589832 | tf_op jit(solution)/shard_map/ppermute | solution.py:324
  33.0 1.1 %collective-permute-start.9 = (f32[12,4,8,128]{3,2,1,0:T(8,128)S(1)}, f32[12,4,8,128]{3,2,1,0:T(8,128)S(1)}, u32[]{:S(2)}, u32[]{:S(2)}) collective-permute-start(f32[12,4,8,128]{3,2,1,0:T(8,128)S(1)} %collective-permute-done.8.refs_5_), channel_id=1, source_target_pairs={{1,4},{4,1},{5,8},{8,5},{9,12},{12,9},{3,6},{6,3},{7,10},{10,7},{1... | collective-permute-start | bytes 589832 | tf_op jit(solution)/shard_map/ppermute | solution.py:331
  38.7 18.8 %all-to-all-start = ((f32[16,8,128]{2,1,0:T(8,128)}), f32[16,8,128]{2,1,0:T(8,128)S(1)}, u32[]{:S(2)}, u32[]{:S(2)}) async-start(f32[16,8,128]{2,1,0:T(8,128)} %get-tuple-element.21), calls=%async_computation | async-start | bytes 131072 | tf_op jit(solution)/shard_map/all_to_all | solution.py:441

commit v7 on v6

--- a/solution.py
+++ b/solution.py
@@ -81,6 +81,133 @@
     return product[:rows, :columns] + small
 
 
+def unpack(strips, st, scale_ref, layers, planes, eps, rows_own, gy):
+    rows = rows_own + 2 * HALF
+    low_half = lax.broadcasted_iota(jnp.int32, (8, 128), 0) < HALF
+    low_half_at = jnp.where(low_half, 0, 1)
+    for l in layers:
+        for c in range(planes):
+            if strips.shape[0] == 2:
+                lo, hi = strips[0, c, l], strips[1, c, l]
+                left = jnp.where(low_half, hi, pltpu.roll(lo, HALF, 0))
+                right = jnp.where(low_half, pltpu.roll(hi, HALF, 0), lo)
+            else:
+                v = strips[0, c, l]
+                w = pltpu.roll(v, HALF, 0)
+                keep = low_half_at == gy
+                left = jnp.where(keep, jnp.where(low_half, v, w), 0.0)
+                right = jnp.where(keep, jnp.where(low_half, w, v), 0.0)
+            tile = jnp.concatenate([left, right], axis=1)
+            if c == 12:
+                scale_ref[l, rows_own:rows, :] = courant * tile
+                scale_ref[l, :rows_own, :] = courant * eps[l]
+            else:
+                st[c, l, rows_own:rows, :] = tile
+
+
+def updates(st, scale_ref, depth, rows_own):
+    rows, nx = st.shape[-2:]
+    n_z, n_gy = 2 * lax.axis_size("gz"), lax.axis_size("gy")
+    gy = lax.axis_index("gy")
+    first_layer = (2 * lax.axis_index("gz") + lax.axis_index("col")) * depth
+    row_at = lax.broadcasted_iota(jnp.int32, (rows, nx), 0)
+    lane_at = lax.broadcasted_iota(jnp.int32, (rows, 128), 1)
+    last_lane, first_lane = lane_at == 127, lane_at == 0
+    ahead = jnp.where(gy < n_gy - 1, courant, 0.0)
+    behind = jnp.where(gy > 0, courant, 0.0)
+    coef_in = jnp.where(row_at < rows_own, courant, jnp.where(row_at < rows_own + HALF, ahead, behind))
+    low_layer = depth - first_layer
+    high_layer = low_layer + depth * n_z
+
+    def y_ahead(f):
+        return pltpu.roll(f, rows - 1, 0)
+
+    def y_behind(f):
+        return pltpu.roll(f, 1, 0)
+
+    def x_ahead(f):
+        a, b = pltpu.roll(f[:, :128], 127, 1), pltpu.roll(f[:, 128:], 127, 1)
+        return jnp.concatenate([jnp.where(last_lane, b, a), jnp.where(last_lane, 0.0, b)], axis=1)
+
+    def x_behind(f):
+        a, b = pltpu.roll(f[:, :128], 1, 1), pltpu.roll(f[:, 128:], 1, 1)
+        return jnp.concatenate([jnp.where(first_lane, 0.0, a), jnp.where(first_lane, a, b)], axis=1)
+
+    def magnetic(z, whole):
+        coef = coef_in * jnp.where((z >= low_layer) & (z < high_layer), 1.0, 0.0)
+        for b in (0, 6):
+            ex, ey, ez = st[b, z], st[b + 1, z], st[b + 2, z]
+            ex_n, ey_n = st[b, z + 1], st[b + 1, z + 1]
+            st[b + 3, z] = st[b + 3, z] - coef * ((y_ahead(ez) - ez) - (ey_n - ey))
+            st[b + 4, z] = st[b + 4, z] - coef * ((ex_n - ex) - (x_ahead(ez) - ez))
+            if whole:
+                st[b + 5, z] = st[b + 5, z] - coef * ((x_ahead(ey) - ey) - (y_ahead(ex) - ex))
+
+    def electric(z, b):
+        scale = scale_ref[z]
+        hx_p, hy_p = st[b + 3, z - 1], st[b + 4, z - 1]
+        hx, hy, hz = st[b + 3, z], st[b + 4, z], st[b + 5, z]
+        ex = st[b, z] + scale * ((hz - y_behind(hz)) - (hy - hy_p))
+        ey = st[b + 1, z] + scale * ((hx - hx_p) - (hz - x_behind(hz)))
+        ez = st[b + 2, z] + scale * ((hy - x_behind(hy)) - (hx - y_behind(hx)))
+        return ex, ey, ez, hx, hy, hz
+
+    def first_step(magnetic_layers, electric_layers):
+        for z in magnetic_layers:
+            magnetic(z, z >= 1)
+        for z in electric_layers:
+            for b in (0, 6):
+                for c, f in enumerate(electric(z, b)[:3]):
+                    st[b + c, z] = f
+
+    return magnetic, electric, first_step
+
+
+def early_kernel(cfg, *refs):
+    depth, rows_own, sides, second = cfg
+    it = iter(refs)
+    take = lambda n: [next(it) for _ in range(n)]
+    full = take(2)
+    strip_in = [take(2) for _ in range(sides)]
+    if second:
+        (scale_ref, st, strips, sem_full, sem_strip) = take(5)
+        eps = eps_in = None
+    else:
+        (eps_sib, st, scale_ref, strips, eps, sem_full, sem_strip, sem_eps) = take(8)
+        eps_in = [full[0].at[12], eps_sib]
+    gy, core = lax.axis_index("gy"), lax.axis_index("col")
+    planes = 12 if second else 13
+
+    def run(places, base):
+        copies = []
+        for b, place in enumerate(places):
+            layers = pl.ds(place * depth, depth)
+            copies.append(
+                pltpu.make_async_copy(
+                    full[b].at[pl.ds(0, 12)], st.at[:, layers, pl.ds(0, rows_own), :], sem_full.at[b]
+                )
+            )
+            for s in range(sides):
+                copies.append(pltpu.make_async_copy(strip_in[s][b], strips.at[s, :, layers], sem_strip.at[s, b]))
+            if not second:
+                copies.append(pltpu.make_async_copy(eps_in[b], eps.at[layers], sem_eps.at[b]))
+        for copy in copies:
+            copy.start()
+        for copy in copies:
+            copy.wait()
+        unpack(strips, st, scale_ref, range(base, base + 2 * depth), planes, eps, rows_own, gy)
+        first_step = updates(st, scale_ref, depth, rows_own)[2]
+        first_step(range(base, base + 2 * depth - 1), range(base + 1, base + 2 * depth - 1))
+
+    @pl.when(core == 0)
+    def _():
+        run((1, 2), depth)
+
+    @pl.when(core != 0)
+    def _():
+        run((1, 0), 0)
+
+
 def window_kernel(cfg, *refs):
     depth, rows_own, sides, second = cfg
     it = iter(refs)
@@ -89,141 +216,84 @@
     core, gy = lax.axis_index("col"), lax.axis_index("gy")
     first_layer = (2 * lax.axis_index("gz") + core) * depth
     layer_start = depth * n_z // 2 - depth - depth // 2
-    pieces = 2 if second else 1
-    full = [take(pieces), take(1), take(1)]
-    strip_in = [take(3) for _ in range(sides)]
+    near = take(2 if second else 1)
+    strip_in = take(sides)
+    take(1)
+    (scale_ref,) = take(1)
     if second:
-        (scale_ref, acc_in) = take(2)
+        (acc_in,) = take(1)
         row_wide, col_table, slope, basis_x, basis_xt, basis_y, basis_yt, response = take(8)
-        out, share = take(2)
-        st, strips, acc, done, sem_full, sem_strip, sem_out = take(7)
+        st, out, share = take(3)
+        strips, acc, done, sem_full, sem_strip, sem_out = take(6)
     else:
+        st, scale_ref = take(2)
         done = take(3)
-        scale_ref, acc = take(2)
+        (acc,) = take(1)
         strip_out = take(sides)
-        st, strips, eps, sem_full, sem_strip, sem_eps = take(6)
-
-    def copies_of(b, place):
+        strips, eps, sem_full, sem_strip, sem_eps = take(5)
+    nx = st.shape[-1]
+    n_layers = 3 * depth
+    magnetic, electric, first_step = updates(st, scale_ref, depth, rows_own)
+
+    def start(place):
         layers = pl.ds(place * depth, depth)
-        found = []
-        for p, ref in enumerate(full[b]):
+        copies = []
+        for p, ref in enumerate(near):
             count = min(ref.shape[0], 12)
-            planes = pl.ds(count * p, count)
-            found.append(
+            copies.append(
                 pltpu.make_async_copy(
-                    ref.at[pl.ds(0, count)], st.at[planes, layers, pl.ds(0, rows_own), :], sem_full.at[p, place]
+                    ref.at[pl.ds(0, count)],
+                    st.at[pl.ds(count * p, count), layers, pl.ds(0, rows_own), :],
+                    sem_full.at[p],
                 )
             )
         for s in range(sides):
-            found.append(pltpu.make_async_copy(strip_in[s][b], strips.at[s, :, layers], sem_strip.at[s, place]))
+            copies.append(pltpu.make_async_copy(strip_in[s], strips.at[s, :, layers], sem_strip.at[s]))
         if not second:
-            found.append(pltpu.make_async_copy(full[b][0].at[12], eps.at[layers], sem_eps.at[place]))
-        return found
+            copies.append(pltpu.make_async_copy(near[0].at[12], eps.at[layers], sem_eps))
+        for copy in copies:
+            copy.start()
+        for copy in copies:
+            copy.wait()
+        layers = range(place * depth, (place + 1) * depth)
+        unpack(strips, st, scale_ref, layers, 12 if second else 13, None if second else eps, rows_own, gy)
 
     @pl.when(core == 0)
     def _():
-        for b in range(3):
-            for copy in copies_of(b, b):
-                copy.start()
+        start(0)
+        first_step(range(depth), range(1, depth + 1))
 
     @pl.when(core != 0)
     def _():
-        for b in (2, 1, 0):
-            for copy in copies_of(b, 2 - b):
-                copy.start()
-
-    nx = st.shape[-1]
-    rows = st.shape[-2]
-    low_half = lax.broadcasted_iota(jnp.int32, (8, 128), 0) < HALF
-    low_half_at = jnp.where(low_half, 0, 1)
-    n_layers = 3 * depth
-
-    def arrive(place):
-        if place == 1:
-            for copy in copies_of(1, 1):
-                copy.wait()
-        else:
-            here = core == place // 2
-
-            @pl.when(here)
-            def _():
-                for copy in copies_of(0, place):
-                    copy.wait()
-
-            @pl.when(jnp.logical_not(here))
-            def _():
-                for copy in copies_of(2, place):
-                    copy.wait()
-
-        for l in range(place * depth, (place + 1) * depth):
-            for c in range(12 if second else 13):
-                if sides == 2:
-                    lo, hi = strips[0, c, l], strips[1, c, l]
-                    left = jnp.where(low_half, hi, pltpu.roll(lo, HALF, 0))
-                    right = jnp.where(low_half, pltpu.roll(hi, HALF, 0), lo)
-                else:
-                    v = strips[0, c, l]
-                    w = pltpu.roll(v, HALF, 0)
-                    keep = low_half_at == gy
-                    left = jnp.where(keep, jnp.where(low_half, v, w), 0.0)
-                    right = jnp.where(keep, jnp.where(low_half, w, v), 0.0)
-                tile = jnp.concatenate([left, right], axis=1)
-                if c == 12:
-                    scale_ref[l, rows_own:rows, :] = courant * tile
-                    scale_ref[l, :rows_own, :] = courant * eps[l]
-                else:
-                    st[c, l, rows_own:rows, :] = tile
-
-    row_at = lax.broadcasted_iota(jnp.int32, (rows, nx), 0)
-    lane_at = lax.broadcasted_iota(jnp.int32, (rows, 128), 1)
-    last_lane, first_lane = lane_at == 127, lane_at == 0
-    ahead = jnp.where(gy < n_gy - 1, courant, 0.0)
-    behind = jnp.where(gy > 0, courant, 0.0)
-    coef_in = jnp.where(row_at < rows_own, courant, jnp.where(row_at < rows_own + HALF, ahead, behind))
-    low_layer = depth - first_layer
-    high_layer = low_layer + depth * n_z
-
-    def y_ahead(f):
-        return pltpu.roll(f, rows - 1, 0)
-
-    def y_behind(f):
-        return pltpu.roll(f, 1, 0)
-
-    def x_ahead(f):
-        a, b = pltpu.roll(f[:, :128], 127, 1), pltpu.roll(f[:, 128:], 127, 1)
-        return jnp.concatenate([jnp.where(last_lane, b, a), jnp.where(last_lane, 0.0, b)], axis=1)
-
-    def x_behind(f):
-        a, b = pltpu.roll(f[:, :128], 1, 1), pltpu.roll(f[:, 128:], 1, 1)
-        return jnp.concatenate([jnp.where(first_lane, 0.0, a), jnp.where(first_lane, a, b)], axis=1)
-
-    for m in range(1, HALF + 1):
+        start(2)
+        layers = range(2 * depth - 1, n_layers - 1)
+        first_step(layers, layers)
+
+    angle = omega_step * (1 + (HALF if second else 0))
+    w_re, w_im = math.cos(angle), math.sin(angle)
+    for own in range(depth):
+        for k in range(6):
+            e = st[6 * (k // 3) + k % 3, depth + own, :rows_own, :]
+            if second:
+                acc[0, k, own] = acc_in[0, k, own] + e * w_re
+                acc[1, k, own] = acc_in[1, k, own] - e * w_im
+            else:
+                acc[0, k, own] = e * w_re
+                acc[1, k, own] = -(e * w_im)
+
+    column_sum = jnp.zeros((rows_own, nx), jnp.float32)
+    for m in range(2, HALF + 1):
         angle = omega_step * (m + (HALF if second else 0))
         w_re, w_im = math.cos(angle), math.sin(angle)
         for z in range(m - 1, n_layers - m):
-            if m == 1 and z == 0:
-                arrive(0)
-            if m == 1 and (z + 1) % depth == 0:
-                arrive((z + 1) // depth)
-            coef = coef_in * jnp.where((z >= low_layer) & (z < high_layer), 1.0, 0.0)
-            for b in (0, 6):
-                ex, ey, ez = st[b, z], st[b + 1, z], st[b + 2, z]
-                ex_n, ey_n = st[b, z + 1], st[b + 1, z + 1]
-                st[b + 3, z] = st[b + 3, z] - coef * ((y_ahead(ez) - ez) - (ey_n - ey))
-                st[b + 4, z] = st[b + 4, z] - coef * ((ex_n - ex) - (x_ahead(ez) - ez))
-                if z >= m:
-                    st[b + 5, z] = st[b + 5, z] - coef * ((x_ahead(ey) - ey) - (y_ahead(ex) - ex))
+            magnetic(z, z >= m)
         for z in range(m, n_layers - m):
-            scale = scale_ref[z]
             own = z - depth
+            last = []
             for r in range(2):
                 b = 6 * r
-                hx_p, hy_p = st[b + 3, z - 1], st[b + 4, z - 1]
-                hx, hy, hz = st[b + 3, z], st[b + 4, z], st[b + 5, z]
-                ex = st[b, z] + scale * ((hz - y_behind(hz)) - (hy - hy_p))
-                ey = st[b + 1, z] + scale * ((hx - hx_p) - (hz - x_behind(hz)))
-                ez = st[b + 2, z] + scale * ((hy - x_behind(hy)) - (hx - y_behind(hx)))
-                for c, f in enumerate((ex, ey, ez, hx, hy, hz)):
+                now = electric(z, b)
+                for c, f in enumerate(now):
                     if m < HALF:
                         if c < 3:
                             st[b + c, z] = f
@@ -240,30 +310,24 @@
                         else:
                             strip_out[0][b + c, own] = jnp.where(gy == 0, strip_of(up, True), strip_of(down, False))
                 if 0 <= own < depth:
-                    for c, e in enumerate((ex, ey, ez)):
+                    for c, e in enumerate(now[:3]):
                         e = e[:rows_own]
-                        re, im = e * w_re, e * w_im
-                        if m > 1:
-                            acc[0, 3 * r + c, own] = acc[0, 3 * r + c, own] + re
-                            acc[1, 3 * r + c, own] = acc[1, 3 * r + c, own] - im
-                        elif second:
-                            acc[0, 3 * r + c, own] = acc_in[0, 3 * r + c, own] + re
-                            acc[1, 3 * r + c, own] = acc_in[1, 3 * r + c, own] - im
+                        re = acc[0, 3 * r + c, own] + e * w_re
+                        im = acc[1, 3 * r + c, own] - e * w_im
+                        if second and m == HALF:
+                            last += [re, im]
                         else:
-                            acc[0, 3 * r + c, own] = re
-                            acc[1, 3 * r + c, own] = -im
+                            acc[0, 3 * r + c, own], acc[1, 3 * r + c, own] = re, im
+            if last:
+                g = jnp.zeros((rows_own, nx), jnp.float32)
+                for c in range(3):
+                    g = g + last[2 * c] * last[2 * c + 6] - last[2 * c + 1] * last[2 * c + 7]
+                layer = first_layer + own - layer_start
+                column_sum = column_sum + jnp.where((layer >= 0) & (layer < 3 * depth), g, 0.0)
 
     if second:
         result = pltpu.make_async_copy(done, out, sem_out)
         result.start()
-        column_sum = jnp.zeros((rows_own, nx), jnp.float32)
-        for own in range(depth):
-            g = jnp.zeros((rows_own, nx), jnp.float32)
-            for c in range(3):
-                g = g + acc[0, c, own] * acc[0, 3 + c, own] - acc[1, c, own] * acc[1, 3 + c, own]
-            layer = first_layer + own - layer_start
-            in_layer = (layer >= 0) & (layer < 3 * depth)
-            column_sum = column_sum + jnp.where(in_layer, g, 0.0)
         pooled = jnp.zeros(row_wide.shape[1:], jnp.float32)
         for k in range(rows_own):
             pooled = pooled + row_wide[k] * column_sum[k : k + 1]
@@ -319,6 +383,7 @@
     assert HALF == depth and rows_own == 16 and nx == 256
     rows = rows_own + 2 * HALF
     own = jnp.concatenate([fields.reshape(runs * comps, depth, rows_own, nx), eps_inv[None]])
+    own = lax.optimization_barrier(own)
 
     def swap_core(x):
         return lax.ppermute(x, "col", [(0, 1), (1, 0)])
@@ -353,39 +418,59 @@
             sent += [far, mine, swap_core(mine)]
         return sent
 
+    def here(sent):
+        return [strip for at, strip in enumerate(sent) if at % 3]
+
     starts = [(1 - gy) * (rows_own - HALF)] if sides == 1 else [rows_own - HALF, 0]
     strips = []
     for start in starts:
         edge = lax.dynamic_slice_in_dim(own, start, HALF, 2)
         strips.append(jnp.concatenate([edge[..., :128], edge[..., 128:]], 2))
     sent = strips_sent(strips)
-    operands = [cross(own), own, swap_core(own)] + sent
+    near = cross(own)
     cost = pl.CostEstimate(flops=20_000_000, bytes_accessed=4_000_000, transcendentals=0)
-    window = pltpu.VMEM((12, 3 * depth, rows, nx), jnp.float32)
-    block = pltpu.VMEM((12, depth, rows_own, nx), jnp.float32)
-    arrivals = [pltpu.SemaphoreType.DMA((2, 3)), pltpu.SemaphoreType.DMA((sides, 3))]
-    half_0, half_1, state, scale, acc, *strips = pl.pallas_call(
+    wide = (12, 3 * depth, rows, nx)
+    sems = pltpu.SemaphoreType.DMA
+    sibling = swap_core(fields.reshape(runs * comps, depth, rows_own, nx))
+    window, scale = pl.pallas_call(
+        functools.partial(early_kernel, (depth, rows_own, sides, False)),
+        out_shape=(shape(*wide), shape(3 * depth, rows, nx)),
+        in_specs=[anywhere] * (3 + 2 * sides),
+        out_specs=(vmem, vmem),
+        scratch_shapes=[
+            pltpu.VMEM((sides, 13, 3 * depth, 8, 128), jnp.float32),
+            pltpu.VMEM((3 * depth, rows_own, nx), jnp.float32),
+            sems((2,)),
+            sems((sides, 2)),
+            sems((2,)),
+        ],
+        compiler_params=limit,
+        cost_estimate=cost,
+    )(own, sibling, *here(sent), swap_core(eps_inv))
+    window, scale, half_0, half_1, state, acc, *strips = pl.pallas_call(
         functools.partial(window_kernel, (depth, rows_own, sides, False)),
         out_shape=(
+            shape(*wide),
+            shape(3 * depth, rows, nx),
             shape(comps, depth, rows_own, nx),
             shape(comps, depth, rows_own, nx),
             shape(runs * comps, depth, rows_own, nx),
-            shape(3 * depth, rows, nx),
             shape(2, 6, depth, rows_own, nx),
         )
         + (shape(12, depth, 8, 128),) * sides,
-        in_specs=[anywhere] * (3 + 3 * sides),
-        out_specs=(vmem,) * (5 + sides),
+        in_specs=[anywhere] * (1 + sides) + [vmem] * 2,
+        out_specs=(vmem,) * (6 + sides),
+        input_output_aliases={1 + sides: 0, 2 + sides: 1},
         scratch_shapes=[
-            window,
             pltpu.VMEM((sides, 13, 3 * depth, 8, 128), jnp.float32),
             pltpu.VMEM((3 * depth, rows_own, nx), jnp.float32),
-        ]
-        + arrivals
-        + [pltpu.SemaphoreType.DMA((3,))],
+            sems((2,)),
+            sems((sides,)),
+            sems,
+        ],
         compiler_params=limit,
         cost_estimate=cost,
-    )(*operands)
+    )(near, *sent[::3], window, scale)
 
     band, design_cols = density.shape
     tall = band * n_gy
@@ -416,24 +501,41 @@
         return const(np.concatenate([high, matrix - high], axis=1))
 
     sent = strips_sent(strips)
-    operands = [cross(half_0), cross(half_1), state, swap_core(state)]
-    operands += sent + [scale, acc]
+    window = pl.pallas_call(
+        functools.partial(early_kernel, (depth, rows_own, sides, True)),
+        out_shape=shape(*wide),
+        in_specs=[anywhere] * (2 + 2 * sides) + [vmem],
+        out_specs=vmem,
+        scratch_shapes=[
+            pltpu.VMEM((sides, 12, 3 * depth, 8, 128), jnp.float32),
+            sems((2,)),
+            sems((sides, 2)),
+        ],
+        compiler_params=limit,
+        cost_estimate=cost,
+    )(state, swap_core(state), *here(sent), scale)
+    operands = [cross(half_0), cross(half_1), *sent[::3], window, scale, acc]
     operands += [row_wide, col_table, slope_of(density), halves(basis_x), halves(basis_x.T)]
     operands += [const(tables[0]), const(tables[1]), const(response)]
     n_all = n_z * n_gy
-    fields_out, share = pl.pallas_call(
+    _, fields_out, share = pl.pallas_call(
         functools.partial(window_kernel, (depth, rows_own, sides, True)),
-        out_shape=(shape(runs * comps, depth, rows_own, nx), shape(n_all, band, design_cols)),
-        in_specs=[anywhere] * (4 + 3 * sides) + [vmem] * 10,
-        out_specs=(anywhere, vmem),
+        out_shape=(
+            shape(*wide),
+            shape(runs * comps, depth, rows_own, nx),
+            shape(n_all, band, design_cols),
+        ),
+        in_specs=[anywhere] * (2 + sides) + [vmem] * 11,
+        out_specs=(vmem, anywhere, vmem),
+        input_output_aliases={2 + sides: 0},
         scratch_shapes=[
-            window,
             pltpu.VMEM((sides, 12, 3 * depth, 8, 128), jnp.float32),
             pltpu.VMEM((2, 6, depth, rows_own, nx), jnp.float32),
-            block,
-        ]
-        + arrivals
-        + [pltpu.SemaphoreType.DMA],
+            pltpu.VMEM((12, depth, rows_own, nx), jnp.float32),
+            sems((2,)),
+            sems((sides,)),
+            sems,
+        ],
         compiler_params=limit,
         cost_estimate=cost,
     )(*operands)

time: 58.5 us -> 57.5 us (0.983)
  starting transfers between devices: 29.3 us -> 27.8 us
    pallas_call x0 -> x2, Pallas kernels: none -> 1.83 us  [the longest x1 0.99 us: body(): pl.pallas_call(functools.partial(early_kernel, (depth, rows_own, sides, F...]
    pallas_call x2, Pallas kernels: 7.68 us -> 6.38 us  [body(): pl.pallas_call(functools.partial(window_kernel, (depth, rows_own, sides,...]
    all_to_all x1, starting transfers between devices: 11.9 us -> 11.1 us  [body(): got = lax.all_to_all(share, ('gz', 'gy', 'col'), 0, 0)]
    ppermute x4 -> x5, starting transfers between devices: 11 us -> 10.3 us  [swap_core(): return lax.ppermute(x, 'col', [(0, 1), (1, 0)])]
    concatenate x2 -> x1, other arithmetic: 1.37 us -> 1.25 us  [body(): jnp.concatenate([fields.reshape(runs * comps, depth, rows_own, nx), eps_i...]
    ppermute x4 -> x5, waiting for transfers between devices: 1.47 us -> 1.5 us  [swap_core(): return lax.ppermute(x, 'col', [(0, 1), (1, 0)])]
  transfers between devices with their start and end apart: 12 -> 13, of which waited for: 5 -> 5; matrix products, arithmetic and copies ran while one was open for 0% -> 0% of each run, Pallas kernels for 1% -> 4%
where the time goes in v7:
time: 57.5 us; the launch traced here: 57.2 us
  starting transfers between devices  27.8 us (48%)
  waiting for transfers between devices  17.4 us (30%)
  Pallas kernels  8.92 us (16%)
  other arithmetic  1.34 us (2%)
  between operations  0.91 us (2%)
  local copies, waits for them, and re-layouts  0.85 us (1%)
    all_to_all x1, starting transfers between devices, body(): got = lax.all_to_all(share, ('gz', 'gy', 'col'), 0, 0)  11.1 us
    ppermute x5, starting transfers between devices, swap_core(): return lax.ppermute(x, 'col', [(0, 1), (1, 0)])  10.3 us
    ppermute x2, waiting for transfers between devices, along_y(): return lax.ppermute(x, 'gy', list(ways[s].items()))  8.98 us
    all_to_all x1, waiting for transfers between devices, body(): got = lax.all_to_all(share, ('gz', 'gy', 'col'), 0, 0)  6.89 us
    pallas_call x2, Pallas kernels, body(): pl.pallas_call(functools.partial(window_kernel, (depth, rows_own, sides,...  6.38 us
    ppermute x5, starting transfers between devices, cross(): return lax.ppermute(x, Z, pairs)  3.4 us
    ppermute x2, starting transfers between devices, along_y(): return lax.ppermute(x, 'gy', list(ways[s].items()))  3.05 us
    ppermute x5, waiting for transfers between devices, swap_core(): return lax.ppermute(x, 'col', [(0, 1), (1, 0)])  1.5 us
  transfers between devices with their start and end apart: 13, of which 5 were waited for; matrix products, arithmetic and copies ran while one was open for 0% of the time, Pallas kernels for 4%

profile of v7, /device:TPU:0, one launch (start us, length us, event | category | flops | bytes accessed | tf_op | source)
XLA Modules:
  0.0 57.2 jit_solution(13744497841115899529)
XLA Ops:
  0.6 1.3 %pad_maximum_fusion.refs_0_ = f32[13,4,16,256]{3,2,1,0:T(8,128)S(1)} fusion(f32[1,4,16,256]{3,2,1,0:T(8,128)} %bitcast.7, f32[12,4,16,256]{3,2,1,0:T(8,128)} %bitcast.5), kind=kLoop, calls=%fused_computation | loop fusion | flops 212992 | bytes 1703936 | tf_op jit(solution)/shard_map/concatenate | solution.py:385
  1.9 0.7 %collective-permute-start = (f32[13,4,16,256]{3,2,1,0:T(8,128)S(1)}, f32[13,4,16,256]{3,2,1,0:T(8,128)S(1)}, u32[]{:S(2)}, u32[]{:S(2)}) collective-permute-start(f32[13,4,16,256]{3,2,1,0:T(8,128)S(1)} %pad_maximum_fusion.refs_0_), channel_id=1, source_target_pairs={{1,4},{4,1},{5,8},{8,5},{9,12},{12,9},{3,6},{6,3},{7,10},{10,7},{1... | collective-permute-start | bytes 2555912 | tf_op jit(solution)/shard_map/ppermute | solution.py:396
  2.6 4.4 %collective-permute-start.3 = (f32[12,4,16,256]{3,2,1,0:T(8,128)}, f32[12,4,16,256]{3,2,1,0:T(8,128)S(1)}, u32[]{:S(2)}, u32[]{:S(2)}) collective-permute-start(f32[12,4,16,256]{3,2,1,0:T(8,128)} %bitcast.6), channel_id=1, source_target_pairs={{0,1},{1,0},{2,3},{3,2},{4,5},{5,4},{6,7},{7,6},{8,9},{9,8},{10,11... | collective-permute-start | bytes 2359304 | tf_op jit(solution)/shard_map/ppermute | solution.py:389
  7.0 0.1 constant_dynamic-slice_fusion
  7.1 0.1 pad_maximum_fusion.1
  7.2 0.0 copy-start.5
  7.2 0.0 copy-start.6
  7.2 0.0 copy-start.7
  7.2 1.6 %collective-permute-start.1 = (f32[13,4,8,128]{3,2,1,0:T(8,128)S(1)}, f32[13,4,8,128]{3,2,1,0:T(8,128)S(1)}, u32[]{:S(2)}, u32[]{:S(2)}) collective-permute-start(f32[13,4,8,128]{3,2,1,0:T(8,128)S(1)} %pad_maximum_fusion.1), channel_id=1, source_target_pairs={{0,2},{2,0},{1,3},{3,1},{4,6},{6,4},{5,7},{7,5},{8,10},{10,8},{9,1... | collective-permute-start | bytes 638984 | tf_op jit(solution)/shard_map/ppermute | solution.py:405
  8.8 5.7 %collective-permute-done.1.refs_2_ = f32[13,4,8,128]{3,2,1,0:T(8,128)S(1)} collective-permute-done((f32[13,4,8,128]{3,2,1,0:T(8,128)S(1)}, f32[13,4,8,128]{3,2,1,0:T(8,128)S(1)}, u32[]{:S(2)}, u32[]{:S(2)}) %collective-permute-start.1) | collective-permute-done | bytes 213024 | tf_op jit(solution)/shard_map/ppermute | solution.py:405
  14.5 0.0 collective-permute-start.4
  14.5 0.7 %collective-permute-start.2 = (f32[13,4,8,128]{3,2,1,0:T(8,128)S(1)}, f32[13,4,8,128]{3,2,1,0:T(8,128)S(1)}, u32[]{:S(2)}, u32[]{:S(2)}) collective-permute-start(f32[13,4,8,128]{3,2,1,0:T(8,128)S(1)} %collective-permute-done.1.refs_2_), channel_id=1, source_target_pairs={{1,4},{4,1},{5,8},{8,5},{9,12},{12,9},{3,6},{6,3},{7,10},{10,7},{1... | collective-permute-start | bytes 638984 | tf_op jit(solution)/shard_map/ppermute | solution.py:396
  15.2 3.0 %collective-permute-start.5 = (f32[4,16,256]{2,1,0:T(8,128)}, f32[4,16,256]{2,1,0:T(8,128)S(1)}, u32[]{:S(2)}, u32[]{:S(2)}) collective-permute-start(f32[4,16,256]{2,1,0:T(8,128)} %param.11), channel_id=1, source_target_pairs={{0,1},{1,0},{2,3},{3,2},{4,5},{5,4},{6,7},{7,6},{8,9},{9,8},{10,11... | collective-permute-start | bytes 196616 | tf_op jit(solution)/shard_map/ppermute | solution.py:389
  18.2 1.1 %collective-permute-done.5.refs_4_ = f32[4,16,256]{2,1,0:T(8,128)S(1)} collective-permute-done((f32[4,16,256]{2,1,0:T(8,128)}, f32[4,16,256]{2,1,0:T(8,128)S(1)}, u32[]{:S(2)}, u32[]{:S(2)}) %collective-permute-start.5) | collective-permute-done | bytes 65568 | tf_op jit(solution)/shard_map/ppermute | solution.py:389
  19.3 0.0 collective-permute-done.4.refs_3_
  19.3 0.0 collective-permute-done.3.refs_1_
  19.3 1.0 %shard_map.113 = (f32[12,12,24,256]{3,2,1,0:T(8,128)S(1)}, f32[12,24,256]{2,1,0:T(8,128)S(1)}) custom-call(f32[13,4,16,256]{3,2,1,0:T(8,128)S(1)} %pad_maximum_fusion.refs_0_, f32[12,4,16,256]{3,2,1,0:T(8,128)S(1)} %collective-permute-done.3.refs_1_, f32[13,4,8,128]{3,2,1,0:T(8,128)S(1)} %collective-permute-done.1.refs_2_, ...), custom_call_target="tpu_custom_call" | custom-call | flops 20000000 | bytes 4000000 | tf_op jit(solution)/shard_map/pallas_call | solution.py:435
  20.3 0.0 collective-permute-done.2.refs_1_
  20.3 0.0 collective-permute-done.refs_0_
  20.3 2.3 %shard_map.114 = (f32[12,12,24,256]{3,2,1,0:T(8,128)S(1)}, f32[12,24,256]{2,1,0:T(8,128)S(1)}, f32[6,4,16,256]{3,2,1,0:T(8,128)S(1)}, f32[6,4,16,256]{3,2,1,0:T(...) custom-call(f32[13,4,16,256]{3,2,1,0:T(8,128)S(1)} %collective-permu, ...), custom_call_target="tpu_custom_call", output_to_operand_aliasing={{0}: (2, {}), {1}: (3, {})} | custom-call | flops 20000000 | bytes 4000000 | tf_op jit(solution)/shard_map/pallas_call | solution.py:450
  22.6 0.0 copy-start
  22.6 0.0 copy-start.1
  22.6 0.0 copy-start.2
  22.6 0.0 copy-start.3
  22.6 0.0 copy-start.4
  22.6 1.9 %collective-permute-start.10 = (f32[12,4,16,256]{3,2,1,0:T(8,128)S(1)}, f32[12,4,16,256]{3,2,1,0:T(8,128)S(1)}, u32[]{:S(2)}, u32[]{:S(2)}) collective-permute-start(f32[12,4,16,256]{3,2,1,0:T(8,128)S(1)} %get-tuple-element.19.refs_0_), channel_id=1, source_target_pairs={{0,1},{1,0},{2,3},{3,2},{4,5},{5,4},{6,7},{7,6},{8,9},{9,8},{10,11... | collective-permute-start | bytes 2359304 | tf_op jit(solution)/shard_map/ppermute | solution.py:389
  24.6 1.5 %collective-permute-start.8 = (f32[12,4,8,128]{3,2,1,0:T(8,128)S(1)}, f32[12,4,8,128]{3,2,1,0:T(8,128)S(1)}, u32[]{:S(2)}, u32[]{:S(2)}) collective-permute-start(f32[12,4,8,128]{3,2,1,0:T(8,128)S(1)} %get-tuple-element.18), channel_id=1, source_target_pairs={{0,2},{2,0},{1,3},{3,1},{4,6},{6,4},{5,7},{7,5},{8,10},{10,8},{9,1... | collective-permute-start | bytes 589832 | tf_op jit(solution)/shard_map/ppermute | solution.py:405
  26.0 0.7 %collective-permute-start.6 = (f32[6,4,16,256]{3,2,1,0:T(8,128)S(1)}, f32[6,4,16,256]{3,2,1,0:T(8,128)S(1)}, u32[]{:S(2)}, u32[]{:S(2)}) collective-permute-start(f32[6,4,16,256]{3,2,1,0:T(8,128)S(1)} %get-tuple-element.16), channel_id=1, source_target_pairs={{1,4},{4,1},{5,8},{8,5},{9,12},{12,9},{3,6},{6,3},{7,10},{10,7},{1... | collective-permute-start | bytes 1179656 | tf_op jit(solution)/shard_map/ppermute | solution.py:396
  26.7 0.7 %collective-permute-start.7 = (f32[6,4,16,256]{3,2,1,0:T(8,128)S(1)}, f32[6,4,16,256]{3,2,1,0:T(8,128)S(1)}, u32[]{:S(2)}, u32[]{:S(2)}) collective-permute-start(f32[6,4,16,256]{3,2,1,0:T(8,128)S(1)} %get-tuple-element.17), channel_id=1, source_target_pairs={{1,4},{4,1},{5,8},{8,5},{9,12},{12,9},{3,6},{6,3},{7,10},{10,7},{1... | collective-permute-start | bytes 1179656 | tf_op jit(solution)/shard_map/ppermute | solution.py:396
  27.4 0.0 copy-done.5
  27.4 0.0 copy-done.6
  27.4 0.7 %shard_map.116 = (f32[16,8,256]{2,1,0:T(8,128)S(1)}, f32[256,128]{1,0:T(8,128)S(1)}) custom-call(s32[1,8]{1,0:T(1,128)S(1)} %copy-done.5, s32[1,128]{1,0:T(1,128)S(1)} %bitcast.4), custom_call_target="tpu_custom_call" | custom-call | tf_op jit(solution)/shard_map/pallas_call | solution.py:477
  28.1 3.3 %collective-permute-done.8.refs_2_ = f32[12,4,8,128]{3,2,1,0:T(8,128)S(1)} collective-permute-done((f32[12,4,8,128]{3,2,1,0:T(8,128)S(1)}, f32[12,4,8,128]{3,2,1,0:T(8,128)S(1)}, u32[]{:S(2)}, u32[]{:S(2)}) %collective-permute-start.8) | collective-permute-done | bytes 196640 | tf_op jit(solution)/shard_map/ppermute | solution.py:405
  31.4 0.9 %collective-permute-start.11 = (f32[12,4,8,128]{3,2,1,0:T(8,128)S(1)}, f32[12,4,8,128]{3,2,1,0:T(8,128)S(1)}, u32[]{:S(2)}, u32[]{:S(2)}) collective-permute-start(f32[12,4,8,128]{3,2,1,0:T(8,128)S(1)} %collective-permute-done.8.refs_2_), channel_id=1, source_target_pairs={{0,1},{1,0},{2,3},{3,2},{4,5},{5,4},{6,7},{7,6},{8,9},{9,8},{10,11... | collective-permute-start | bytes 589832 | tf_op jit(solution)/shard_map/ppermute | solution.py:389
  32.4 0.7 %collective-permute-start.9 = (f32[12,4,8,128]{3,2,1,0:T(8,128)S(1)}, f32[12,4,8,128]{3,2,1,0:T(8,128)S(1)}, u32[]{:S(2)}, u32[]{:S(2)}) collective-permute-start(f32[12,4,8,128]{3,2,1,0:T(8,128)S(1)} %collective-permute-done.8.refs_2_), channel_id=1, source_target_pairs={{1,4},{4,1},{5,8},{8,5},{9,12},{12,9},{3,6},{6,3},{7,10},{10,7},{1... | collective-permute-start | bytes 589832 | tf_op jit(solution)/shard_map/ppermute | solution.py:396
  33.0 0.0 copy-done.7
  33.1 0.4 collective-permute-done.11.refs_3_
  33.4 0.0 collective-permute-done.10.refs_1_
  33.4 0.8 %shard_map.115.refs_3_ = f32[12,12,24,256]{3,2,1,0:T(8,128)S(1)} custom-call(f32[12,4,16,256]{3,2,1,0:T(8,128)S(1)} %get-tuple-element.19.refs_0_, f32[12,4,16,256]{3,2,1,0:T(8,128)S(1)} %collective-permute-done.10.refs_1_, f32[12,4,8,128]{3,2,1,0:T(8,128)S(1)} %collective-permute-done.8.refs_2_, f32[12,4,8,128]{3,2,1,0:T(8,128)S(1)} %collective-permute-done.11.refs_3_, ...), custom_call_target="tpu_custom_call" | custom-call | flops 20000000 | bytes 4000000 | tf_op jit(solution)/shard_map/pallas_call | solution.py:504
  34.3 0.0 collective-permute-done.9.refs_2_
  34.3 0.0 collective-permute-done.6.refs_0_
  34.3 0.0 collective-permute-done.7.refs_1_
  34.3 0.0 copy-done
  34.3 0.0 copy-done.1
  34.3 0.0 copy-done.2
  34.4 0.0 copy-done.3
  34.4 0.0 copy-done.4
  34.4 4.1 %shard_map.117 = (f32[12,12,24,256]{3,2,1,0:T(8,128)S(1)}, f32[12,4,16,256]{3,2,1,0:T(8,128)}, f32[16,8,128]{2,1,0:T(8,128)}) custom-call(f32[6,4,16,256]{3,2,1,0:T(8,128)S(1)} %collective-permute-done.6.refs_0_, f32[6,4,16,256]{3,2,1,0:T(8,128)S(1)} %collective-permute-done.7.refs_1_, ...), custom_call_target="tpu_custom_call", output_to_operand_aliasing={{0}: (3, {})} | custom-call | flops 20000000 | bytes 4000000 | tf_op jit(solution)/shard_map/pallas_call | solution.py:521
  38.5 11.1 %all-to-all-start = ((f32[16,8,128]{2,1,0:T(8,128)}), f32[16,8,128]{2,1,0:T(8,128)S(1)}, u32[]{:S(2)}, u32[]{:S(2)}) async-start(f32[16,8,128]{2,1,0:T(8,128)} %get-tuple-element.25), calls=%async_computation | async-start | bytes 131072 | tf_op jit(solution)/shard_map/all_to_all | solution.py:543
  49.6 6.9 %all-to-all-done = f32[16,8,128]{2,1,0:T(8,128)S(1)} async-done(((f32[16,8,128]{2,1,0:T(8,128)}), f32[16,8,128]{2,1,0:T(8,128)S(1)}, u32[]{:S(2)}, u32[]{:S(2)}) %all-to-all-start) | async-done | bytes 65568 | tf_op jit(solution)/shard_map/all_to_all | solution.py:543
  56.5 0.7 %constant_dynamic-slice_fusion.1 = f32[8,16]{1,0:T(8,128)} fusion(f32[8,128]{1,0:T(8,128)S(1)} %reduce_sum.9, s32[]{:T(128)S(6)} %select_n.7), kind=kLoop, calls=%fused_computation.4 | loop fusion | bytes 1028 | tf_op jit(solution)/shard_map/dynamic_slice | solution.py:545
  (2 shorter events, 0.0 us)
Async XLA Ops:
  1.9 18.4 %collective-permute-start = (f32[13,4,16,256]{3,2,1,0:T(8,128)S(1)}, f32[13,4,16,256]{3,2,1,0:T(8,128)S(1)}, u32[]{:S(2)}, u32[]{:S(2)}) collective-permute-start(f32[13,4,16,256]{3,2,1,0:T(8,128)S(1)} %pad_maximum_fusion.refs_0_), channel_id=1, source_target_pairs={{1,4},{4,1},{5,8},{8,5},{9,12},{12,9},{3,6},{6,3},{7,10},{10,7},{1... | collective-permute-start | bytes 2555912 | tf_op jit(solution)/shard_map/ppermute | solution.py:396
  2.6 16.7 %collective-permute-start.3 = (f32[12,4,16,256]{3,2,1,0:T(8,128)}, f32[12,4,16,256]{3,2,1,0:T(8,128)S(1)}, u32[]{:S(2)}, u32[]{:S(2)}) collective-permute-start(f32[12,4,16,256]{3,2,1,0:T(8,128)} %bitcast.6), channel_id=1, source_target_pairs={{0,1},{1,0},{2,3},{3,2},{4,5},{5,4},{6,7},{7,6},{8,9},{9,8},{10,11... | collective-permute-start | bytes 2359304 | tf_op jit(solution)/shard_map/ppermute | solution.py:389
  7.2 20.2 %copy-start.5 = (s32[1,8]{1,0:T(1,128)S(1)}, s32[1,8]{1,0:T(1,128)}, u32[]{:S(2)}) copy-start(s32[1,8]{1,0:T(1,128)} %row_counts.1) | copy-start | bytes 100
  7.2 20.2 %copy-start.6 = (s32[128]{0:T(128)S(1)}, s32[128]{0:T(128)}, u32[]{:S(2)}) copy-start(s32[128]{0:T(128)} %param.13) | copy-start | bytes 1540
  7.2 25.8 %copy-start.7 = (f32[8,128]{1,0:T(8,128)S(1)}, f32[8,128]{1,0:T(8,128)}, u32[]{:S(2)}) copy-start(f32[8,128]{1,0:T(8,128)} %param.14) | copy-start | bytes 12292
  7.2 7.2 %collective-permute-start.1 = (f32[13,4,8,128]{3,2,1,0:T(8,128)S(1)}, f32[13,4,8,128]{3,2,1,0:T(8,128)S(1)}, u32[]{:S(2)}, u32[]{:S(2)}) collective-permute-start(f32[13,4,8,128]{3,2,1,0:T(8,128)S(1)} %pad_maximum_fusion.1), channel_id=1, source_target_pairs={{0,2},{2,0},{1,3},{3,1},{4,6},{6,4},{5,7},{7,5},{8,10},{10,8},{9,1... | collective-permute-start | bytes 638984 | tf_op jit(solution)/shard_map/ppermute | solution.py:405
  14.5 4.8 %collective-permute-start.4 = (f32[13,4,8,128]{3,2,1,0:T(8,128)S(1)}, f32[13,4,8,128]{3,2,1,0:T(8,128)S(1)}, u32[]{:S(2)}, u32[]{:S(2)}) collective-permute-start(f32[13,4,8,128]{3,2,1,0:T(8,128)S(1)} %collective-permute-done.1.refs_2_), channel_id=1, source_target_pairs={{0,1},{1,0},{2,3},{3,2},{4,5},{5,4},{6,7},{7,6},{8,9},{9,8},{10,11... | collective-permute-start | bytes 638984 | tf_op jit(solution)/shard_map/ppermute | solution.py:389
  14.5 5.8 %collective-permute-start.2 = (f32[13,4,8,128]{3,2,1,0:T(8,128)S(1)}, f32[13,4,8,128]{3,2,1,0:T(8,128)S(1)}, u32[]{:S(2)}, u32[]{:S(2)}) collective-permute-start(f32[13,4,8,128]{3,2,1,0:T(8,128)S(1)} %collective-permute-done.1.refs_2_), channel_id=1, source_target_pairs={{1,4},{4,1},{5,8},{8,5},{9,12},{12,9},{3,6},{6,3},{7,10},{10,7},{1... | collective-permute-start | bytes 638984 | tf_op jit(solution)/shard_map/ppermute | solution.py:396
  15.2 4.1 %collective-permute-start.5 = (f32[4,16,256]{2,1,0:T(8,128)}, f32[4,16,256]{2,1,0:T(8,128)S(1)}, u32[]{:S(2)}, u32[]{:S(2)}) collective-permute-start(f32[4,16,256]{2,1,0:T(8,128)} %param.11), channel_id=1, source_target_pairs={{0,1},{1,0},{2,3},{3,2},{4,5},{5,4},{6,7},{7,6},{8,9},{9,8},{10,11... | collective-permute-start | bytes 196616 | tf_op jit(solution)/shard_map/ppermute | solution.py:389
  22.6 11.8 %copy-start = (f32[128,256]{1,0:T(8,128)S(1)}, f32[128,256]{1,0:T(8,128)}, u32[]{:S(2)}) copy-start(f32[128,256]{1,0:T(8,128)} %constant.46.clone.refs_9_) | copy-start | bytes 393220
  22.6 11.8 %copy-start.1 = (f32[128,256]{1,0:T(8,128)S(1)}, f32[128,256]{1,0:T(8,128)}, u32[]{:S(2)}) copy-start(f32[128,256]{1,0:T(8,128)} %constant.47.clone.refs_10_) | copy-start | bytes 393220
  22.6 11.8 %copy-start.2 = (f32[16,16,128]{2,1,0:T(8,128)S(1)}, f32[16,16,128]{2,1,0:T(8,128)}, u32[]{:S(2)}) copy-start(f32[16,16,128]{2,1,0:T(8,128)} %constant.48.clone.refs_11_) | copy-start | bytes 393220
  22.6 11.8 %copy-start.3 = (f32[16,16,128]{2,1,0:T(8,128)S(1)}, f32[16,16,128]{2,1,0:T(8,128)}, u32[]{:S(2)}) copy-start(f32[16,16,128]{2,1,0:T(8,128)} %constant.49.clone.refs_12_) | copy-start | bytes 393220
  22.6 11.8 %copy-start.4 = (f32[16,128]{1,0:T(8,128)S(1)}, f32[16,128]{1,0:T(8,128)}, u32[]{:S(2)}) copy-start(f32[16,128]{1,0:T(8,128)} %constant.50.clone.refs_13_) | copy-start | bytes 24580
  22.6 10.8 %collective-permute-start.10 = (f32[12,4,16,256]{3,2,1,0:T(8,128)S(1)}, f32[12,4,16,256]{3,2,1,0:T(8,128)S(1)}, u32[]{:S(2)}, u32[]{:S(2)}) collective-permute-start(f32[12,4,16,256]{3,2,1,0:T(8,128)S(1)} %get-tuple-element.19.refs_0_), channel_id=1, source_target_pairs={{0,1},{1,0},{2,3},{3,2},{4,5},{5,4},{6,7},{7,6},{8,9},{9,8},{10,11... | collective-permute-start | bytes 2359304 | tf_op jit(solution)/shard_map/ppermute | solution.py:389
  24.6 6.9 %collective-permute-start.8 = (f32[12,4,8,128]{3,2,1,0:T(8,128)S(1)}, f32[12,4,8,128]{3,2,1,0:T(8,128)S(1)}, u32[]{:S(2)}, u32[]{:S(2)}) collective-permute-start(f32[12,4,8,128]{3,2,1,0:T(8,128)S(1)} %get-tuple-element.18), channel_id=1, source_target_pairs={{0,2},{2,0},{1,3},{3,1},{4,6},{6,4},{5,7},{7,5},{8,10},{10,8},{9,1... | collective-permute-start | bytes 589832 | tf_op jit(solution)/shard_map/ppermute | solution.py:405
  26.0 8.3 %collective-permute-start.6 = (f32[6,4,16,256]{3,2,1,0:T(8,128)S(1)}, f32[6,4,16,256]{3,2,1,0:T(8,128)S(1)}, u32[]{:S(2)}, u32[]{:S(2)}) collective-permute-start(f32[6,4,16,256]{3,2,1,0:T(8,128)S(1)} %get-tuple-element.16), channel_id=1, source_target_pairs={{1,4},{4,1},{5,8},{8,5},{9,12},{12,9},{3,6},{6,3},{7,10},{10,7},{1... | collective-permute-start | bytes 1179656 | tf_op jit(solution)/shard_map/ppermute | solution.py:396
  26.7 7.6 %collective-permute-start.7 = (f32[6,4,16,256]{3,2,1,0:T(8,128)S(1)}, f32[6,4,16,256]{3,2,1,0:T(8,128)S(1)}, u32[]{:S(2)}, u32[]{:S(2)}) collective-permute-start(f32[6,4,16,256]{3,2,1,0:T(8,128)S(1)} %get-tuple-element.17), channel_id=1, source_target_pairs={{1,4},{4,1},{5,8},{8,5},{9,12},{12,9},{3,6},{6,3},{7,10},{10,7},{1... | collective-permute-start | bytes 1179656 | tf_op jit(solution)/shard_map/ppermute | solution.py:396
  31.4 2.0 %collective-permute-start.11 = (f32[12,4,8,128]{3,2,1,0:T(8,128)S(1)}, f32[12,4,8,128]{3,2,1,0:T(8,128)S(1)}, u32[]{:S(2)}, u32[]{:S(2)}) collective-permute-start(f32[12,4,8,128]{3,2,1,0:T(8,128)S(1)} %collective-permute-done.8.refs_2_), channel_id=1, source_target_pairs={{0,1},{1,0},{2,3},{3,2},{4,5},{5,4},{6,7},{7,6},{8,9},{9,8},{10,11... | collective-permute-start | bytes 589832 | tf_op jit(solution)/shard_map/ppermute | solution.py:389
  32.4 1.9 %collective-permute-start.9 = (f32[12,4,8,128]{3,2,1,0:T(8,128)S(1)}, f32[12,4,8,128]{3,2,1,0:T(8,128)S(1)}, u32[]{:S(2)}, u32[]{:S(2)}) collective-permute-start(f32[12,4,8,128]{3,2,1,0:T(8,128)S(1)} %collective-permute-done.8.refs_2_), channel_id=1, source_target_pairs={{1,4},{4,1},{5,8},{8,5},{9,12},{12,9},{3,6},{6,3},{7,10},{10,7},{1... | collective-permute-start | bytes 589832 | tf_op jit(solution)/shard_map/ppermute | solution.py:396
  38.5 18.0 %all-to-all-start = ((f32[16,8,128]{2,1,0:T(8,128)}), f32[16,8,128]{2,1,0:T(8,128)S(1)}, u32[]{:S(2)}, u32[]{:S(2)}) async-start(f32[16,8,128]{2,1,0:T(8,128)} %get-tuple-element.25), calls=%async_computation | async-start | bytes 131072 | tf_op jit(solution)/shard_map/all_to_all | solution.py:543

commit v8 on v7

--- a/solution.py
+++ b/solution.py
@@ -152,15 +152,27 @@
         ez = st[b + 2, z] + scale * ((hy - x_behind(hy)) - (hx - y_behind(hx)))
         return ex, ey, ez, hx, hy, hz
 
-    def first_step(magnetic_layers, electric_layers):
+    def step(m, magnetic_layers, electric_layers, acc, second):
         for z in magnetic_layers:
-            magnetic(z, z >= 1)
+            magnetic(z, z >= m)
+        angle = omega_step * (m + (HALF if second else 0))
+        w_re, w_im = math.cos(angle), math.sin(angle)
         for z in electric_layers:
-            for b in (0, 6):
-                for c, f in enumerate(electric(z, b)[:3]):
-                    st[b + c, z] = f
-
-    return magnetic, electric, first_step
+            own = z - depth
+            for r in range(2):
+                for c, e in enumerate(electric(z, 6 * r)[:3]):
+                    st[6 * r + c, z] = e
+                    if not 0 <= own < depth:
+                        continue
+                    k = 3 * r + c
+                    re, im = e[:rows_own] * w_re, e[:rows_own] * w_im
+                    if m == 1 and not second:
+                        acc[0, k, own], acc[1, k, own] = re, -im
+                    else:
+                        acc[0, k, own] = acc[0, k, own] + re
+                        acc[1, k, own] = acc[1, k, own] - im
+
+    return magnetic, electric, step
 
 
 def early_kernel(cfg, *refs):
@@ -170,10 +182,10 @@
     full = take(2)
     strip_in = [take(2) for _ in range(sides)]
     if second:
-        (scale_ref, st, strips, sem_full, sem_strip) = take(5)
+        (scale_ref, _, st, acc, strips, sem_full, sem_strip) = take(7)
         eps = eps_in = None
     else:
-        (eps_sib, st, scale_ref, strips, eps, sem_full, sem_strip, sem_eps) = take(8)
+        (eps_sib, st, scale_ref, acc, strips, eps, sem_full, sem_strip, sem_eps) = take(9)
         eps_in = [full[0].at[12], eps_sib]
     gy, core = lax.axis_index("gy"), lax.axis_index("col")
     planes = 12 if second else 13
@@ -196,8 +208,10 @@
         for copy in copies:
             copy.wait()
         unpack(strips, st, scale_ref, range(base, base + 2 * depth), planes, eps, rows_own, gy)
-        first_step = updates(st, scale_ref, depth, rows_own)[2]
-        first_step(range(base, base + 2 * depth - 1), range(base + 1, base + 2 * depth - 1))
+        step = updates(st, scale_ref, depth, rows_own)[2]
+        for m in range(1, HALF):
+            top = base + 2 * depth - m
+            step(m, range(base + m - 1, top), range(base + m, top), acc, second)
 
     @pl.when(core == 0)
     def _():
@@ -219,12 +233,11 @@
     near = take(2 if second else 1)
     strip_in = take(sides)
     take(1)
-    (scale_ref,) = take(1)
+    scale_ref, _ = take(2)
     if second:
-        (acc_in,) = take(1)
         row_wide, col_table, slope, basis_x, basis_xt, basis_y, basis_yt, response = take(8)
-        st, out, share = take(3)
-        strips, acc, done, sem_full, sem_strip, sem_out = take(6)
+        st, acc, out, share = take(4)
+        strips, done, sem_full, sem_strip, sem_out = take(5)
     else:
         st, scale_ref = take(2)
         done = take(3)
@@ -233,7 +246,7 @@
         strips, eps, sem_full, sem_strip, sem_eps = take(5)
     nx = st.shape[-1]
     n_layers = 3 * depth
-    magnetic, electric, first_step = updates(st, scale_ref, depth, rows_own)
+    magnetic, electric, step = updates(st, scale_ref, depth, rows_own)
 
     def start(place):
         layers = pl.ds(place * depth, depth)
@@ -261,28 +274,18 @@
     @pl.when(core == 0)
     def _():
         start(0)
-        first_step(range(depth), range(1, depth + 1))
+        for m in range(1, HALF):
+            step(m, range(m - 1, m + depth - 1), range(m, m + depth), acc, second)
 
     @pl.when(core != 0)
     def _():
         start(2)
-        layers = range(2 * depth - 1, n_layers - 1)
-        first_step(layers, layers)
-
-    angle = omega_step * (1 + (HALF if second else 0))
-    w_re, w_im = math.cos(angle), math.sin(angle)
-    for own in range(depth):
-        for k in range(6):
-            e = st[6 * (k // 3) + k % 3, depth + own, :rows_own, :]
-            if second:
-                acc[0, k, own] = acc_in[0, k, own] + e * w_re
-                acc[1, k, own] = acc_in[1, k, own] - e * w_im
-            else:
-                acc[0, k, own] = e * w_re
-                acc[1, k, own] = -(e * w_im)
+        for m in range(1, HALF):
+            layers = range(2 * depth - m, n_layers - m)
+            step(m, layers, layers, acc, second)
 
     column_sum = jnp.zeros((rows_own, nx), jnp.float32)
-    for m in range(2, HALF + 1):
+    for m in range(HALF, HALF + 1):
         angle = omega_step * (m + (HALF if second else 0))
         w_re, w_im = math.cos(angle), math.sin(angle)
         for z in range(m - 1, n_layers - m):
@@ -432,11 +435,11 @@
     wide = (12, 3 * depth, rows, nx)
     sems = pltpu.SemaphoreType.DMA
     sibling = swap_core(fields.reshape(runs * comps, depth, rows_own, nx))
-    window, scale = pl.pallas_call(
+    window, scale, acc = pl.pallas_call(
         functools.partial(early_kernel, (depth, rows_own, sides, False)),
-        out_shape=(shape(*wide), shape(3 * depth, rows, nx)),
+        out_shape=(shape(*wide), shape(3 * depth, rows, nx), shape(2, 6, depth, rows_own, nx)),
         in_specs=[anywhere] * (3 + 2 * sides),
-        out_specs=(vmem, vmem),
+        out_specs=(vmem, vmem, vmem),
         scratch_shapes=[
             pltpu.VMEM((sides, 13, 3 * depth, 8, 128), jnp.float32),
             pltpu.VMEM((3 * depth, rows_own, nx), jnp.float32),
@@ -458,9 +461,9 @@
             shape(2, 6, depth, rows_own, nx),
         )
         + (shape(12, depth, 8, 128),) * sides,
-        in_specs=[anywhere] * (1 + sides) + [vmem] * 2,
+        in_specs=[anywhere] * (1 + sides) + [vmem] * 3,
         out_specs=(vmem,) * (6 + sides),
-        input_output_aliases={1 + sides: 0, 2 + sides: 1},
+        input_output_aliases={1 + sides: 0, 2 + sides: 1, 3 + sides: 5},
         scratch_shapes=[
             pltpu.VMEM((sides, 13, 3 * depth, 8, 128), jnp.float32),
             pltpu.VMEM((3 * depth, rows_own, nx), jnp.float32),
@@ -470,7 +473,7 @@
         ],
         compiler_params=limit,
         cost_estimate=cost,
-    )(near, *sent[::3], window, scale)
+    )(near, *sent[::3], window, scale, acc)
 
     band, design_cols = density.shape
     tall = band * n_gy
@@ -501,11 +504,12 @@
         return const(np.concatenate([high, matrix - high], axis=1))
 
     sent = strips_sent(strips)
-    window = pl.pallas_call(
+    window, acc = pl.pallas_call(
         functools.partial(early_kernel, (depth, rows_own, sides, True)),
-        out_shape=shape(*wide),
-        in_specs=[anywhere] * (2 + 2 * sides) + [vmem],
-        out_specs=vmem,
+        out_shape=(shape(*wide), shape(2, 6, depth, rows_own, nx)),
+        in_specs=[anywhere] * (2 + 2 * sides) + [vmem] * 2,
+        out_specs=(vmem, vmem),
+        input_output_aliases={3 + 2 * sides: 1},
         scratch_shapes=[
             pltpu.VMEM((sides, 12, 3 * depth, 8, 128), jnp.float32),
             sems((2,)),
@@ -513,24 +517,24 @@
         ],
         compiler_params=limit,
         cost_estimate=cost,
-    )(state, swap_core(state), *here(sent), scale)
+    )(state, swap_core(state), *here(sent), scale, acc)
     operands = [cross(half_0), cross(half_1), *sent[::3], window, scale, acc]
     operands += [row_wide, col_table, slope_of(density), halves(basis_x), halves(basis_x.T)]
     operands += [const(tables[0]), const(tables[1]), const(response)]
     n_all = n_z * n_gy
-    _, fields_out, share = pl.pallas_call(
+    _, _, fields_out, share = pl.pallas_call(
         functools.partial(window_kernel, (depth, rows_own, sides, True)),
         out_shape=(
             shape(*wide),
+            shape(2, 6, depth, rows_own, nx),
             shape(runs * comps, depth, rows_own, nx),
             shape(n_all, band, design_cols),
         ),
         in_specs=[anywhere] * (2 + sides) + [vmem] * 11,
-        out_specs=(vmem, anywhere, vmem),
-        input_output_aliases={2 + sides: 0},
+        out_specs=(vmem, vmem, anywhere, vmem),
+        input_output_aliases={2 + sides: 0, 4 + sides: 1},
         scratch_shapes=[
             pltpu.VMEM((sides, 12, 3 * depth, 8, 128), jnp.float32),
-            pltpu.VMEM((2, 6, depth, rows_own, nx), jnp.float32),
             pltpu.VMEM((12, depth, rows_own, nx), jnp.float32),
             sems((2,)),
             sems((sides,)),

time: 57.5 us -> 55.9 us (0.972)
  starting transfers between devices: 27.8 us -> 26.6 us
    pallas_call x2, Pallas kernels: 6.38 us -> 4.73 us  [body(): pl.pallas_call(functools.partial(window_kernel, (depth, rows_own, sides,...]
    pallas_call x1, Pallas kernels: 0.99 us -> 1.65 us  [body(): pl.pallas_call(functools.partial(early_kernel, (depth, rows_own, sides, F...]
    pallas_call x1, Pallas kernels: 0.84 us -> 1.45 us  [body(): pl.pallas_call(functools.partial(early_kernel, (depth, rows_own, sides, T...]
    all_to_all x1, starting transfers between devices: 11.1 us -> 10.5 us  [body(): got = lax.all_to_all(share, ('gz', 'gy', 'col'), 0, 0)]
    ppermute x5, starting transfers between devices: 10.3 us -> 9.66 us  [swap_core(): return lax.ppermute(x, 'col', [(0, 1), (1, 0)])]
  transfers between devices with their start and end apart: 13 -> 13, of which waited for: 5 -> 5; matrix products, arithmetic and copies ran while one was open for 0% -> 0% of each run, Pallas kernels for 4% -> 7%
where the time goes in v8:
time: 55.9 us; the launch traced here: 55.6 us
  starting transfers between devices  26.6 us (48%)
  waiting for transfers between devices  17.4 us (31%)
  Pallas kernels  8.53 us (15%)
  other arithmetic  1.34 us (2%)
  between operations  0.91 us (2%)
  local copies, waits for them, and re-layouts  0.85 us (2%)
    all_to_all x1, starting transfers between devices, body(): got = lax.all_to_all(share, ('gz', 'gy', 'col'), 0, 0)  10.5 us
    ppermute x5, starting transfers between devices, swap_core(): return lax.ppermute(x, 'col', [(0, 1), (1, 0)])  9.66 us
    ppermute x2, waiting for transfers between devices, along_y(): return lax.ppermute(x, 'gy', list(ways[s].items()))  8.98 us
    all_to_all x1, waiting for transfers between devices, body(): got = lax.all_to_all(share, ('gz', 'gy', 'col'), 0, 0)  6.89 us
    pallas_call x2, Pallas kernels, body(): pl.pallas_call(functools.partial(window_kernel, (depth, rows_own, sides,...  4.73 us
    ppermute x5, starting transfers between devices, cross(): return lax.ppermute(x, Z, pairs)  3.4 us
    ppermute x2, starting transfers between devices, along_y(): return lax.ppermute(x, 'gy', list(ways[s].items()))  3.05 us
    pallas_call x1, Pallas kernels, body(): pl.pallas_call(functools.partial(early_kernel, (depth, rows_own, sides, F...  1.65 us
  transfers between devices with their start and end apart: 13, of which 5 were waited for; matrix products, arithmetic and copies ran while one was open for 0% of the time, Pallas kernels for 7%

profile of v8, /device:TPU:0, one launch (start us, length us, event | category | flops | bytes accessed | tf_op | source)
XLA Modules:
  0.0 55.6 jit_solution(13357349761712147387)
XLA Ops:
  0.6 1.3 %pad_maximum_fusion.refs_0_ = f32[13,4,16,256]{3,2,1,0:T(8,128)S(1)} fusion(f32[1,4,16,256]{3,2,1,0:T(8,128)} %bitcast.7, f32[12,4,16,256]{3,2,1,0:T(8,128)} %bitcast.5), kind=kLoop, calls=%fused_computation | loop fusion | flops 212992 | bytes 1703936 | tf_op jit(solution)/shard_map/concatenate | solution.py:388
  1.9 0.7 %collective-permute-start = (f32[13,4,16,256]{3,2,1,0:T(8,128)S(1)}, f32[13,4,16,256]{3,2,1,0:T(8,128)S(1)}, u32[]{:S(2)}, u32[]{:S(2)}) collective-permute-start(f32[13,4,16,256]{3,2,1,0:T(8,128)S(1)} %pad_maximum_fusion.refs_0_), channel_id=1, source_target_pairs={{1,4},{4,1},{5,8},{8,5},{9,12},{12,9},{3,6},{6,3},{7,10},{10,7},{1... | collective-permute-start | bytes 2555912 | tf_op jit(solution)/shard_map/ppermute | solution.py:399
  2.6 4.4 %collective-permute-start.3 = (f32[12,4,16,256]{3,2,1,0:T(8,128)}, f32[12,4,16,256]{3,2,1,0:T(8,128)S(1)}, u32[]{:S(2)}, u32[]{:S(2)}) collective-permute-start(f32[12,4,16,256]{3,2,1,0:T(8,128)} %bitcast.6), channel_id=1, source_target_pairs={{0,1},{1,0},{2,3},{3,2},{4,5},{5,4},{6,7},{7,6},{8,9},{9,8},{10,11... | collective-permute-start | bytes 2359304 | tf_op jit(solution)/shard_map/ppermute | solution.py:392
  7.0 0.1 constant_dynamic-slice_fusion
  7.1 0.1 pad_maximum_fusion.1
  7.2 0.0 copy-start.5
  7.2 0.0 copy-start.6
  7.2 0.0 copy-start.7
  7.2 1.6 %collective-permute-start.1 = (f32[13,4,8,128]{3,2,1,0:T(8,128)S(1)}, f32[13,4,8,128]{3,2,1,0:T(8,128)S(1)}, u32[]{:S(2)}, u32[]{:S(2)}) collective-permute-start(f32[13,4,8,128]{3,2,1,0:T(8,128)S(1)} %pad_maximum_fusion.1), channel_id=1, source_target_pairs={{0,2},{2,0},{1,3},{3,1},{4,6},{6,4},{5,7},{7,5},{8,10},{10,8},{9,1... | collective-permute-start | bytes 638984 | tf_op jit(solution)/shard_map/ppermute | solution.py:408
  8.8 5.7 %collective-permute-done.1.refs_2_ = f32[13,4,8,128]{3,2,1,0:T(8,128)S(1)} collective-permute-done((f32[13,4,8,128]{3,2,1,0:T(8,128)S(1)}, f32[13,4,8,128]{3,2,1,0:T(8,128)S(1)}, u32[]{:S(2)}, u32[]{:S(2)}) %collective-permute-start.1) | collective-permute-done | bytes 213024 | tf_op jit(solution)/shard_map/ppermute | solution.py:408
  14.5 0.0 collective-permute-start.4
  14.5 0.7 %collective-permute-start.2 = (f32[13,4,8,128]{3,2,1,0:T(8,128)S(1)}, f32[13,4,8,128]{3,2,1,0:T(8,128)S(1)}, u32[]{:S(2)}, u32[]{:S(2)}) collective-permute-start(f32[13,4,8,128]{3,2,1,0:T(8,128)S(1)} %collective-permute-done.1.refs_2_), channel_id=1, source_target_pairs={{1,4},{4,1},{5,8},{8,5},{9,12},{12,9},{3,6},{6,3},{7,10},{10,7},{1... | collective-permute-start | bytes 638984 | tf_op jit(solution)/shard_map/ppermute | solution.py:399
  15.2 3.0 %collective-permute-start.5 = (f32[4,16,256]{2,1,0:T(8,128)}, f32[4,16,256]{2,1,0:T(8,128)S(1)}, u32[]{:S(2)}, u32[]{:S(2)}) collective-permute-start(f32[4,16,256]{2,1,0:T(8,128)} %param.11), channel_id=1, source_target_pairs={{0,1},{1,0},{2,3},{3,2},{4,5},{5,4},{6,7},{7,6},{8,9},{9,8},{10,11... | collective-permute-start | bytes 196616 | tf_op jit(solution)/shard_map/ppermute | solution.py:392
  18.2 1.1 %collective-permute-done.5.refs_4_ = f32[4,16,256]{2,1,0:T(8,128)S(1)} collective-permute-done((f32[4,16,256]{2,1,0:T(8,128)}, f32[4,16,256]{2,1,0:T(8,128)S(1)}, u32[]{:S(2)}, u32[]{:S(2)}) %collective-permute-start.5) | collective-permute-done | bytes 65568 | tf_op jit(solution)/shard_map/ppermute | solution.py:392
  19.3 0.0 collective-permute-done.4.refs_3_
  19.3 0.0 collective-permute-done.3.refs_1_
  19.3 1.7 %shard_map.113 = (f32[12,12,24,256]{3,2,1,0:T(8,128)S(1)}, f32[12,24,256]{2,1,0:T(8,128)S(1)}, f32[2,6,4,16,256]{4,3,2,1,0:T(8,128)S(1)}) custom-call(f32[13,4,16,256]{3,2,1,0:T(8,128)S(1)} %pad_maximum_fusion.refs_0_, f32[12,4,16,256]{3,2,1,0:T(8,128)S(1)} %collective-permute-done.3.refs_1_, f32[13,4,8,128]{3,2,1,0:T(8,128)S(1)} %collective-permute-done.1.refs_2_, ...), custom_call_target="tpu_custom_call" | custom-call | flops 20000000 | bytes 4000000 | tf_op jit(solution)/shard_map/pallas_call | solution.py:438
  20.9 0.0 collective-permute-done.2.refs_1_
  20.9 0.0 collective-permute-done.refs_0_
  21.0 0.0 copy-start
  21.0 0.0 copy-start.1
  21.0 0.0 copy-start.2
  21.0 0.0 copy-start.3
  21.0 0.0 copy-start.4
  21.0 1.6 %shard_map.114 = (f32[12,12,24,256]{3,2,1,0:T(8,128)S(1)}, f32[12,24,256]{2,1,0:T(8,128)S(1)}, f32[6,4,16,256]{3,2,1,0:T(8,128)S(1)}, f32[6,4,16,256]{3,2,1,0:T(...) custom-call(f32[13,4,16,256]{3,2,1,0:T(8,128)S(1)} %collective-permu, ...), custom_call_target="tpu_custom_call", output_to_operand_aliasing={{0}: (2, {}), {1}: (3, {}), {5}: (4, {})} | custom-call | flops 20000000 | bytes 4000000 | tf_op jit(solution)/shard_map/pallas_call | solution.py:453
  22.7 1.3 %collective-permute-start.10 = (f32[12,4,16,256]{3,2,1,0:T(8,128)S(1)}, f32[12,4,16,256]{3,2,1,0:T(8,128)S(1)}, u32[]{:S(2)}, u32[]{:S(2)}) collective-permute-start(f32[12,4,16,256]{3,2,1,0:T(8,128)S(1)} %get-tuple-element.23.refs_0_), channel_id=1, source_target_pairs={{0,1},{1,0},{2,3},{3,2},{4,5},{5,4},{6,7},{7,6},{8,9},{9,8},{10,11... | collective-permute-start | bytes 2359304 | tf_op jit(solution)/shard_map/ppermute | solution.py:392
  24.0 1.5 %collective-permute-start.8 = (f32[12,4,8,128]{3,2,1,0:T(8,128)S(1)}, f32[12,4,8,128]{3,2,1,0:T(8,128)S(1)}, u32[]{:S(2)}, u32[]{:S(2)}) collective-permute-start(f32[12,4,8,128]{3,2,1,0:T(8,128)S(1)} %get-tuple-element.22), channel_id=1, source_target_pairs={{0,2},{2,0},{1,3},{3,1},{4,6},{6,4},{5,7},{7,5},{8,10},{10,8},{9,1... | collective-permute-start | bytes 589832 | tf_op jit(solution)/shard_map/ppermute | solution.py:408
  25.5 0.7 %collective-permute-start.6 = (f32[6,4,16,256]{3,2,1,0:T(8,128)S(1)}, f32[6,4,16,256]{3,2,1,0:T(8,128)S(1)}, u32[]{:S(2)}, u32[]{:S(2)}) collective-permute-start(f32[6,4,16,256]{3,2,1,0:T(8,128)S(1)} %get-tuple-element.20), channel_id=1, source_target_pairs={{1,4},{4,1},{5,8},{8,5},{9,12},{12,9},{3,6},{6,3},{7,10},{10,7},{1... | collective-permute-start | bytes 1179656 | tf_op jit(solution)/shard_map/ppermute | solution.py:399
  26.2 0.7 %collective-permute-start.7 = (f32[6,4,16,256]{3,2,1,0:T(8,128)S(1)}, f32[6,4,16,256]{3,2,1,0:T(8,128)S(1)}, u32[]{:S(2)}, u32[]{:S(2)}) collective-permute-start(f32[6,4,16,256]{3,2,1,0:T(8,128)S(1)} %get-tuple-element.21), channel_id=1, source_target_pairs={{1,4},{4,1},{5,8},{8,5},{9,12},{12,9},{3,6},{6,3},{7,10},{10,7},{1... | collective-permute-start | bytes 1179656 | tf_op jit(solution)/shard_map/ppermute | solution.py:399
  26.9 0.0 copy-done.5
  26.9 0.0 copy-done.6
  26.9 0.7 %shard_map.116 = (f32[16,8,256]{2,1,0:T(8,128)S(1)}, f32[256,128]{1,0:T(8,128)S(1)}) custom-call(s32[1,8]{1,0:T(1,128)S(1)} %copy-done.5, s32[1,128]{1,0:T(1,128)S(1)} %bitcast.4), custom_call_target="tpu_custom_call" | custom-call | tf_op jit(solution)/shard_map/pallas_call | solution.py:480
  27.6 3.3 %collective-permute-done.8.refs_2_ = f32[12,4,8,128]{3,2,1,0:T(8,128)S(1)} collective-permute-done((f32[12,4,8,128]{3,2,1,0:T(8,128)S(1)}, f32[12,4,8,128]{3,2,1,0:T(8,128)S(1)}, u32[]{:S(2)}, u32[]{:S(2)}) %collective-permute-start.8) | collective-permute-done | bytes 196640 | tf_op jit(solution)/shard_map/ppermute | solution.py:408
  30.9 0.9 %collective-permute-start.11 = (f32[12,4,8,128]{3,2,1,0:T(8,128)S(1)}, f32[12,4,8,128]{3,2,1,0:T(8,128)S(1)}, u32[]{:S(2)}, u32[]{:S(2)}) collective-permute-start(f32[12,4,8,128]{3,2,1,0:T(8,128)S(1)} %collective-permute-done.8.refs_2_), channel_id=1, source_target_pairs={{0,1},{1,0},{2,3},{3,2},{4,5},{5,4},{6,7},{7,6},{8,9},{9,8},{10,11... | collective-permute-start | bytes 589832 | tf_op jit(solution)/shard_map/ppermute | solution.py:392
  31.8 0.7 %collective-permute-start.9 = (f32[12,4,8,128]{3,2,1,0:T(8,128)S(1)}, f32[12,4,8,128]{3,2,1,0:T(8,128)S(1)}, u32[]{:S(2)}, u32[]{:S(2)}) collective-permute-start(f32[12,4,8,128]{3,2,1,0:T(8,128)S(1)} %collective-permute-done.8.refs_2_), channel_id=1, source_target_pairs={{1,4},{4,1},{5,8},{8,5},{9,12},{12,9},{3,6},{6,3},{7,10},{10,7},{1... | collective-permute-start | bytes 589832 | tf_op jit(solution)/shard_map/ppermute | solution.py:399
  32.5 0.0 copy-done.7
  32.5 0.4 collective-permute-done.11.refs_3_
  32.9 0.0 collective-permute-done.10.refs_1_
  32.9 1.4 %shard_map.115 = (f32[12,12,24,256]{3,2,1,0:T(8,128)S(1)}, f32[2,6,4,16,256]{4,3,2,1,0:T(8,128)S(1)}) custom-call(f32[12,4,16,256]{3,2,1,0:T(8,128)S(1)} %get-tuple-element.23.refs_0_, f32[12,4,16,256]{3,2,1,0:T(8,128)S(1)} %collective-permute-done.10.refs_1_, f32[12,4,8,128]{3,2,1,0:T(8,128)S(1)} %collective-permute-done.8.refs_2_, ...), custom_call_target="tpu_custom_call", output_to_operand_aliasing={{1}: (5, {})} | custom-call | flops 20000000 | bytes 4000000 | tf_op jit(solution)/shard_map/pallas_call | solution.py:507
  34.3 0.0 collective-permute-done.9.refs_2_
  34.4 0.0 collective-permute-done.6.refs_0_
  34.4 0.0 collective-permute-done.7.refs_1_
  34.4 0.0 copy-done
  34.4 0.0 copy-done.1
  34.4 0.0 copy-done.2
  34.4 0.0 copy-done.3
  34.4 0.0 copy-done.4
  34.4 3.1 %shard_map.117 = (f32[12,12,24,256]{3,2,1,0:T(8,128)S(1)}, f32[2,6,4,16,256]{4,3,2,1,0:T(8,128)S(1)}, f32[12,4,16,256]{3,2,1,0:T(8,128)}, f32[16,8,128]{2,1,0:T(8,128)}) custom-call(f32[6,4,16,256]{3,2,1,0:T(8,128)S(1)} %collective-permute-done.6.refs_0_, ...), custom_call_target="tpu_custom_call", output_to_operand_aliasing={{0}: (3, {}), {1}: (5, {})} | custom-call | flops 20000000 | bytes 4000000 | tf_op jit(solution)/shard_map/pallas_call | solution.py:525
  37.5 10.5 %all-to-all-start = ((f32[16,8,128]{2,1,0:T(8,128)}), f32[16,8,128]{2,1,0:T(8,128)S(1)}, u32[]{:S(2)}, u32[]{:S(2)}) async-start(f32[16,8,128]{2,1,0:T(8,128)} %get-tuple-element.31), calls=%async_computation | async-start | bytes 131072 | tf_op jit(solution)/shard_map/all_to_all | solution.py:547
  48.0 6.9 %all-to-all-done = f32[16,8,128]{2,1,0:T(8,128)S(1)} async-done(((f32[16,8,128]{2,1,0:T(8,128)}), f32[16,8,128]{2,1,0:T(8,128)S(1)}, u32[]{:S(2)}, u32[]{:S(2)}) %all-to-all-start) | async-done | bytes 65568 | tf_op jit(solution)/shard_map/all_to_all | solution.py:547
  54.9 0.7 %constant_dynamic-slice_fusion.1 = f32[8,16]{1,0:T(8,128)} fusion(f32[8,128]{1,0:T(8,128)S(1)} %reduce_sum.9, s32[]{:T(128)S(6)} %select_n.7), kind=kLoop, calls=%fused_computation.4 | loop fusion | bytes 1028 | tf_op jit(solution)/shard_map/dynamic_slice | solution.py:549
  (2 shorter events, 0.0 us)
Async XLA Ops:
  1.9 19.1 %collective-permute-start = (f32[13,4,16,256]{3,2,1,0:T(8,128)S(1)}, f32[13,4,16,256]{3,2,1,0:T(8,128)S(1)}, u32[]{:S(2)}, u32[]{:S(2)}) collective-permute-start(f32[13,4,16,256]{3,2,1,0:T(8,128)S(1)} %pad_maximum_fusion.refs_0_), channel_id=1, source_target_pairs={{1,4},{4,1},{5,8},{8,5},{9,12},{12,9},{3,6},{6,3},{7,10},{10,7},{1... | collective-permute-start | bytes 2555912 | tf_op jit(solution)/shard_map/ppermute | solution.py:399
  2.6 16.7 %collective-permute-start.3 = (f32[12,4,16,256]{3,2,1,0:T(8,128)}, f32[12,4,16,256]{3,2,1,0:T(8,128)S(1)}, u32[]{:S(2)}, u32[]{:S(2)}) collective-permute-start(f32[12,4,16,256]{3,2,1,0:T(8,128)} %bitcast.6), channel_id=1, source_target_pairs={{0,1},{1,0},{2,3},{3,2},{4,5},{5,4},{6,7},{7,6},{8,9},{9,8},{10,11... | collective-permute-start | bytes 2359304 | tf_op jit(solution)/shard_map/ppermute | solution.py:392
  7.2 19.7 %copy-start.5 = (s32[1,8]{1,0:T(1,128)S(1)}, s32[1,8]{1,0:T(1,128)}, u32[]{:S(2)}) copy-start(s32[1,8]{1,0:T(1,128)} %row_counts.1) | copy-start | bytes 100
  7.2 19.7 %copy-start.6 = (s32[128]{0:T(128)S(1)}, s32[128]{0:T(128)}, u32[]{:S(2)}) copy-start(s32[128]{0:T(128)} %param.13) | copy-start | bytes 1540
  7.2 25.3 %copy-start.7 = (f32[8,128]{1,0:T(8,128)S(1)}, f32[8,128]{1,0:T(8,128)}, u32[]{:S(2)}) copy-start(f32[8,128]{1,0:T(8,128)} %param.14) | copy-start | bytes 12292
  7.2 7.2 %collective-permute-start.1 = (f32[13,4,8,128]{3,2,1,0:T(8,128)S(1)}, f32[13,4,8,128]{3,2,1,0:T(8,128)S(1)}, u32[]{:S(2)}, u32[]{:S(2)}) collective-permute-start(f32[13,4,8,128]{3,2,1,0:T(8,128)S(1)} %pad_maximum_fusion.1), channel_id=1, source_target_pairs={{0,2},{2,0},{1,3},{3,1},{4,6},{6,4},{5,7},{7,5},{8,10},{10,8},{9,1... | collective-permute-start | bytes 638984 | tf_op jit(solution)/shard_map/ppermute | solution.py:408
  14.5 4.8 %collective-permute-start.4 = (f32[13,4,8,128]{3,2,1,0:T(8,128)S(1)}, f32[13,4,8,128]{3,2,1,0:T(8,128)S(1)}, u32[]{:S(2)}, u32[]{:S(2)}) collective-permute-start(f32[13,4,8,128]{3,2,1,0:T(8,128)S(1)} %collective-permute-done.1.refs_2_), channel_id=1, source_target_pairs={{0,1},{1,0},{2,3},{3,2},{4,5},{5,4},{6,7},{7,6},{8,9},{9,8},{10,11... | collective-permute-start | bytes 638984 | tf_op jit(solution)/shard_map/ppermute | solution.py:392
  14.5 6.4 %collective-permute-start.2 = (f32[13,4,8,128]{3,2,1,0:T(8,128)S(1)}, f32[13,4,8,128]{3,2,1,0:T(8,128)S(1)}, u32[]{:S(2)}, u32[]{:S(2)}) collective-permute-start(f32[13,4,8,128]{3,2,1,0:T(8,128)S(1)} %collective-permute-done.1.refs_2_), channel_id=1, source_target_pairs={{1,4},{4,1},{5,8},{8,5},{9,12},{12,9},{3,6},{6,3},{7,10},{10,7},{1... | collective-permute-start | bytes 638984 | tf_op jit(solution)/shard_map/ppermute | solution.py:399
  15.2 4.1 %collective-permute-start.5 = (f32[4,16,256]{2,1,0:T(8,128)}, f32[4,16,256]{2,1,0:T(8,128)S(1)}, u32[]{:S(2)}, u32[]{:S(2)}) collective-permute-start(f32[4,16,256]{2,1,0:T(8,128)} %param.11), channel_id=1, source_target_pairs={{0,1},{1,0},{2,3},{3,2},{4,5},{5,4},{6,7},{7,6},{8,9},{9,8},{10,11... | collective-permute-start | bytes 196616 | tf_op jit(solution)/shard_map/ppermute | solution.py:392
  21.0 13.4 %copy-start = (f32[128,256]{1,0:T(8,128)S(1)}, f32[128,256]{1,0:T(8,128)}, u32[]{:S(2)}) copy-start(f32[128,256]{1,0:T(8,128)} %constant.46.clone.refs_9_) | copy-start | bytes 393220
  21.0 13.4 %copy-start.1 = (f32[128,256]{1,0:T(8,128)S(1)}, f32[128,256]{1,0:T(8,128)}, u32[]{:S(2)}) copy-start(f32[128,256]{1,0:T(8,128)} %constant.47.clone.refs_10_) | copy-start | bytes 393220
  21.0 13.4 %copy-start.2 = (f32[16,16,128]{2,1,0:T(8,128)S(1)}, f32[16,16,128]{2,1,0:T(8,128)}, u32[]{:S(2)}) copy-start(f32[16,16,128]{2,1,0:T(8,128)} %constant.48.clone.refs_11_) | copy-start | bytes 393220
  21.0 13.4 %copy-start.3 = (f32[16,16,128]{2,1,0:T(8,128)S(1)}, f32[16,16,128]{2,1,0:T(8,128)}, u32[]{:S(2)}) copy-start(f32[16,16,128]{2,1,0:T(8,128)} %constant.49.clone.refs_12_) | copy-start | bytes 393220
  21.0 13.4 %copy-start.4 = (f32[16,128]{1,0:T(8,128)S(1)}, f32[16,128]{1,0:T(8,128)}, u32[]{:S(2)}) copy-start(f32[16,128]{1,0:T(8,128)} %constant.50.clone.refs_13_) | copy-start | bytes 24580
  22.7 10.2 %collective-permute-start.10 = (f32[12,4,16,256]{3,2,1,0:T(8,128)S(1)}, f32[12,4,16,256]{3,2,1,0:T(8,128)S(1)}, u32[]{:S(2)}, u32[]{:S(2)}) collective-permute-start(f32[12,4,16,256]{3,2,1,0:T(8,128)S(1)} %get-tuple-element.23.refs_0_), channel_id=1, source_target_pairs={{0,1},{1,0},{2,3},{3,2},{4,5},{5,4},{6,7},{7,6},{8,9},{9,8},{10,11... | collective-permute-start | bytes 2359304 | tf_op jit(solution)/shard_map/ppermute | solution.py:392
  24.0 6.9 %collective-permute-start.8 = (f32[12,4,8,128]{3,2,1,0:T(8,128)S(1)}, f32[12,4,8,128]{3,2,1,0:T(8,128)S(1)}, u32[]{:S(2)}, u32[]{:S(2)}) collective-permute-start(f32[12,4,8,128]{3,2,1,0:T(8,128)S(1)} %get-tuple-element.22), channel_id=1, source_target_pairs={{0,2},{2,0},{1,3},{3,1},{4,6},{6,4},{5,7},{7,5},{8,10},{10,8},{9,1... | collective-permute-start | bytes 589832 | tf_op jit(solution)/shard_map/ppermute | solution.py:408
  25.5 8.9 %collective-permute-start.6 = (f32[6,4,16,256]{3,2,1,0:T(8,128)S(1)}, f32[6,4,16,256]{3,2,1,0:T(8,128)S(1)}, u32[]{:S(2)}, u32[]{:S(2)}) collective-permute-start(f32[6,4,16,256]{3,2,1,0:T(8,128)S(1)} %get-tuple-element.20), channel_id=1, source_target_pairs={{1,4},{4,1},{5,8},{8,5},{9,12},{12,9},{3,6},{6,3},{7,10},{10,7},{1... | collective-permute-start | bytes 1179656 | tf_op jit(solution)/shard_map/ppermute | solution.py:399
  26.2 8.2 %collective-permute-start.7 = (f32[6,4,16,256]{3,2,1,0:T(8,128)S(1)}, f32[6,4,16,256]{3,2,1,0:T(8,128)S(1)}, u32[]{:S(2)}, u32[]{:S(2)}) collective-permute-start(f32[6,4,16,256]{3,2,1,0:T(8,128)S(1)} %get-tuple-element.21), channel_id=1, source_target_pairs={{1,4},{4,1},{5,8},{8,5},{9,12},{12,9},{3,6},{6,3},{7,10},{10,7},{1... | collective-permute-start | bytes 1179656 | tf_op jit(solution)/shard_map/ppermute | solution.py:399
  30.9 2.0 %collective-permute-start.11 = (f32[12,4,8,128]{3,2,1,0:T(8,128)S(1)}, f32[12,4,8,128]{3,2,1,0:T(8,128)S(1)}, u32[]{:S(2)}, u32[]{:S(2)}) collective-permute-start(f32[12,4,8,128]{3,2,1,0:T(8,128)S(1)} %collective-permute-done.8.refs_2_), channel_id=1, source_target_pairs={{0,1},{1,0},{2,3},{3,2},{4,5},{5,4},{6,7},{7,6},{8,9},{9,8},{10,11... | collective-permute-start | bytes 589832 | tf_op jit(solution)/shard_map/ppermute | solution.py:392
  31.8 2.5 %collective-permute-start.9 = (f32[12,4,8,128]{3,2,1,0:T(8,128)S(1)}, f32[12,4,8,128]{3,2,1,0:T(8,128)S(1)}, u32[]{:S(2)}, u32[]{:S(2)}) collective-permute-start(f32[12,4,8,128]{3,2,1,0:T(8,128)S(1)} %collective-permute-done.8.refs_2_), channel_id=1, source_target_pairs={{1,4},{4,1},{5,8},{8,5},{9,12},{12,9},{3,6},{6,3},{7,10},{10,7},{1... | collective-permute-start | bytes 589832 | tf_op jit(solution)/shard_map/ppermute | solution.py:399
  37.5 17.4 %all-to-all-start = ((f32[16,8,128]{2,1,0:T(8,128)}), f32[16,8,128]{2,1,0:T(8,128)S(1)}, u32[]{:S(2)}, u32[]{:S(2)}) async-start(f32[16,8,128]{2,1,0:T(8,128)} %get-tuple-element.31), calls=%async_computation | async-start | bytes 131072 | tf_op jit(solution)/shard_map/all_to_all | solution.py:547

commit v9 on v8

--- a/solution.py
+++ b/solution.py
@@ -185,8 +185,8 @@
         (scale_ref, _, st, acc, strips, sem_full, sem_strip) = take(7)
         eps = eps_in = None
     else:
-        (eps_sib, st, scale_ref, acc, strips, eps, sem_full, sem_strip, sem_eps) = take(9)
-        eps_in = [full[0].at[12], eps_sib]
+        (st, scale_ref, acc, strips, eps, sem_full, sem_strip, sem_eps) = take(8)
+        eps_in = [full[0].at[12], full[1].at[12]]
     gy, core = lax.axis_index("gy"), lax.axis_index("col")
     planes = 12 if second else 13
 
@@ -434,11 +434,11 @@
     cost = pl.CostEstimate(flops=20_000_000, bytes_accessed=4_000_000, transcendentals=0)
     wide = (12, 3 * depth, rows, nx)
     sems = pltpu.SemaphoreType.DMA
-    sibling = swap_core(fields.reshape(runs * comps, depth, rows_own, nx))
+    sibling = swap_core(own)
     window, scale, acc = pl.pallas_call(
         functools.partial(early_kernel, (depth, rows_own, sides, False)),
         out_shape=(shape(*wide), shape(3 * depth, rows, nx), shape(2, 6, depth, rows_own, nx)),
-        in_specs=[anywhere] * (3 + 2 * sides),
+        in_specs=[anywhere] * (2 + 2 * sides),
         out_specs=(vmem, vmem, vmem),
         scratch_shapes=[
             pltpu.VMEM((sides, 13, 3 * depth, 8, 128), jnp.float32),
@@ -449,7 +449,7 @@
         ],
         compiler_params=limit,
         cost_estimate=cost,
-    )(own, sibling, *here(sent), swap_core(eps_inv))
+    )(own, sibling, *here(sent))
     window, scale, half_0, half_1, state, acc, *strips = pl.pallas_call(
         functools.partial(window_kernel, (depth, rows_own, sides, False)),
         out_shape=(

time: 55.9 us -> 55.5 us (level)
  waiting for transfers between devices: 17.4 us -> 14.6 us
  starting transfers between devices: 26.6 us -> 29 us
    ppermute x2, waiting for transfers between devices: 8.98 us -> 6.87 us  [along_y(): return lax.ppermute(x, 'gy', list(ways[s].items()))]
    ppermute x2, starting transfers between devices: 3.05 us -> 4.59 us  [along_y(): return lax.ppermute(x, 'gy', list(ways[s].items()))]
    ppermute x5 -> x4, starting transfers between devices: 9.66 us -> 10.6 us  [swap_core(): return lax.ppermute(x, 'col', [(0, 1), (1, 0)])]
    ppermute x5 -> x4, waiting for transfers between devices: 1.5 us -> 0.8 us  [swap_core(): return lax.ppermute(x, 'col', [(0, 1), (1, 0)])]
  transfers between devices with their start and end apart: 13 -> 12, of which waited for: 5 -> 5; matrix products, arithmetic and copies ran while one was open for 0% -> 0% of each run, Pallas kernels for 7% -> 7%
where the time goes in v9:
time: 55.5 us; the launch traced here: 55.2 us
  starting transfers between devices  29 us (52%)
  waiting for transfers between devices  14.6 us (26%)
  Pallas kernels  8.54 us (15%)
  other arithmetic  1.34 us (2%)
  between operations  0.92 us (2%)
  local copies, waits for them, and re-layouts  0.85 us (2%)
    ppermute x4, starting transfers between devices, swap_core(): return lax.ppermute(x, 'col', [(0, 1), (1, 0)])  10.6 us
    all_to_all x1, starting transfers between devices, body(): got = lax.all_to_all(share, ('gz', 'gy', 'col'), 0, 0)  10.5 us
    all_to_all x1, waiting for transfers between devices, body(): got = lax.all_to_all(share, ('gz', 'gy', 'col'), 0, 0)  6.89 us
    ppermute x2, waiting for transfers between devices, along_y(): return lax.ppermute(x, 'gy', list(ways[s].items()))  6.87 us
    pallas_call x2, Pallas kernels, body(): pl.pallas_call(functools.partial(window_kernel, (depth, rows_own, sides,...  4.74 us
    ppermute x2, starting transfers between devices, along_y(): return lax.ppermute(x, 'gy', list(ways[s].items()))  4.59 us
    ppermute x5, starting transfers between devices, cross(): return lax.ppermute(x, Z, pairs)  3.39 us
    pallas_call x1, Pallas kernels, body(): pl.pallas_call(functools.partial(early_kernel, (depth, rows_own, sides, F...  1.65 us
  transfers between devices with their start and end apart: 12, of which 5 were waited for; matrix products, arithmetic and copies ran while one was open for 0% of the time, Pallas kernels for 7%

profile of v9, /device:TPU:0, one launch (start us, length us, event | category | flops | bytes accessed | tf_op | source)
XLA Modules:
  0.0 55.2 jit_solution(8743354066683297172)
XLA Ops:
  0.6 1.3 %pad_maximum_fusion.refs_0_ = f32[13,4,16,256]{3,2,1,0:T(8,128)S(1)} fusion(f32[1,4,16,256]{3,2,1,0:T(8,128)} %bitcast.6, f32[12,4,16,256]{3,2,1,0:T(8,128)} %bitcast.5), kind=kLoop, calls=%fused_computation | loop fusion | flops 212992 | bytes 1703936 | tf_op jit(solution)/shard_map/concatenate | solution.py:388
  1.9 0.5 collective-permute-start.3
  2.4 0.7 %collective-permute-start = (f32[13,4,16,256]{3,2,1,0:T(8,128)S(1)}, f32[13,4,16,256]{3,2,1,0:T(8,128)S(1)}, u32[]{:S(2)}, u32[]{:S(2)}) collective-permute-start(f32[13,4,16,256]{3,2,1,0:T(8,128)S(1)} %pad_maximum_fusion.refs_0_), channel_id=1, source_target_pairs={{1,4},{4,1},{5,8},{8,5},{9,12},{12,9},{3,6},{6,3},{7,10},{10,7},{1... | collective-permute-start | bytes 2555912 | tf_op jit(solution)/shard_map/ppermute | solution.py:399
  3.1 0.1 constant_dynamic-slice_fusion
  3.3 0.1 pad_maximum_fusion.1
  3.3 0.0 copy-start.5
  3.3 0.0 copy-start.6
  3.3 0.0 copy-start.7
  3.4 2.6 %collective-permute-start.1 = (f32[13,4,8,128]{3,2,1,0:T(8,128)S(1)}, f32[13,4,8,128]{3,2,1,0:T(8,128)S(1)}, u32[]{:S(2)}, u32[]{:S(2)}) collective-permute-start(f32[13,4,8,128]{3,2,1,0:T(8,128)S(1)} %pad_maximum_fusion.1), channel_id=1, source_target_pairs={{0,2},{2,0},{1,3},{3,1},{4,6},{6,4},{5,7},{7,5},{8,10},{10,8},{9,1... | collective-permute-start | bytes 638984 | tf_op jit(solution)/shard_map/ppermute | solution.py:408
  5.9 3.8 %collective-permute-done.1.refs_2_ = f32[13,4,8,128]{3,2,1,0:T(8,128)S(1)} collective-permute-done((f32[13,4,8,128]{3,2,1,0:T(8,128)S(1)}, f32[13,4,8,128]{3,2,1,0:T(8,128)S(1)}, u32[]{:S(2)}, u32[]{:S(2)}) %collective-permute-start.1) | collective-permute-done | bytes 213024 | tf_op jit(solution)/shard_map/ppermute | solution.py:408
  9.8 2.3 %collective-permute-start.4 = (f32[13,4,8,128]{3,2,1,0:T(8,128)S(1)}, f32[13,4,8,128]{3,2,1,0:T(8,128)S(1)}, u32[]{:S(2)}, u32[]{:S(2)}) collective-permute-start(f32[13,4,8,128]{3,2,1,0:T(8,128)S(1)} %collective-permute-done.1.refs_2_), channel_id=1, source_target_pairs={{0,1},{1,0},{2,3},{3,2},{4,5},{5,4},{6,7},{7,6},{8,9},{9,8},{10,11... | collective-permute-start | bytes 638984 | tf_op jit(solution)/shard_map/ppermute | solution.py:392
  12.0 0.7 %collective-permute-start.2 = (f32[13,4,8,128]{3,2,1,0:T(8,128)S(1)}, f32[13,4,8,128]{3,2,1,0:T(8,128)S(1)}, u32[]{:S(2)}, u32[]{:S(2)}) collective-permute-start(f32[13,4,8,128]{3,2,1,0:T(8,128)S(1)} %collective-permute-done.1.refs_2_), channel_id=1, source_target_pairs={{1,4},{4,1},{5,8},{8,5},{9,12},{12,9},{3,6},{6,3},{7,10},{10,7},{1... | collective-permute-start | bytes 638984 | tf_op jit(solution)/shard_map/ppermute | solution.py:399
  12.7 0.4 collective-permute-done.4.refs_3_
  13.1 0.0 collective-permute-done.3.refs_1_
  13.1 1.6 %shard_map.113 = (f32[12,12,24,256]{3,2,1,0:T(8,128)S(1)}, f32[12,24,256]{2,1,0:T(8,128)S(1)}, f32[2,6,4,16,256]{4,3,2,1,0:T(8,128)S(1)}) custom-call(f32[13,4,16,256]{3,2,1,0:T(8,128)S(1)} %pad_maximum_fusion.refs_0_, f32[13,4,16,256]{3,2,1,0:T(8,128)S(1)} %collective-permute-done.3.refs_1_, f32[13,4,8,128]{3,2,1,0:T(8,128)S(1)} %collective-permute-done.1.refs_2_, ...), custom_call_target="tpu_custom_call" | custom-call | flops 20000000 | bytes 4000000 | tf_op jit(solution)/shard_map/pallas_call | solution.py:438
  14.8 0.0 collective-permute-done.2.refs_1_
  14.8 0.0 collective-permute-done.refs_0_
  14.8 0.0 copy-start
  14.8 0.0 copy-start.1
  14.8 0.0 copy-start.2
  14.8 0.0 copy-start.3
  14.8 0.0 copy-start.4
  14.9 1.6 %shard_map.114 = (f32[12,12,24,256]{3,2,1,0:T(8,128)S(1)}, f32[12,24,256]{2,1,0:T(8,128)S(1)}, f32[6,4,16,256]{3,2,1,0:T(8,128)S(1)}, f32[6,4,16,256]{3,2,1,0:T(...) custom-call(f32[13,4,16,256]{3,2,1,0:T(8,128)S(1)} %collective-permu, ...), custom_call_target="tpu_custom_call", output_to_operand_aliasing={{0}: (2, {}), {1}: (3, {}), {5}: (4, {})} | custom-call | flops 20000000 | bytes 4000000 | tf_op jit(solution)/shard_map/pallas_call | solution.py:453
  16.5 6.3 %collective-permute-start.9 = (f32[12,4,16,256]{3,2,1,0:T(8,128)S(1)}, f32[12,4,16,256]{3,2,1,0:T(8,128)S(1)}, u32[]{:S(2)}, u32[]{:S(2)}) collective-permute-start(f32[12,4,16,256]{3,2,1,0:T(8,128)S(1)} %get-tuple-element.23.refs_0_), channel_id=1, source_target_pairs={{0,1},{1,0},{2,3},{3,2},{4,5},{5,4},{6,7},{7,6},{8,9},{9,8},{10,11... | collective-permute-start | bytes 2359304 | tf_op jit(solution)/shard_map/ppermute | solution.py:392
  22.8 2.0 %collective-permute-start.7 = (f32[12,4,8,128]{3,2,1,0:T(8,128)S(1)}, f32[12,4,8,128]{3,2,1,0:T(8,128)S(1)}, u32[]{:S(2)}, u32[]{:S(2)}) collective-permute-start(f32[12,4,8,128]{3,2,1,0:T(8,128)S(1)} %get-tuple-element.22), channel_id=1, source_target_pairs={{0,2},{2,0},{1,3},{3,1},{4,6},{6,4},{5,7},{7,5},{8,10},{10,8},{9,1... | collective-permute-start | bytes 589832 | tf_op jit(solution)/shard_map/ppermute | solution.py:408
  24.9 0.7 %collective-permute-start.5 = (f32[6,4,16,256]{3,2,1,0:T(8,128)S(1)}, f32[6,4,16,256]{3,2,1,0:T(8,128)S(1)}, u32[]{:S(2)}, u32[]{:S(2)}) collective-permute-start(f32[6,4,16,256]{3,2,1,0:T(8,128)S(1)} %get-tuple-element.20), channel_id=1, source_target_pairs={{1,4},{4,1},{5,8},{8,5},{9,12},{12,9},{3,6},{6,3},{7,10},{10,7},{1... | collective-permute-start | bytes 1179656 | tf_op jit(solution)/shard_map/ppermute | solution.py:399
  25.5 0.7 %collective-permute-start.6 = (f32[6,4,16,256]{3,2,1,0:T(8,128)S(1)}, f32[6,4,16,256]{3,2,1,0:T(8,128)S(1)}, u32[]{:S(2)}, u32[]{:S(2)}) collective-permute-start(f32[6,4,16,256]{3,2,1,0:T(8,128)S(1)} %get-tuple-element.21), channel_id=1, source_target_pairs={{1,4},{4,1},{5,8},{8,5},{9,12},{12,9},{3,6},{6,3},{7,10},{10,7},{1... | collective-permute-start | bytes 1179656 | tf_op jit(solution)/shard_map/ppermute | solution.py:399
  26.2 0.0 copy-done.5
  26.2 0.0 copy-done.6
  26.3 0.7 %shard_map.116 = (f32[16,8,256]{2,1,0:T(8,128)S(1)}, f32[256,128]{1,0:T(8,128)S(1)}) custom-call(s32[1,8]{1,0:T(1,128)S(1)} %copy-done.5, s32[1,128]{1,0:T(1,128)S(1)} %bitcast.4), custom_call_target="tpu_custom_call" | custom-call | tf_op jit(solution)/shard_map/pallas_call | solution.py:480
  27.0 3.0 %collective-permute-done.7.refs_2_ = f32[12,4,8,128]{3,2,1,0:T(8,128)S(1)} collective-permute-done((f32[12,4,8,128]{3,2,1,0:T(8,128)S(1)}, f32[12,4,8,128]{3,2,1,0:T(8,128)S(1)}, u32[]{:S(2)}, u32[]{:S(2)}) %collective-permute-start.7) | collective-permute-done | bytes 196640 | tf_op jit(solution)/shard_map/ppermute | solution.py:408
  30.0 1.4 %collective-permute-start.10 = (f32[12,4,8,128]{3,2,1,0:T(8,128)S(1)}, f32[12,4,8,128]{3,2,1,0:T(8,128)S(1)}, u32[]{:S(2)}, u32[]{:S(2)}) collective-permute-start(f32[12,4,8,128]{3,2,1,0:T(8,128)S(1)} %collective-permute-done.7.refs_2_), channel_id=1, source_target_pairs={{0,1},{1,0},{2,3},{3,2},{4,5},{5,4},{6,7},{7,6},{8,9},{9,8},{10,11... | collective-permute-start | bytes 589832 | tf_op jit(solution)/shard_map/ppermute | solution.py:392
  31.4 0.7 %collective-permute-start.8 = (f32[12,4,8,128]{3,2,1,0:T(8,128)S(1)}, f32[12,4,8,128]{3,2,1,0:T(8,128)S(1)}, u32[]{:S(2)}, u32[]{:S(2)}) collective-permute-start(f32[12,4,8,128]{3,2,1,0:T(8,128)S(1)} %collective-permute-done.7.refs_2_), channel_id=1, source_target_pairs={{1,4},{4,1},{5,8},{8,5},{9,12},{12,9},{3,6},{6,3},{7,10},{10,7},{1... | collective-permute-start | bytes 589832 | tf_op jit(solution)/shard_map/ppermute | solution.py:399
  32.1 0.0 copy-done.7
  32.1 0.4 collective-permute-done.10.refs_3_
  32.5 0.0 collective-permute-done.9.refs_1_
  32.5 1.4 %shard_map.115 = (f32[12,12,24,256]{3,2,1,0:T(8,128)S(1)}, f32[2,6,4,16,256]{4,3,2,1,0:T(8,128)S(1)}) custom-call(f32[12,4,16,256]{3,2,1,0:T(8,128)S(1)} %get-tuple-element.23.refs_0_, f32[12,4,16,256]{3,2,1,0:T(8,128)S(1)} %collective-permute-done.9.refs_1_, f32[12,4,8,128]{3,2,1,0:T(8,128)S(1)} %collective-permute-done.7.refs_2_, ...), custom_call_target="tpu_custom_call", output_to_operand_aliasing={{1}: (5, {})} | custom-call | flops 20000000 | bytes 4000000 | tf_op jit(solution)/shard_map/pallas_call | solution.py:507
  34.0 0.0 collective-permute-done.8.refs_2_
  34.0 0.0 collective-permute-done.5.refs_0_
  34.0 0.0 collective-permute-done.6.refs_1_
  34.0 0.0 copy-done
  34.0 0.0 copy-done.1
  34.0 0.0 copy-done.2
  34.0 0.0 copy-done.3
  34.0 0.0 copy-done.4
  34.1 3.1 %shard_map.117 = (f32[12,12,24,256]{3,2,1,0:T(8,128)S(1)}, f32[2,6,4,16,256]{4,3,2,1,0:T(8,128)S(1)}, f32[12,4,16,256]{3,2,1,0:T(8,128)}, f32[16,8,128]{2,1,0:T(8,128)}) custom-call(f32[6,4,16,256]{3,2,1,0:T(8,128)S(1)} %collective-permute-done.5.refs_0_, ...), custom_call_target="tpu_custom_call", output_to_operand_aliasing={{0}: (3, {}), {1}: (5, {})} | custom-call | flops 20000000 | bytes 4000000 | tf_op jit(solution)/shard_map/pallas_call | solution.py:525
  37.2 10.5 %all-to-all-start = ((f32[16,8,128]{2,1,0:T(8,128)}), f32[16,8,128]{2,1,0:T(8,128)S(1)}, u32[]{:S(2)}, u32[]{:S(2)}) async-start(f32[16,8,128]{2,1,0:T(8,128)} %get-tuple-element.31), calls=%async_computation | async-start | bytes 131072 | tf_op jit(solution)/shard_map/all_to_all | solution.py:547
  47.7 6.9 %all-to-all-done = f32[16,8,128]{2,1,0:T(8,128)S(1)} async-done(((f32[16,8,128]{2,1,0:T(8,128)}), f32[16,8,128]{2,1,0:T(8,128)S(1)}, u32[]{:S(2)}, u32[]{:S(2)}) %all-to-all-start) | async-done | bytes 65568 | tf_op jit(solution)/shard_map/all_to_all | solution.py:547
  54.6 0.7 %constant_dynamic-slice_fusion.1 = f32[8,16]{1,0:T(8,128)} fusion(f32[8,128]{1,0:T(8,128)S(1)} %reduce_sum.9, s32[]{:T(128)S(6)} %select_n.7), kind=kLoop, calls=%fused_computation.4 | loop fusion | bytes 1028 | tf_op jit(solution)/shard_map/dynamic_slice | solution.py:549
  (2 shorter events, 0.0 us)
Async XLA Ops:
  1.9 11.2 %collective-permute-start.3 = (f32[13,4,16,256]{3,2,1,0:T(8,128)S(1)}, f32[13,4,16,256]{3,2,1,0:T(8,128)S(1)}, u32[]{:S(2)}, u32[]{:S(2)}) collective-permute-start(f32[13,4,16,256]{3,2,1,0:T(8,128)S(1)} %pad_maximum_fusion.refs_0_), channel_id=1, source_target_pairs={{0,1},{1,0},{2,3},{3,2},{4,5},{5,4},{6,7},{7,6},{8,9},{9,8},{10,11... | collective-permute-start | bytes 2555912 | tf_op jit(solution)/shard_map/ppermute | solution.py:392
  2.4 12.4 %collective-permute-start = (f32[13,4,16,256]{3,2,1,0:T(8,128)S(1)}, f32[13,4,16,256]{3,2,1,0:T(8,128)S(1)}, u32[]{:S(2)}, u32[]{:S(2)}) collective-permute-start(f32[13,4,16,256]{3,2,1,0:T(8,128)S(1)} %pad_maximum_fusion.refs_0_), channel_id=1, source_target_pairs={{1,4},{4,1},{5,8},{8,5},{9,12},{12,9},{3,6},{6,3},{7,10},{10,7},{1... | collective-permute-start | bytes 2555912 | tf_op jit(solution)/shard_map/ppermute | solution.py:399
  3.3 22.9 %copy-start.5 = (s32[1,8]{1,0:T(1,128)S(1)}, s32[1,8]{1,0:T(1,128)}, u32[]{:S(2)}) copy-start(s32[1,8]{1,0:T(1,128)} %row_counts.1) | copy-start | bytes 100
  3.3 22.9 %copy-start.6 = (s32[128]{0:T(128)S(1)}, s32[128]{0:T(128)}, u32[]{:S(2)}) copy-start(s32[128]{0:T(128)} %param.13) | copy-start | bytes 1540
  3.3 28.8 %copy-start.7 = (f32[8,128]{1,0:T(8,128)S(1)}, f32[8,128]{1,0:T(8,128)}, u32[]{:S(2)}) copy-start(f32[8,128]{1,0:T(8,128)} %param.14) | copy-start | bytes 12292
  3.4 6.4 %collective-permute-start.1 = (f32[13,4,8,128]{3,2,1,0:T(8,128)S(1)}, f32[13,4,8,128]{3,2,1,0:T(8,128)S(1)}, u32[]{:S(2)}, u32[]{:S(2)}) collective-permute-start(f32[13,4,8,128]{3,2,1,0:T(8,128)S(1)} %pad_maximum_fusion.1), channel_id=1, source_target_pairs={{0,2},{2,0},{1,3},{3,1},{4,6},{6,4},{5,7},{7,5},{8,10},{10,8},{9,1... | collective-permute-start | bytes 638984 | tf_op jit(solution)/shard_map/ppermute | solution.py:408
  9.8 3.4 %collective-permute-start.4 = (f32[13,4,8,128]{3,2,1,0:T(8,128)S(1)}, f32[13,4,8,128]{3,2,1,0:T(8,128)S(1)}, u32[]{:S(2)}, u32[]{:S(2)}) collective-permute-start(f32[13,4,8,128]{3,2,1,0:T(8,128)S(1)} %collective-permute-done.1.refs_2_), channel_id=1, source_target_pairs={{0,1},{1,0},{2,3},{3,2},{4,5},{5,4},{6,7},{7,6},{8,9},{9,8},{10,11... | collective-permute-start | bytes 638984 | tf_op jit(solution)/shard_map/ppermute | solution.py:392
  12.0 2.8 %collective-permute-start.2 = (f32[13,4,8,128]{3,2,1,0:T(8,128)S(1)}, f32[13,4,8,128]{3,2,1,0:T(8,128)S(1)}, u32[]{:S(2)}, u32[]{:S(2)}) collective-permute-start(f32[13,4,8,128]{3,2,1,0:T(8,128)S(1)} %collective-permute-done.1.refs_2_), channel_id=1, source_target_pairs={{1,4},{4,1},{5,8},{8,5},{9,12},{12,9},{3,6},{6,3},{7,10},{10,7},{1... | collective-permute-start | bytes 638984 | tf_op jit(solution)/shard_map/ppermute | solution.py:399
  14.8 19.2 %copy-start = (f32[128,256]{1,0:T(8,128)S(1)}, f32[128,256]{1,0:T(8,128)}, u32[]{:S(2)}) copy-start(f32[128,256]{1,0:T(8,128)} %constant.46.clone.refs_9_) | copy-start | bytes 393220
  14.8 19.2 %copy-start.1 = (f32[128,256]{1,0:T(8,128)S(1)}, f32[128,256]{1,0:T(8,128)}, u32[]{:S(2)}) copy-start(f32[128,256]{1,0:T(8,128)} %constant.47.clone.refs_10_) | copy-start | bytes 393220
  14.8 19.2 %copy-start.2 = (f32[16,16,128]{2,1,0:T(8,128)S(1)}, f32[16,16,128]{2,1,0:T(8,128)}, u32[]{:S(2)}) copy-start(f32[16,16,128]{2,1,0:T(8,128)} %constant.48.clone.refs_11_) | copy-start | bytes 393220
  14.8 19.2 %copy-start.3 = (f32[16,16,128]{2,1,0:T(8,128)S(1)}, f32[16,16,128]{2,1,0:T(8,128)}, u32[]{:S(2)}) copy-start(f32[16,16,128]{2,1,0:T(8,128)} %constant.49.clone.refs_12_) | copy-start | bytes 393220
  14.8 19.2 %copy-start.4 = (f32[16,128]{1,0:T(8,128)S(1)}, f32[16,128]{1,0:T(8,128)}, u32[]{:S(2)}) copy-start(f32[16,128]{1,0:T(8,128)} %constant.50.clone.refs_13_) | copy-start | bytes 24580
  16.5 16.0 %collective-permute-start.9 = (f32[12,4,16,256]{3,2,1,0:T(8,128)S(1)}, f32[12,4,16,256]{3,2,1,0:T(8,128)S(1)}, u32[]{:S(2)}, u32[]{:S(2)}) collective-permute-start(f32[12,4,16,256]{3,2,1,0:T(8,128)S(1)} %get-tuple-element.23.refs_0_), channel_id=1, source_target_pairs={{0,1},{1,0},{2,3},{3,2},{4,5},{5,4},{6,7},{7,6},{8,9},{9,8},{10,11... | collective-permute-start | bytes 2359304 | tf_op jit(solution)/shard_map/ppermute | solution.py:392
  22.8 7.2 %collective-permute-start.7 = (f32[12,4,8,128]{3,2,1,0:T(8,128)S(1)}, f32[12,4,8,128]{3,2,1,0:T(8,128)S(1)}, u32[]{:S(2)}, u32[]{:S(2)}) collective-permute-start(f32[12,4,8,128]{3,2,1,0:T(8,128)S(1)} %get-tuple-element.22), channel_id=1, source_target_pairs={{0,2},{2,0},{1,3},{3,1},{4,6},{6,4},{5,7},{7,5},{8,10},{10,8},{9,1... | collective-permute-start | bytes 589832 | tf_op jit(solution)/shard_map/ppermute | solution.py:408
  24.9 9.1 %collective-permute-start.5 = (f32[6,4,16,256]{3,2,1,0:T(8,128)S(1)}, f32[6,4,16,256]{3,2,1,0:T(8,128)S(1)}, u32[]{:S(2)}, u32[]{:S(2)}) collective-permute-start(f32[6,4,16,256]{3,2,1,0:T(8,128)S(1)} %get-tuple-element.20), channel_id=1, source_target_pairs={{1,4},{4,1},{5,8},{8,5},{9,12},{12,9},{3,6},{6,3},{7,10},{10,7},{1... | collective-permute-start | bytes 1179656 | tf_op jit(solution)/shard_map/ppermute | solution.py:399
  25.5 8.5 %collective-permute-start.6 = (f32[6,4,16,256]{3,2,1,0:T(8,128)S(1)}, f32[6,4,16,256]{3,2,1,0:T(8,128)S(1)}, u32[]{:S(2)}, u32[]{:S(2)}) collective-permute-start(f32[6,4,16,256]{3,2,1,0:T(8,128)S(1)} %get-tuple-element.21), channel_id=1, source_target_pairs={{1,4},{4,1},{5,8},{8,5},{9,12},{12,9},{3,6},{6,3},{7,10},{10,7},{1... | collective-permute-start | bytes 1179656 | tf_op jit(solution)/shard_map/ppermute | solution.py:399
  30.0 2.5 %collective-permute-start.10 = (f32[12,4,8,128]{3,2,1,0:T(8,128)S(1)}, f32[12,4,8,128]{3,2,1,0:T(8,128)S(1)}, u32[]{:S(2)}, u32[]{:S(2)}) collective-permute-start(f32[12,4,8,128]{3,2,1,0:T(8,128)S(1)} %collective-permute-done.7.refs_2_), channel_id=1, source_target_pairs={{0,1},{1,0},{2,3},{3,2},{4,5},{5,4},{6,7},{7,6},{8,9},{9,8},{10,11... | collective-permute-start | bytes 589832 | tf_op jit(solution)/shard_map/ppermute | solution.py:392
  31.4 2.5 %collective-permute-start.8 = (f32[12,4,8,128]{3,2,1,0:T(8,128)S(1)}, f32[12,4,8,128]{3,2,1,0:T(8,128)S(1)}, u32[]{:S(2)}, u32[]{:S(2)}) collective-permute-start(f32[12,4,8,128]{3,2,1,0:T(8,128)S(1)} %collective-permute-done.7.refs_2_), channel_id=1, source_target_pairs={{1,4},{4,1},{5,8},{8,5},{9,12},{12,9},{3,6},{6,3},{7,10},{10,7},{1... | collective-permute-start | bytes 589832 | tf_op jit(solution)/shard_map/ppermute | solution.py:399
  37.2 17.4 %all-to-all-start = ((f32[16,8,128]{2,1,0:T(8,128)}), f32[16,8,128]{2,1,0:T(8,128)S(1)}, u32[]{:S(2)}, u32[]{:S(2)}) async-start(f32[16,8,128]{2,1,0:T(8,128)} %get-tuple-element.31), calls=%async_computation | async-start | bytes 131072 | tf_op jit(solution)/shard_map/all_to_all | solution.py:547
